TPU v7x, 32 devices: a whole 2x2x4 slice. The times are simulated.
32 devices in a mesh: seq: 4 (over y, core), blk: 8 (over z, x).
Axes of the slice: x: 2, y: 2, z: 4, core: 2. Of those that a mesh axis runs over, the one named last changes fastest.
Arguments:
- tokens: bfloat16 [4, 2048, 1024], P('seq', 'blk'), may hold values from -20 to 20
- lengths: int32 [4, 1], P('seq'), may hold values from 768 to 1536, as said below
- attend_weight: bfloat16 [1024, 3072], replicated, may hold values from -0.1875 to 0.1875
- merge_weight: bfloat16 [1024, 1024], replicated, may hold values from -4 to 4
- expand_weight: bfloat16 [1024, 4096], replicated, may hold values from -0.1875 to 0.1875
- contract_weight: bfloat16 [4096, 1024], replicated, may hold values from -0.09375 to 0.09375
- gain_first: float32 [1024], replicated, may hold values from 0.1 to 1.9
- shift_first: float32 [1024], replicated, may hold values from -3 to 3
- gain_second: float32 [1024], replicated, may hold values from 0.1 to 1.9
- shift_second: float32 [1024], replicated, may hold values from -3 to 3
- bias_table: float32 [32, 16], replicated, may hold values from -4 to 4
- cotangent: bfloat16 [4, 2048, 1024], P('seq', 'blk'), may hold values from -6 to 6
Outputs:
- output: bfloat16 [4, 2048, 1024], P('seq', 'blk')
- tokens_grad: float32 [4, 2048, 1024], P('seq', 'blk')
- attend_grad: float32 [1024, 3072], P('blk')
- merge_grad: float32 [1024, 1024], P('blk')
- expand_grad: float32 [1024, 4096], P('blk')
- contract_grad: float32 [4096, 1024], P('blk')
- gain_first_grad: float32 [1024], P('blk')
- shift_first_grad: float32 [1024], P('blk')
- gain_second_grad: float32 [1024], P('blk')
- shift_second_grad: float32 [1024], P('blk')
- table_grad: float32 [32, 16], replicated
Inputs may be any that keep to these rules, and one draw needn't show every extreme that they name: Row s holds the lengths of the 1 items packed in order from the start of sequence s, one of them exactly 1536; the tokens after the last item are padding.
All inputs are finite; a program needn't handle non-finite values.
Results may differ from a plain program's by a relative error of at most 0.013.
Values may be sent and summed in bfloat16 or wider, within the bound.
No kernel may reach another device: no remote copies, remote signals or barrier semaphores. Data moves between devices by JAX's collectives and lax.ppermute only.
A program may use at most 256 MiB of HBM per device.

v0:
```python
from functools import partial
import math

import jax
import jax.numpy as jnp
from jax import lax
from jax.sharding import PartitionSpec as P

HOPS = 6


epsilon = 1e-05
masked_score = -1e30
highest = lax.Precision.HIGHEST
bucket_edges = [math.ceil(16 * 8 ** (t / 16)) for t in range(1, 16)]


def shifted(array, axis, by):
    peers = lax.axis_size(axis)
    pairs = [(i, i + by) for i in range(peers) if 0 <= i + by < peers]
    return lax.ppermute(array, axis, pairs)


def shortened(array):

    def short(part):
        return part.astype(jnp.bfloat16) if part.dtype == jnp.float32 else part

    return jax.tree.map(short, array)


def bucket_of(distance):
    total = jnp.minimum(jnp.maximum(distance, 0), 16)
    for edge in bucket_edges:
        total = total + (distance >= edge).astype(jnp.int32)
    return total


def segment_of(position, ends):
    return jnp.sum((position[:, None] >= ends[None, :]).astype(jnp.int32), axis=1)


def layer_norm(value, gain, shift):
    mean = jnp.mean(value, axis=-1, keepdims=True)
    centred = value - mean
    variance = jnp.mean(centred * centred, axis=-1, keepdims=True)
    return centred * lax.rsqrt(variance + epsilon) * gain + shift


def diagonal_sums(grid, count):
    heads = grid.shape[0]
    padded = jnp.pad(jnp.flip(grid, axis=-1), ((0, 0), (0, 0), (0, count)))
    flat = padded.reshape(heads, 2 * count * count)[:, : count * (2 * count - 1)]
    return jnp.sum(flat.reshape(heads, count, 2 * count - 1), axis=1)


def band_matrix(line, count):
    heads = line.shape[0]
    flipped = jnp.flip(line, axis=-1)
    tiled = jnp.tile(flipped, (1, count))
    window = tiled[:, count - 1 : count - 1 + count * (2 * count - 2)]
    return window.reshape(heads, count, 2 * count - 2)[:, :, :count]


def fetch_earlier(block):
    earlier = []
    moving = block
    for hop in range(HOPS):
        moving = shifted(moving, "blk", 1)
        earlier.append(moving)
    return earlier


def return_parts(parts):
    carried = jnp.zeros_like(parts[0])
    for hop in range(HOPS, 0, -1):
        carried = shifted(shortened(carried + parts[hop - 1]), "blk", -1)
    return carried


def local(
    tokens,
    lengths,
    attend_weight,
    merge_weight,
    expand_weight,
    contract_weight,
    gain_first,
    shift_first,
    gain_second,
    shift_second,
    bias_table,
    cotangent,
):
    rows = tokens.shape[1]
    width = tokens.shape[2]
    heads = bias_table.shape[1]
    buckets = bias_table.shape[0]
    head_size = width // heads
    items = lengths.shape[1]
    start = lax.axis_index("blk") * rows
    query_pos = start + jnp.arange(rows, dtype=jnp.int32)
    ends = jnp.cumsum(lengths[0])
    query_seg = segment_of(query_pos, ends)
    band = jnp.arange(2 * rows - 1, dtype=jnp.int32) - (rows - 1)
    bucket_ids = jnp.arange(buckets, dtype=jnp.int32)

    def pair_setup(hop):
        key_pos = query_pos - hop * rows
        key_seg = segment_of(key_pos, ends)
        key_valid = (key_pos >= 0) & (key_seg < items)
        same = key_pos[None, :] == query_pos[:, None]
        allowed = (
            (query_seg[:, None] == key_seg[None, :])
            & (key_pos[None, :] <= query_pos[:, None])
            & (key_valid[None, :] | same)
        )
        onehot = (bucket_of(hop * rows + band)[:, None] == bucket_ids[None, :]).astype(jnp.float32)
        band_bias = jnp.dot(onehot, bias_table, precision=highest).T
        bias = band_matrix(band_bias, rows)
        additive = jnp.where(allowed[None], bias, masked_score)
        return (jnp.any(allowed), onehot, additive)

    pairs = [pair_setup(hop) for hop in range(HOPS + 1)]
    residual = tokens[0].astype(jnp.float32)
    normed_first, norm_first_pull = jax.vjp(layer_norm, residual, gain_first, shift_first)
    act_first = normed_first.astype(jnp.bfloat16)
    projected = jnp.dot(act_first, attend_weight, preferred_element_type=jnp.float32).astype(
        jnp.bfloat16
    )
    query = projected[:, :width].reshape(rows, heads, head_size)
    keys_values = jnp.stack([projected[:, width : 2 * width], projected[:, 2 * width :]])
    blocks = [keys_values] + fetch_earlier(keys_values)

    def scores_of(block, pair):
        key = block[0].reshape(rows, heads, head_size)
        raw = jnp.einsum("qhe,khe->hqk", query, key, preferred_element_type=jnp.float32) * 0.125
        return raw + pair[2]

    def empty_total():
        return jnp.full((heads, rows), masked_score, jnp.float32)

    def empty_scores():
        return jnp.full((heads, rows, rows), masked_score, jnp.float32)

    log_total = empty_total()
    kept_scores = []
    for block, pair in zip(blocks, pairs):

        def part_total(block=block, pair=pair):
            scores = scores_of(block, pair)
            peak = jnp.max(scores, axis=-1)
            return (peak + jnp.log(jnp.sum(jnp.exp(scores - peak[..., None]), axis=-1)), scores)

        def skip_total():
            return (empty_total(), empty_scores())

        part_log, scores = lax.cond(pair[0], part_total, skip_total)
        log_total = jnp.logaddexp(log_total, part_log)
        kept_scores.append(scores)

    def empty_heads():
        return jnp.zeros((rows, heads, head_size), jnp.float32)

    attended = empty_heads()
    for block, pair, scores in zip(blocks, pairs, kept_scores):

        def part_mix(block=block, scores=scores):
            weights = jnp.exp(scores - log_total[..., None]).astype(jnp.bfloat16)
            value = block[1].reshape(rows, heads, head_size)
            return jnp.einsum("hqk,khe->qhe", weights, value, preferred_element_type=jnp.float32)

        attended = attended + lax.cond(pair[0], part_mix, empty_heads)
    attn_low = attended.reshape(rows, width).astype(jnp.bfloat16)
    middle = residual + jnp.dot(attn_low, merge_weight, preferred_element_type=jnp.float32)
    normed_second, norm_second_pull = jax.vjp(layer_norm, middle, gain_second, shift_second)
    act_second = normed_second.astype(jnp.bfloat16)
    hidden_pre = jnp.dot(act_second, expand_weight, preferred_element_type=jnp.float32)
    hidden, gelu_pull = jax.vjp(partial(jax.nn.gelu, approximate=False), hidden_pre)
    hidden_low = hidden.astype(jnp.bfloat16)
    output = (
        middle + jnp.dot(hidden_low, contract_weight, preferred_element_type=jnp.float32)
    ).astype(jnp.bfloat16)
    grad_out = cotangent[0]
    contract_grad = jnp.einsum(
        "tf,td->fd", hidden_low, grad_out, preferred_element_type=jnp.float32
    )
    grad_hidden = jnp.einsum(
        "td,fd->tf", grad_out, contract_weight, preferred_element_type=jnp.float32
    )
    grad_pre = gelu_pull(grad_hidden)[0].astype(jnp.bfloat16)
    expand_grad = jnp.einsum("td,tf->df", act_second, grad_pre, preferred_element_type=jnp.float32)
    grad_second = jnp.einsum(
        "tf,df->td", grad_pre, expand_weight, preferred_element_type=jnp.float32
    )
    grad_middle_norm, gain_second_grad, shift_second_grad = norm_second_pull(grad_second)
    grad_middle = grad_out.astype(jnp.float32) + grad_middle_norm
    grad_middle_low = grad_middle.astype(jnp.bfloat16)
    merge_grad = jnp.einsum(
        "td,te->de", attn_low, grad_middle_low, preferred_element_type=jnp.float32
    )
    grad_heads = (
        jnp.einsum("te,de->td", grad_middle_low, merge_weight, preferred_element_type=jnp.float32)
        .astype(jnp.bfloat16)
        .reshape(rows, heads, head_size)
    )
    row_dot = jnp.sum(grad_heads.astype(jnp.float32) * attended, axis=-1).T
    back_blocks = [keys_values] + fetch_earlier(keys_values)

    def empty_grads():
        return (
            empty_heads(),
            jnp.zeros((2, rows, width), jnp.float32),
            jnp.zeros((buckets, heads), jnp.float32),
        )

    grad_query = empty_heads()
    table_local = jnp.zeros((buckets, heads), jnp.float32)
    parts = []
    for block, pair in zip(back_blocks, pairs):

        def part_grads(block=block, pair=pair):
            key = block[0].reshape(rows, heads, head_size)
            value = block[1].reshape(rows, heads, head_size)
            weights = jnp.exp(scores_of(block, pair) - log_total[..., None])
            weights_low = weights.astype(jnp.bfloat16)
            grad_weights = jnp.einsum(
                "qhe,khe->hqk", grad_heads, value, preferred_element_type=jnp.float32
            )
            grad_scores = (weights * (grad_weights - row_dot[..., None])).astype(jnp.bfloat16)
            query_part = (
                jnp.einsum("hqk,khe->qhe", grad_scores, key, preferred_element_type=jnp.float32)
                * 0.125
            )
            key_part = (
                jnp.einsum("hqk,qhe->khe", grad_scores, query, preferred_element_type=jnp.float32)
                * 0.125
            )
            value_part = jnp.einsum(
                "hqk,qhe->khe", weights_low, grad_heads, preferred_element_type=jnp.float32
            )
            line_grad = diagonal_sums(grad_scores.astype(jnp.float32), rows)
            table_part = jnp.dot(pair[1].T, line_grad.T, precision=highest)
            return (
                query_part,
                jnp.stack([key_part.reshape(rows, width), value_part.reshape(rows, width)]),
                table_part,
            )

        query_part, pair_part, table_part = lax.cond(pair[0], part_grads, empty_grads)
        grad_query = grad_query + query_part
        table_local = table_local + table_part
        parts.append(pair_part)
    owned = (parts[0] + return_parts(parts[1:])).astype(jnp.bfloat16)
    grad_project = jnp.concatenate(
        [grad_query.reshape(rows, width).astype(jnp.bfloat16), owned[0], owned[1]], axis=1
    )
    attend_grad = jnp.einsum(
        "td,te->de", act_first, grad_project, preferred_element_type=jnp.float32
    )
    grad_first = jnp.einsum(
        "te,de->td", grad_project, attend_weight, preferred_element_type=jnp.float32
    )
    grad_input_norm, gain_first_grad, shift_first_grad = norm_first_pull(grad_first)
    tokens_grad = grad_middle + grad_input_norm
    results = (
        lax.psum_scatter(attend_grad, "blk", scatter_dimension=0, tiled=True),
        lax.psum_scatter(merge_grad, "blk", scatter_dimension=0, tiled=True),
        lax.psum_scatter(expand_grad, "blk", scatter_dimension=0, tiled=True),
        lax.psum_scatter(contract_grad, "blk", scatter_dimension=0, tiled=True),
        lax.psum_scatter(gain_first_grad, "blk", scatter_dimension=0, tiled=True),
        lax.psum_scatter(shift_first_grad, "blk", scatter_dimension=0, tiled=True),
        lax.psum_scatter(gain_second_grad, "blk", scatter_dimension=0, tiled=True),
        lax.psum_scatter(shift_second_grad, "blk", scatter_dimension=0, tiled=True),
    )
    results = (
        lax.psum(results[0].astype(jnp.bfloat16), "seq").astype(jnp.float32),
        lax.psum(results[1].astype(jnp.bfloat16), "seq").astype(jnp.float32),
        lax.psum(results[2].astype(jnp.bfloat16), "seq").astype(jnp.float32),
        lax.psum(results[3].astype(jnp.bfloat16), "seq").astype(jnp.float32),
        lax.psum(results[4].astype(jnp.bfloat16), "seq").astype(jnp.float32),
        lax.psum(results[5].astype(jnp.bfloat16), "seq").astype(jnp.float32),
        lax.psum(results[6].astype(jnp.bfloat16), "seq").astype(jnp.float32),
        lax.psum(results[7].astype(jnp.bfloat16), "seq").astype(jnp.float32),
    )
    table_grad = lax.psum(table_local, ("seq", "blk"))
    return (
        output[None],
        tokens_grad[None],
        results[0],
        results[1],
        results[2],
        results[3],
        results[4],
        results[5],
        results[6],
        results[7],
        table_grad,
    )


def solution(mesh):
    in_specs = (
        P("seq", "blk", None),
        P("seq", None),
        P(),
        P(),
        P(),
        P(),
        P(),
        P(),
        P(),
        P(),
        P(),
        P("seq", "blk", None),
    )
    out_specs = (
        P("seq", "blk", None),
        P("seq", "blk", None),
        P("blk", None),
        P("blk", None),
        P("blk", None),
        P("blk", None),
        P("blk"),
        P("blk"),
        P("blk"),
        P("blk"),
        P(),
    )
    return jax.shard_map(local, mesh=mesh, in_specs=in_specs, out_specs=out_specs, check_vma=False)
```

profile of v0, /device:TPU:0, one launch (start us, length us, event | category | flops | bytes accessed | tf_op | source)
XLA Modules:
  0.0 1942.7 jit_solution(4368288595920992620)
XLA Ops:
  25.3 20.6 %collective-permute-done = bf16[2,256,1024]{2,1,0:T(8,128)(2,1)} collective-permute-done((bf16[2,256,1024]{2,1,0:T(8,128)(2,1)}, bf16[2,256,1024]{2,1,0:T(8,128)(2,1)}, u32[]{:S(2)}, u32[]{:S(2)}) %collective-permute-start) | collective-permute-done | bytes 1048608 | tf_op jit(solution)/shard_map/ppermute | solution.py:21
  54.4 17.7 collective-permute-done.1
  99.8 12.1 reshape.1436
  149.5 12.1 reshape.1434
  167.0 9.0 tile.33
  184.9 12.2 reshape.1433
  219.8 12.3 reshape.1437
  255.0 12.1 reshape.1432
  272.4 9.0 tile.29
  290.2 12.1 reshape.1431
  325.1 12.3 reshape.1435
  351.4 14.4 conditional.21
  403.4 10.9 conditional.28
  425.7 15.4 multiply_convert_fusion.7
  441.1 10.8 add_convert_fusion
  466.0 11.6 conditional.41
  487.7 36.2 %collective-permute-done.6 = bf16[2,256,1024]{1,2,0:T(8,128)(2,1)} collective-permute-done((bf16[2,256,1024]{1,2,0:T(8,128)(2,1)}, bf16[2,256,1024]{1,2,0:T(8,128)(2,1)}, u32[]{:S(2)}, u32[]{:S(2)}) %collective-permute-start.6) | collective-permute-done | bytes 1048608 | tf_op jit(solution)/shard_map/ppermute | solution.py:21
  531.2 46.0 %collective-permute-done.7 = bf16[2,256,1024]{1,2,0:T(8,128)(2,1)} collective-permute-done((bf16[2,256,1024]{1,2,0:T(8,128)(2,1)}, bf16[2,256,1024]{1,2,0:T(8,128)(2,1)}, u32[]{:S(2)}, u32[]{:S(2)}) %collective-permute-start.7) | collective-permute-done | bytes 1048608 | tf_op jit(solution)/shard_map/ppermute | solution.py:21
  583.7 49.9 %collective-permute-done.8 = bf16[2,256,1024]{1,2,0:T(8,128)(2,1)} collective-permute-done((bf16[2,256,1024]{1,2,0:T(8,128)(2,1)}, bf16[2,256,1024]{1,2,0:T(8,128)(2,1)}, u32[]{:S(2)}, u32[]{:S(2)}) %collective-permute-start.8) | collective-permute-done | bytes 1048608 | tf_op jit(solution)/shard_map/ppermute | solution.py:21
  640.8 76.4 %collective-permute-done.9 = bf16[2,256,1024]{1,2,0:T(8,128)(2,1)} collective-permute-done((bf16[2,256,1024]{1,2,0:T(8,128)(2,1)}, bf16[2,256,1024]{1,2,0:T(8,128)(2,1)}, u32[]{:S(2)}, u32[]{:S(2)}) %collective-permute-start.9) | collective-permute-done | bytes 1048608 | tf_op jit(solution)/shard_map/ppermute | solution.py:21
  723.7 56.6 %collective-permute-done.10 = bf16[2,256,1024]{1,2,0:T(8,128)(2,1)} collective-permute-done((bf16[2,256,1024]{1,2,0:T(8,128)(2,1)}, bf16[2,256,1024]{1,2,0:T(8,128)(2,1)}, u32[]{:S(2)}, u32[]{:S(2)}) %collective-permute-start.10) | collective-permute-done | bytes 1048608 | tf_op jit(solution)/shard_map/ppermute | solution.py:21
  784.9 72.7 %conditional.35 = (f32[256,16,64]{0,2,1:T(8,128)}, f32[2,256,1024]{1,2,0:T(8,128)S(1)}, f32[32,16]{0,1:T(8,128)S(1)}) conditional(s32[]{:T(128)} %convert_element_type.1327, () %tuple.190, (bf16[256,1024]{1,0:T(8,128)(2,1)}, bf16[256,16,64]{0,2,1:T(8,128)(2,1)S(1)}, f32[16,256,256]{2,1,0:T(8,128)}, f32[16,256]{1,0:T(8,128)S(1)}, ...), branch_computations={%region_56.57_spmd, %region_57.59_spmd} | conditional | flops 684701696 | bytes 141117280 | solution.py:250
  796.6 32.3 %rev.30 = f32[16,256,256]{2,1,0:T(8,128)} reverse(bf16[16,256,256]{2,1,0:T(8,128)(2,1)} %copy-done.9), dimensions={2} | reverse | bytes 6291456 | tf_op jit(solution)/shard_map/cond/branch_1_fun/jit(_flip)/rev | solution.py:52
  840.8 11.8 reshape.1396
  872.9 9.9 fusion.204
  883.8 9.7 fusion.65
  895.5 250.1 %psum.71 = f32[32,16]{0,1:T(8,128)} all-reduce(f32[32,16]{0,1:T(8,128)S(1)} %add_add_fusion.4), channel_id=1, replica_groups=mesh['seq'=4,'blk'=8] {'seq','blk'}, use_global_device_ids=true, to_apply=%region_99.100 | all-reduce | flops 512 | bytes 4096 | tf_op jit(solution)/shard_map/psum | solution.py:286
  1154.5 130.7 %reduce-scatter.5.cloned.1.call-done = f32[128,3072]{1,0:T(8,128)} async-done(((f32[1024,3072]{1,0:T(8,128)}), f32[128,3072]{1,0:T(8,128)}) %reduce-scatter.5.cloned.1.call-update) | async-done | bytes 1572880 | tf_op jit(solution)/shard_map/reduce_scatter | solution.py:267
  1287.5 283.8 %reduce-scatter.9.cloned.1.call-done = f32[128,4096]{1,0:T(8,128)} async-done(((f32[1024,4096]{1,0:T(8,128)}), f32[128,4096]{1,0:T(8,128)}) %reduce-scatter.9.cloned.1.call-update) | async-done | bytes 2097168 | tf_op jit(solution)/shard_map/reduce_scatter | solution.py:269
  1574.0 282.6 %reduce-scatter.11.cloned.1.call-done = f32[512,1024]{1,0:T(8,128)} async-done(((f32[4096,1024]{1,0:T(8,128)}), f32[512,1024]{1,0:T(8,128)}) %reduce-scatter.11.cloned.1.call-update) | async-done | bytes 2097168 | tf_op jit(solution)/shard_map/reduce_scatter | solution.py:270
  1866.0 35.3 %all-reduce.11 = (bf16[1024]{0:T(1024)(128)(2,1)S(1)}, bf16[1024]{0:T(1024)(128)(2,1)S(1)}, bf16[1024]{0:T(1024)(128)(2,1)S(1)}, bf16[1024]{0:T(1024)(128)(2,1)S(1)}) all-reduce(f32[1024]{0:T(1024)S(1)} %get-tuple-element.656, f32[1024]{0:T(1024)S(1)} %get-tuple-element.659, ...), channel_id=6, replica_groups=mesh['seq'=4,'blk'=8] {'blk'}, use_global_device_ids=true, to_apply=%region_88.89.clone | all-reduce | flops 4096 | bytes 24576
  1912.5 15.6 all-reduce.16.cloned.1.call-done
  (389 shorter events, 447.1 us)
Async XLA Ops:
  7.2 417.4 %copy-start = (bf16[1024,1024]{1,0:T(8,128)(2,1)S(1)}, bf16[1024,1024]{1,0:T(8,128)(2,1)}, u32[]{:S(2)}) copy-start(bf16[1024,1024]{1,0:T(8,128)(2,1)} %param.57) | copy-start | bytes 6291460
  7.2 1145.5 %reduce-scatter.7.cloned.1.call-start = ((), (), s32[]{:S(2)}) async-start(), calls=%async_computation.5 | async-start | bytes 4718592 | tf_op jit(solution)/shard_map/reduce_scatter | solution.py:268
  17.2 334.2 %copy-start.21 = (bf16[256,1024]{1,0:T(8,128)(2,1)}, bf16[256,1024]{1,0:T(8,128)(2,1)S(1)}, u32[]{:S(2)}) copy-start(bf16[256,1024]{1,0:T(8,128)(2,1)S(1)} %get-tuple-element.721) | copy-start | bytes 1572868
  18.3 27.6 %collective-permute-start = (bf16[2,256,1024]{2,1,0:T(8,128)(2,1)}, bf16[2,256,1024]{2,1,0:T(8,128)(2,1)}, u32[]{:S(2)}, u32[]{:S(2)}) collective-permute-start(bf16[2,256,1024]{2,1,0:T(8,128)(2,1)} %pad_maximum_fusion.8), channel_id=1, source_target_pairs={{0,1},{1,2},{2,3},{3,4},{4,5},{5,6},{6,7},{8,9},{9,10},{10,11},{11... | collective-permute-start | bytes 3145736 | tf_op jit(solution)/shard_map/ppermute | solution.py:21
  24.9 57.5 %copy-start.72 = (s32[511]{0:T(512)}, s32[511]{0:T(512)S(1)}, u32[]{:S(2)}) copy-start(s32[511]{0:T(512)S(1)} %convert_add_fusion.1) | copy-start | bytes 6136
  24.9 57.5 %copy-start.68 = (s32[511]{0:T(512)}, s32[511]{0:T(512)S(1)}, u32[]{:S(2)}) copy-start(s32[511]{0:T(512)S(1)} %convert_add_fusion.3) | copy-start | bytes 6136
  24.9 57.5 %copy-start.66 = (s32[511]{0:T(512)}, s32[511]{0:T(512)S(1)}, u32[]{:S(2)}) copy-start(s32[511]{0:T(512)S(1)} %convert_add_fusion.4) | copy-start | bytes 6136
  25.0 57.4 %copy-start.64 = (s32[511]{0:T(512)}, s32[511]{0:T(512)S(1)}, u32[]{:S(2)}) copy-start(s32[511]{0:T(512)S(1)} %convert_add_fusion.5) | copy-start | bytes 6136
  45.9 26.2 %collective-permute-start.1 = (bf16[2,256,1024]{2,1,0:T(8,128)(2,1)}, bf16[2,256,1024]{2,1,0:T(8,128)(2,1)}, u32[]{:S(2)}, u32[]{:S(2)}) collective-permute-start(bf16[2,256,1024]{2,1,0:T(8,128)(2,1)} %collective-permute-done), channel_id=1, source_target_pairs={{0,1},{1,2},{2,3},{3,4},{4,5},{5,6},{6,7},{8,9},{9,10},{10,11},{11... | collective-permute-start | bytes 3145736 | tf_op jit(solution)/shard_map/ppermute | solution.py:21
  51.2 60.7 %copy-start.62 = (s32[511]{0:T(512)}, s32[511]{0:T(512)S(1)}, u32[]{:S(2)}) copy-start(s32[511]{0:T(512)S(1)} %convert_add_fusion.6) | copy-start | bytes 6136
  72.1 47.0 %collective-permute-start.2 = (bf16[2,256,1024]{2,1,0:T(8,128)(2,1)}, bf16[2,256,1024]{2,1,0:T(8,128)(2,1)}, u32[]{:S(2)}, u32[]{:S(2)}) collective-permute-start(bf16[2,256,1024]{2,1,0:T(8,128)(2,1)} %collective-permute-done.1), channel_id=1, source_target_pairs={{0,1},{1,2},{2,3},{3,4},{4,5},{5,6},{6,7},{8,9},{9,10},{10,11},{11... | collective-permute-start | bytes 3145736 | tf_op jit(solution)/shard_map/ppermute | solution.py:21
  119.1 228.0 %collective-permute-start.3 = (bf16[2,256,1024]{2,1,0:T(8,128)(2,1)}, bf16[2,256,1024]{2,1,0:T(8,128)(2,1)}, u32[]{:S(2)}, u32[]{:S(2)}) collective-permute-start(bf16[2,256,1024]{2,1,0:T(8,128)(2,1)} %collective-permute-done.2), channel_id=1, source_target_pairs={{0,1},{1,2},{2,3},{3,4},{4,5},{5,6},{6,7},{8,9},{9,10},{10,11},{11... | collective-permute-start | bytes 3145736 | tf_op jit(solution)/shard_map/ppermute | solution.py:21
  347.0 28.9 %collective-permute-start.4 = (bf16[2,256,1024]{2,1,0:T(8,128)(2,1)}, bf16[2,256,1024]{2,1,0:T(8,128)(2,1)}, u32[]{:S(2)}, u32[]{:S(2)}) collective-permute-start(bf16[2,256,1024]{2,1,0:T(8,128)(2,1)} %collective-permute-done.3), channel_id=1, source_target_pairs={{0,1},{1,2},{2,3},{3,4},{4,5},{5,6},{6,7},{8,9},{9,10},{10,11},{11... | collective-permute-start | bytes 3145736 | tf_op jit(solution)/shard_map/ppermute | solution.py:21
  375.9 23.8 %collective-permute-start.5 = (bf16[2,256,1024]{2,1,0:T(8,128)(2,1)}, bf16[2,256,1024]{2,1,0:T(8,128)(2,1)}, u32[]{:S(2)}, u32[]{:S(2)}) collective-permute-start(bf16[2,256,1024]{2,1,0:T(8,128)(2,1)} %collective-permute-done.4), channel_id=1, source_target_pairs={{0,1},{1,2},{2,3},{3,4},{4,5},{5,6},{6,7},{8,9},{9,10},{10,11},{11... | collective-permute-start | bytes 3145736 | tf_op jit(solution)/shard_map/ppermute | solution.py:21
  477.6 46.3 %collective-permute-start.6 = (bf16[2,256,1024]{1,2,0:T(8,128)(2,1)}, bf16[2,256,1024]{1,2,0:T(8,128)(2,1)}, u32[]{:S(2)}, u32[]{:S(2)}) collective-permute-start(bf16[2,256,1024]{1,2,0:T(8,128)(2,1)} %get-tuple-element.365), channel_id=1, source_target_pairs={{1,0},{2,1},{3,2},{4,3},{5,4},{6,5},{7,6},{9,8},{10,9},{11,10},{12... | collective-permute-start | bytes 3145736 | tf_op jit(solution)/shard_map/ppermute | solution.py:21
  482.7 802.5 %reduce-scatter.5.cloned.1.call-start = ((), (), s32[]{:S(2)}) async-start(), calls=%async_computation.4 | async-start | bytes 14155776 | tf_op jit(solution)/shard_map/reduce_scatter | solution.py:267
  527.0 50.2 %collective-permute-start.7 = (bf16[2,256,1024]{1,2,0:T(8,128)(2,1)}, bf16[2,256,1024]{1,2,0:T(8,128)(2,1)}, u32[]{:S(2)}, u32[]{:S(2)}) collective-permute-start(bf16[2,256,1024]{1,2,0:T(8,128)(2,1)} %add_convert_fusion.6), channel_id=1, source_target_pairs={{1,0},{2,1},{3,2},{4,3},{5,4},{6,5},{7,6},{9,8},{10,9},{11,10},{12... | collective-permute-start | bytes 3145736 | tf_op jit(solution)/shard_map/ppermute | solution.py:21
  531.2 50.5 %copy-start.54 = (f32[32,16]{0,1:T(8,128)}, f32[32,16]{0,1:T(8,128)S(1)}, u32[]{:S(2)}) copy-start(f32[32,16]{0,1:T(8,128)S(1)} %get-tuple-element.375) | copy-start | bytes 6148
  531.2 50.3 %copy-start.69 = (s32[511]{0:T(512)S(1)}, s32[511]{0:T(512)}, u32[]{:S(2)}) copy-start(s32[511]{0:T(512)} %copy-done.68) | copy-start | bytes 6136
  580.2 53.3 %collective-permute-start.8 = (bf16[2,256,1024]{1,2,0:T(8,128)(2,1)}, bf16[2,256,1024]{1,2,0:T(8,128)(2,1)}, u32[]{:S(2)}, u32[]{:S(2)}) collective-permute-start(bf16[2,256,1024]{1,2,0:T(8,128)(2,1)} %add_convert_fusion.5), channel_id=1, source_target_pairs={{1,0},{2,1},{3,2},{4,3},{5,4},{6,5},{7,6},{9,8},{10,9},{11,10},{12... | collective-permute-start | bytes 3145736 | tf_op jit(solution)/shard_map/ppermute | solution.py:21
  583.7 54.4 %copy-start.25 = (f32[256,16,64]{0,2,1:T(8,128)}, f32[256,16,64]{0,2,1:T(8,128)S(1)}, u32[]{:S(2)}) copy-start(f32[256,16,64]{0,2,1:T(8,128)S(1)} %get-tuple-element.360) | copy-start | bytes 3145732
  583.7 54.2 %copy-start.67 = (s32[511]{0:T(512)S(1)}, s32[511]{0:T(512)}, u32[]{:S(2)}) copy-start(s32[511]{0:T(512)} %copy-done.66) | copy-start | bytes 6136
  636.6 80.6 %collective-permute-start.9 = (bf16[2,256,1024]{1,2,0:T(8,128)(2,1)}, bf16[2,256,1024]{1,2,0:T(8,128)(2,1)}, u32[]{:S(2)}, u32[]{:S(2)}) collective-permute-start(bf16[2,256,1024]{1,2,0:T(8,128)(2,1)} %add_convert_fusion.4), channel_id=1, source_target_pairs={{1,0},{2,1},{3,2},{4,3},{5,4},{6,5},{7,6},{9,8},{10,9},{11,10},{12... | collective-permute-start | bytes 3145736 | tf_op jit(solution)/shard_map/ppermute | solution.py:21
  640.8 80.8 %copy-start.65 = (s32[511]{0:T(512)S(1)}, s32[511]{0:T(512)}, u32[]{:S(2)}) copy-start(s32[511]{0:T(512)} %copy-done.64) | copy-start | bytes 6136
  720.3 60.0 %collective-permute-start.10 = (bf16[2,256,1024]{1,2,0:T(8,128)(2,1)}, bf16[2,256,1024]{1,2,0:T(8,128)(2,1)}, u32[]{:S(2)}, u32[]{:S(2)}) collective-permute-start(bf16[2,256,1024]{1,2,0:T(8,128)(2,1)} %add_convert_fusion.3), channel_id=1, source_target_pairs={{1,0},{2,1},{3,2},{4,3},{5,4},{6,5},{7,6},{9,8},{10,9},{11,10},{12... | collective-permute-start | bytes 3145736 | tf_op jit(solution)/shard_map/ppermute | solution.py:21
  723.7 61.2 %copy-start.26 = (f32[256,16,64]{0,2,1:T(8,128)}, f32[256,16,64]{0,2,1:T(8,128)S(1)}, u32[]{:S(2)}) copy-start(f32[256,16,64]{0,2,1:T(8,128)S(1)} %get-tuple-element.358) | copy-start | bytes 3145732
  723.7 61.0 %copy-start.63 = (s32[511]{0:T(512)S(1)}, s32[511]{0:T(512)}, u32[]{:S(2)}) copy-start(s32[511]{0:T(512)} %copy-done.62) | copy-start | bytes 6136
  783.4 79.2 %collective-permute-start.11 = (bf16[2,256,1024]{1,2,0:T(8,128)(2,1)}, bf16[2,256,1024]{1,2,0:T(8,128)(2,1)}, u32[]{:S(2)}, u32[]{:S(2)}) collective-permute-start(bf16[2,256,1024]{1,2,0:T(8,128)(2,1)} %add_convert_fusion.2), channel_id=1, source_target_pairs={{1,0},{2,1},{3,2},{4,3},{5,4},{6,5},{7,6},{9,8},{10,9},{11,10},{12... | collective-permute-start | bytes 3145736 | tf_op jit(solution)/shard_map/ppermute | solution.py:21
  871.7 699.6 %reduce-scatter.9.cloned.1.call-start = ((), (), s32[]{:S(2)}) async-start(), calls=%async_computation.6 | async-start | bytes 18874368 | tf_op jit(solution)/shard_map/reduce_scatter | solution.py:269
  882.8 973.8 %reduce-scatter.11.cloned.1.call-start = ((), (), s32[]{:S(2)}) async-start(), calls=%async_computation.7 | async-start | bytes 18874368 | tf_op jit(solution)/shard_map/reduce_scatter | solution.py:270
  893.6 1034.5 %all-reduce.16.cloned.1.call-start = ((), (), s32[]{:S(2)}) async-start(), calls=%async_computation.8 | async-start | bytes 6291456 | tf_op jit(solution)/shard_map/psum | solution.py:277
  1859.4 50.4 %copy-start.15 = (f32[256,1024]{1,0:T(8,128)S(1)}, f32[256,1024]{1,0:T(8,128)}, u32[]{:S(2)}) copy-start(f32[256,1024]{1,0:T(8,128)} %copy-done.14) | copy-start | bytes 3145732
  (62 other events, 557.0 us)
Sparse Core Ops, SparseCore 0:
  482.8 252.4 reduce-scatter.6
  871.9 413.2 reduce-scatter.4
  1289.4 281.8 reduce-scatter.8
  1575.0 281.6 reduce-scatter.10
  1859.8 68.2 all-reduce.15
where the time goes:
time: 1970 us; the launch traced here: 1940 us
  waiting for transfers between devices  1020 us (52%)
  local copies, waits for them, and re-layouts  357 us (18%)
  blocking collectives  291 us (15%)
  matrix products  108 us (5%)
  other arithmetic  96.2 us (5%)
  starting transfers between devices  37 us (2%)
  between operations  21 us (1%)
    ppermute x12, waiting for transfers between devices, shifted(): return lax.ppermute(array, axis, pairs)  305 us
    reduce_scatter x1, waiting for transfers between devices, local(): lax.psum_scatter(expand_grad, 'blk', scatter_dimension=0, tiled=True)  284 us
    reduce_scatter x1, waiting for transfers between devices, local(): lax.psum_scatter(contract_grad, 'blk', scatter_dimension=0, tiled=True)  283 us
    psum x1, blocking collectives, local(): table_grad = lax.psum(table_local, ('seq', 'blk'))  250 us
    reduce_scatter x1, waiting for transfers between devices, local(): lax.psum_scatter(attend_grad, 'blk', scatter_dimension=0, tiled=True)  131 us
    another operation x14, local copies, waits for them, and re-layouts, band_matrix(): tiled = jnp.tile(flipped, (1, count))  91.4 us
    reshape x7, local copies, waits for them, and re-layouts, band_matrix(): return window.reshape(heads, count, 2 * count - 2)[:, :, :count]  85.2 us
    slice x7, local copies, waits for them, and re-layouts, band_matrix(): window = tiled[:, count - 1:count - 1 + count * (2 * count - 2)]  61.8 us
  transfers between devices with their start and end apart: 17, of which 12 were waited for; matrix products, arithmetic and copies ran while one was open for 24% of the time, Pallas kernels for 0%

commit v1 on v0

--- a/solution.py
+++ b/solution.py
@@ -4,6 +4,8 @@
 import jax
 import jax.numpy as jnp
 from jax import lax
+from jax.experimental import pallas as pl
+from jax.experimental.pallas import tpu as pltpu
 from jax.sharding import PartitionSpec as P
 
 HOPS = 6
@@ -78,7 +80,7 @@
     return carried
 
 
-def local(
+def local_by_runs(
     tokens,
     lengths,
     attend_weight,
@@ -299,6 +301,727 @@
     )
 
 
+def _segments(position, meta_ref, first, items):
+    total = jnp.zeros(position.shape, jnp.int32)
+    for item in range(items):
+        total = total + (position >= meta_ref[first + item]).astype(jnp.int32)
+    return total
+
+def _allowed(meta_ref, peers, items, rows, i, j, diagonal):
+    first = 1 + 2 * peers
+    q_seg = _segments(i * rows + lax.broadcasted_iota(jnp.int32, (1, rows), 1), meta_ref, first, items)
+    k_seg = _segments(j * rows + lax.broadcasted_iota(jnp.int32, (rows, 1), 0), meta_ref, first, items)
+    k_seg = jnp.where(k_seg < items, k_seg, -1)
+    same = q_seg == k_seg
+    if diagonal:
+        key = lax.broadcasted_iota(jnp.int32, (rows, rows), 0)
+        query = lax.broadcasted_iota(jnp.int32, (rows, rows), 1)
+        return (same & (key < query)) | (key == query)
+    return same
+
+def _dot(a, b, dims):
+    return lax.dot_general(a, b, (dims, ((), ())), preferred_element_type=jnp.float32)
+
+def _turned(array):
+    return jnp.transpose(array.astype(jnp.float32))
+
+def _split(array, axis=1):
+    wide = array.astype(jnp.float32)
+    left = lax.broadcasted_iota(jnp.int32, array.shape, axis) < 64
+    return jnp.where(left, wide, 0.0).astype(jnp.bfloat16), jnp.where(left, 0.0, wide).astype(jnp.bfloat16)
+
+def _fold(value, op):
+    while value.shape[0] > 8:
+        half = value.shape[0] // 2
+        value = op(value[:half], value[half:])
+    return value
+
+def _put_bias(bias, line_ref, rows):
+    for head in range(2):
+        line = jnp.broadcast_to(line_ref[head:head + 1, :], (rows, 2 * rows))
+        bias[head] = pltpu.roll(line, 0, 1, stride=1, stride_axis=0)
+
+def _biased(raw, bias, far_ref, head, which, rows):
+    if which == 0:
+        return raw + bias[head, :, :rows]
+    if which == 1:
+        return raw + bias[head, :, rows:]
+    return raw + far_ref[head]
+
+def attend_kernel(peers, items, rows, meta_ref, far_ref, line_ref, *refs):
+    parts = refs[:peers]
+    outs = refs[peers:2 * peers]
+    wide_ref, log_ref = refs[2 * peers:2 * peers + 2]
+    qkv, turned, bias, scores, mixed = refs[2 * peers + 2:]
+    me = meta_ref[0]
+    for slot in range(peers):
+        qkv[me ^ slot] = parts[slot][...]
+        turned[me ^ slot] = _turned(parts[slot][2]).astype(jnp.bfloat16)
+    _put_bias(bias, line_ref, rows)
+    upper = lax.broadcasted_iota(jnp.int32, (128, rows), 0) < 64
+
+    def one_row(i, _):
+        low = meta_ref[1 + i]
+        whole = jnp.minimum(meta_ref[1 + peers + i], i - 1)
+        queries = _split(qkv[i, 0].astype(jnp.float32) * 0.125)
+
+        def put(j, which, masked, peaks):
+            key = qkv[j, 1]
+            if masked:
+                allowed = _allowed(meta_ref, peers, items, rows, i, j, which == 0)
+            new = []
+            for head in range(2):
+                raw = _biased(_dot(key, queries[head], ((1,), (1,))), bias, far_ref, head, which, rows)
+                if masked:
+                    raw = jnp.where(allowed, raw, masked_score)
+                scores[head, j] = raw
+                new.append(jnp.maximum(peaks[head], _fold(raw, jnp.maximum)))
+            return tuple(new)
+
+        start = jnp.full((8, rows), masked_score, jnp.float32)
+        peaks = put(i, 0, True, (start, start))
+        peaks = lax.cond(low < i, lambda p: put(i - 1, 1, True, p), lambda p: p, peaks)
+        peaks = lax.fori_loop(low, whole, lambda j, p: put(j, 2, True, p), peaks)
+        peaks = lax.fori_loop(jnp.maximum(low, whole), i - 1, lambda j, p: put(j, 2, False, p), peaks)
+        tops = [jnp.max(peak, axis=0, keepdims=True) for peak in peaks]
+
+        def mix(j, carry):
+            sums, total = carry
+            value = turned[j]
+            new = []
+            both = []
+            for head in range(2):
+                weight = jnp.exp(scores[head, j] - tops[head])
+                new.append(sums[head] + _fold(weight, jnp.add))
+                both.append(_dot(value[64 * head:64 * head + 64], weight.astype(jnp.bfloat16), ((1,), (0,))))
+            return tuple(new), total + jnp.concatenate(both)
+
+        nothing = jnp.zeros((8, rows), jnp.float32)
+        sums, total = lax.fori_loop(low, i + 1, mix, ((nothing, nothing), jnp.zeros((128, rows), jnp.float32)))
+        sums = [jnp.sum(s, axis=0, keepdims=True) for s in sums]
+        total = total / jnp.where(upper, sums[0], sums[1])
+        wide_ref[i] = total
+        for head in range(2):
+            log_ref[i, head:head + 1, :] = tops[head] + jnp.log(sums[head])
+        mixed[i] = jnp.transpose(total).astype(jnp.bfloat16)
+        return 0
+
+    lax.fori_loop(0, peers, one_row, 0)
+    for slot in range(peers):
+        outs[slot][...] = mixed[me ^ slot]
+
+def attend(meta, far, line, parts, items):
+    peers = len(parts)
+    rows = parts[0].shape[1]
+    smem = pl.BlockSpec(memory_space=pltpu.SMEM)
+    vmem = pl.BlockSpec(memory_space=pltpu.VMEM)
+    shapes = [jax.ShapeDtypeStruct((rows, 128), jnp.bfloat16)] * peers + [
+        jax.ShapeDtypeStruct((peers, 128, rows), jnp.float32),
+        jax.ShapeDtypeStruct((peers, 8, rows), jnp.float32),
+    ]
+    res = pl.pallas_call(
+        partial(attend_kernel, peers, items, rows),
+        out_shape=shapes,
+        in_specs=[smem, smem] + [vmem] * (peers + 1),
+        out_specs=[vmem] * (peers + 2),
+        scratch_shapes=[
+            pltpu.VMEM((peers, 3, rows, 128), jnp.bfloat16),
+            pltpu.VMEM((peers, 128, rows), jnp.bfloat16),
+            pltpu.VMEM((2, rows, 2 * rows), jnp.float32),
+            pltpu.VMEM((2, peers, rows, rows), jnp.float32),
+            pltpu.VMEM((peers, rows, 128), jnp.bfloat16),
+        ],
+        compiler_params=pltpu.CompilerParams(vmem_limit_bytes=40 * 2**20),
+        cost_estimate=pl.CostEstimate(flops=8 * 10**9, bytes_accessed=4 * 2**20, transcendentals=3 * 10**6),
+        name="attend",
+    )(meta, far, line, *parts)
+    return res[:peers], res[peers], res[peers + 1]
+
+def attend_back_kernel(peers, items, rows, meta_ref, far_ref, line_ref, wide_ref, log_ref, *refs):
+    parts = refs[:peers]
+    grads = refs[peers:2 * peers]
+    outs = refs[2 * peers:3 * peers]
+    all_ref, table_ref = refs[3 * peers:3 * peers + 2]
+    qkv, cot, turned, bias, near, far_sum, dkey, dvalue = refs[3 * peers + 2:]
+    me = meta_ref[0]
+    for slot in range(peers):
+        qkv[me ^ slot] = parts[slot][...]
+        cot[me ^ slot] = grads[slot][...]
+        turned[me ^ slot] = _turned(parts[slot][1]).astype(jnp.bfloat16)
+    _put_bias(bias, line_ref, rows)
+    near[...] = jnp.zeros_like(near)
+    far_sum[...] = jnp.zeros_like(far_sum)
+    dkey[...] = jnp.zeros_like(dkey)
+    dvalue[...] = jnp.zeros_like(dvalue)
+
+    def one_row(i, _):
+        low = meta_ref[1 + i]
+        whole = jnp.minimum(meta_ref[1 + peers + i], i - 1)
+        queries = _split(qkv[i, 0].astype(jnp.float32) * 0.125)
+        grad = cot[i]
+        grads_ = _split(grad)
+        product = _turned(grad) * wide_ref[i]
+        dots = [jnp.sum(product[64 * head:64 * head + 64], axis=0, keepdims=True) for head in range(2)]
+        logs = [log_ref[i, head:head + 1, :] for head in range(2)]
+
+        def step(j, which, masked, dquery):
+            key = qkv[j, 1]
+            value = qkv[j, 2]
+            across = turned[j]
+            if masked:
+                allowed = _allowed(meta_ref, peers, items, rows, i, j, which == 0)
+            dk = jnp.zeros((rows, 128), jnp.float32)
+            dv = jnp.zeros((rows, 128), jnp.float32)
+            both = []
+            for head in range(2):
+                raw = _biased(_dot(key, queries[head], ((1,), (1,))), bias, far_ref, head, which, rows)
+                if masked:
+                    raw = jnp.where(allowed, raw, masked_score)
+                weight = jnp.exp(raw - logs[head])
+                dweight = _dot(value, grads_[head], ((1,), (1,)))
+                dscore = weight * (dweight - dots[head])
+                low_score = dscore.astype(jnp.bfloat16)
+                if which == 0:
+                    near[head, :, :rows] += dscore
+                elif which == 1:
+                    near[head, :, rows:] += dscore
+                else:
+                    far_sum[head] += _fold(dscore, jnp.add)
+                both.append(_dot(across[64 * head:64 * head + 64], low_score, ((1,), (0,))))
+                dk = dk + _dot(low_score, queries[head], ((1,), (0,)))
+                dv = dv + _dot(weight.astype(jnp.bfloat16), grads_[head], ((1,), (0,)))
+            dkey[j] += dk
+            dvalue[j] += dv
+            return dquery + jnp.concatenate(both)
+
+        dquery = step(i, 0, True, jnp.zeros((128, rows), jnp.float32))
+        dquery = lax.cond(low < i, lambda d: step(i - 1, 1, True, d), lambda d: d, dquery)
+        dquery = lax.fori_loop(low, whole, lambda j, d: step(j, 2, True, d), dquery)
+        dquery = lax.fori_loop(jnp.maximum(low, whole), i - 1, lambda j, d: step(j, 2, False, d), dquery)
+        all_ref[i, 0] = (jnp.transpose(dquery) * 0.125).astype(jnp.bfloat16)
+        return 0
+
+    lax.fori_loop(0, peers, one_row, 0)
+    for i in range(peers):
+        all_ref[i, 1] = dkey[i].astype(jnp.bfloat16)
+        all_ref[i, 2] = dvalue[i].astype(jnp.bfloat16)
+    for slot in range(peers):
+        outs[slot][...] = all_ref[me ^ slot]
+    wide = 2 * rows
+    sub = lax.broadcasted_iota(jnp.int32, (8, wide), 0)
+    for head in range(2):
+        part = near[head]
+        count = rows
+        while count > 8:
+            count //= 2
+            part = part[:count] + pltpu.roll(part[count:], wide - count, 1)
+        for bit in (4, 2, 1):
+            part = jnp.where((sub & bit) != 0, pltpu.roll(part, wide - bit, 1), part)
+        total = far_sum[head]
+        table_ref[head, :, :rows] = part[:, :rows]
+        table_ref[head, :, rows:] = part[:, rows:] + jnp.concatenate([jnp.zeros((8, rows - 128), jnp.float32), total[:, :128] + total[:, 128:]], axis=1)
+
+def attend_back(meta, far, line, wide, logs, parts, grads, items):
+    peers = len(parts)
+    rows = parts[0].shape[1]
+    smem = pl.BlockSpec(memory_space=pltpu.SMEM)
+    vmem = pl.BlockSpec(memory_space=pltpu.VMEM)
+    shapes = [jax.ShapeDtypeStruct((3, rows, 128), jnp.bfloat16)] * peers + [
+        jax.ShapeDtypeStruct((peers, 3, rows, 128), jnp.bfloat16),
+        jax.ShapeDtypeStruct((2, 8, 2 * rows), jnp.float32),
+    ]
+    res = pl.pallas_call(
+        partial(attend_back_kernel, peers, items, rows),
+        out_shape=shapes,
+        in_specs=[smem, smem] + [vmem] * (2 * peers + 3),
+        out_specs=[vmem] * (peers + 2),
+        scratch_shapes=[
+            pltpu.VMEM((peers, 3, rows, 128), jnp.bfloat16),
+            pltpu.VMEM((peers, rows, 128), jnp.bfloat16),
+            pltpu.VMEM((peers, 128, rows), jnp.bfloat16),
+            pltpu.VMEM((2, rows, 2 * rows), jnp.float32),
+            pltpu.VMEM((2, rows, 2 * rows), jnp.float32),
+            pltpu.VMEM((2, 8, rows), jnp.float32),
+            pltpu.VMEM((peers, rows, 128), jnp.float32),
+            pltpu.VMEM((peers, rows, 128), jnp.float32),
+        ],
+        compiler_params=pltpu.CompilerParams(vmem_limit_bytes=40 * 2**20),
+        cost_estimate=pl.CostEstimate(flops=20 * 10**9, bytes_accessed=8 * 2**20, transcendentals=3 * 10**6),
+        name="attend_back",
+    )(meta, far, line, wide, logs, *parts, *grads)
+    return res[:peers], res[peers], jnp.sum(res[peers + 1], axis=1)
+
+def plan(lengths, me, peers, rows):
+    ends = jnp.cumsum(lengths)
+    items = lengths.shape[0]
+    place = jnp.arange(peers, dtype=jnp.int32)
+    first = jnp.sum((place[:, None] * rows >= ends[None]).astype(jnp.int32), axis=1)
+    last = jnp.sum((place[:, None] * rows + rows - 1 >= ends[None]).astype(jnp.int32), axis=1)
+    low = jnp.sum((last[None, :] < first[:, None]).astype(jnp.int32), axis=1)
+    low = jnp.where(first < items, jnp.minimum(low, place), place)
+    whole = jnp.sum((first[None, :] < last[:, None]).astype(jnp.int32), axis=1)
+    return jnp.concatenate([me[None].astype(jnp.int32), low, whole, ends.astype(jnp.int32)])
+def bucket_lines(rows, buckets):
+    k = jnp.arange(2 * rows, dtype=jnp.int32)
+    return (bucket_of(k)[None, :] == jnp.arange(buckets, dtype=jnp.int32)[:, None]).astype(jnp.float32)
+
+
+def _unit(value):
+    mean = jnp.mean(value, axis=-1, keepdims=True)
+    centred = value - mean
+    variance = jnp.mean(centred * centred, axis=-1, keepdims=True)
+    scale = lax.rsqrt(variance + epsilon)
+    return centred * scale, scale
+
+
+def _norm_back(grad, unit, scale, gain, sums_ref):
+    inner = grad * gain
+    first = jnp.mean(inner, axis=-1, keepdims=True)
+    second = jnp.mean(inner * unit, axis=-1, keepdims=True)
+    sums_ref[0:1, :] = jnp.sum(grad * unit, axis=0, keepdims=True)
+    sums_ref[1:2, :] = jnp.sum(grad, axis=0, keepdims=True)
+    return scale * (inner - first - unit * second)
+
+
+def _lanes(index):
+    return pl.ds(pl.multiple_of(index * 128, 128), 128)
+
+
+def _specs(*kinds):
+    places = {"s": pltpu.SMEM, "v": pltpu.VMEM, "a": pl.ANY}
+    return [pl.BlockSpec(memory_space=places[kind]) for word in kinds for kind in word]
+
+
+def _params(**more):
+    return pltpu.CompilerParams(vmem_limit_bytes=44 * 2**20, **more)
+
+
+def project_kernel(peers, meta_ref, tokens_ref, gain_ref, shift_ref, weight_ref, *refs):
+    outs, act_ref, held, arrived = refs[:peers], refs[peers], refs[peers + 1], refs[peers + 2]
+    me = meta_ref[0]
+    copies = []
+    for slot in range(peers):
+        for block in range(3):
+            columns = _lanes(block * peers + (me ^ slot))
+            copies.append(pltpu.make_async_copy(weight_ref.at[:, columns], held.at[slot, block], arrived.at[slot, block]))
+            copies[-1].start()
+    unit, _ = _unit(tokens_ref[...].astype(jnp.float32))
+    act = (unit * gain_ref[...] + shift_ref[...]).astype(jnp.bfloat16)
+    act_ref[...] = act
+    for slot in range(peers):
+        for block in range(3):
+            copies[3 * slot + block].wait()
+            outs[slot][block] = _dot(act, held[slot, block], ((1,), (0,))).astype(jnp.bfloat16)
+
+
+def project(meta, tokens, gain, shift, weight, peers):
+    rows, width = tokens.shape
+    return pl.pallas_call(
+        partial(project_kernel, peers),
+        out_shape=[jax.ShapeDtypeStruct((3, rows, 128), jnp.bfloat16)] * peers + [jax.ShapeDtypeStruct((rows, width), jnp.bfloat16)],
+        in_specs=_specs("svvva"),
+        out_specs=_specs("v" * (peers + 1)),
+        scratch_shapes=[pltpu.VMEM((peers, 3, width, 128), jnp.bfloat16), pltpu.SemaphoreType.DMA((peers, 3))],
+        compiler_params=_params(),
+        cost_estimate=pl.CostEstimate(flops=4 * 10**9, bytes_accessed=8 * 2**20, transcendentals=0),
+        name="project",
+    )(meta, tokens, gain, shift, weight)
+
+
+def merge_kernel(peers, meta_ref, tokens_ref, gain_ref, shift_ref, weight_ref, *refs):
+    parts = refs[:peers]
+    low_ref, middle_ref, act_ref = refs[peers:]
+    me = meta_ref[0]
+    for slot in range(peers):
+        low_ref[:, _lanes(me ^ slot)] = parts[slot][...]
+    middle = tokens_ref[...].astype(jnp.float32) + _dot(low_ref[...], weight_ref[...], ((1,), (0,)))
+    middle_ref[...] = middle
+    unit, _ = _unit(middle)
+    act_ref[...] = (unit * gain_ref[...] + shift_ref[...]).astype(jnp.bfloat16)
+
+
+def merge(meta, tokens, gain, shift, weight, parts):
+    shape, peers = tokens.shape, len(parts)
+    return pl.pallas_call(
+        partial(merge_kernel, peers),
+        out_shape=[jax.ShapeDtypeStruct(shape, t) for t in (jnp.bfloat16, jnp.float32, jnp.bfloat16)],
+        in_specs=_specs("svvvv", "v" * peers),
+        out_specs=_specs("vvv"),
+        compiler_params=_params(),
+        cost_estimate=pl.CostEstimate(flops=10**9, bytes_accessed=5 * 2**20, transcendentals=0),
+        name="merge",
+    )(meta, tokens, gain, shift, weight, *parts)
+
+
+def feed_kernel(
+    peers, rows, part, meta_ref, act_mine, act_other, grad_mine, grad_other, expand_ref, contract_ref,
+    out_keep, out_send, in_keep, in_send, c_one_keep, c_one_send, c_two_keep, c_two_send,
+    e_one_keep, e_one_send, e_two_keep, e_two_send, acts, grads, out_total, in_total, block_grad,
+):
+    step = pl.program_id(0)
+    x, y = meta_ref[1], meta_ref[2]
+    cut = c_one_keep.shape[2]
+    group = block_grad.shape[1]
+    half = group // 2
+
+    @pl.when(step == 0)
+    def _():
+        acts[:rows] = act_mine[...]
+        acts[rows:] = act_other[...]
+        grads[:rows] = grad_mine[...]
+        grads[rows:] = grad_other[...]
+
+    before = _dot(acts[...], expand_ref[...], ((1,), (0,)))
+    pulled = _dot(grads[...], contract_ref[...], ((1,), (1,)))
+    rate = 0.5 * (1.0 + lax.erf(before * math.sqrt(0.5)))
+    low = (before * rate).astype(jnp.bfloat16)
+    slope = rate + before * jnp.exp(-0.5 * before * before) * (1.0 / math.sqrt(2.0 * math.pi))
+    back = (pulled * slope).astype(jnp.bfloat16)
+    out_part = _dot(low, contract_ref[...], ((1,), (0,)))
+    in_part = _dot(back, expand_ref[...], ((1,), (1,)))
+
+    @pl.when(step == 0)
+    def _():
+        out_total[...] = out_part
+        in_total[...] = in_part
+
+    @pl.when(step > 0)
+    def _():
+        out_total[...] += out_part
+        in_total[...] += in_part
+
+    contract_grad = _dot(low, grads[...], ((0,), (0,))).astype(jnp.bfloat16)
+    level = step // 2
+
+    @pl.when(step % 2 == x)
+    def _():
+        c_one_keep[level] = contract_grad[:, :cut]
+
+    @pl.when(step % 2 != x)
+    def _():
+        c_one_send[level] = contract_grad[:, :cut]
+
+    @pl.when(y == 0)
+    def _():
+        c_two_keep[step] = contract_grad[: part // 2, cut:]
+        c_two_send[step] = contract_grad[part // 2 :, cut:]
+
+    @pl.when(y != 0)
+    def _():
+        c_two_keep[step] = contract_grad[part // 2 :, cut:]
+        c_two_send[step] = contract_grad[: part // 2, cut:]
+
+    expand_grad = _dot(acts[...], back, ((0,), (0,))).astype(jnp.bfloat16)
+    block_grad[...] = expand_grad.reshape(peers, group, part)
+    near = peers // 2
+
+    @pl.when(step < near)
+    def _():
+        columns = pl.ds(pl.multiple_of(step * part, part), part)
+        for place in range(near):
+            e_one_keep[place, :, columns] = block_grad[2 * place + x]
+            e_one_send[place, :, columns] = block_grad[2 * place + 1 - x]
+
+    @pl.when(step >= near)
+    def _():
+        columns = pl.ds(pl.multiple_of((step - near) * part, part), part)
+        for place in range(peers):
+            e_two_keep[place, :, columns] = block_grad[place, pl.ds(pl.multiple_of(y * half, half), half), :]
+            e_two_send[place, :, columns] = block_grad[place, pl.ds(pl.multiple_of((1 - y) * half, half), half), :]
+
+    @pl.when(step == peers - 1)
+    def _():
+        out_keep[...] = out_total[:rows]
+        out_send[...] = out_total[rows:].astype(jnp.bfloat16)
+        in_keep[...] = in_total[:rows]
+        in_send[...] = in_total[rows:]
+
+
+def feed(meta, act_mine, act_other, grad_mine, grad_other, expand_weight, contract_weight, peers):
+    rows, width = act_mine.shape
+    part = expand_weight.shape[1] // (2 * peers)
+    group, cut = width // peers, width // 2
+    whole = lambda *shape: pl.BlockSpec(shape, lambda step, meta_ref: (0,) * len(shape))
+    shapes = [
+        ((rows, width), jnp.float32),
+        ((rows, width), jnp.bfloat16),
+        ((rows, width), jnp.float32),
+        ((rows, width), jnp.float32),
+        ((peers // 2, part, cut), jnp.bfloat16),
+        ((peers // 2, part, cut), jnp.bfloat16),
+        ((peers, part // 2, cut), jnp.bfloat16),
+        ((peers, part // 2, cut), jnp.bfloat16),
+        ((peers // 2, group, part * peers // 2), jnp.bfloat16),
+        ((peers // 2, group, part * peers // 2), jnp.bfloat16),
+        ((peers, group // 2, part * peers // 2), jnp.bfloat16),
+        ((peers, group // 2, part * peers // 2), jnp.bfloat16),
+    ]
+    return pl.pallas_call(
+        partial(feed_kernel, peers, rows, part),
+        out_shape=[jax.ShapeDtypeStruct(*shape) for shape in shapes],
+        grid_spec=pltpu.PrefetchScalarGridSpec(
+            num_scalar_prefetch=1,
+            grid=(peers,),
+            in_specs=[whole(rows, width)] * 4
+            + [
+                pl.BlockSpec((width, part), lambda step, meta_ref: (0, 2 * step + meta_ref[3])),
+                pl.BlockSpec((part, width), lambda step, meta_ref: (2 * step + meta_ref[3], 0)),
+            ],
+            out_specs=[whole(*shape) for shape, _ in shapes],
+            scratch_shapes=[
+                pltpu.VMEM((2 * rows, width), jnp.bfloat16),
+                pltpu.VMEM((2 * rows, width), jnp.bfloat16),
+                pltpu.VMEM((2 * rows, width), jnp.float32),
+                pltpu.VMEM((2 * rows, width), jnp.float32),
+                pltpu.VMEM((peers, group, part), jnp.bfloat16),
+            ],
+        ),
+        compiler_params=_params(),
+        cost_estimate=pl.CostEstimate(flops=13 * 10**9, bytes_accessed=24 * 2**20, transcendentals=2 * 10**6),
+        name="feed",
+    )(meta, act_mine, act_other, grad_mine, grad_other, expand_weight, contract_weight)
+
+
+def turn_kernel(peers, meta_ref, in_mine, in_other, middle_ref, grad_ref, gain_ref, weight_ref, *refs):
+    outs = refs[:peers]
+    total_ref, keep_ref, send_ref, sums_ref, held = refs[peers:]
+    me, core = meta_ref[0], meta_ref[3]
+    half = keep_ref.shape[1]
+    unit, scale = _unit(middle_ref[...])
+    total = grad_ref[...].astype(jnp.float32) + _norm_back(in_mine[...] + in_other[...], unit, scale, gain_ref[...], sums_ref)
+    total_ref[...] = total
+    low = total.astype(jnp.bfloat16)
+
+    @pl.when(core == 0)
+    def _():
+        keep_ref[...] = low[:, :half]
+        send_ref[...] = low[:, half:]
+
+    @pl.when(core != 0)
+    def _():
+        keep_ref[...] = low[:, half:]
+        send_ref[...] = low[:, :half]
+
+    held[...] = _dot(low, weight_ref[...], ((1,), (1,))).astype(jnp.bfloat16)
+    for slot in range(peers):
+        outs[slot][...] = held[:, _lanes(me ^ slot)]
+
+
+def turn(meta, in_mine, in_other, middle, grad, gain, weight, peers):
+    rows, width = middle.shape
+    shapes = [((rows, 128), jnp.bfloat16)] * peers + [
+        ((rows, width), jnp.float32),
+        ((rows, width // 2), jnp.bfloat16),
+        ((rows, width // 2), jnp.bfloat16),
+        ((2, width), jnp.float32),
+    ]
+    return pl.pallas_call(
+        partial(turn_kernel, peers),
+        out_shape=[jax.ShapeDtypeStruct(*shape) for shape in shapes],
+        in_specs=_specs("svvvvvv"),
+        out_specs=_specs("v" * len(shapes)),
+        scratch_shapes=[pltpu.VMEM((rows, width), jnp.bfloat16)],
+        compiler_params=_params(),
+        cost_estimate=pl.CostEstimate(flops=10**9, bytes_accessed=8 * 2**20, transcendentals=0),
+        name="turn",
+    )(meta, in_mine, in_other, middle, grad, gain, weight)
+
+
+def close_kernel(peers, meta_ref, tokens_ref, grad_ref, gain_ref, weight_ref, *refs):
+    parts = refs[:peers]
+    out_ref, sums_ref, held = refs[peers:]
+    me = meta_ref[0]
+    for slot in range(peers):
+        for block in range(3):
+            held[:, _lanes(block * peers + (me ^ slot))] = parts[slot][block]
+    back = _dot(held[...], weight_ref[...], ((1,), (1,)))
+    unit, scale = _unit(tokens_ref[...].astype(jnp.float32))
+    out_ref[...] = grad_ref[...] + _norm_back(back, unit, scale, gain_ref[...], sums_ref)
+
+
+def close(meta, tokens, grad, gain, weight, parts):
+    rows, width = tokens.shape
+    peers = len(parts)
+    return pl.pallas_call(
+        partial(close_kernel, peers),
+        out_shape=[jax.ShapeDtypeStruct((rows, width), jnp.float32), jax.ShapeDtypeStruct((2, width), jnp.float32)],
+        in_specs=_specs("svvvv", "v" * peers),
+        out_specs=_specs("vv"),
+        scratch_shapes=[pltpu.VMEM((rows, 3 * width), jnp.bfloat16)],
+        compiler_params=_params(),
+        cost_estimate=pl.CostEstimate(flops=2 * 10**9, bytes_accessed=10 * 2**20, transcendentals=0),
+        name="close",
+    )(meta, tokens, grad, gain, weight, *parts)
+
+
+def flipped(array, axis, mask):
+    peers = lax.axis_size(axis)
+    return lax.ppermute(array, axis, [(i, i ^ mask) for i in range(peers)])
+
+
+def pick(array, index, axis):
+    return lax.dynamic_index_in_dim(array, index, axis, keepdims=False)
+
+
+def added(a, b):
+    return (a.astype(jnp.float32) + b.astype(jnp.float32)).astype(jnp.bfloat16)
+
+
+def in_order(mine, other, bit, axis):
+    lower = jnp.where(bit == 0, mine, other)
+    upper = jnp.where(bit == 0, other, mine)
+    return jnp.concatenate([lower, upper], axis=axis)
+
+
+def over_chips(one_keep, one_send, two_keep, two_send, place):
+    z, x, y = place
+    levels, rows, cut = one_keep.shape
+    half = rows // 2
+    one_got = flipped(one_send, "blk", 1)
+    two_got = flipped(two_send, "seq", 2)
+
+    def sums(keep, got, shape, index, axis):
+        return added(pick(keep.reshape(shape), index, axis), pick(got.reshape(shape), index, axis))
+
+    tall, wide = (levels, 2, half, cut), (levels, 2, half, cut)
+    one_next = flipped(sums(one_keep, one_got, tall, 1 - y, 1), "seq", 2)
+    two_next = flipped(sums(two_keep, two_got, wide, 1 - x, 1), "blk", 1)
+    one = added(sums(one_keep, one_got, tall, y, 1), one_next)
+    two = added(sums(two_keep, two_got, wide, x, 1), two_next)
+    both = jnp.concatenate([one, two], axis=-1)
+    total = pick(both, z, 0).astype(jnp.float32)
+    for step in range(1, levels):
+        total = total + flipped(pick(both, z ^ step, 0), "blk", 2 * step).astype(jnp.float32)
+    return total.astype(jnp.bfloat16)
+
+
+def local_by_heads(
+    tokens,
+    lengths,
+    attend_weight,
+    merge_weight,
+    expand_weight,
+    contract_weight,
+    gain_first,
+    shift_first,
+    gain_second,
+    shift_second,
+    bias_table,
+    cotangent,
+):
+    rows, width = tokens.shape[1], tokens.shape[2]
+    buckets, heads = bias_table.shape
+    hidden = expand_weight.shape[1]
+    items = lengths.shape[1]
+    peers = lax.axis_size("blk")
+    levels = peers // 2
+    group = width // peers
+    part = hidden // (2 * peers)
+    me, line_of = lax.axis_index("blk"), lax.axis_index("seq")
+    z, x, y, core = me // 2, me % 2, line_of // 2, line_of % 2
+    place = (z, x, y)
+    here = jnp.stack([me, x, y, core]).astype(jnp.int32)
+    gain_first, shift_first, gain_second, shift_second = (
+        v.reshape(1, width) for v in (gain_first, shift_first, gain_second, shift_second)
+    )
+
+    own, grad_out = tokens[0], cotangent[0]
+    grad_other = flipped(grad_out, "seq", 1)
+    meta = plan(lengths[0], me, peers, rows)
+    hot = bucket_lines(rows, buckets)
+    table_mine = lax.dynamic_slice_in_dim(bias_table, 2 * me, 2, 1)
+    lines = jnp.dot(table_mine.T, hot, precision=highest)
+    far = table_mine[buckets - 1]
+
+    def exchanged(parts):
+        return [parts[0]] + [flipped(parts[step], "blk", step) for step in range(1, peers)]
+
+    def ordered(parts):
+        stack = jnp.stack(parts)
+        return jnp.stack([pick(stack, me ^ peer, 0) for peer in range(peers)])
+
+    *parts, act_first = project(here, own, gain_first, shift_first, attend_weight, peers)
+    parts = exchanged(parts)
+    act_all = lax.all_gather(act_first, "blk", axis=0, tiled=True)
+    mixed, wide, logs = attend(meta, far, lines, parts, items)
+    attn_low, middle, act_second = merge(here, own, gain_second, shift_second, merge_weight, exchanged(mixed))
+    act_other = flipped(act_second, "seq", 1)
+    out_keep, out_send, in_keep, in_send, *grads = feed(
+        here, act_second, act_other, grad_out, grad_other, expand_weight, contract_weight, peers
+    )
+    *grad_heads, grad_middle, keep_low, send_low, sums_second = turn(
+        here, in_keep, flipped(in_send, "seq", 1), middle, grad_out, gain_second, merge_weight, peers
+    )
+    back_parts, back_all, line_grad = attend_back(meta, far, lines, wide, logs, parts, exchanged(grad_heads), items)
+    tokens_grad, sums_first = close(here, own, grad_middle, gain_first, attend_weight, exchanged(back_parts))
+    output = (middle + out_keep + flipped(out_send, "seq", 1).astype(jnp.float32)).astype(jnp.bfloat16)
+
+    contract_grad = over_chips(*grads[:4], place)
+    expand_grad = over_chips(*grads[4:], place)
+    attn_both = jnp.concatenate([attn_low, flipped(attn_low, "seq", 1)])
+    merge_right = jnp.concatenate([keep_low, flipped(send_low, "seq", 1)])
+    merge_grad = jnp.einsum("td,te->de", attn_both, merge_right, preferred_element_type=jnp.float32).astype(jnp.bfloat16)
+    merge_grad = merge_grad.reshape(levels, 2, group, width // 2)
+    one, two = merge_grad[..., : width // 4], merge_grad[..., width // 4 :].reshape(levels, 2, 2, group // 2, width // 4)
+    merge_grad = over_chips(pick(one, x, 1), pick(one, 1 - x, 1), pick(two, y, 2), pick(two, 1 - y, 2), place)
+    attend_grad = jnp.einsum(
+        "td,te->de",
+        act_all,
+        back_all.transpose(0, 2, 1, 3).reshape(peers * rows, 3 * group),
+        preferred_element_type=jnp.float32,
+    ).astype(jnp.bfloat16)
+    attend_grad = attend_grad.reshape(peers, 2, group // 2, 3 * group)
+    attend_grad = added(pick(attend_grad, core, 1), flipped(pick(attend_grad, 1 - core, 1), "seq", 1))
+    attend_grad = attend_grad.reshape(peers, 2, group // 4, 3 * group)
+    attend_grad = added(pick(attend_grad, y, 1), flipped(pick(attend_grad, 1 - y, 1), "seq", 2))
+    attend_grad = ordered(exchanged([pick(attend_grad, me ^ slot, 0) for slot in range(peers)]))
+
+    contract_grad = in_order(contract_grad, flipped(contract_grad, "seq", 2), y, 0)
+    contract_grad = in_order(contract_grad, flipped(contract_grad, "seq", 1), core, 0).astype(jnp.float32)
+    expand_grad = in_order(expand_grad, flipped(expand_grad, "seq", 2), y, 0)
+    expand_other = flipped(expand_grad, "seq", 1)
+    expand_halves = [jnp.where(core == side, expand_grad, expand_other) for side in range(2)]
+    expand_grad = jnp.concatenate(
+        [expand_halves[side][:, part * peer : part * (peer + 1)] for peer in range(peers) for side in range(2)], axis=1
+    ).astype(jnp.float32)
+    merge_grad = in_order(merge_grad, flipped(merge_grad, "seq", 2), y, 0)
+    merge_grad = in_order(merge_grad, flipped(merge_grad, "seq", 1), core, 1).astype(jnp.float32)
+    attend_grad = in_order(attend_grad, flipped(attend_grad, "seq", 2), y, 1)
+    attend_grad = in_order(attend_grad, flipped(attend_grad, "seq", 1), core, 1)
+    attend_grad = attend_grad.reshape(peers, group, 3, group).transpose(1, 2, 0, 3).reshape(group, 3 * width).astype(jnp.float32)
+
+    table_mine = jnp.dot(hot, line_grad.T, precision=highest)
+    table_local = lax.dynamic_update_slice(jnp.zeros((buckets, heads), jnp.float32), table_mine, (0, 2 * me))
+    table_row = jnp.pad(table_local.reshape(1, buckets * heads), ((0, 0), (0, width - buckets * heads)))
+    small = jnp.concatenate([sums_first, sums_second, table_row])
+    for axis, mask in (("seq", 1), ("seq", 2), ("blk", 1), ("blk", 2), ("blk", 4)):
+        small = small + flipped(small, axis, mask)
+    table_grad = small[4, : buckets * heads].reshape(buckets, heads)
+    vectors = lax.dynamic_slice_in_dim(small, me * group, group, 1)
+    return (
+        output[None],
+        tokens_grad[None],
+        attend_grad,
+        merge_grad,
+        expand_grad,
+        contract_grad,
+        vectors[0],
+        vectors[1],
+        vectors[2],
+        vectors[3],
+        table_grad,
+    )
+
+
+def local(*arguments):
+    heads = arguments[10].shape[1]
+    rows = arguments[0].shape[1]
+    peers = lax.axis_size("blk")
+    if peers == 8 and lax.axis_size("seq") == 4 and heads == 2 * peers and rows == 256:
+        return local_by_heads(*arguments)
+    return local_by_runs(*arguments)
+
+
 def solution(mesh):
     in_specs = (
         P("seq", "blk", None),

time: 1970 us -> 455 us (0.23); the launches traced: 1940 us -> 448 us
  waiting for transfers between devices: 1020 us -> 163 us
  local copies, waits for them, and re-layouts: 357 us -> 39.3 us
  blocking collectives: 291 us -> 0 us
  matrix products: 108 us -> 7.79 us
  Pallas kernels: 0 us -> 82.2 us
  starting transfers between devices: 37 us -> 114 us
  other arithmetic: 96.2 us -> 25.6 us
    reduce_scatter x4 -> x0, waiting for transfers between devices: 697 us -> none  [the longest x1 284 us: local(): lax.psum_scatter(expand_grad, 'blk', scatter_dimension=0, tiled=True)]
    psum x2 -> x0, blocking collectives: 256 us -> none  [the longest x1 250 us: local(): table_grad = lax.psum(table_local, ('seq', 'blk'))]
    ppermute x12 -> x77, waiting for transfers between devices: 305 us -> 163 us  [flipped(): return lax.ppermute(array, axis, [(i, i ^ mask) for i in range(peers)])]
    another operation x56 -> x3, local copies, waits for them, and re-layouts: 138 us -> 0.11 us  [the longest x1 0.08 us: local_by_heads(): table_grad = small[4, :buckets * heads].reshape(buckets, heads)]
    dot_general x27 -> x4, matrix products: 108 us -> 7.79 us  [the longest x1 5.05 us: local_by_heads(): jnp.einsum('td,te->de', act_all, back_all.transpose(0, 2, 1, 3).reshape(p...]
    reshape x8 -> x1, local copies, waits for them, and re-layouts: 97 us -> 1.38 us  [local_by_heads(): table_local.reshape(1, buckets * heads)]
    pallas_call x0 -> x7, Pallas kernels: none -> 82.2 us  [the longest x1 28 us: feed(): pl.pallas_call(partial(feed_kernel, peers, rows, part), out_shape=[jax.Sh...]
    ppermute x12 -> x77, starting transfers between devices: 36.8 us -> 114 us  [flipped(): return lax.ppermute(array, axis, [(i, i ^ mask) for i in range(peers)])]
  transfers between devices with their start and end apart: 17 -> 78, of which waited for: 12 -> 32; matrix products, arithmetic and copies ran while one was open for 24% -> 10% of each run, Pallas kernels for 0% -> 7%
where the time goes in v1:
time: 455 us; the launch traced here: 448 us
  waiting for transfers between devices  163 us (36%)
  starting transfers between devices  114 us (25%)
  Pallas kernels  82.2 us (18%)
  local copies, waits for them, and re-layouts  39.3 us (9%)
  other arithmetic  25.6 us (6%)
  between operations  16.5 us (4%)
  matrix products  7.79 us (2%)
    ppermute x77, waiting for transfers between devices, flipped(): return lax.ppermute(array, axis, [(i, i ^ mask) for i in range(peers)])  163 us
    ppermute x77, starting transfers between devices, flipped(): return lax.ppermute(array, axis, [(i, i ^ mask) for i in range(peers)])  114 us
    unnamed x181, local copies, waits for them, and re-layouts  28.3 us
    pallas_call x1, Pallas kernels, feed(): pl.pallas_call(partial(feed_kernel, peers, rows, part), out_shape=[jax.Sh...  28 us
    pallas_call x1, Pallas kernels, attend_back(): pl.pallas_call(partial(attend_back_kernel, peers, items, rows), out_shape...  21.3 us
    convert_element_type x14, other arithmetic, added(): return (a.astype(jnp.float32) + b.astype(jnp.float32)).astype(jnp.bfloat16)  14.7 us
    pallas_call x1, Pallas kernels, attend(): pl.pallas_call(partial(attend_kernel, peers, items, rows), out_shape=shap...  12.8 us
    pallas_call x1, Pallas kernels, project(): pl.pallas_call(partial(project_kernel, peers), out_shape=[jax.ShapeDtypeS...  10.2 us
  transfers between devices with their start and end apart: 78, of which 32 were waited for; matrix products, arithmetic and copies ran while one was open for 10% of the time, Pallas kernels for 7%

profile of v1, /device:TPU:0, one launch (start us, length us, event | category | flops | bytes accessed | tf_op | source)
XLA Modules:
  0.0 447.7 jit_solution(8562782362901544499)
XLA Ops:
  12.6 10.2 %project.1 = (bf16[3,256,128]{2,1,0:T(8,128)(2,1)S(1)}, bf16[3,256,128]{2,1,0:T(8,128)(2,1)S(1)}, bf16[3,256,128]{2,1,0:T(8,128)(2,1)S(1)}, bf16[3,256,128]{2,1,...) custom-call(s32[4]{0:T(128)S(1)} %pad_add_fusion.meta_ref, ...), custom_call_target="tpu_custom_call" | custom-call | flops 4000000000 | bytes 8388608 | tf_op jit(solution)/shard_map/project/pallas_call | solution.py:619
  24.9 2.9 collective-permute-start
  29.4 3.0 collective-permute-start.3
  34.9 3.7 collective-permute-start.5
  38.6 4.6 %collective-permute-done.1.refs_2_ = bf16[3,256,128]{2,1,0:T(8,128)(2,1)S(1)} collective-permute-done((bf16[3,256,128]{2,1,0:T(8,128)(2,1)S(1)}, bf16[3,256,128]{2,1,0:T(8,128)(2,1)S(1)}, u32[]{:S(2)}, u32[]{:S(2)}) %collective-permute-start.1) | collective-permute-done | bytes 196640 | tf_op jit(solution)/shard_map/ppermute | solution.py:859
  45.1 15.2 %collective-permute-done.4.refs_5_ = bf16[3,256,128]{2,1,0:T(8,128)(2,1)S(1)} collective-permute-done((bf16[3,256,128]{2,1,0:T(8,128)(2,1)}, bf16[3,256,128]{2,1,0:T(8,128)(2,1)S(1)}, u32[]{:S(2)}, u32[]{:S(2)}) %collective-permute-start.4) | collective-permute-done | bytes 196640 | tf_op jit(solution)/shard_map/ppermute | solution.py:859
  61.5 12.8 %attend.1 = (bf16[256,128]{1,0:T(8,128)(2,1)S(1)}, bf16[256,128]{1,0:T(8,128)(2,1)S(1)}, bf16[256,128]{1,0:T(8,128)(2,1)S(1)}, bf16[256,128]{1,0:T(8,128)(2,1)S(...) custom-call(s32[18]{0:T(128)S(1)} %pad_add_fusion.1.meta_ref, ...), custom_call_target="tpu_custom_call" | custom-call | flops 8000000000 | bytes 4194304 | tf_op jit(solution)/shard_map/attend/pallas_call | solution.py:422
  76.3 7.6 %collective-permute-start.8 = (bf16[256,128]{1,0:T(8,128)(2,1)S(1)}, bf16[256,128]{1,0:T(8,128)(2,1)S(1)}, u32[]{:S(2)}, u32[]{:S(2)}) collective-permute-start(bf16[256,128]{1,0:T(8,128)(2,1)S(1)} %get-tuple-element.79), channel_id=1, source_target_pairs={{0,2},{1,3},{2,0},{3,1},{4,6},{5,7},{6,4},{7,5},{8,10},{9,11},{10,... | collective-permute-start | bytes 196616 | tf_op jit(solution)/shard_map/ppermute | solution.py:859
  84.6 4.2 collective-permute-start.10
  101.9 28.0 %feed.1 = (f32[256,1024]{1,0:T(8,128)S(1)}, bf16[256,1024]{1,0:T(8,128)(2,1)}, f32[256,1024]{1,0:T(8,128)S(1)}, f32[256,1024]{1,0:T(8,128)}, bf16[4,256,512]{2,1...) custom-call(s32[4]{0:T(128)S(1)} %pad_add_fusion.meta_ref, ...), custom_call_target="tpu_custom_call" | custom-call | flops 12999999488 | bytes 25165824 | tf_op jit(solution)/shard_map/feed/pallas_call | solution.py:759
  140.2 3.2 turn.1
  151.4 9.4 %collective-permute-done.56 = bf16[8,64,1024]{2,1,0:T(8,128)(2,1)} collective-permute-done((bf16[8,64,1024]{2,1,0:T(8,128)(2,1)}, bf16[8,64,1024]{2,1,0:T(8,128)(2,1)}, u32[]{:S(2)}, u32[]{:S(2)}) %collective-permute-start.56) | collective-permute-done | bytes 1048608 | tf_op jit(solution)/shard_map/ppermute | solution.py:859
  175.9 21.3 %attend_back.1 = (bf16[3,256,128]{2,1,0:T(8,128)(2,1)S(1)}, bf16[3,256,128]{2,1,0:T(8,128)(2,1)}, bf16[3,256,128]{2,1,0:T(8,128)(2,1)}, bf16[3,256,128]{2,1,0:T(...) custom-call(s32[18]{0:T(128)S(1)} %pad_add_fusion.1.meta_ref, ...), custom_call_target="tpu_custom_call" | custom-call | flops 20000000000 | bytes 8388608 | tf_op jit(solution)/shard_map/attend_back/pallas_call | solution.py:533
  199.7 15.8 %collective-permute-done.54 = bf16[4,128,1024]{2,1,0:T(8,128)(2,1)S(1)} collective-permute-done((bf16[4,128,1024]{2,1,0:T(8,128)(2,1)S(1)}, bf16[4,128,1024]{2,1,0:T(8,128)(2,1)S(1)}, u32[]{:S(2)}, u32[]{:S(2)}) %collective-permute-start.54) | collective-permute-done | bytes 1048608 | tf_op jit(solution)/shard_map/ppermute | solution.py:859
  216.7 29.2 %collective-permute-done.63 = bf16[4,256,512]{2,1,0:T(8,128)(2,1)S(1)} collective-permute-done((bf16[4,256,512]{2,1,0:T(8,128)(2,1)S(1)}, bf16[4,256,512]{2,1,0:T(8,128)(2,1)S(1)}, u32[]{:S(2)}, u32[]{:S(2)}) %collective-permute-start.63) | collective-permute-done | bytes 1048608 | tf_op jit(solution)/shard_map/ppermute | solution.py:859
  252.3 3.2 collective-permute-start.31
  259.6 9.8 %collective-permute-done.28.refs_4_ = bf16[3,256,128]{2,1,0:T(8,128)(2,1)} collective-permute-done((bf16[3,256,128]{2,1,0:T(8,128)(2,1)}, bf16[3,256,128]{2,1,0:T(8,128)(2,1)}, u32[]{:S(2)}, u32[]{:S(2)}) %collective-permute-start.28) | collective-permute-done | bytes 196640 | tf_op jit(solution)/shard_map/ppermute | solution.py:859
  269.4 4.6 %collective-permute-done.29.refs_5_ = bf16[3,256,128]{2,1,0:T(8,128)(2,1)} collective-permute-done((bf16[3,256,128]{2,1,0:T(8,128)(2,1)}, bf16[3,256,128]{2,1,0:T(8,128)(2,1)}, u32[]{:S(2)}, u32[]{:S(2)}) %collective-permute-start.29) | collective-permute-done | bytes 196640 | tf_op jit(solution)/shard_map/ppermute | solution.py:859
  280.8 5.1 %close.1 = (f32[256,1024]{1,0:T(8,128)}, f32[2,1024]{1,0:T(2,128)S(1)}) custom-call(s32[4]{0:T(128)S(1)} %copy-done.25, bf16[256,1024]{1,0:T(8,128)(2,1)S(1)} %bitcast.229, f32[256,1024]{1,0:T(8,128)S(1)} %copy-done.8, f32[1,1024]{1,0:T(1,128)S(1)} %bitcast.234, bf16[1024,3072]{1,0:T(8,128)(2,1)S(1)} %copy-done.3, ...), custom_call_target="tpu_custom_call" | custom-call | flops 2000000000 | bytes 10485760 | tf_op jit(solution)/shard_map/close/pallas_call | solution.py:845
  290.0 3.1 copy.149
  297.1 11.2 %collective-permute-done.73 = f32[5,1024]{1,0:T(8,128)S(1)} collective-permute-done((f32[5,1024]{1,0:T(8,128)S(1)}, f32[5,1024]{1,0:T(8,128)S(1)}, u32[]{:S(2)}, u32[]{:S(2)}) %collective-permute-start.73) | collective-permute-done | bytes 20512 | tf_op jit(solution)/shard_map/ppermute | solution.py:859
  309.4 2.9 collective-permute-done.74
  312.3 7.0 %collective-permute-start.75 = (f32[5,1024]{1,0:T(8,128)S(1)}, f32[5,1024]{1,0:T(8,128)S(1)}, u32[]{:S(2)}, u32[]{:S(2)}) collective-permute-start(f32[5,1024]{1,0:T(8,128)S(1)} %add.481), channel_id=1, source_target_pairs={{0,2},{1,3},{2,0},{3,1},{4,6},{5,7},{6,4},{7,5},{8,10},{9,11},{10,... | collective-permute-start | bytes 61448 | tf_op jit(solution)/shard_map/ppermute | solution.py:859
  330.7 3.4 collective-permute-done.47
  351.4 6.8 %collective-permute-done.51 = bf16[64,512]{1,0:T(8,128)(2,1)S(1)} collective-permute-done((bf16[64,512]{1,0:T(8,128)(2,1)S(1)}, bf16[64,512]{1,0:T(8,128)(2,1)S(1)}, u32[]{:S(2)}, u32[]{:S(2)}) %collective-permute-start.51) | collective-permute-done | bytes 65568 | tf_op jit(solution)/shard_map/ppermute | solution.py:859
  358.2 8.0 %collective-permute-start.49 = (bf16[64,512]{1,0:T(8,128)(2,1)S(1)}, bf16[64,512]{1,0:T(8,128)(2,1)S(1)}, u32[]{:S(2)}, u32[]{:S(2)}) collective-permute-start(bf16[64,512]{1,0:T(8,128)(2,1)S(1)} %get-tuple-element.197), channel_id=1, source_target_pairs={{0,2},{1,3},{2,0},{3,1},{4,6},{5,7},{6,4},{7,5},{8,10},{9,11},{10,... | collective-permute-start | bytes 196616 | tf_op jit(solution)/shard_map/ppermute | solution.py:859
  378.1 10.4 %collective-permute-done.68 = bf16[128,1024]{1,0:T(8,128)(2,1)S(1)} collective-permute-done((bf16[128,1024]{1,0:T(8,128)(2,1)S(1)}, bf16[128,1024]{1,0:T(8,128)(2,1)S(1)}, u32[]{:S(2)}, u32[]{:S(2)}) %collective-permute-start.68) | collective-permute-done | bytes 262176 | tf_op jit(solution)/shard_map/ppermute | solution.py:859
  390.2 4.9 %collective-permute-done.70 = bf16[128,1024]{1,0:T(8,128)(2,1)S(1)} collective-permute-done((bf16[128,1024]{1,0:T(8,128)(2,1)S(1)}, bf16[128,1024]{1,0:T(8,128)(2,1)S(1)}, u32[]{:S(2)}, u32[]{:S(2)}) %collective-permute-start.70) | collective-permute-done | bytes 262176 | tf_op jit(solution)/shard_map/ppermute | solution.py:859
  396.4 5.1 %convolution_convert_fusion.1 = bf16[1024,384]{1,0:T(8,128)(2,1)S(1)} fusion(bf16[2048,1024]{1,0:T(8,128)(2,1)} %all-gather.2.cloned.1.call-done, bf16[2048,384]{0,1:T(8,128)(2,1)} %bitcast.245), kind=kOutput, calls=%fused_computation.17 | convolution fusion | flops 1611005952 | bytes 6553600 | tf_op jit(solution)/shard_map/td,te->de/dot_general | solution.py:967
  404.1 6.8 %collective-permute-done.33 = bf16[8,32,384]{2,1,0:T(8,128)(2,1)S(1)} collective-permute-done((bf16[8,32,384]{2,1,0:T(8,128)(2,1)S(1)}, bf16[8,32,384]{2,1,0:T(8,128)(2,1)S(1)}, u32[]{:S(2)}, u32[]{:S(2)}) %collective-permute-start.33) | collective-permute-done | bytes 196640 | tf_op jit(solution)/shard_map/ppermute | solution.py:859
  415.1 3.1 collective-permute-start.38
  428.7 3.6 collective-permute-done.41
  (388 shorter events, 161.1 us)
Async XLA Ops:
  7.2 389.2 %all-gather.2.cloned.1.call-start = ((), (), s32[]{:S(2)}) async-start(), calls=%async_computation | async-start | bytes 4718592 | tf_op jit(solution)/shard_map/all_gather | solution.py:945
  32.4 27.9 %collective-permute-start.4 = (bf16[3,256,128]{2,1,0:T(8,128)(2,1)}, bf16[3,256,128]{2,1,0:T(8,128)(2,1)S(1)}, u32[]{:S(2)}, u32[]{:S(2)}) collective-permute-start(bf16[3,256,128]{2,1,0:T(8,128)(2,1)} %get-tuple-element.74), channel_id=1, source_target_pairs={{0,5},{1,4},{2,7},{3,6},{4,1},{5,0},{6,3},{7,2},{8,13},{9,12},{10,... | collective-permute-start | bytes 589832 | tf_op jit(solution)/shard_map/ppermute | solution.py:859
  34.9 25.4 %collective-permute-start.5 = (bf16[3,256,128]{2,1,0:T(8,128)(2,1)}, bf16[3,256,128]{2,1,0:T(8,128)(2,1)S(1)}, u32[]{:S(2)}, u32[]{:S(2)}) collective-permute-start(bf16[3,256,128]{2,1,0:T(8,128)(2,1)} %copy-done.53), channel_id=1, source_target_pairs={{0,6},{1,7},{2,4},{3,5},{4,2},{5,3},{6,0},{7,1},{8,14},{9,15},{10,... | collective-permute-start | bytes 589832 | tf_op jit(solution)/shard_map/ppermute | solution.py:859
  43.2 17.1 %collective-permute-start.6 = (bf16[3,256,128]{2,1,0:T(8,128)(2,1)S(1)}, bf16[3,256,128]{2,1,0:T(8,128)(2,1)S(1)}, u32[]{:S(2)}, u32[]{:S(2)}) collective-permute-start(bf16[3,256,128]{2,1,0:T(8,128)(2,1)S(1)} %get-tuple-element.76), channel_id=1, source_target_pairs={{0,7},{1,6},{2,5},{3,4},{4,3},{5,2},{6,1},{7,0},{8,15},{9,14},{10,... | collective-permute-start | bytes 589832 | tf_op jit(solution)/shard_map/ppermute | solution.py:859
  135.0 25.8 %collective-permute-start.56 = (bf16[8,64,1024]{2,1,0:T(8,128)(2,1)}, bf16[8,64,1024]{2,1,0:T(8,128)(2,1)}, u32[]{:S(2)}, u32[]{:S(2)}) collective-permute-start(bf16[8,64,1024]{2,1,0:T(8,128)(2,1)} %get-tuple-element.119), channel_id=1, source_target_pairs={{0,16},{8,24},{16,0},{24,8},{1,17},{9,25},{17,1},{25,9},{2,18},{10... | collective-permute-start | bytes 3145736 | tf_op jit(solution)/shard_map/ppermute | solution.py:859
  143.4 19.7 %collective-permute-start.18 = (bf16[256,128]{1,0:T(8,128)(2,1)S(1)}, bf16[256,128]{1,0:T(8,128)(2,1)S(1)}, u32[]{:S(2)}, u32[]{:S(2)}) collective-permute-start(bf16[256,128]{1,0:T(8,128)(2,1)S(1)} %get-tuple-element.95), channel_id=1, source_target_pairs={{0,1},{1,0},{2,3},{3,2},{4,5},{5,4},{6,7},{7,6},{8,9},{9,8},{10,11... | collective-permute-start | bytes 196616 | tf_op jit(solution)/shard_map/ppermute | solution.py:859
  144.9 20.4 %collective-permute-start.19 = (bf16[256,128]{1,0:T(8,128)(2,1)S(1)}, bf16[256,128]{1,0:T(8,128)(2,1)S(1)}, u32[]{:S(2)}, u32[]{:S(2)}) collective-permute-start(bf16[256,128]{1,0:T(8,128)(2,1)S(1)} %get-tuple-element.96), channel_id=1, source_target_pairs={{0,2},{1,3},{2,0},{3,1},{4,6},{5,7},{6,4},{7,5},{8,10},{9,11},{10,... | collective-permute-start | bytes 196616 | tf_op jit(solution)/shard_map/ppermute | solution.py:859
  148.5 21.2 %collective-permute-start.20 = (bf16[256,128]{1,0:T(8,128)(2,1)S(1)}, bf16[256,128]{1,0:T(8,128)(2,1)S(1)}, u32[]{:S(2)}, u32[]{:S(2)}) collective-permute-start(bf16[256,128]{1,0:T(8,128)(2,1)S(1)} %get-tuple-element.97), channel_id=1, source_target_pairs={{0,3},{1,2},{2,1},{3,0},{4,7},{5,6},{6,5},{7,4},{8,11},{9,10},{10,... | collective-permute-start | bytes 196616 | tf_op jit(solution)/shard_map/ppermute | solution.py:859
  149.5 21.1 %collective-permute-start.21 = (bf16[256,128]{1,0:T(8,128)(2,1)S(1)}, bf16[256,128]{1,0:T(8,128)(2,1)S(1)}, u32[]{:S(2)}, u32[]{:S(2)}) collective-permute-start(bf16[256,128]{1,0:T(8,128)(2,1)S(1)} %get-tuple-element.98), channel_id=1, source_target_pairs={{0,4},{1,5},{2,6},{3,7},{4,0},{5,1},{6,2},{7,3},{8,12},{9,13},{10,... | collective-permute-start | bytes 196616 | tf_op jit(solution)/shard_map/ppermute | solution.py:859
  169.7 45.9 %collective-permute-start.54 = (bf16[4,128,1024]{2,1,0:T(8,128)(2,1)S(1)}, bf16[4,128,1024]{2,1,0:T(8,128)(2,1)S(1)}, u32[]{:S(2)}, u32[]{:S(2)}) collective-permute-start(bf16[4,128,1024]{2,1,0:T(8,128)(2,1)S(1)} %copy-done.74), channel_id=1, source_target_pairs={{0,1},{1,0},{2,3},{3,2},{4,5},{5,4},{6,7},{7,6},{8,9},{9,8},{10,11... | collective-permute-start | bytes 3145736 | tf_op jit(solution)/shard_map/ppermute | solution.py:859
  170.5 75.4 %collective-permute-start.63 = (bf16[4,256,512]{2,1,0:T(8,128)(2,1)S(1)}, bf16[4,256,512]{2,1,0:T(8,128)(2,1)S(1)}, u32[]{:S(2)}, u32[]{:S(2)}) collective-permute-start(bf16[4,256,512]{2,1,0:T(8,128)(2,1)S(1)} %copy-done.30), channel_id=1, source_target_pairs={{0,1},{1,0},{2,3},{3,2},{4,5},{5,4},{6,7},{7,6},{8,9},{9,8},{10,11... | collective-permute-start | bytes 3145736 | tf_op jit(solution)/shard_map/ppermute | solution.py:859
  174.3 111.6 %collective-permute-start.65 = (bf16[8,128,512]{2,1,0:T(8,128)(2,1)}, bf16[8,128,512]{2,1,0:T(8,128)(2,1)}, u32[]{:S(2)}, u32[]{:S(2)}) collective-permute-start(bf16[8,128,512]{2,1,0:T(8,128)(2,1)} %get-tuple-element.123), channel_id=1, source_target_pairs={{0,16},{8,24},{16,0},{24,8},{1,17},{9,25},{17,1},{25,9},{2,18},{10... | collective-permute-start | bytes 3145736 | tf_op jit(solution)/shard_map/ppermute | solution.py:859
  197.2 51.5 %collective-permute-start.25 = (bf16[3,256,128]{2,1,0:T(8,128)(2,1)}, bf16[3,256,128]{2,1,0:T(8,128)(2,1)S(1)}, u32[]{:S(2)}, u32[]{:S(2)}) collective-permute-start(bf16[3,256,128]{2,1,0:T(8,128)(2,1)} %get-tuple-element.103), channel_id=1, source_target_pairs={{0,1},{1,0},{2,3},{3,2},{4,5},{5,4},{6,7},{7,6},{8,9},{9,8},{10,11... | collective-permute-start | bytes 589832 | tf_op jit(solution)/shard_map/ppermute | solution.py:859
  197.9 52.9 %collective-permute-start.26 = (bf16[3,256,128]{2,1,0:T(8,128)(2,1)}, bf16[3,256,128]{2,1,0:T(8,128)(2,1)}, u32[]{:S(2)}, u32[]{:S(2)}) collective-permute-start(bf16[3,256,128]{2,1,0:T(8,128)(2,1)} %get-tuple-element.104), channel_id=1, source_target_pairs={{0,2},{1,3},{2,0},{3,1},{4,6},{5,7},{6,4},{7,5},{8,10},{9,11},{10,... | collective-permute-start | bytes 589832 | tf_op jit(solution)/shard_map/ppermute | solution.py:859
  215.6 36.7 %collective-permute-start.27 = (bf16[3,256,128]{2,1,0:T(8,128)(2,1)}, bf16[3,256,128]{2,1,0:T(8,128)(2,1)}, u32[]{:S(2)}, u32[]{:S(2)}) collective-permute-start(bf16[3,256,128]{2,1,0:T(8,128)(2,1)} %get-tuple-element.105), channel_id=1, source_target_pairs={{0,3},{1,2},{2,1},{3,0},{4,7},{5,6},{6,5},{7,4},{8,11},{9,10},{10,... | collective-permute-start | bytes 589832 | tf_op jit(solution)/shard_map/ppermute | solution.py:859
  247.0 22.5 %collective-permute-start.28 = (bf16[3,256,128]{2,1,0:T(8,128)(2,1)}, bf16[3,256,128]{2,1,0:T(8,128)(2,1)}, u32[]{:S(2)}, u32[]{:S(2)}) collective-permute-start(bf16[3,256,128]{2,1,0:T(8,128)(2,1)} %get-tuple-element.106), channel_id=1, source_target_pairs={{0,4},{1,5},{2,6},{3,7},{4,0},{5,1},{6,2},{7,3},{8,12},{9,13},{10,... | collective-permute-start | bytes 589832 | tf_op jit(solution)/shard_map/ppermute | solution.py:859
  248.7 25.3 %collective-permute-start.29 = (bf16[3,256,128]{2,1,0:T(8,128)(2,1)}, bf16[3,256,128]{2,1,0:T(8,128)(2,1)}, u32[]{:S(2)}, u32[]{:S(2)}) collective-permute-start(bf16[3,256,128]{2,1,0:T(8,128)(2,1)} %copy-done.52), channel_id=1, source_target_pairs={{0,5},{1,4},{2,7},{3,6},{4,1},{5,0},{6,3},{7,2},{8,13},{9,12},{10,... | collective-permute-start | bytes 589832 | tf_op jit(solution)/shard_map/ppermute | solution.py:859
  250.8 23.3 %collective-permute-start.30 = (bf16[3,256,128]{2,1,0:T(8,128)(2,1)}, bf16[3,256,128]{2,1,0:T(8,128)(2,1)}, u32[]{:S(2)}, u32[]{:S(2)}) collective-permute-start(bf16[3,256,128]{2,1,0:T(8,128)(2,1)} %copy-done.51), channel_id=1, source_target_pairs={{0,6},{1,7},{2,4},{3,5},{4,2},{5,3},{6,0},{7,1},{8,14},{9,15},{10,... | collective-permute-start | bytes 589832 | tf_op jit(solution)/shard_map/ppermute | solution.py:859
  252.3 23.2 %collective-permute-start.31 = (bf16[3,256,128]{2,1,0:T(8,128)(2,1)}, bf16[3,256,128]{2,1,0:T(8,128)(2,1)}, u32[]{:S(2)}, u32[]{:S(2)}) collective-permute-start(bf16[3,256,128]{2,1,0:T(8,128)(2,1)} %copy-done.50), channel_id=1, source_target_pairs={{0,7},{1,6},{2,5},{3,4},{4,3},{5,2},{6,1},{7,0},{8,15},{9,14},{10,... | collective-permute-start | bytes 589832 | tf_op jit(solution)/shard_map/ppermute | solution.py:859
  269.4 24.3 %collective-permute-start.43 = (bf16[256,1024]{1,0:T(8,128)(2,1)}, bf16[256,1024]{1,0:T(8,128)(2,1)}, u32[]{:S(2)}, u32[]{:S(2)}) collective-permute-start(bf16[256,1024]{1,0:T(8,128)(2,1)} %copy-done.31), channel_id=1, source_target_pairs={{0,8},{8,0},{16,24},{24,16},{1,9},{9,1},{17,25},{25,17},{2,10},{10... | collective-permute-start | bytes 1572872 | tf_op jit(solution)/shard_map/ppermute | solution.py:859
  274.1 21.2 %collective-permute-start.44 = (bf16[256,512]{1,0:T(8,128)(2,1)}, bf16[256,512]{1,0:T(8,128)(2,1)}, u32[]{:S(2)}, u32[]{:S(2)}) collective-permute-start(bf16[256,512]{1,0:T(8,128)(2,1)} %copy-done.35), channel_id=1, source_target_pairs={{0,8},{8,0},{16,24},{24,16},{1,9},{9,1},{17,25},{25,17},{2,10},{10... | collective-permute-start | bytes 786440 | tf_op jit(solution)/shard_map/ppermute | solution.py:859
  274.1 62.5 %collective-permute-start.55 = (bf16[4,64,1024]{2,1,0:T(8,128)(2,1)}, bf16[4,64,1024]{2,1,0:T(8,128)(2,1)}, u32[]{:S(2)}, u32[]{:S(2)}) collective-permute-start(bf16[4,64,1024]{2,1,0:T(8,128)(2,1)} %fusion.10), channel_id=1, source_target_pairs={{0,16},{8,24},{16,0},{24,8},{1,17},{9,25},{17,1},{25,9},{2,18},{10... | collective-permute-start | bytes 1572872 | tf_op jit(solution)/shard_map/ppermute | solution.py:859
  275.5 63.6 %collective-permute-start.57 = (bf16[4,64,1024]{2,1,0:T(8,128)(2,1)}, bf16[4,64,1024]{2,1,0:T(8,128)(2,1)}, u32[]{:S(2)}, u32[]{:S(2)}) collective-permute-start(bf16[4,64,1024]{2,1,0:T(8,128)(2,1)} %fusion.12), channel_id=1, source_target_pairs={{0,1},{1,0},{2,3},{3,2},{4,5},{5,4},{6,7},{7,6},{8,9},{9,8},{10,11... | collective-permute-start | bytes 1572872 | tf_op jit(solution)/shard_map/ppermute | solution.py:859
  293.2 49.5 %collective-permute-start.64 = (bf16[4,128,512]{2,1,0:T(8,128)(2,1)}, bf16[4,128,512]{2,1,0:T(8,128)(2,1)S(1)}, u32[]{:S(2)}, u32[]{:S(2)}) collective-permute-start(bf16[4,128,512]{2,1,0:T(8,128)(2,1)} %fusion.14), channel_id=1, source_target_pairs={{0,16},{8,24},{16,0},{24,8},{1,17},{9,25},{17,1},{25,9},{2,18},{10... | collective-permute-start | bytes 1572872 | tf_op jit(solution)/shard_map/ppermute | solution.py:859
  328.8 20.6 %collective-permute-start.66 = (bf16[4,128,512]{2,1,0:T(8,128)(2,1)}, bf16[4,128,512]{2,1,0:T(8,128)(2,1)S(1)}, u32[]{:S(2)}, u32[]{:S(2)}) collective-permute-start(bf16[4,128,512]{2,1,0:T(8,128)(2,1)} %fusion.16), channel_id=1, source_target_pairs={{0,1},{1,0},{2,3},{3,2},{4,5},{5,4},{6,7},{7,6},{8,9},{9,8},{10,11... | collective-permute-start | bytes 1572872 | tf_op jit(solution)/shard_map/ppermute | solution.py:859
  340.8 30.9 %collective-permute-start.60 = (bf16[64,2048]{1,0:T(8,128)(2,1)S(1)}, bf16[64,2048]{1,0:T(8,128)(2,1)S(1)}, u32[]{:S(2)}, u32[]{:S(2)}) collective-permute-start(bf16[64,2048]{1,0:T(8,128)(2,1)S(1)} %get-tuple-element.182), channel_id=1, source_target_pairs={{0,6},{1,7},{2,4},{3,5},{4,2},{5,3},{6,0},{7,1},{8,14},{9,15},{10,... | collective-permute-start | bytes 786440 | tf_op jit(solution)/shard_map/ppermute | solution.py:859
  342.7 29.8 %collective-permute-start.59 = (bf16[64,2048]{1,0:T(8,128)(2,1)S(1)}, bf16[64,2048]{1,0:T(8,128)(2,1)S(1)}, u32[]{:S(2)}, u32[]{:S(2)}) collective-permute-start(bf16[64,2048]{1,0:T(8,128)(2,1)S(1)} %get-tuple-element.181), channel_id=1, source_target_pairs={{0,4},{1,5},{2,6},{3,7},{4,0},{5,1},{6,2},{7,3},{8,12},{9,13},{10,... | collective-permute-start | bytes 786440 | tf_op jit(solution)/shard_map/ppermute | solution.py:859
  344.5 28.4 %collective-permute-start.58 = (bf16[64,2048]{1,0:T(8,128)(2,1)S(1)}, bf16[64,2048]{1,0:T(8,128)(2,1)S(1)}, u32[]{:S(2)}, u32[]{:S(2)}) collective-permute-start(bf16[64,2048]{1,0:T(8,128)(2,1)S(1)} %get-tuple-element.180), channel_id=1, source_target_pairs={{0,2},{1,3},{2,0},{3,1},{4,6},{5,7},{6,4},{7,5},{8,10},{9,11},{10,... | collective-permute-start | bytes 786440 | tf_op jit(solution)/shard_map/ppermute | solution.py:859
  350.6 16.4 %collective-permute-start.50 = (bf16[64,512]{1,0:T(8,128)(2,1)S(1)}, bf16[64,512]{1,0:T(8,128)(2,1)S(1)}, u32[]{:S(2)}, u32[]{:S(2)}) collective-permute-start(bf16[64,512]{1,0:T(8,128)(2,1)S(1)} %get-tuple-element.198), channel_id=1, source_target_pairs={{0,4},{1,5},{2,6},{3,7},{4,0},{5,1},{6,2},{7,3},{8,12},{9,13},{10,... | collective-permute-start | bytes 196616 | tf_op jit(solution)/shard_map/ppermute | solution.py:859
  369.9 18.6 %collective-permute-start.68 = (bf16[128,1024]{1,0:T(8,128)(2,1)S(1)}, bf16[128,1024]{1,0:T(8,128)(2,1)S(1)}, u32[]{:S(2)}, u32[]{:S(2)}) collective-permute-start(bf16[128,1024]{1,0:T(8,128)(2,1)S(1)} %get-tuple-element.176), channel_id=1, source_target_pairs={{0,4},{1,5},{2,6},{3,7},{4,0},{5,1},{6,2},{7,3},{8,12},{9,13},{10,... | collective-permute-start | bytes 786440 | tf_op jit(solution)/shard_map/ppermute | solution.py:859
  371.7 16.8 %collective-permute-start.67 = (bf16[128,1024]{1,0:T(8,128)(2,1)S(1)}, bf16[128,1024]{1,0:T(8,128)(2,1)S(1)}, u32[]{:S(2)}, u32[]{:S(2)}) collective-permute-start(bf16[128,1024]{1,0:T(8,128)(2,1)S(1)} %get-tuple-element.175), channel_id=1, source_target_pairs={{0,2},{1,3},{2,0},{3,1},{4,6},{5,7},{6,4},{7,5},{8,10},{9,11},{10,... | collective-permute-start | bytes 786440 | tf_op jit(solution)/shard_map/ppermute | solution.py:859
  396.0 36.5 %collective-permute-start.71 = (bf16[256,1024]{1,0:T(8,128)(2,1)}, bf16[256,1024]{1,0:T(8,128)(2,1)}, u32[]{:S(2)}, u32[]{:S(2)}) collective-permute-start(bf16[256,1024]{1,0:T(8,128)(2,1)} %pad_maximum_fusion.1), channel_id=1, source_target_pairs={{0,8},{8,0},{16,24},{24,16},{1,9},{9,1},{17,25},{25,17},{2,10},{10... | collective-permute-start | bytes 1572872 | tf_op jit(solution)/shard_map/ppermute | solution.py:859
  (121 other events, 2118.1 us)
Sparse Core Ops, SparseCore 0:
  136.8 107.8 all-gather.1

commit v2 on v1

--- a/solution.py
+++ b/solution.py
@@ -350,9 +350,7 @@
 
 def attend_kernel(peers, items, rows, meta_ref, far_ref, line_ref, *refs):
     parts = refs[:peers]
-    outs = refs[peers:2 * peers]
-    wide_ref, log_ref = refs[2 * peers:2 * peers + 2]
-    qkv, turned, bias, scores, mixed = refs[2 * peers + 2:]
+    mixed, wide_ref, log_ref, qkv, turned, bias, scores = refs[peers:]
     me = meta_ref[0]
     for slot in range(peers):
         qkv[me ^ slot] = parts[slot][...]
@@ -407,15 +405,14 @@
         return 0
 
     lax.fori_loop(0, peers, one_row, 0)
-    for slot in range(peers):
-        outs[slot][...] = mixed[me ^ slot]
 
 def attend(meta, far, line, parts, items):
     peers = len(parts)
     rows = parts[0].shape[1]
     smem = pl.BlockSpec(memory_space=pltpu.SMEM)
     vmem = pl.BlockSpec(memory_space=pltpu.VMEM)
-    shapes = [jax.ShapeDtypeStruct((rows, 128), jnp.bfloat16)] * peers + [
+    shapes = [
+        jax.ShapeDtypeStruct((peers, rows, 128), jnp.bfloat16),
         jax.ShapeDtypeStruct((peers, 128, rows), jnp.float32),
         jax.ShapeDtypeStruct((peers, 8, rows), jnp.float32),
     ]
@@ -423,30 +420,25 @@
         partial(attend_kernel, peers, items, rows),
         out_shape=shapes,
         in_specs=[smem, smem] + [vmem] * (peers + 1),
-        out_specs=[vmem] * (peers + 2),
+        out_specs=[vmem] * 3,
         scratch_shapes=[
             pltpu.VMEM((peers, 3, rows, 128), jnp.bfloat16),
             pltpu.VMEM((peers, 128, rows), jnp.bfloat16),
             pltpu.VMEM((2, rows, 2 * rows), jnp.float32),
             pltpu.VMEM((2, peers, rows, rows), jnp.float32),
-            pltpu.VMEM((peers, rows, 128), jnp.bfloat16),
         ],
-        compiler_params=pltpu.CompilerParams(vmem_limit_bytes=40 * 2**20),
+        compiler_params=pltpu.CompilerParams(vmem_limit_bytes=24 * 2**20),
         cost_estimate=pl.CostEstimate(flops=8 * 10**9, bytes_accessed=4 * 2**20, transcendentals=3 * 10**6),
         name="attend",
     )(meta, far, line, *parts)
-    return res[:peers], res[peers], res[peers + 1]
-
-def attend_back_kernel(peers, items, rows, meta_ref, far_ref, line_ref, wide_ref, log_ref, *refs):
+    return res
+
+def attend_back_kernel(peers, items, rows, meta_ref, far_ref, line_ref, wide_ref, log_ref, cot, *refs):
     parts = refs[:peers]
-    grads = refs[peers:2 * peers]
-    outs = refs[2 * peers:3 * peers]
-    all_ref, table_ref = refs[3 * peers:3 * peers + 2]
-    qkv, cot, turned, bias, near, far_sum, dkey, dvalue = refs[3 * peers + 2:]
+    all_ref, table_ref, qkv, turned, bias, near, far_sum, dkey, dvalue = refs[peers:]
     me = meta_ref[0]
     for slot in range(peers):
         qkv[me ^ slot] = parts[slot][...]
-        cot[me ^ slot] = grads[slot][...]
         turned[me ^ slot] = _turned(parts[slot][1]).astype(jnp.bfloat16)
     _put_bias(bias, line_ref, rows)
     near[...] = jnp.zeros_like(near)
@@ -505,8 +497,6 @@
     for i in range(peers):
         all_ref[i, 1] = dkey[i].astype(jnp.bfloat16)
         all_ref[i, 2] = dvalue[i].astype(jnp.bfloat16)
-    for slot in range(peers):
-        outs[slot][...] = all_ref[me ^ slot]
     wide = 2 * rows
     sub = lax.broadcasted_iota(jnp.int32, (8, wide), 0)
     for head in range(2):
@@ -526,18 +516,17 @@
     rows = parts[0].shape[1]
     smem = pl.BlockSpec(memory_space=pltpu.SMEM)
     vmem = pl.BlockSpec(memory_space=pltpu.VMEM)
-    shapes = [jax.ShapeDtypeStruct((3, rows, 128), jnp.bfloat16)] * peers + [
+    shapes = [
         jax.ShapeDtypeStruct((peers, 3, rows, 128), jnp.bfloat16),
         jax.ShapeDtypeStruct((2, 8, 2 * rows), jnp.float32),
     ]
     res = pl.pallas_call(
         partial(attend_back_kernel, peers, items, rows),
         out_shape=shapes,
-        in_specs=[smem, smem] + [vmem] * (2 * peers + 3),
-        out_specs=[vmem] * (peers + 2),
+        in_specs=[smem, smem] + [vmem] * (peers + 4),
+        out_specs=[vmem] * 2,
         scratch_shapes=[
             pltpu.VMEM((peers, 3, rows, 128), jnp.bfloat16),
-            pltpu.VMEM((peers, rows, 128), jnp.bfloat16),
             pltpu.VMEM((peers, 128, rows), jnp.bfloat16),
             pltpu.VMEM((2, rows, 2 * rows), jnp.float32),
             pltpu.VMEM((2, rows, 2 * rows), jnp.float32),
@@ -545,11 +534,11 @@
             pltpu.VMEM((peers, rows, 128), jnp.float32),
             pltpu.VMEM((peers, rows, 128), jnp.float32),
         ],
-        compiler_params=pltpu.CompilerParams(vmem_limit_bytes=40 * 2**20),
+        compiler_params=pltpu.CompilerParams(vmem_limit_bytes=24 * 2**20),
         cost_estimate=pl.CostEstimate(flops=20 * 10**9, bytes_accessed=8 * 2**20, transcendentals=3 * 10**6),
         name="attend_back",
-    )(meta, far, line, wide, logs, *parts, *grads)
-    return res[:peers], res[peers], jnp.sum(res[peers + 1], axis=1)
+    )(meta, far, line, wide, logs, grads, *parts)
+    return res[0], jnp.sum(res[1], axis=1)
 
 def plan(lengths, me, peers, rows):
     ends = jnp.cumsum(lengths)
@@ -588,204 +577,289 @@
 
 
 def _specs(*kinds):
-    places = {"s": pltpu.SMEM, "v": pltpu.VMEM, "a": pl.ANY}
+    places = {"s": pltpu.SMEM, "v": pltpu.VMEM, "h": pltpu.HBM}
     return [pl.BlockSpec(memory_space=places[kind]) for word in kinds for kind in word]
 
 
-def _params(**more):
-    return pltpu.CompilerParams(vmem_limit_bytes=44 * 2**20, **more)
+def _params(mebibytes):
+    return pltpu.CompilerParams(vmem_limit_bytes=mebibytes * 2**20)
 
 
 def project_kernel(peers, meta_ref, tokens_ref, gain_ref, shift_ref, weight_ref, *refs):
-    outs, act_ref, held, arrived = refs[:peers], refs[peers], refs[peers + 1], refs[peers + 2]
+    outs, act_ref, held, done, arrived = refs[:peers], refs[peers], refs[peers + 1], refs[peers + 2], refs[peers + 3]
     me = meta_ref[0]
+    pieces, _, span = held.shape
     copies = []
-    for slot in range(peers):
-        for block in range(3):
-            columns = _lanes(block * peers + (me ^ slot))
-            copies.append(pltpu.make_async_copy(weight_ref.at[:, columns], held.at[slot, block], arrived.at[slot, block]))
-            copies[-1].start()
+    for piece in range(pieces):
+        copies.append(pltpu.make_async_copy(weight_ref.at[:, pl.ds(piece * span, span)], held.at[piece], arrived.at[piece]))
+        copies[-1].start()
     unit, _ = _unit(tokens_ref[...].astype(jnp.float32))
     act = (unit * gain_ref[...] + shift_ref[...]).astype(jnp.bfloat16)
     act_ref[...] = act
+    for piece in range(pieces):
+        copies[piece].wait()
+        got = _dot(act, held[piece], ((1,), (0,))).astype(jnp.bfloat16)
+        for block in range(span // 128):
+            done[piece * (span // 128) + block] = got[:, 128 * block : 128 * block + 128]
     for slot in range(peers):
         for block in range(3):
-            copies[3 * slot + block].wait()
-            outs[slot][block] = _dot(act, held[slot, block], ((1,), (0,))).astype(jnp.bfloat16)
+            outs[slot][block] = done[block * peers + (me ^ slot)]
 
 
 def project(meta, tokens, gain, shift, weight, peers):
     rows, width = tokens.shape
+    span = 512
+    pieces = weight.shape[1] // span
     return pl.pallas_call(
         partial(project_kernel, peers),
         out_shape=[jax.ShapeDtypeStruct((3, rows, 128), jnp.bfloat16)] * peers + [jax.ShapeDtypeStruct((rows, width), jnp.bfloat16)],
-        in_specs=_specs("svvva"),
+        in_specs=_specs("svvvh"),
         out_specs=_specs("v" * (peers + 1)),
-        scratch_shapes=[pltpu.VMEM((peers, 3, width, 128), jnp.bfloat16), pltpu.SemaphoreType.DMA((peers, 3))],
-        compiler_params=_params(),
+        scratch_shapes=[
+            pltpu.VMEM((pieces, width, span), jnp.bfloat16),
+            pltpu.VMEM((3 * peers, rows, 128), jnp.bfloat16),
+            pltpu.SemaphoreType.DMA((pieces,)),
+        ],
+        compiler_params=_params(60),
         cost_estimate=pl.CostEstimate(flops=4 * 10**9, bytes_accessed=8 * 2**20, transcendentals=0),
         name="project",
     )(meta, tokens, gain, shift, weight)
 
 
-def merge_kernel(peers, meta_ref, tokens_ref, gain_ref, shift_ref, weight_ref, *refs):
-    parts = refs[:peers]
-    low_ref, middle_ref, act_ref = refs[peers:]
-    me = meta_ref[0]
-    for slot in range(peers):
-        low_ref[:, _lanes(me ^ slot)] = parts[slot][...]
+def merge_kernel(parts_ref, tokens_ref, gain_ref, shift_ref, weight_ref, low_ref, middle_ref, act_ref):
+    for part in range(parts_ref.shape[0]):
+        low_ref[:, 128 * part : 128 * part + 128] = parts_ref[part]
     middle = tokens_ref[...].astype(jnp.float32) + _dot(low_ref[...], weight_ref[...], ((1,), (0,)))
     middle_ref[...] = middle
     unit, _ = _unit(middle)
     act_ref[...] = (unit * gain_ref[...] + shift_ref[...]).astype(jnp.bfloat16)
 
 
-def merge(meta, tokens, gain, shift, weight, parts):
-    shape, peers = tokens.shape, len(parts)
+def merge(parts, tokens, gain, shift, weight):
     return pl.pallas_call(
-        partial(merge_kernel, peers),
-        out_shape=[jax.ShapeDtypeStruct(shape, t) for t in (jnp.bfloat16, jnp.float32, jnp.bfloat16)],
-        in_specs=_specs("svvvv", "v" * peers),
+        merge_kernel,
+        out_shape=[jax.ShapeDtypeStruct(tokens.shape, t) for t in (jnp.bfloat16, jnp.float32, jnp.bfloat16)],
+        in_specs=_specs("vvvvv"),
         out_specs=_specs("vvv"),
-        compiler_params=_params(),
+        compiler_params=_params(16),
         cost_estimate=pl.CostEstimate(flops=10**9, bytes_accessed=5 * 2**20, transcendentals=0),
         name="merge",
-    )(meta, tokens, gain, shift, weight, *parts)
+    )(parts, tokens, gain, shift, weight)
+
+
+def _both(ref, mine, other):
+    rows = mine.shape[0]
+    ref[:rows] = mine[...]
+    ref[rows:] = other[...]
+
+
+def _whole(*shape):
+    return pl.BlockSpec(shape, lambda step, meta_ref: (0,) * len(shape))
+
+
+def _across(rows, columns):
+    return pl.BlockSpec((rows, columns), lambda step, meta_ref: (0, step))
+
+
+def pull_kernel(meta_ref, mine, other, contract_ref, out_ref, grads):
+    @pl.when(pl.program_id(0) == 0)
+    def _():
+        _both(grads, mine, other)
+
+    out_ref[...] = _dot(grads[...], contract_ref[...], ((1,), (1,)))
+
+
+def pull(meta, mine, other, contract_weight, peers):
+    rows, width = mine.shape
+    part = contract_weight.shape[0] // (2 * peers)
+    return pl.pallas_call(
+        pull_kernel,
+        out_shape=jax.ShapeDtypeStruct((2 * rows, peers * part), jnp.float32),
+        grid_spec=pltpu.PrefetchScalarGridSpec(
+            num_scalar_prefetch=1,
+            grid=(peers,),
+            in_specs=[_whole(rows, width)] * 2 + [pl.BlockSpec((part, width), lambda step, meta_ref: (2 * step + meta_ref[3], 0))],
+            out_specs=_across(2 * rows, part),
+            scratch_shapes=[pltpu.VMEM((2 * rows, width), jnp.bfloat16)],
+        ),
+        compiler_params=_params(16),
+        cost_estimate=pl.CostEstimate(flops=3 * 10**9, bytes_accessed=9 * 2**20, transcendentals=0),
+        name="pull",
+    )(meta, mine, other, contract_weight)
 
 
 def feed_kernel(
-    peers, rows, part, meta_ref, act_mine, act_other, grad_mine, grad_other, expand_ref, contract_ref,
-    out_keep, out_send, in_keep, in_send, c_one_keep, c_one_send, c_two_keep, c_two_send,
-    e_one_keep, e_one_send, e_two_keep, e_two_send, acts, grads, out_total, in_total, block_grad,
+    rows, part, meta_ref, act_mine, act_other, grad_mine, grad_other, pulled_ref, expand_ref,
+    in_keep, in_send, low_ref, back_ref, one_keep, one_send, two_keep, two_send, acts, grads, total,
 ):
     step = pl.program_id(0)
     x, y = meta_ref[1], meta_ref[2]
-    cut = c_one_keep.shape[2]
-    group = block_grad.shape[1]
-    half = group // 2
+    cut, half = one_keep.shape[2], part // 2
 
     @pl.when(step == 0)
     def _():
-        acts[:rows] = act_mine[...]
-        acts[rows:] = act_other[...]
-        grads[:rows] = grad_mine[...]
-        grads[rows:] = grad_other[...]
+        _both(acts, act_mine, act_other)
+        _both(grads, grad_mine, grad_other)
+        total[...] = jnp.zeros_like(total)
 
     before = _dot(acts[...], expand_ref[...], ((1,), (0,)))
-    pulled = _dot(grads[...], contract_ref[...], ((1,), (1,)))
     rate = 0.5 * (1.0 + lax.erf(before * math.sqrt(0.5)))
     low = (before * rate).astype(jnp.bfloat16)
+    low_ref[...] = low
+    contract_grad = _dot(low, grads[...], ((0,), (0,))).astype(jnp.bfloat16)
     slope = rate + before * jnp.exp(-0.5 * before * before) * (1.0 / math.sqrt(2.0 * math.pi))
-    back = (pulled * slope).astype(jnp.bfloat16)
-    out_part = _dot(low, contract_ref[...], ((1,), (0,)))
-    in_part = _dot(back, expand_ref[...], ((1,), (1,)))
-
-    @pl.when(step == 0)
-    def _():
-        out_total[...] = out_part
-        in_total[...] = in_part
-
-    @pl.when(step > 0)
-    def _():
-        out_total[...] += out_part
-        in_total[...] += in_part
-
-    contract_grad = _dot(low, grads[...], ((0,), (0,))).astype(jnp.bfloat16)
+    back = (pulled_ref[...] * slope).astype(jnp.bfloat16)
+    back_ref[...] = back
+    total[...] += _dot(back, expand_ref[...], ((1,), (1,)))
     level = step // 2
 
     @pl.when(step % 2 == x)
     def _():
-        c_one_keep[level] = contract_grad[:, :cut]
+        one_keep[level] = contract_grad[:, :cut]
 
     @pl.when(step % 2 != x)
     def _():
-        c_one_send[level] = contract_grad[:, :cut]
+        one_send[level] = contract_grad[:, :cut]
 
     @pl.when(y == 0)
     def _():
-        c_two_keep[step] = contract_grad[: part // 2, cut:]
-        c_two_send[step] = contract_grad[part // 2 :, cut:]
+        two_keep[step] = contract_grad[:half, cut:]
+        two_send[step] = contract_grad[half:, cut:]
 
     @pl.when(y != 0)
     def _():
-        c_two_keep[step] = contract_grad[part // 2 :, cut:]
-        c_two_send[step] = contract_grad[: part // 2, cut:]
-
-    expand_grad = _dot(acts[...], back, ((0,), (0,))).astype(jnp.bfloat16)
-    block_grad[...] = expand_grad.reshape(peers, group, part)
-    near = peers // 2
-
-    @pl.when(step < near)
-    def _():
-        columns = pl.ds(pl.multiple_of(step * part, part), part)
-        for place in range(near):
-            e_one_keep[place, :, columns] = block_grad[2 * place + x]
-            e_one_send[place, :, columns] = block_grad[2 * place + 1 - x]
-
-    @pl.when(step >= near)
-    def _():
-        columns = pl.ds(pl.multiple_of((step - near) * part, part), part)
-        for place in range(peers):
-            e_two_keep[place, :, columns] = block_grad[place, pl.ds(pl.multiple_of(y * half, half), half), :]
-            e_two_send[place, :, columns] = block_grad[place, pl.ds(pl.multiple_of((1 - y) * half, half), half), :]
-
-    @pl.when(step == peers - 1)
-    def _():
-        out_keep[...] = out_total[:rows]
-        out_send[...] = out_total[rows:].astype(jnp.bfloat16)
-        in_keep[...] = in_total[:rows]
-        in_send[...] = in_total[rows:]
-
-
-def feed(meta, act_mine, act_other, grad_mine, grad_other, expand_weight, contract_weight, peers):
+        two_keep[step] = contract_grad[half:, cut:]
+        two_send[step] = contract_grad[:half, cut:]
+
+    @pl.when(step == pl.num_programs(0) - 1)
+    def _():
+        in_keep[...] = total[:rows]
+        in_send[...] = total[rows:]
+
+
+def feed(meta, act_mine, act_other, grad_mine, grad_other, pulled, expand_weight, peers):
     rows, width = act_mine.shape
     part = expand_weight.shape[1] // (2 * peers)
-    group, cut = width // peers, width // 2
-    whole = lambda *shape: pl.BlockSpec(shape, lambda step, meta_ref: (0,) * len(shape))
+    cut = width // 2
     shapes = [
         ((rows, width), jnp.float32),
-        ((rows, width), jnp.bfloat16),
         ((rows, width), jnp.float32),
-        ((rows, width), jnp.float32),
+        ((2 * rows, peers * part), jnp.bfloat16),
+        ((2 * rows, peers * part), jnp.bfloat16),
         ((peers // 2, part, cut), jnp.bfloat16),
         ((peers // 2, part, cut), jnp.bfloat16),
         ((peers, part // 2, cut), jnp.bfloat16),
         ((peers, part // 2, cut), jnp.bfloat16),
-        ((peers // 2, group, part * peers // 2), jnp.bfloat16),
-        ((peers // 2, group, part * peers // 2), jnp.bfloat16),
-        ((peers, group // 2, part * peers // 2), jnp.bfloat16),
-        ((peers, group // 2, part * peers // 2), jnp.bfloat16),
     ]
     return pl.pallas_call(
-        partial(feed_kernel, peers, rows, part),
+        partial(feed_kernel, rows, part),
         out_shape=[jax.ShapeDtypeStruct(*shape) for shape in shapes],
         grid_spec=pltpu.PrefetchScalarGridSpec(
             num_scalar_prefetch=1,
             grid=(peers,),
-            in_specs=[whole(rows, width)] * 4
-            + [
-                pl.BlockSpec((width, part), lambda step, meta_ref: (0, 2 * step + meta_ref[3])),
-                pl.BlockSpec((part, width), lambda step, meta_ref: (2 * step + meta_ref[3], 0)),
-            ],
-            out_specs=[whole(*shape) for shape, _ in shapes],
+            in_specs=[_whole(rows, width)] * 4
+            + [_across(2 * rows, part), pl.BlockSpec((width, part), lambda step, meta_ref: (0, 2 * step + meta_ref[3]))],
+            out_specs=[_whole(rows, width)] * 2 + [_across(2 * rows, part)] * 2 + [_whole(*shape) for shape, _ in shapes[4:]],
             scratch_shapes=[
                 pltpu.VMEM((2 * rows, width), jnp.bfloat16),
                 pltpu.VMEM((2 * rows, width), jnp.bfloat16),
                 pltpu.VMEM((2 * rows, width), jnp.float32),
+            ],
+        ),
+        compiler_params=_params(40),
+        cost_estimate=pl.CostEstimate(flops=10 * 10**9, bytes_accessed=20 * 2**20, transcendentals=2 * 10**6),
+        name="feed",
+    )(meta, act_mine, act_other, grad_mine, grad_other, pulled, expand_weight)
+
+
+def weigh_kernel(
+    peers, rows, part, meta_ref, act_mine, act_other, mix_mine, mix_other, right_mine, right_other, low_ref, back_ref, contract_ref,
+    out_keep, out_send, one_keep, one_send, two_keep, two_send, turned, total, block_grad,
+):
+    step = pl.program_id(0)
+    x, y = meta_ref[1], meta_ref[2]
+    group = block_grad.shape[1]
+    half, near = group // 2, peers // 2
+
+    def over_x(columns):
+        for place in range(near):
+            one_keep[place, :, columns] = block_grad[2 * place + x]
+            one_send[place, :, columns] = block_grad[2 * place + 1 - x]
+
+    def over_y(columns):
+        for place in range(peers):
+            two_keep[place, :, columns] = block_grad[place, pl.ds(pl.multiple_of(y * half, half), half), :]
+            two_send[place, :, columns] = block_grad[place, pl.ds(pl.multiple_of((1 - y) * half, half), half), :]
+
+    @pl.when(step == 0)
+    def _():
+        turned[:, :rows] = _turned(mix_mine[...]).astype(jnp.bfloat16)
+        turned[:, rows:] = _turned(mix_other[...]).astype(jnp.bfloat16)
+        right = jnp.concatenate([right_mine[...], right_other[...]])
+        grad = _dot(turned[...], right, ((1,), (0,))).astype(jnp.bfloat16)
+        tail = pl.ds(near * part, part)
+        block_grad[...] = grad[:, :part].reshape(peers, group, part)
+        over_x(tail)
+        block_grad[...] = grad[:, part:].reshape(peers, group, part)
+        over_y(tail)
+        turned[:, :rows] = _turned(act_mine[...]).astype(jnp.bfloat16)
+        turned[:, rows:] = _turned(act_other[...]).astype(jnp.bfloat16)
+        total[...] = jnp.zeros_like(total)
+
+    total[...] += _dot(low_ref[...], contract_ref[...], ((1,), (0,)))
+    block_grad[...] = _dot(turned[...], back_ref[...], ((1,), (0,))).astype(jnp.bfloat16).reshape(peers, group, part)
+
+    @pl.when(step < near)
+    def _():
+        over_x(pl.ds(pl.multiple_of(step * part, part), part))
+
+    @pl.when(step >= near)
+    def _():
+        over_y(pl.ds(pl.multiple_of((step - near) * part, part), part))
+
+    @pl.when(step == peers - 1)
+    def _():
+        out_keep[...] = total[:rows]
+        out_send[...] = total[rows:].astype(jnp.bfloat16)
+
+
+def weigh(meta, act_mine, act_other, mix_mine, mix_other, right_mine, right_other, low, back, contract_weight, peers):
+    rows, width = act_mine.shape
+    part = contract_weight.shape[0] // (2 * peers)
+    group, span = width // peers, part * (peers // 2 + 1)
+    shapes = [
+        ((rows, width), jnp.float32),
+        ((rows, width), jnp.bfloat16),
+        ((peers // 2, group, span), jnp.bfloat16),
+        ((peers // 2, group, span), jnp.bfloat16),
+        ((peers, group // 2, span), jnp.bfloat16),
+        ((peers, group // 2, span), jnp.bfloat16),
+    ]
+    return pl.pallas_call(
+        partial(weigh_kernel, peers, rows, part),
+        out_shape=[jax.ShapeDtypeStruct(*shape) for shape in shapes],
+        grid_spec=pltpu.PrefetchScalarGridSpec(
+            num_scalar_prefetch=1,
+            grid=(peers,),
+            in_specs=[_whole(rows, width)] * 4
+            + [_whole(rows, width // 2)] * 2
+            + [_across(2 * rows, part)] * 2
+            + [pl.BlockSpec((part, width), lambda step, meta_ref: (2 * step + meta_ref[3], 0))],
+            out_specs=[_whole(*shape) for shape, _ in shapes],
+            scratch_shapes=[
+                pltpu.VMEM((width, 2 * rows), jnp.bfloat16),
                 pltpu.VMEM((2 * rows, width), jnp.float32),
                 pltpu.VMEM((peers, group, part), jnp.bfloat16),
             ],
         ),
-        compiler_params=_params(),
-        cost_estimate=pl.CostEstimate(flops=13 * 10**9, bytes_accessed=24 * 2**20, transcendentals=2 * 10**6),
-        name="feed",
-    )(meta, act_mine, act_other, grad_mine, grad_other, expand_weight, contract_weight)
-
-
-def turn_kernel(peers, meta_ref, in_mine, in_other, middle_ref, grad_ref, gain_ref, weight_ref, *refs):
-    outs = refs[:peers]
-    total_ref, keep_ref, send_ref, sums_ref, held = refs[peers:]
-    me, core = meta_ref[0], meta_ref[3]
+        compiler_params=_params(36),
+        cost_estimate=pl.CostEstimate(flops=8 * 10**9, bytes_accessed=20 * 2**20, transcendentals=0),
+        name="weigh",
+    )(meta, act_mine, act_other, mix_mine, mix_other, right_mine, right_other, low, back, contract_weight)
+
+
+def turn_kernel(meta_ref, in_mine, in_other, middle_ref, grad_ref, gain_ref, weight_ref, heads_ref, total_ref, keep_ref, send_ref, sums_ref):
+    core = meta_ref[3]
     half = keep_ref.shape[1]
     unit, scale = _unit(middle_ref[...])
     total = grad_ref[...].astype(jnp.float32) + _norm_back(in_mine[...] + in_other[...], unit, scale, gain_ref[...], sums_ref)
@@ -802,56 +876,81 @@
         keep_ref[...] = low[:, half:]
         send_ref[...] = low[:, :half]
 
-    held[...] = _dot(low, weight_ref[...], ((1,), (1,))).astype(jnp.bfloat16)
-    for slot in range(peers):
-        outs[slot][...] = held[:, _lanes(me ^ slot)]
+    heads = _dot(low, weight_ref[...], ((1,), (1,))).astype(jnp.bfloat16)
+    for part in range(heads_ref.shape[0]):
+        heads_ref[part] = heads[:, 128 * part : 128 * part + 128]
 
 
 def turn(meta, in_mine, in_other, middle, grad, gain, weight, peers):
     rows, width = middle.shape
-    shapes = [((rows, 128), jnp.bfloat16)] * peers + [
+    shapes = [
+        ((peers, rows, width // peers), jnp.bfloat16),
         ((rows, width), jnp.float32),
         ((rows, width // 2), jnp.bfloat16),
         ((rows, width // 2), jnp.bfloat16),
         ((2, width), jnp.float32),
     ]
     return pl.pallas_call(
-        partial(turn_kernel, peers),
+        turn_kernel,
         out_shape=[jax.ShapeDtypeStruct(*shape) for shape in shapes],
         in_specs=_specs("svvvvvv"),
         out_specs=_specs("v" * len(shapes)),
-        scratch_shapes=[pltpu.VMEM((rows, width), jnp.bfloat16)],
-        compiler_params=_params(),
+        compiler_params=_params(20),
         cost_estimate=pl.CostEstimate(flops=10**9, bytes_accessed=8 * 2**20, transcendentals=0),
         name="turn",
     )(meta, in_mine, in_other, middle, grad, gain, weight)
 
 
-def close_kernel(peers, meta_ref, tokens_ref, grad_ref, gain_ref, weight_ref, *refs):
-    parts = refs[:peers]
-    out_ref, sums_ref, held = refs[peers:]
-    me = meta_ref[0]
-    for slot in range(peers):
+def close_kernel(parts_ref, tokens_ref, grad_ref, gain_ref, weight_ref, out_ref, sums_ref, held):
+    peers = parts_ref.shape[0]
+    for peer in range(peers):
         for block in range(3):
-            held[:, _lanes(block * peers + (me ^ slot))] = parts[slot][block]
+            at = 128 * (block * peers + peer)
+            held[:, at : at + 128] = parts_ref[peer, block]
     back = _dot(held[...], weight_ref[...], ((1,), (1,)))
     unit, scale = _unit(tokens_ref[...].astype(jnp.float32))
     out_ref[...] = grad_ref[...] + _norm_back(back, unit, scale, gain_ref[...], sums_ref)
 
 
-def close(meta, tokens, grad, gain, weight, parts):
+def close(parts, tokens, grad, gain, weight):
     rows, width = tokens.shape
-    peers = len(parts)
     return pl.pallas_call(
-        partial(close_kernel, peers),
+        close_kernel,
         out_shape=[jax.ShapeDtypeStruct((rows, width), jnp.float32), jax.ShapeDtypeStruct((2, width), jnp.float32)],
-        in_specs=_specs("svvvv", "v" * peers),
+        in_specs=_specs("vvvvv"),
         out_specs=_specs("vv"),
         scratch_shapes=[pltpu.VMEM((rows, 3 * width), jnp.bfloat16)],
-        compiler_params=_params(),
+        compiler_params=_params(24),
         cost_estimate=pl.CostEstimate(flops=2 * 10**9, bytes_accessed=10 * 2**20, transcendentals=0),
         name="close",
-    )(meta, tokens, grad, gain, weight, *parts)
+    )(parts, tokens, grad, gain, weight)
+
+
+def attend_weigh_kernel(meta_ref, act_ref, back_ref, keep_ref, send_ref, held):
+    core = meta_ref[3]
+    peers, _, half, _ = held.shape
+    for block in range(3):
+        back = jnp.concatenate([back_ref[peer, block] for peer in range(peers)])
+        grad = jnp.transpose(_dot(back, act_ref[...], ((0,), (0,)))).astype(jnp.bfloat16)
+        held[:, :, :, 128 * block : 128 * block + 128] = grad.reshape(peers, 2, half, 128)
+    for peer in range(peers):
+        keep_ref[peer] = held[peer, core]
+        send_ref[peer] = held[peer, 1 - core]
+
+
+def attend_weigh(meta, act, back):
+    peers = back.shape[0]
+    shape = (peers, act.shape[1] // (2 * peers), 3 * back.shape[3])
+    return pl.pallas_call(
+        attend_weigh_kernel,
+        out_shape=[jax.ShapeDtypeStruct(shape, jnp.bfloat16)] * 2,
+        in_specs=_specs("svv"),
+        out_specs=_specs("vv"),
+        scratch_shapes=[pltpu.VMEM((peers, 2) + shape[1:], jnp.bfloat16)],
+        compiler_params=_params(20),
+        cost_estimate=pl.CostEstimate(flops=3 * 10**9, bytes_accessed=7 * 2**20, transcendentals=0),
+        name="attend_weigh",
+    )(meta, act, back)
 
 
 def flipped(array, axis, mask):
@@ -873,26 +972,46 @@
     return jnp.concatenate([lower, upper], axis=axis)
 
 
-def over_chips(one_keep, one_send, two_keep, two_send, place):
-    z, x, y = place
+def after(value, *others):
+    return lax.optimization_barrier((value, others))[0]
+
+
+def over_first(one_keep, one_send, two_keep, two_send):
+    return one_keep, flipped(one_send, "blk", 1), two_keep, flipped(two_send, "seq", 2)
+
+
+def over_second(place, one_keep, one_got, two_keep, two_got):
+    _, x, y = place
     levels, rows, cut = one_keep.shape
-    half = rows // 2
-    one_got = flipped(one_send, "blk", 1)
-    two_got = flipped(two_send, "seq", 2)
-
-    def sums(keep, got, shape, index, axis):
-        return added(pick(keep.reshape(shape), index, axis), pick(got.reshape(shape), index, axis))
-
-    tall, wide = (levels, 2, half, cut), (levels, 2, half, cut)
-    one_next = flipped(sums(one_keep, one_got, tall, 1 - y, 1), "seq", 2)
-    two_next = flipped(sums(two_keep, two_got, wide, 1 - x, 1), "blk", 1)
-    one = added(sums(one_keep, one_got, tall, y, 1), one_next)
-    two = added(sums(two_keep, two_got, wide, x, 1), two_next)
-    both = jnp.concatenate([one, two], axis=-1)
-    total = pick(both, z, 0).astype(jnp.float32)
-    for step in range(1, levels):
-        total = total + flipped(pick(both, z ^ step, 0), "blk", 2 * step).astype(jnp.float32)
-    return total.astype(jnp.bfloat16)
+    shape = (levels, 2, rows // 2, cut)
+
+    def sums(keep, got, index):
+        return added(pick(keep.reshape(shape), index, 1), pick(got.reshape(shape), index, 1))
+
+    one_next = flipped(sums(one_keep, one_got, 1 - y), "seq", 2)
+    two_next = flipped(sums(two_keep, two_got, 1 - x), "blk", 1)
+    return sums(one_keep, one_got, y), one_next, sums(two_keep, two_got, x), two_next
+
+
+def over_near(place, one, one_next, two, two_next):
+    side = place[0] % 2
+    levels = one.shape[0]
+    shape = (levels // 2, 2) + one.shape[1:]
+
+    def of(index):
+        parts = [(pick(a.reshape(shape), index, 1), pick(b.reshape(shape), index, 1)) for a, b in ((one, one_next), (two, two_next))]
+        return jnp.concatenate([added(a, b) for a, b in parts], axis=-1)
+
+    return of(side), flipped(of(1 - side), "blk", 2)
+
+
+def over_far(place, keep, got):
+    upper = place[0] // 2
+
+    def of(index):
+        return added(pick(keep, index, 0), pick(got, index, 0))
+
+    return of(upper), flipped(of(1 - upper), "blk", 4)
 
 
 def local_by_heads(
@@ -933,59 +1052,57 @@
     lines = jnp.dot(table_mine.T, hot, precision=highest)
     far = table_mine[buckets - 1]
 
-    def exchanged(parts):
-        return [parts[0]] + [flipped(parts[step], "blk", step) for step in range(1, peers)]
-
-    def ordered(parts):
-        stack = jnp.stack(parts)
-        return jnp.stack([pick(stack, me ^ peer, 0) for peer in range(peers)])
+    def to_all(array):
+        return lax.all_to_all(array, "blk", split_axis=0, concat_axis=0, tiled=True)
 
     *parts, act_first = project(here, own, gain_first, shift_first, attend_weight, peers)
-    parts = exchanged(parts)
-    act_all = lax.all_gather(act_first, "blk", axis=0, tiled=True)
-    mixed, wide, logs = attend(meta, far, lines, parts, items)
-    attn_low, middle, act_second = merge(here, own, gain_second, shift_second, merge_weight, exchanged(mixed))
+    parts = [parts[0]] + [flipped(parts[step], "blk", step) for step in range(1, peers)]
+    pulled = pull(here, grad_out, grad_other, contract_weight, peers)
+    mixed, wide, logs = attend(meta, after(far, pulled), lines, parts, items)
+    act_all = lax.all_gather(after(act_first, mixed), "blk", axis=0, tiled=True)
+    attn_low, middle, act_second = merge(to_all(mixed), own, gain_second, shift_second, merge_weight)
     act_other = flipped(act_second, "seq", 1)
-    out_keep, out_send, in_keep, in_send, *grads = feed(
-        here, act_second, act_other, grad_out, grad_other, expand_weight, contract_weight, peers
-    )
-    *grad_heads, grad_middle, keep_low, send_low, sums_second = turn(
+    attn_other = flipped(attn_low, "seq", 1)
+    in_keep, in_send, hidden_low, hidden_back, *contract_parts = feed(
+        here, act_second, act_other, grad_out, grad_other, pulled, expand_weight, peers
+    )
+    grad_heads, grad_middle, keep_low, send_low, sums_second = turn(
         here, in_keep, flipped(in_send, "seq", 1), middle, grad_out, gain_second, merge_weight, peers
     )
-    back_parts, back_all, line_grad = attend_back(meta, far, lines, wide, logs, parts, exchanged(grad_heads), items)
-    tokens_grad, sums_first = close(here, own, grad_middle, gain_first, attend_weight, exchanged(back_parts))
+    contract_parts = over_first(*contract_parts)
+    out_keep, out_send, *expand_parts = weigh(
+        here, act_second, act_other, attn_low, attn_other, keep_low, flipped(send_low, "seq", 1), hidden_low, hidden_back, contract_weight, peers
+    )
+    expand_parts = over_first(*expand_parts)
+
+    grad_heads, out_send, *contract_parts = lax.optimization_barrier((to_all(grad_heads), out_send, *contract_parts))
+    contract_parts = over_second(place, *contract_parts)
+    back_all, line_grad = attend_back(meta, far, lines, wide, logs, parts, grad_heads, items)
+    act_all, back_all, *sums = lax.optimization_barrier((act_all, back_all, *contract_parts, *expand_parts))
+    contract_parts = over_near(place, *sums[:4])
+    expand_parts = over_second(place, *sums[4:])
+    attend_keep, attend_send = attend_weigh(here, act_all, back_all)
+    owned, attend_keep, attend_send, *sums = lax.optimization_barrier((to_all(back_all), attend_keep, attend_send, *contract_parts, *expand_parts))
+    contract_parts = over_far(place, *sums[:2])
+    expand_parts = over_near(place, *sums[2:])
     output = (middle + out_keep + flipped(out_send, "seq", 1).astype(jnp.float32)).astype(jnp.bfloat16)
-
-    contract_grad = over_chips(*grads[:4], place)
-    expand_grad = over_chips(*grads[4:], place)
-    attn_both = jnp.concatenate([attn_low, flipped(attn_low, "seq", 1)])
-    merge_right = jnp.concatenate([keep_low, flipped(send_low, "seq", 1)])
-    merge_grad = jnp.einsum("td,te->de", attn_both, merge_right, preferred_element_type=jnp.float32).astype(jnp.bfloat16)
-    merge_grad = merge_grad.reshape(levels, 2, group, width // 2)
-    one, two = merge_grad[..., : width // 4], merge_grad[..., width // 4 :].reshape(levels, 2, 2, group // 2, width // 4)
-    merge_grad = over_chips(pick(one, x, 1), pick(one, 1 - x, 1), pick(two, y, 2), pick(two, 1 - y, 2), place)
-    attend_grad = jnp.einsum(
-        "td,te->de",
-        act_all,
-        back_all.transpose(0, 2, 1, 3).reshape(peers * rows, 3 * group),
-        preferred_element_type=jnp.float32,
-    ).astype(jnp.bfloat16)
-    attend_grad = attend_grad.reshape(peers, 2, group // 2, 3 * group)
-    attend_grad = added(pick(attend_grad, core, 1), flipped(pick(attend_grad, 1 - core, 1), "seq", 1))
-    attend_grad = attend_grad.reshape(peers, 2, group // 4, 3 * group)
-    attend_grad = added(pick(attend_grad, y, 1), flipped(pick(attend_grad, 1 - y, 1), "seq", 2))
-    attend_grad = ordered(exchanged([pick(attend_grad, me ^ slot, 0) for slot in range(peers)]))
+    tokens_grad, sums_first = close(owned, own, grad_middle, gain_first, attend_weight)
+    contract_grad = added(*contract_parts)
+    expand_grad = added(*over_far(place, *expand_parts))
+    attend_keep = added(attend_keep, flipped(attend_send, "seq", 1)).reshape(peers, 2, group // 4, 3 * group)
+    attend_keep, attend_send = pick(attend_keep, y, 1), pick(attend_keep, 1 - y, 1)
+
+    attend_grad = to_all(added(attend_keep, flipped(attend_send, "seq", 2)))
 
     contract_grad = in_order(contract_grad, flipped(contract_grad, "seq", 2), y, 0)
     contract_grad = in_order(contract_grad, flipped(contract_grad, "seq", 1), core, 0).astype(jnp.float32)
+    span = part * (peers // 2 + 1)
     expand_grad = in_order(expand_grad, flipped(expand_grad, "seq", 2), y, 0)
     expand_other = flipped(expand_grad, "seq", 1)
-    expand_halves = [jnp.where(core == side, expand_grad, expand_other) for side in range(2)]
-    expand_grad = jnp.concatenate(
-        [expand_halves[side][:, part * peer : part * (peer + 1)] for peer in range(peers) for side in range(2)], axis=1
-    ).astype(jnp.float32)
-    merge_grad = in_order(merge_grad, flipped(merge_grad, "seq", 2), y, 0)
-    merge_grad = in_order(merge_grad, flipped(merge_grad, "seq", 1), core, 1).astype(jnp.float32)
+    halves = [jnp.where(core == side, expand_grad, expand_other).astype(jnp.float32) for side in range(2)]
+    at = [part * peer if peer < peers // 2 else part * (peer + 1) for peer in range(peers)]
+    expand_grad = jnp.concatenate([halves[side][:, start : start + part] for start in at for side in range(2)], axis=1)
+    merge_grad = jnp.concatenate([halves[side][:, start - part : start] for side in range(2) for start in (span, 2 * span)], axis=1)
     attend_grad = in_order(attend_grad, flipped(attend_grad, "seq", 2), y, 1)
     attend_grad = in_order(attend_grad, flipped(attend_grad, "seq", 1), core, 1)
     attend_grad = attend_grad.reshape(peers, group, 3, group).transpose(1, 2, 0, 3).reshape(group, 3 * width).astype(jnp.float32)

time: 455 us -> 342 us (0.75); the launches traced: 448 us -> 340 us
  waiting for transfers between devices: 163 us -> 76.4 us
  starting transfers between devices: 114 us -> 53.3 us
  blocking collectives: 0 us -> 35.8 us
  matrix products: 7.79 us -> 0.29 us
  other arithmetic: 25.6 us -> 31.6 us
    ppermute x77 -> x38, waiting for transfers between devices: 163 us -> 67.5 us  [flipped(): return lax.ppermute(array, axis, [(i, i ^ mask) for i in range(peers)])]
    ppermute x77 -> x38, starting transfers between devices: 114 us -> 39.5 us  [flipped(): return lax.ppermute(array, axis, [(i, i ^ mask) for i in range(peers)])]
    all_to_all x0 -> x1, blocking collectives: none -> 35.8 us  [to_all(): return lax.all_to_all(array, 'blk', split_axis=0, concat_axis=0, tiled=True)]
    all_to_all x0 -> x3, starting transfers between devices: none -> 13.8 us  [to_all(): return lax.all_to_all(array, 'blk', split_axis=0, concat_axis=0, tiled=True)]
    all_to_all x0 -> x3, waiting for transfers between devices: none -> 8.83 us  [to_all(): return lax.all_to_all(array, 'blk', split_axis=0, concat_axis=0, tiled=True)]
    pallas_call x4 -> x7, Pallas kernels: 38 us -> 45.3 us  [the longest x1 18.8 us: feed(): pl.pallas_call(partial(feed_kernel, rows, part), out_shape=[jax.ShapeDtyp...]
    dot_general x2 -> x0, matrix products: 6.9 us -> none  [the longest x1 5.05 us: local_by_heads(): jnp.einsum('td,te->de', act_all, back_all.transpose(0, 2, 1, 3).reshape(p...]
    unnamed x181 -> x167, local copies, waits for them, and re-layouts: 28.3 us -> 35 us
  transfers between devices with their start and end apart: 78 -> 42, of which waited for: 32 -> 15; matrix products, arithmetic and copies ran while one was open for 10% -> 11% of each run, Pallas kernels for 7% -> 20%
where the time goes in v2:
time: 342 us; the launch traced here: 340 us
  Pallas kernels  85 us (25%)
  waiting for transfers between devices  76.4 us (22%)
  starting transfers between devices  53.3 us (16%)
  local copies, waits for them, and re-layouts  42 us (12%)
  blocking collectives  35.8 us (10%)
  other arithmetic  31.6 us (9%)
  between operations  15.7 us (5%)
    ppermute x38, waiting for transfers between devices, flipped(): return lax.ppermute(array, axis, [(i, i ^ mask) for i in range(peers)])  67.5 us
    ppermute x38, starting transfers between devices, flipped(): return lax.ppermute(array, axis, [(i, i ^ mask) for i in range(peers)])  39.5 us
    all_to_all x1, blocking collectives, to_all(): return lax.all_to_all(array, 'blk', split_axis=0, concat_axis=0, tiled=True)  35.8 us
    unnamed x167, local copies, waits for them, and re-layouts  35 us
    pallas_call x1, Pallas kernels, attend_back(): pl.pallas_call(partial(attend_back_kernel, peers, items, rows), out_shape...  20.7 us
    pallas_call x1, Pallas kernels, feed(): pl.pallas_call(partial(feed_kernel, rows, part), out_shape=[jax.ShapeDtyp...  18.8 us
    convert_element_type x16, other arithmetic, added(): return (a.astype(jnp.float32) + b.astype(jnp.float32)).astype(jnp.bfloat16)  18.2 us
    all_to_all x3, starting transfers between devices, to_all(): return lax.all_to_all(array, 'blk', split_axis=0, concat_axis=0, tiled=True)  13.8 us
  transfers between devices with their start and end apart: 42, of which 15 were waited for; matrix products, arithmetic and copies ran while one was open for 11% of the time, Pallas kernels for 20%

profile of v2, /device:TPU:0, one launch (start us, length us, event | category | flops | bytes accessed | tf_op | source)
XLA Modules:
  0.0 340.2 jit_solution(10244280005338950264)
XLA Ops:
  8.4 6.3 %project.1 = (bf16[3,256,128]{2,1,0:T(8,128)(2,1)}, bf16[3,256,128]{2,1,0:T(8,128)(2,1)}, bf16[3,256,128]{2,1,0:T(8,128)(2,1)}, bf16[3,256,128]{2,1,0:T(8,128)(2...) custom-call(s32[4]{0:T(128)} %pad_add_fusion.1.meta_ref, ...), custom_call_target="tpu_custom_call" | custom-call | flops 4000000000 | bytes 8388608 | tf_op jit(solution)/shard_map/project/pallas_call | solution.py:613
  14.7 2.6 collective-permute-start.1
  18.9 3.0 collective-permute-start.4
  23.2 3.6 %collective-permute-start.5 = (bf16[3,256,128]{2,1,0:T(8,128)(2,1)}, bf16[3,256,128]{2,1,0:T(8,128)(2,1)S(1)}, u32[]{:S(2)}, u32[]{:S(2)}) collective-permute-start(bf16[3,256,128]{2,1,0:T(8,128)(2,1)} %get-tuple-element.84), channel_id=1, source_target_pairs={{0,5},{1,4},{2,7},{3,6},{4,1},{5,0},{6,3},{7,2},{8,13},{9,12},{10,... | collective-permute-start | bytes 589832 | tf_op jit(solution)/shard_map/ppermute | solution.py:958
  26.8 5.7 %collective-permute-done.2.refs_2_ = bf16[3,256,128]{2,1,0:T(8,128)(2,1)S(1)} collective-permute-done((bf16[3,256,128]{2,1,0:T(8,128)(2,1)}, bf16[3,256,128]{2,1,0:T(8,128)(2,1)S(1)}, u32[]{:S(2)}, u32[]{:S(2)}) %collective-permute-start.2) | collective-permute-done | bytes 196640 | tf_op jit(solution)/shard_map/ppermute | solution.py:958
  35.8 3.4 copy-done.2
  39.2 4.7 %pull.1.pulled_ref = f32[512,2048]{1,0:T(8,128)S(1)} custom-call(s32[4]{0:T(128)S(1)} %copy-done.22, bf16[256,1024]{1,0:T(8,128)(2,1)S(1)} %bitcast.160, bf16[256,1024]{1,0:T(8,128)(2,1)S(1)} %collective-permute-done.other.grad_other, bf16[4096,1024]{1,0:T(8,128)(2,1)S(1)} %copy-done.2), custom_call_target="tpu_custom_call" | custom-call | flops 3000000000 | bytes 9437184 | tf_op jit(solution)/shard_map/pull/pallas_call | solution.py:675
  46.0 4.0 %collective-permute-done.5.refs_5_ = bf16[3,256,128]{2,1,0:T(8,128)(2,1)S(1)} collective-permute-done((bf16[3,256,128]{2,1,0:T(8,128)(2,1)}, bf16[3,256,128]{2,1,0:T(8,128)(2,1)S(1)}, u32[]{:S(2)}, u32[]{:S(2)}) %collective-permute-start.5) | collective-permute-done | bytes 196640 | tf_op jit(solution)/shard_map/ppermute | solution.py:958
  50.0 12.7 %attend.1 = (bf16[8,256,128]{2,1,0:T(8,128)(2,1)S(1)}, f32[8,128,256]{2,1,0:T(8,128)S(1)}, f32[8,8,256]{2,1,0:T(8,128)S(1)}) custom-call(s32[18]{0:T(128)S(1)} %pad_add_fusion.meta_ref, f32[2]{0:T(128)S(1)} %slice_reduce_fusion.1.far_ref, f32[2,512]{1,0:T(2,128)S(1)} %fusion.27.line_ref, bf16[3,256,128]{2,1,0:T(8,128)(2,1)S(1)} %copy-done.55, ...), custom_call_target="tpu_custom_call" | custom-call | flops 8000000000 | bytes 4194304 | tf_op jit(solution)/shard_map/attend/pallas_call | solution.py:419
  63.9 35.8 %all_to_all.20.parts_ref = bf16[8,256,128]{2,1,0:T(8,128)(2,1)S(1)} all-to-all(bf16[8,256,128]{2,1,0:T(8,128)(2,1)S(1)} %get-tuple-element.87), channel_id=1, replica_groups=mesh['seq'=4,'blk'=8] {'blk'}, dimensions={0} | all-to-all | bytes 1048576 | tf_op jit(solution)/shard_map/all_to_all | solution.py:1056
  104.3 18.8 %feed.1 = (f32[256,1024]{1,0:T(8,128)S(1)}, f32[256,1024]{1,0:T(8,128)S(1)}, bf16[512,2048]{1,0:T(8,128)(2,1)S(1)}, bf16[512,2048]{1,0:T(8,128)(2,1)S(1)}, bf16[...) custom-call(s32[4]{0:T(128)S(1)} %copy-done.22, ...), custom_call_target="tpu_custom_call" | custom-call | flops 10000000000 | bytes 20971520 | tf_op jit(solution)/shard_map/feed/pallas_call | solution.py:754
  130.1 2.7 turn.1
  134.6 4.3 %all-to-all-start.1 = ((bf16[8,256,128]{2,1,0:T(8,128)(2,1)}), bf16[8,256,128]{2,1,0:T(8,128)(2,1)}, u32[]{:S(2)}, u32[]{:S(2)}) async-start(bf16[8,256,128]{2,1,0:T(8,128)(2,1)} %copy-done.19), calls=%async_computation.1 | async-start | bytes 1048576 | tf_op jit(solution)/shard_map/all_to_all | solution.py:1056
  146.0 12.1 %weigh.1 = (f32[256,1024]{1,0:T(8,128)S(1)}, bf16[256,1024]{1,0:T(8,128)(2,1)S(1)}, bf16[4,128,1280]{2,1,0:T(8,128)(2,1)S(1)}, bf16[4,128,1280]{2,1,0:T(8,128)(2...) custom-call(s32[4]{0:T(128)S(1)} %copy-done.22, bf16[256,1024]{1,0:T(8,128)(2,1)S(1)} %copy-done.29, ...), custom_call_target="tpu_custom_call" | custom-call | flops 8000000000 | bytes 20971520 | tf_op jit(solution)/shard_map/weigh/pallas_call | solution.py:838
  164.4 2.6 fusion.9
  171.4 20.7 %attend_back.1 = (bf16[8,3,256,128]{3,2,1,0:T(8,128)(2,1)S(1)}, f32[2,8,512]{2,1,0:T(8,128)S(1)}) custom-call(s32[18]{0:T(128)S(1)} %pad_add_fusion.meta_ref, f32[2]{0:T(128)S(1)} %slice_reduce_fusion.1.far_ref, f32[2,512]{1,0:T(2,128)S(1)} %fusion.27.line_ref, f32[8,128,256]{2,1,0:T(8,128)S(1)} %copy-done.58, f32[8,8,256]{2,1,0:T(8,128)S(1)} %get-tuple-element.108.log_ref, ...), custom_call_target="tpu_custom_call" | custom-call | flops 20000000000 | bytes 8388608 | tf_op jit(solution)/shard_map/attend_back/pallas_call | solution.py:523
  193.2 11.4 %collective-permute-done.16 = bf16[4,128,512]{2,1,0:T(8,128)(2,1)S(1)} collective-permute-done((bf16[4,128,512]{2,1,0:T(8,128)(2,1)S(1)}, bf16[4,128,512]{2,1,0:T(8,128)(2,1)S(1)}, u32[]{:S(2)}, u32[]{:S(2)}) %collective-permute-start.16) | collective-permute-done | bytes 524320 | tf_op jit(solution)/shard_map/ppermute | solution.py:958
  206.6 5.2 %all-to-all-start.2 = ((bf16[8,3,256,128]{3,2,1,0:T(8,128)(2,1)}), bf16[8,3,256,128]{3,2,1,0:T(8,128)(2,1)S(1)}, u32[]{:S(2)}, u32[]{:S(2)}) async-start(bf16[8,3,256,128]{3,2,1,0:T(8,128)(2,1)} %copy-done.8), calls=%async_computation.2 | async-start | bytes 3145728 | tf_op jit(solution)/shard_map/all_to_all | solution.py:1056
  214.0 2.6 fusion.5
  216.5 2.7 fusion.3
  221.3 2.7 fusion.1
  231.1 19.2 %collective-permute-done.19 = bf16[2,128,1024]{2,1,0:T(8,128)(2,1)S(1)} collective-permute-done((bf16[2,128,1024]{2,1,0:T(8,128)(2,1)S(1)}, bf16[2,128,1024]{2,1,0:T(8,128)(2,1)S(1)}, u32[]{:S(2)}, u32[]{:S(2)}) %collective-permute-start.19) | collective-permute-done | bytes 524320 | tf_op jit(solution)/shard_map/ppermute | solution.py:958
  252.0 2.8 copy-done.3
  255.5 3.4 close.1
  262.6 3.6 %collective-permute-done.34 = f32[5,1024]{1,0:T(8,128)S(1)} collective-permute-done((f32[5,1024]{1,0:T(8,128)S(1)}, f32[5,1024]{1,0:T(8,128)S(1)}, u32[]{:S(2)}, u32[]{:S(2)}) %collective-permute-start.34) | collective-permute-done | bytes 20512 | tf_op jit(solution)/shard_map/ppermute | solution.py:958
  271.4 4.5 %collective-permute-done.36 = f32[5,1024]{1,0:T(8,128)S(1)} collective-permute-done((f32[5,1024]{1,0:T(8,128)S(1)}, f32[5,1024]{1,0:T(8,128)S(1)}, u32[]{:S(2)}, u32[]{:S(2)}) %collective-permute-start.36) | collective-permute-done | bytes 20512 | tf_op jit(solution)/shard_map/ppermute | solution.py:958
  285.5 4.6 %collective-permute-done.23 = bf16[8,32,384]{2,1,0:T(8,128)(2,1)S(1)} collective-permute-done((bf16[8,32,384]{2,1,0:T(8,128)(2,1)S(1)}, bf16[8,32,384]{2,1,0:T(8,128)(2,1)S(1)}, u32[]{:S(2)}, u32[]{:S(2)}) %collective-permute-start.23) | collective-permute-done | bytes 196640 | tf_op jit(solution)/shard_map/ppermute | solution.py:958
  290.8 4.3 %all-to-all-start.3 = ((bf16[8,32,384]{2,1,0:T(8,128)(2,1)}), bf16[8,32,384]{2,1,0:T(8,128)(2,1)}, u32[]{:S(2)}, u32[]{:S(2)}) async-start(bf16[8,32,384]{2,1,0:T(8,128)(2,1)} %fusion.11), calls=%async_computation.3 | async-start | bytes 393216 | tf_op jit(solution)/shard_map/all_to_all | solution.py:1056
  296.2 2.8 collective-permute-start.27
  299.1 8.8 %all-to-all-done.3 = bf16[8,32,384]{2,1,0:T(8,128)(2,1)} async-done(((bf16[8,32,384]{2,1,0:T(8,128)(2,1)}), bf16[8,32,384]{2,1,0:T(8,128)(2,1)}, u32[]{:S(2)}, u32[]{:S(2)}) %all-to-all-start.3) | async-done | bytes 196640 | tf_op jit(solution)/shard_map/all_to_all | solution.py:1056
  309.8 4.1 %collective-permute-done.27 = bf16[64,2560]{1,0:T(8,128)(2,1)} collective-permute-done((bf16[64,2560]{1,0:T(8,128)(2,1)S(1)}, bf16[64,2560]{1,0:T(8,128)(2,1)}, u32[]{:S(2)}, u32[]{:S(2)}) %collective-permute-start.27) | collective-permute-done | bytes 327712 | tf_op jit(solution)/shard_map/ppermute | solution.py:958
  321.2 2.6 collective-permute-done.28
  (295 shorter events, 96.4 us)
Async XLA Ops:
  7.2 198.6 %all-gather.2.cloned.1.call-start = ((), (), s32[]{:S(2)}) async-start(), calls=%async_computation.4 | async-start | bytes 4718592 | tf_op jit(solution)/shard_map/all_gather | solution.py:1062
  7.2 26.8 %collective-permute-start = (bf16[256,1024]{1,0:T(8,128)(2,1)}, bf16[256,1024]{1,0:T(8,128)(2,1)S(1)}, u32[]{:S(2)}, u32[]{:S(2)}) collective-permute-start(bf16[256,1024]{1,0:T(8,128)(2,1)} %bitcast.159), channel_id=1, source_target_pairs={{0,8},{8,0},{16,24},{24,16},{1,9},{9,1},{17,25},{25,17},{2,10},{10... | collective-permute-start | bytes 1572872 | tf_op jit(solution)/shard_map/ppermute | solution.py:958
  14.7 8.5 %collective-permute-start.1 = (bf16[3,256,128]{2,1,0:T(8,128)(2,1)}, bf16[3,256,128]{2,1,0:T(8,128)(2,1)S(1)}, u32[]{:S(2)}, u32[]{:S(2)}) collective-permute-start(bf16[3,256,128]{2,1,0:T(8,128)(2,1)} %get-tuple-element.80), channel_id=1, source_target_pairs={{0,1},{1,0},{2,3},{3,2},{4,5},{5,4},{6,7},{7,6},{8,9},{9,8},{10,11... | collective-permute-start | bytes 589832 | tf_op jit(solution)/shard_map/ppermute | solution.py:958
  17.3 15.2 %collective-permute-start.2 = (bf16[3,256,128]{2,1,0:T(8,128)(2,1)}, bf16[3,256,128]{2,1,0:T(8,128)(2,1)S(1)}, u32[]{:S(2)}, u32[]{:S(2)}) collective-permute-start(bf16[3,256,128]{2,1,0:T(8,128)(2,1)} %get-tuple-element.81), channel_id=1, source_target_pairs={{0,2},{1,3},{2,0},{3,1},{4,6},{5,7},{6,4},{7,5},{8,10},{9,11},{10,... | collective-permute-start | bytes 589832 | tf_op jit(solution)/shard_map/ppermute | solution.py:958
  18.9 27.1 %collective-permute-start.3 = (bf16[3,256,128]{2,1,0:T(8,128)(2,1)}, bf16[3,256,128]{2,1,0:T(8,128)(2,1)S(1)}, u32[]{:S(2)}, u32[]{:S(2)}) collective-permute-start(bf16[3,256,128]{2,1,0:T(8,128)(2,1)} %get-tuple-element.82), channel_id=1, source_target_pairs={{0,3},{1,2},{2,1},{3,0},{4,7},{5,6},{6,5},{7,4},{8,11},{9,10},{10,... | collective-permute-start | bytes 589832 | tf_op jit(solution)/shard_map/ppermute | solution.py:958
  18.9 27.1 %collective-permute-start.4 = (bf16[3,256,128]{2,1,0:T(8,128)(2,1)}, bf16[3,256,128]{2,1,0:T(8,128)(2,1)S(1)}, u32[]{:S(2)}, u32[]{:S(2)}) collective-permute-start(bf16[3,256,128]{2,1,0:T(8,128)(2,1)} %get-tuple-element.83), channel_id=1, source_target_pairs={{0,4},{1,5},{2,6},{3,7},{4,0},{5,1},{6,2},{7,3},{8,12},{9,13},{10,... | collective-permute-start | bytes 589832 | tf_op jit(solution)/shard_map/ppermute | solution.py:958
  23.2 26.7 %collective-permute-start.5 = (bf16[3,256,128]{2,1,0:T(8,128)(2,1)}, bf16[3,256,128]{2,1,0:T(8,128)(2,1)S(1)}, u32[]{:S(2)}, u32[]{:S(2)}) collective-permute-start(bf16[3,256,128]{2,1,0:T(8,128)(2,1)} %get-tuple-element.84), channel_id=1, source_target_pairs={{0,5},{1,4},{2,7},{3,6},{4,1},{5,0},{6,3},{7,2},{8,13},{9,12},{10,... | collective-permute-start | bytes 589832 | tf_op jit(solution)/shard_map/ppermute | solution.py:958
  32.5 17.5 %collective-permute-start.6 = (bf16[3,256,128]{2,1,0:T(8,128)(2,1)}, bf16[3,256,128]{2,1,0:T(8,128)(2,1)S(1)}, u32[]{:S(2)}, u32[]{:S(2)}) collective-permute-start(bf16[3,256,128]{2,1,0:T(8,128)(2,1)} %get-tuple-element.85), channel_id=1, source_target_pairs={{0,6},{1,7},{2,4},{3,5},{4,2},{5,3},{6,0},{7,1},{8,14},{9,15},{10,... | collective-permute-start | bytes 589832 | tf_op jit(solution)/shard_map/ppermute | solution.py:958
  34.1 15.9 %collective-permute-start.7 = (bf16[3,256,128]{2,1,0:T(8,128)(2,1)}, bf16[3,256,128]{2,1,0:T(8,128)(2,1)S(1)}, u32[]{:S(2)}, u32[]{:S(2)}) collective-permute-start(bf16[3,256,128]{2,1,0:T(8,128)(2,1)} %get-tuple-element.86), channel_id=1, source_target_pairs={{0,7},{1,6},{2,5},{3,4},{4,3},{5,2},{6,1},{7,0},{8,15},{9,14},{10,... | collective-permute-start | bytes 589832 | tf_op jit(solution)/shard_map/ppermute | solution.py:958
  125.9 13.0 %collective-permute-start.9 = (bf16[256,1024]{1,0:T(8,128)(2,1)}, bf16[256,1024]{1,0:T(8,128)(2,1)}, u32[]{:S(2)}, u32[]{:S(2)}) collective-permute-start(bf16[256,1024]{1,0:T(8,128)(2,1)} %get-tuple-element.90.mix_mine), channel_id=1, source_target_pairs={{0,8},{8,0},{16,24},{24,16},{1,9},{9,1},{17,25},{25,17},{2,10},{10... | collective-permute-start | bytes 1572872 | tf_op jit(solution)/shard_map/ppermute | solution.py:958
  126.3 38.0 %collective-permute-start.12 = (bf16[4,256,512]{2,1,0:T(8,128)(2,1)}, bf16[4,256,512]{2,1,0:T(8,128)(2,1)}, u32[]{:S(2)}, u32[]{:S(2)}) collective-permute-start(bf16[4,256,512]{2,1,0:T(8,128)(2,1)} %get-tuple-element.101), channel_id=1, source_target_pairs={{0,1},{1,0},{2,3},{3,2},{4,5},{5,4},{6,7},{7,6},{8,9},{9,8},{10,11... | collective-permute-start | bytes 3145736 | tf_op jit(solution)/shard_map/ppermute | solution.py:958
  128.6 35.7 %collective-permute-start.13 = (bf16[8,128,512]{2,1,0:T(8,128)(2,1)}, bf16[8,128,512]{2,1,0:T(8,128)(2,1)}, u32[]{:S(2)}, u32[]{:S(2)}) collective-permute-start(bf16[8,128,512]{2,1,0:T(8,128)(2,1)} %get-tuple-element.103), channel_id=1, source_target_pairs={{0,16},{8,24},{16,0},{24,8},{1,17},{9,25},{17,1},{25,9},{2,18},{10... | collective-permute-start | bytes 3145736 | tf_op jit(solution)/shard_map/ppermute | solution.py:958
  134.6 29.8 %all-to-all-start.1 = ((bf16[8,256,128]{2,1,0:T(8,128)(2,1)}), bf16[8,256,128]{2,1,0:T(8,128)(2,1)}, u32[]{:S(2)}, u32[]{:S(2)}) async-start(bf16[8,256,128]{2,1,0:T(8,128)(2,1)} %copy-done.19), calls=%async_computation.1 | async-start | bytes 1048576 | tf_op jit(solution)/shard_map/all_to_all | solution.py:1056
  162.1 43.6 %collective-permute-start.17 = (bf16[4,128,1280]{2,1,0:T(8,128)(2,1)}, bf16[4,128,1280]{2,1,0:T(8,128)(2,1)}, u32[]{:S(2)}, u32[]{:S(2)}) collective-permute-start(bf16[4,128,1280]{2,1,0:T(8,128)(2,1)} %get-tuple-element.116), channel_id=1, source_target_pairs={{0,1},{1,0},{2,3},{3,2},{4,5},{5,4},{6,7},{7,6},{8,9},{9,8},{10,11... | collective-permute-start | bytes 3932168 | tf_op jit(solution)/shard_map/ppermute | solution.py:958
  163.6 42.1 %collective-permute-start.18 = (bf16[8,64,1280]{2,1,0:T(8,128)(2,1)}, bf16[8,64,1280]{2,1,0:T(8,128)(2,1)}, u32[]{:S(2)}, u32[]{:S(2)}) collective-permute-start(bf16[8,64,1280]{2,1,0:T(8,128)(2,1)} %get-tuple-element.118), channel_id=1, source_target_pairs={{0,16},{8,24},{16,0},{24,8},{1,17},{9,25},{17,1},{25,9},{2,18},{10... | collective-permute-start | bytes 3932168 | tf_op jit(solution)/shard_map/ppermute | solution.py:958
  167.0 37.6 %collective-permute-start.16 = (bf16[4,128,512]{2,1,0:T(8,128)(2,1)S(1)}, bf16[4,128,512]{2,1,0:T(8,128)(2,1)S(1)}, u32[]{:S(2)}, u32[]{:S(2)}) collective-permute-start(bf16[4,128,512]{2,1,0:T(8,128)(2,1)S(1)} %get-tuple-element.206), channel_id=1, source_target_pairs={{0,1},{1,0},{2,3},{3,2},{4,5},{5,4},{6,7},{7,6},{8,9},{9,8},{10,11... | collective-permute-start | bytes 1572872 | tf_op jit(solution)/shard_map/ppermute | solution.py:958
  169.7 36.1 %collective-permute-start.15 = (bf16[4,128,512]{2,1,0:T(8,128)(2,1)S(1)}, bf16[4,128,512]{2,1,0:T(8,128)(2,1)S(1)}, u32[]{:S(2)}, u32[]{:S(2)}) collective-permute-start(bf16[4,128,512]{2,1,0:T(8,128)(2,1)S(1)} %get-tuple-element.208), channel_id=1, source_target_pairs={{0,16},{8,24},{16,0},{24,8},{1,17},{9,25},{17,1},{25,9},{2,18},{10... | collective-permute-start | bytes 1572872 | tf_op jit(solution)/shard_map/ppermute | solution.py:958
  206.6 45.4 %all-to-all-start.2 = ((bf16[8,3,256,128]{3,2,1,0:T(8,128)(2,1)}), bf16[8,3,256,128]{3,2,1,0:T(8,128)(2,1)S(1)}, u32[]{:S(2)}, u32[]{:S(2)}) async-start(bf16[8,3,256,128]{3,2,1,0:T(8,128)(2,1)} %copy-done.8), calls=%async_computation.2 | async-start | bytes 3145728 | tf_op jit(solution)/shard_map/all_to_all | solution.py:1056
  219.2 31.1 %collective-permute-start.21 = (bf16[4,64,1280]{2,1,0:T(8,128)(2,1)S(1)}, bf16[4,64,1280]{2,1,0:T(8,128)(2,1)S(1)}, u32[]{:S(2)}, u32[]{:S(2)}) collective-permute-start(bf16[4,64,1280]{2,1,0:T(8,128)(2,1)S(1)} %get-tuple-element.202), channel_id=1, source_target_pairs={{0,1},{1,0},{2,3},{3,2},{4,5},{5,4},{6,7},{7,6},{8,9},{9,8},{10,11... | collective-permute-start | bytes 1966088 | tf_op jit(solution)/shard_map/ppermute | solution.py:958
  224.0 28.0 %collective-permute-start.20 = (bf16[4,64,1280]{2,1,0:T(8,128)(2,1)S(1)}, bf16[4,64,1280]{2,1,0:T(8,128)(2,1)}, u32[]{:S(2)}, u32[]{:S(2)}) collective-permute-start(bf16[4,64,1280]{2,1,0:T(8,128)(2,1)S(1)} %get-tuple-element.204), channel_id=1, source_target_pairs={{0,16},{8,24},{16,0},{24,8},{1,17},{9,25},{17,1},{25,9},{2,18},{10... | collective-permute-start | bytes 1966088 | tf_op jit(solution)/shard_map/ppermute | solution.py:958
  225.3 25.0 %collective-permute-start.19 = (bf16[2,128,1024]{2,1,0:T(8,128)(2,1)S(1)}, bf16[2,128,1024]{2,1,0:T(8,128)(2,1)S(1)}, u32[]{:S(2)}, u32[]{:S(2)}) collective-permute-start(bf16[2,128,1024]{2,1,0:T(8,128)(2,1)S(1)} %pad_maximum_fusion.5), channel_id=1, source_target_pairs={{0,2},{1,3},{2,0},{3,1},{4,6},{5,7},{6,4},{7,5},{8,10},{9,11},{10,... | collective-permute-start | bytes 1572872 | tf_op jit(solution)/shard_map/ppermute | solution.py:958
  259.7 22.5 %collective-permute-start.30 = (bf16[128,1024]{1,0:T(8,128)(2,1)}, bf16[128,1024]{1,0:T(8,128)(2,1)}, u32[]{:S(2)}, u32[]{:S(2)}) collective-permute-start(bf16[128,1024]{1,0:T(8,128)(2,1)} %fusion.25), channel_id=1, source_target_pairs={{0,4},{1,5},{2,6},{3,7},{4,0},{5,1},{6,2},{7,3},{8,12},{9,13},{10,... | collective-permute-start | bytes 786440 | tf_op jit(solution)/shard_map/ppermute | solution.py:958
  270.1 5.8 %collective-permute-start.36 = (f32[5,1024]{1,0:T(8,128)S(1)}, f32[5,1024]{1,0:T(8,128)S(1)}, u32[]{:S(2)}, u32[]{:S(2)}) collective-permute-start(f32[5,1024]{1,0:T(8,128)S(1)} %add.416), channel_id=1, source_target_pairs={{0,2},{1,3},{2,0},{3,1},{4,6},{5,7},{6,4},{7,5},{8,10},{9,11},{10,... | collective-permute-start | bytes 61448 | tf_op jit(solution)/shard_map/ppermute | solution.py:958
  275.8 4.9 %collective-permute-start.37 = (f32[5,1024]{1,0:T(8,128)S(1)}, f32[5,1024]{1,0:T(8,128)S(1)}, u32[]{:S(2)}, u32[]{:S(2)}) collective-permute-start(f32[5,1024]{1,0:T(8,128)S(1)} %add.417), channel_id=1, source_target_pairs={{0,4},{1,5},{2,6},{3,7},{4,0},{5,1},{6,2},{7,3},{8,12},{9,13},{10,... | collective-permute-start | bytes 61448 | tf_op jit(solution)/shard_map/ppermute | solution.py:958
  275.9 19.2 %collective-permute-start.26 = (bf16[2,64,2560]{2,1,0:T(8,128)(2,1)S(1)}, bf16[2,64,2560]{2,1,0:T(8,128)(2,1)}, u32[]{:S(2)}, u32[]{:S(2)}) collective-permute-start(bf16[2,64,2560]{2,1,0:T(8,128)(2,1)S(1)} %pad_maximum_fusion.2), channel_id=1, source_target_pairs={{0,2},{1,3},{2,0},{3,1},{4,6},{5,7},{6,4},{7,5},{8,10},{9,11},{10,... | collective-permute-start | bytes 1966088 | tf_op jit(solution)/shard_map/ppermute | solution.py:958
  282.2 7.9 %collective-permute-start.23 = (bf16[8,32,384]{2,1,0:T(8,128)(2,1)S(1)}, bf16[8,32,384]{2,1,0:T(8,128)(2,1)S(1)}, u32[]{:S(2)}, u32[]{:S(2)}) collective-permute-start(bf16[8,32,384]{2,1,0:T(8,128)(2,1)S(1)} %dynamic-slice_bitcast_fusion), channel_id=1, source_target_pairs={{0,16},{8,24},{16,0},{24,8},{1,17},{9,25},{17,1},{25,9},{2,18},{10... | collective-permute-start | bytes 589832 | tf_op jit(solution)/shard_map/ppermute | solution.py:958
  283.4 15.5 %collective-permute-start.31 = (bf16[128,1024]{1,0:T(8,128)(2,1)S(1)}, bf16[128,1024]{1,0:T(8,128)(2,1)S(1)}, u32[]{:S(2)}, u32[]{:S(2)}) collective-permute-start(bf16[128,1024]{1,0:T(8,128)(2,1)S(1)} %fusion.10), channel_id=1, source_target_pairs={{0,16},{8,24},{16,0},{24,8},{1,17},{9,25},{17,1},{25,9},{2,18},{10... | collective-permute-start | bytes 786440 | tf_op jit(solution)/shard_map/ppermute | solution.py:958
  290.8 17.1 %all-to-all-start.3 = ((bf16[8,32,384]{2,1,0:T(8,128)(2,1)}), bf16[8,32,384]{2,1,0:T(8,128)(2,1)}, u32[]{:S(2)}, u32[]{:S(2)}) async-start(bf16[8,32,384]{2,1,0:T(8,128)(2,1)} %fusion.11), calls=%async_computation.3 | async-start | bytes 393216 | tf_op jit(solution)/shard_map/all_to_all | solution.py:1056
  296.2 17.7 %collective-permute-start.27 = (bf16[64,2560]{1,0:T(8,128)(2,1)S(1)}, bf16[64,2560]{1,0:T(8,128)(2,1)}, u32[]{:S(2)}, u32[]{:S(2)}) collective-permute-start(bf16[64,2560]{1,0:T(8,128)(2,1)S(1)} %fusion.17), channel_id=1, source_target_pairs={{0,4},{1,5},{2,6},{3,7},{4,0},{5,1},{6,2},{7,3},{8,12},{9,13},{10,... | collective-permute-start | bytes 983048 | tf_op jit(solution)/shard_map/ppermute | solution.py:958
  299.0 16.4 %collective-permute-start.32 = (bf16[256,1024]{1,0:T(8,128)(2,1)S(1)}, bf16[256,1024]{1,0:T(8,128)(2,1)}, u32[]{:S(2)}, u32[]{:S(2)}) collective-permute-start(bf16[256,1024]{1,0:T(8,128)(2,1)S(1)} %pad_maximum_fusion.7), channel_id=1, source_target_pairs={{0,8},{8,0},{16,24},{24,16},{1,9},{9,1},{17,25},{25,17},{2,10},{10... | collective-permute-start | bytes 1572872 | tf_op jit(solution)/shard_map/ppermute | solution.py:958
  307.9 10.3 %collective-permute-start.24 = (bf16[8,32,384]{2,1,0:T(8,128)(2,1)}, bf16[8,32,384]{2,1,0:T(8,128)(2,1)}, u32[]{:S(2)}, u32[]{:S(2)}) collective-permute-start(bf16[8,32,384]{2,1,0:T(8,128)(2,1)} %all-to-all-done.3), channel_id=1, source_target_pairs={{0,16},{8,24},{16,0},{24,8},{1,17},{9,25},{17,1},{25,9},{2,18},{10... | collective-permute-start | bytes 589832 | tf_op jit(solution)/shard_map/ppermute | solution.py:958
  315.0 8.7 %collective-permute-start.28 = (bf16[64,2560]{1,0:T(8,128)(2,1)S(1)}, bf16[64,2560]{1,0:T(8,128)(2,1)}, u32[]{:S(2)}, u32[]{:S(2)}) collective-permute-start(bf16[64,2560]{1,0:T(8,128)(2,1)S(1)} %fusion.4), channel_id=1, source_target_pairs={{0,16},{8,24},{16,0},{24,8},{1,17},{9,25},{17,1},{25,9},{2,18},{10... | collective-permute-start | bytes 983048 | tf_op jit(solution)/shard_map/ppermute | solution.py:958
  (85 other events, 617.7 us)
Sparse Core Ops, SparseCore 0:
  64.0 101.8 all-gather.1

commit v3 on v2

--- a/solution.py
+++ b/solution.py
@@ -415,31 +415,28 @@
         jax.ShapeDtypeStruct((peers, rows, 128), jnp.bfloat16),
         jax.ShapeDtypeStruct((peers, 128, rows), jnp.float32),
         jax.ShapeDtypeStruct((peers, 8, rows), jnp.float32),
+        jax.ShapeDtypeStruct((peers, 3, rows, 128), jnp.bfloat16),
     ]
     res = pl.pallas_call(
         partial(attend_kernel, peers, items, rows),
         out_shape=shapes,
         in_specs=[smem, smem] + [vmem] * (peers + 1),
-        out_specs=[vmem] * 3,
+        out_specs=[vmem] * 4,
         scratch_shapes=[
-            pltpu.VMEM((peers, 3, rows, 128), jnp.bfloat16),
             pltpu.VMEM((peers, 128, rows), jnp.bfloat16),
             pltpu.VMEM((2, rows, 2 * rows), jnp.float32),
             pltpu.VMEM((2, peers, rows, rows), jnp.float32),
         ],
-        compiler_params=pltpu.CompilerParams(vmem_limit_bytes=24 * 2**20),
+        compiler_params=pltpu.CompilerParams(vmem_limit_bytes=18 * 2**20),
         cost_estimate=pl.CostEstimate(flops=8 * 10**9, bytes_accessed=4 * 2**20, transcendentals=3 * 10**6),
         name="attend",
     )(meta, far, line, *parts)
     return res
 
-def attend_back_kernel(peers, items, rows, meta_ref, far_ref, line_ref, wide_ref, log_ref, cot, *refs):
-    parts = refs[:peers]
-    all_ref, table_ref, qkv, turned, bias, near, far_sum, dkey, dvalue = refs[peers:]
-    me = meta_ref[0]
-    for slot in range(peers):
-        qkv[me ^ slot] = parts[slot][...]
-        turned[me ^ slot] = _turned(parts[slot][1]).astype(jnp.bfloat16)
+def attend_back_kernel(peers, items, rows, meta_ref, far_ref, line_ref, wide_ref, log_ref, cot, qkv, *refs):
+    all_ref, table_ref, turned, bias, near, far_sum, dkey, dvalue = refs
+    for peer in range(peers):
+        turned[peer] = _turned(qkv[peer, 1]).astype(jnp.bfloat16)
     _put_bias(bias, line_ref, rows)
     near[...] = jnp.zeros_like(near)
     far_sum[...] = jnp.zeros_like(far_sum)
@@ -511,9 +508,8 @@
         table_ref[head, :, :rows] = part[:, :rows]
         table_ref[head, :, rows:] = part[:, rows:] + jnp.concatenate([jnp.zeros((8, rows - 128), jnp.float32), total[:, :128] + total[:, 128:]], axis=1)
 
-def attend_back(meta, far, line, wide, logs, parts, grads, items):
-    peers = len(parts)
-    rows = parts[0].shape[1]
+def attend_back(meta, far, line, wide, logs, qkv, grads, items):
+    peers, _, rows, _ = qkv.shape
     smem = pl.BlockSpec(memory_space=pltpu.SMEM)
     vmem = pl.BlockSpec(memory_space=pltpu.VMEM)
     shapes = [
@@ -523,10 +519,9 @@
     res = pl.pallas_call(
         partial(attend_back_kernel, peers, items, rows),
         out_shape=shapes,
-        in_specs=[smem, smem] + [vmem] * (peers + 4),
+        in_specs=[smem, smem] + [vmem] * 5,
         out_specs=[vmem] * 2,
         scratch_shapes=[
-            pltpu.VMEM((peers, 3, rows, 128), jnp.bfloat16),
             pltpu.VMEM((peers, 128, rows), jnp.bfloat16),
             pltpu.VMEM((2, rows, 2 * rows), jnp.float32),
             pltpu.VMEM((2, rows, 2 * rows), jnp.float32),
@@ -534,10 +529,10 @@
             pltpu.VMEM((peers, rows, 128), jnp.float32),
             pltpu.VMEM((peers, rows, 128), jnp.float32),
         ],
-        compiler_params=pltpu.CompilerParams(vmem_limit_bytes=24 * 2**20),
+        compiler_params=pltpu.CompilerParams(vmem_limit_bytes=18 * 2**20),
         cost_estimate=pl.CostEstimate(flops=20 * 10**9, bytes_accessed=8 * 2**20, transcendentals=3 * 10**6),
         name="attend_back",
-    )(meta, far, line, wide, logs, grads, *parts)
+    )(meta, far, line, wide, logs, grads, qkv)
     return res[0], jnp.sum(res[1], axis=1)
 
 def plan(lengths, me, peers, rows):
@@ -689,87 +684,118 @@
 
 
 def feed_kernel(
-    rows, part, meta_ref, act_mine, act_other, grad_mine, grad_other, pulled_ref, expand_ref,
-    in_keep, in_send, low_ref, back_ref, one_keep, one_send, two_keep, two_send, acts, grads, total,
+    rows, part, meta_ref, act_mine, act_other, pulled_ref, expand_ref, in_keep, in_send, low_ref, back_ref, acts, weights, total, arrived
 ):
-    step = pl.program_id(0)
-    x, y = meta_ref[1], meta_ref[2]
-    cut, half = one_keep.shape[2], part // 2
-
-    @pl.when(step == 0)
-    def _():
-        _both(acts, act_mine, act_other)
-        _both(grads, grad_mine, grad_other)
-        total[...] = jnp.zeros_like(total)
-
-    before = _dot(acts[...], expand_ref[...], ((1,), (0,)))
-    rate = 0.5 * (1.0 + lax.erf(before * math.sqrt(0.5)))
-    low = (before * rate).astype(jnp.bfloat16)
-    low_ref[...] = low
-    contract_grad = _dot(low, grads[...], ((0,), (0,))).astype(jnp.bfloat16)
-    slope = rate + before * jnp.exp(-0.5 * before * before) * (1.0 / math.sqrt(2.0 * math.pi))
-    back = (pulled_ref[...] * slope).astype(jnp.bfloat16)
-    back_ref[...] = back
-    total[...] += _dot(back, expand_ref[...], ((1,), (1,)))
-    level = step // 2
-
-    @pl.when(step % 2 == x)
-    def _():
-        one_keep[level] = contract_grad[:, :cut]
-
-    @pl.when(step % 2 != x)
-    def _():
-        one_send[level] = contract_grad[:, :cut]
-
-    @pl.when(y == 0)
-    def _():
-        two_keep[step] = contract_grad[:half, cut:]
-        two_send[step] = contract_grad[half:, cut:]
-
-    @pl.when(y != 0)
-    def _():
-        two_keep[step] = contract_grad[half:, cut:]
-        two_send[step] = contract_grad[:half, cut:]
-
-    @pl.when(step == pl.num_programs(0) - 1)
-    def _():
-        in_keep[...] = total[:rows]
-        in_send[...] = total[rows:]
-
-
-def feed(meta, act_mine, act_other, grad_mine, grad_other, pulled, expand_weight, peers):
+    core = meta_ref[3]
+    pieces = weights.shape[1] // part
+    copies = []
+    for piece in range(pieces):
+        columns = pl.ds(pl.multiple_of((2 * piece + core) * part, part), part)
+        here = weights.at[:, pl.ds(piece * part, part)]
+        copies.append(pltpu.make_async_copy(expand_ref.at[:, columns], here, arrived.at[piece]))
+        copies[-1].start()
+    _both(acts, act_mine, act_other)
+
+    def before(piece):
+        copies[piece].wait()
+        return _dot(acts[...], weights[:, piece * part : (piece + 1) * part], ((1,), (0,)))
+
+    now = before(0)
+    for piece in range(pieces):
+        later = before(piece + 1) if piece + 1 < pieces else None
+        span = slice(piece * part, (piece + 1) * part)
+        rate = 0.5 * (1.0 + lax.erf(now * math.sqrt(0.5)))
+        low_ref[:, span] = (now * rate).astype(jnp.bfloat16)
+        slope = rate + now * jnp.exp(-0.5 * now * now) * (1.0 / math.sqrt(2.0 * math.pi))
+        back_ref[:, span] = (pulled_ref[:, span] * slope).astype(jnp.bfloat16)
+        if piece % 2 == 1:
+            pair = slice((piece - 1) * part, (piece + 1) * part)
+            got = _dot(back_ref[:, pair], weights[:, pair], ((1,), (1,)))
+            if piece == 1:
+                total[...] = got
+            elif piece + 1 < pieces:
+                total[...] += got
+            else:
+                in_keep[...] = total[:rows] + got[:rows]
+                in_send[...] = total[rows:] + got[rows:]
+        now = later
+
+
+def feed(meta, act_mine, act_other, pulled, expand_weight, peers):
     rows, width = act_mine.shape
     part = expand_weight.shape[1] // (2 * peers)
-    cut = width // 2
     shapes = [
         ((rows, width), jnp.float32),
         ((rows, width), jnp.float32),
         ((2 * rows, peers * part), jnp.bfloat16),
         ((2 * rows, peers * part), jnp.bfloat16),
-        ((peers // 2, part, cut), jnp.bfloat16),
-        ((peers // 2, part, cut), jnp.bfloat16),
-        ((peers, part // 2, cut), jnp.bfloat16),
-        ((peers, part // 2, cut), jnp.bfloat16),
     ]
     return pl.pallas_call(
         partial(feed_kernel, rows, part),
         out_shape=[jax.ShapeDtypeStruct(*shape) for shape in shapes],
+        in_specs=_specs("svvvh"),
+        out_specs=_specs("vvvv"),
+        scratch_shapes=[
+            pltpu.VMEM((2 * rows, width), jnp.bfloat16),
+            pltpu.VMEM((width, peers * part), jnp.bfloat16),
+            pltpu.VMEM((2 * rows, width), jnp.float32),
+            pltpu.SemaphoreType.DMA((peers,)),
+        ],
+        compiler_params=_params(40),
+        cost_estimate=pl.CostEstimate(flops=8 * 10**9, bytes_accessed=20 * 2**20, transcendentals=2 * 10**6),
+        name="feed",
+    )(meta, act_mine, act_other, pulled, expand_weight)
+
+
+def contract_weigh_kernel(part, meta_ref, grad_mine, grad_other, low_ref, one_keep, one_send, two_keep, two_send, grads):
+    step = pl.program_id(0)
+    x, y = meta_ref[1], meta_ref[2]
+    cut, half = one_keep.shape[2], part // 2
+
+    @pl.when(step == 0)
+    def _():
+        _both(grads, grad_mine, grad_other)
+
+    grad = _dot(low_ref[...], grads[...], ((0,), (0,))).astype(jnp.bfloat16)
+    level = step // 2
+
+    @pl.when(step % 2 == x)
+    def _():
+        one_keep[level] = grad[:, :cut]
+
+    @pl.when(step % 2 != x)
+    def _():
+        one_send[level] = grad[:, :cut]
+
+    @pl.when(y == 0)
+    def _():
+        two_keep[step] = grad[:half, cut:]
+        two_send[step] = grad[half:, cut:]
+
+    @pl.when(y != 0)
+    def _():
+        two_keep[step] = grad[half:, cut:]
+        two_send[step] = grad[:half, cut:]
+
+
+def contract_weigh(meta, grad_mine, grad_other, low, peers):
+    rows, width = grad_mine.shape
+    part, cut = low.shape[1] // peers, width // 2
+    shapes = [(peers // 2, part, cut), (peers // 2, part, cut), (peers, part // 2, cut), (peers, part // 2, cut)]
+    return pl.pallas_call(
+        partial(contract_weigh_kernel, part),
+        out_shape=[jax.ShapeDtypeStruct(shape, jnp.bfloat16) for shape in shapes],
         grid_spec=pltpu.PrefetchScalarGridSpec(
             num_scalar_prefetch=1,
             grid=(peers,),
-            in_specs=[_whole(rows, width)] * 4
-            + [_across(2 * rows, part), pl.BlockSpec((width, part), lambda step, meta_ref: (0, 2 * step + meta_ref[3]))],
-            out_specs=[_whole(rows, width)] * 2 + [_across(2 * rows, part)] * 2 + [_whole(*shape) for shape, _ in shapes[4:]],
-            scratch_shapes=[
-                pltpu.VMEM((2 * rows, width), jnp.bfloat16),
-                pltpu.VMEM((2 * rows, width), jnp.bfloat16),
-                pltpu.VMEM((2 * rows, width), jnp.float32),
-            ],
+            in_specs=[_whole(rows, width)] * 2 + [_across(2 * rows, part)],
+            out_specs=[_whole(*shape) for shape in shapes],
+            scratch_shapes=[pltpu.VMEM((2 * rows, width), jnp.bfloat16)],
         ),
-        compiler_params=_params(40),
-        cost_estimate=pl.CostEstimate(flops=10 * 10**9, bytes_accessed=20 * 2**20, transcendentals=2 * 10**6),
-        name="feed",
-    )(meta, act_mine, act_other, grad_mine, grad_other, pulled, expand_weight)
+        compiler_params=_params(12),
+        cost_estimate=pl.CostEstimate(flops=10**8, bytes_accessed=2**20, transcendentals=0),
+        name="contract_weigh",
+    )(meta, grad_mine, grad_other, low)
 
 
 def weigh_kernel(
@@ -852,8 +878,8 @@
                 pltpu.VMEM((peers, group, part), jnp.bfloat16),
             ],
         ),
-        compiler_params=_params(36),
-        cost_estimate=pl.CostEstimate(flops=8 * 10**9, bytes_accessed=20 * 2**20, transcendentals=0),
+        compiler_params=_params(28),
+        cost_estimate=pl.CostEstimate(flops=10**8, bytes_accessed=2**20, transcendentals=0),
         name="weigh",
     )(meta, act_mine, act_other, mix_mine, mix_other, right_mine, right_other, low, back, contract_weight)
 
@@ -895,7 +921,7 @@
         out_shape=[jax.ShapeDtypeStruct(*shape) for shape in shapes],
         in_specs=_specs("svvvvvv"),
         out_specs=_specs("v" * len(shapes)),
-        compiler_params=_params(20),
+        compiler_params=_params(14),
         cost_estimate=pl.CostEstimate(flops=10**9, bytes_accessed=8 * 2**20, transcendentals=0),
         name="turn",
     )(meta, in_mine, in_other, middle, grad, gain, weight)
@@ -920,37 +946,143 @@
         in_specs=_specs("vvvvv"),
         out_specs=_specs("vv"),
         scratch_shapes=[pltpu.VMEM((rows, 3 * width), jnp.bfloat16)],
-        compiler_params=_params(24),
+        compiler_params=_params(20),
         cost_estimate=pl.CostEstimate(flops=2 * 10**9, bytes_accessed=10 * 2**20, transcendentals=0),
         name="close",
     )(parts, tokens, grad, gain, weight)
 
 
-def attend_weigh_kernel(meta_ref, act_ref, back_ref, keep_ref, send_ref, held):
-    core = meta_ref[3]
-    peers, _, half, _ = held.shape
-    for block in range(3):
-        back = jnp.concatenate([back_ref[peer, block] for peer in range(peers)])
-        grad = jnp.transpose(_dot(back, act_ref[...], ((0,), (0,)))).astype(jnp.bfloat16)
-        held[:, :, :, 128 * block : 128 * block + 128] = grad.reshape(peers, 2, half, 128)
-    for peer in range(peers):
-        keep_ref[peer] = held[peer, core]
-        send_ref[peer] = held[peer, 1 - core]
-
-
-def attend_weigh(meta, act, back):
-    peers = back.shape[0]
-    shape = (peers, act.shape[1] // (2 * peers), 3 * back.shape[3])
+def _plus(a, b):
+    return (a.astype(jnp.float32) + b.astype(jnp.float32)).astype(jnp.bfloat16)
+
+
+def second_kernel(meta_ref, one_keep, one_got, two_keep, two_got, one_left, one_send, two_left, two_send):
+    x, y = meta_ref[1], meta_ref[2]
+    levels, half, _ = one_left.shape
+    mine = pl.ds(pl.multiple_of(y * half, half), half)
+    other = pl.ds(pl.multiple_of((1 - y) * half, half), half)
+    for level in range(levels):
+        one_left[level] = _plus(one_keep[level, mine], one_got[level, mine])
+        one_send[level] = _plus(one_keep[level, other], one_got[level, other])
+        two_left[level] = _plus(two_keep[2 * level + x], two_got[2 * level + x])
+        two_send[level] = _plus(two_keep[2 * level + 1 - x], two_got[2 * level + 1 - x])
+
+
+def near_kernel(meta_ref, one_keep, one_got, two_keep, two_got, left, send):
+    side = (meta_ref[0] >> 1) & 1
+    cut = one_keep.shape[2]
+    for level in range(left.shape[0]):
+        for out, at in ((left, 2 * level + side), (send, 2 * level + 1 - side)):
+            out[level, :, :cut] = _plus(one_keep[at], one_got[at])
+            out[level, :, cut:] = _plus(two_keep[at], two_got[at])
+
+
+def far_kernel(meta_ref, keep, got, left, send):
+    upper = meta_ref[0] >> 2
+    left[...] = _plus(keep[upper], got[upper])
+    send[...] = _plus(keep[1 - upper], got[1 - upper])
+
+
+def last_kernel(keep, got, out):
+    out[...] = _plus(keep[...], got[...])
+
+
+def _small_call(kernel, name, shapes, kind, *arguments):
+    size = sum(2 * math.prod(a.shape) for a in arguments[-4:])
+    return pl.pallas_call(
+        kernel,
+        out_shape=[jax.ShapeDtypeStruct(shape, kind) for shape in shapes],
+        in_specs=_specs(*("s" if a.dtype == jnp.int32 else "v" for a in arguments)),
+        out_specs=_specs("v" * len(shapes)),
+        compiler_params=_params(24),
+        cost_estimate=pl.CostEstimate(flops=size, bytes_accessed=3 * size, transcendentals=0),
+        name=name,
+    )(*arguments)
+
+
+def _places(meta_ref, half):
+    y, core = meta_ref[2], meta_ref[3]
+    return [(c, pl.ds(pl.multiple_of(h * half, half), half)) for c in (core, 1 - core) for h in (y, 1 - y)]
+
+
+def finish_contract_kernel(meta_ref, *refs):
+    half = refs[0].shape[0]
+    y, core = meta_ref[2], meta_ref[3]
+    starts = [(2 * c + h) * half for c in (core, 1 - core) for h in (y, 1 - y)]
+    for part, start in zip(refs[:4], starts):
+        refs[4][pl.ds(pl.multiple_of(start, half), half), :] = part[...].astype(jnp.float32)
+
+
+def finish_expand_kernel(part, meta_ref, *refs):
+    expand_ref, merge_ref = refs[4:]
+    half, span = refs[0].shape[0], refs[0].shape[1] // 2
+    near = span // part - 1
+    for source, (core, rows) in zip(refs[:4], _places(meta_ref, half)):
+        for side in range(2):
+            for block in range(near):
+                at = pl.multiple_of((2 * (side * near + block) + core) * part, part)
+                start = side * span + block * part
+                expand_ref[rows, pl.ds(at, part)] = source[:, start : start + part].astype(jnp.float32)
+            at = pl.multiple_of((2 * core + side) * part, part)
+            start = side * span + near * part
+            merge_ref[rows, pl.ds(at, part)] = source[:, start : start + part].astype(jnp.float32)
+
+
+def finish_attend_kernel(meta_ref, *refs):
+    half, wide = refs[0].shape
+    span = wide // 3
+    for source, (core, rows) in zip(refs[:4], _places(meta_ref, half)):
+        for block in range(3):
+            at = pl.multiple_of((2 * block + core) * span, span)
+            refs[4][rows, pl.ds(at, span)] = source[:, block * span : (block + 1) * span].astype(jnp.float32)
+
+
+def attend_weigh_kernel(
+    meta_ref, act_mine, act_other, owned_ref, other_ref, one_keep, one_send, two_keep, two_send, acts, right, held
+):
+    x, y, core = meta_ref[1], meta_ref[2], meta_ref[3]
+    count, blocks, rows, _ = other_ref.shape
+    peers, group, cut = held.shape
+    half = group // 2
+    _both(acts, act_mine, act_other)
+    for block in range(blocks):
+        for place in range(count):
+            at = 128 * (block * count + place)
+            right[:rows, at : at + 128] = owned_ref[core * count + place, block]
+            right[rows:, at : at + 128] = other_ref[place, block]
+    for side in range(2):
+        grad = _dot(acts[...], right[:, side * cut : (side + 1) * cut], ((0,), (0,))).astype(jnp.bfloat16)
+        held[...] = grad.reshape(peers, group, cut)
+        if side == 0:
+            for place in range(peers // 2):
+                one_keep[place] = held[2 * place + x]
+                one_send[place] = held[2 * place + 1 - x]
+        else:
+            for place in range(peers):
+                two_keep[place] = held[place, pl.ds(pl.multiple_of(y * half, half), half), :]
+                two_send[place] = held[place, pl.ds(pl.multiple_of((1 - y) * half, half), half), :]
+
+
+def attend_weigh(meta, act_mine, act_other, owned, other):
+    peers, blocks, rows, _ = owned.shape
+    width = act_mine.shape[1]
+    group, span = width // peers, blocks * width // 2
+    cut = span // 2
+    shapes = [(peers // 2, group, cut), (peers // 2, group, cut), (peers, group // 2, cut), (peers, group // 2, cut)]
     return pl.pallas_call(
         attend_weigh_kernel,
-        out_shape=[jax.ShapeDtypeStruct(shape, jnp.bfloat16)] * 2,
-        in_specs=_specs("svv"),
-        out_specs=_specs("vv"),
-        scratch_shapes=[pltpu.VMEM((peers, 2) + shape[1:], jnp.bfloat16)],
+        out_shape=[jax.ShapeDtypeStruct(shape, jnp.bfloat16) for shape in shapes],
+        in_specs=_specs("svvvv"),
+        out_specs=_specs("vvvv"),
+        scratch_shapes=[
+            pltpu.VMEM((2 * rows, width), jnp.bfloat16),
+            pltpu.VMEM((2 * rows, span), jnp.bfloat16),
+            pltpu.VMEM((peers, group, cut), jnp.bfloat16),
+        ],
         compiler_params=_params(20),
-        cost_estimate=pl.CostEstimate(flops=3 * 10**9, bytes_accessed=7 * 2**20, transcendentals=0),
+        cost_estimate=pl.CostEstimate(flops=2 * 10**9, bytes_accessed=7 * 2**20, transcendentals=0),
         name="attend_weigh",
-    )(meta, act, back)
+    )(meta, act_mine, act_other, owned, other)
 
 
 def flipped(array, axis, mask):
@@ -980,38 +1112,36 @@
     return one_keep, flipped(one_send, "blk", 1), two_keep, flipped(two_send, "seq", 2)
 
 
-def over_second(place, one_keep, one_got, two_keep, two_got):
-    _, x, y = place
+def over_second(here, one_keep, one_got, two_keep, two_got):
     levels, rows, cut = one_keep.shape
-    shape = (levels, 2, rows // 2, cut)
-
-    def sums(keep, got, index):
-        return added(pick(keep.reshape(shape), index, 1), pick(got.reshape(shape), index, 1))
-
-    one_next = flipped(sums(one_keep, one_got, 1 - y), "seq", 2)
-    two_next = flipped(sums(two_keep, two_got, 1 - x), "blk", 1)
-    return sums(one_keep, one_got, y), one_next, sums(two_keep, two_got, x), two_next
-
-
-def over_near(place, one, one_next, two, two_next):
-    side = place[0] % 2
-    levels = one.shape[0]
-    shape = (levels // 2, 2) + one.shape[1:]
-
-    def of(index):
-        parts = [(pick(a.reshape(shape), index, 1), pick(b.reshape(shape), index, 1)) for a, b in ((one, one_next), (two, two_next))]
-        return jnp.concatenate([added(a, b) for a, b in parts], axis=-1)
-
-    return of(side), flipped(of(1 - side), "blk", 2)
-
-
-def over_far(place, keep, got):
-    upper = place[0] // 2
-
-    def of(index):
-        return added(pick(keep, index, 0), pick(got, index, 0))
-
-    return of(upper), flipped(of(1 - upper), "blk", 4)
+    shape = (levels, rows // 2, cut)
+    return _small_call(second_kernel, "second", [shape] * 4, jnp.bfloat16, here, one_keep, one_got, two_keep, two_got)
+
+
+def send_second(one_left, one_send, two_left, two_send):
+    return one_left, flipped(one_send, "seq", 2), two_left, flipped(two_send, "blk", 1)
+
+
+def over_near(here, one_keep, one_got, two_keep, two_got):
+    levels, half, cut = one_keep.shape
+    left, send = _small_call(
+        near_kernel, "near", [(levels // 2, half, 2 * cut)] * 2, jnp.bfloat16, here, one_keep, one_got, two_keep, two_got
+    )
+    return left, flipped(send, "blk", 2)
+
+
+def over_far(here, keep, got):
+    left, send = _small_call(far_kernel, "far", [keep.shape[1:]] * 2, jnp.bfloat16, here, keep, got)
+    return left, flipped(send, "blk", 4)
+
+
+def over_all(keep, got):
+    return _small_call(last_kernel, "last", [keep.shape], jnp.bfloat16, keep, got)[0]
+
+
+def of_all(own):
+    across = flipped(own, "seq", 2)
+    return own, across, flipped(own, "seq", 1), flipped(across, "seq", 1)
 
 
 def local_by_heads(
@@ -1058,63 +1188,63 @@
     *parts, act_first = project(here, own, gain_first, shift_first, attend_weight, peers)
     parts = [parts[0]] + [flipped(parts[step], "blk", step) for step in range(1, peers)]
     pulled = pull(here, grad_out, grad_other, contract_weight, peers)
-    mixed, wide, logs = attend(meta, after(far, pulled), lines, parts, items)
-    act_all = lax.all_gather(after(act_first, mixed), "blk", axis=0, tiled=True)
+    mixed, wide, logs, qkv = attend(meta, after(far, pulled), lines, parts, items)
+    first_other = flipped(act_first, "seq", 1)
     attn_low, middle, act_second = merge(to_all(mixed), own, gain_second, shift_second, merge_weight)
     act_other = flipped(act_second, "seq", 1)
     attn_other = flipped(attn_low, "seq", 1)
-    in_keep, in_send, hidden_low, hidden_back, *contract_parts = feed(
-        here, act_second, act_other, grad_out, grad_other, pulled, expand_weight, peers
-    )
+    in_keep, in_send, hidden_low, hidden_back = feed(here, act_second, act_other, pulled, expand_weight, peers)
     grad_heads, grad_middle, keep_low, send_low, sums_second = turn(
         here, in_keep, flipped(in_send, "seq", 1), middle, grad_out, gain_second, merge_weight, peers
     )
-    contract_parts = over_first(*contract_parts)
+    contract_parts = over_first(*contract_weigh(here, grad_out, grad_other, after(hidden_low, grad_heads), peers))
     out_keep, out_send, *expand_parts = weigh(
         here, act_second, act_other, attn_low, attn_other, keep_low, flipped(send_low, "seq", 1), hidden_low, hidden_back, contract_weight, peers
     )
     expand_parts = over_first(*expand_parts)
 
-    grad_heads, out_send, *contract_parts = lax.optimization_barrier((to_all(grad_heads), out_send, *contract_parts))
-    contract_parts = over_second(place, *contract_parts)
-    back_all, line_grad = attend_back(meta, far, lines, wide, logs, parts, grad_heads, items)
-    act_all, back_all, *sums = lax.optimization_barrier((act_all, back_all, *contract_parts, *expand_parts))
-    contract_parts = over_near(place, *sums[:4])
-    expand_parts = over_second(place, *sums[4:])
-    attend_keep, attend_send = attend_weigh(here, act_all, back_all)
-    owned, attend_keep, attend_send, *sums = lax.optimization_barrier((to_all(back_all), attend_keep, attend_send, *contract_parts, *expand_parts))
-    contract_parts = over_far(place, *sums[:2])
-    expand_parts = over_near(place, *sums[2:])
+    grad_heads, out_send = lax.optimization_barrier((to_all(grad_heads), out_send))
+    back_all, line_grad = attend_back(meta, far, lines, wide, logs, qkv, grad_heads, items)
+    back_all, *sums = lax.optimization_barrier((back_all, *contract_parts, *expand_parts))
+    owned = to_all(back_all)
+    contract_parts = over_near(here, *send_second(*over_second(here, *sums[:4])))
+    expand_parts = send_second(*over_second(here, *sums[4:]))
+    owned, *sums = lax.optimization_barrier((owned, *contract_parts, *expand_parts))
+    contract_parts = over_far(here, *sums[:2])
+    expand_parts = over_near(here, *sums[2:])
+    owned_send = pick(owned.reshape(2, levels, 3, rows, group), 1 - core, 0)
+    attend_parts = over_first(*attend_weigh(here, act_first, first_other, owned, flipped(owned_send, "seq", 1)))
     output = (middle + out_keep + flipped(out_send, "seq", 1).astype(jnp.float32)).astype(jnp.bfloat16)
     tokens_grad, sums_first = close(owned, own, grad_middle, gain_first, attend_weight)
-    contract_grad = added(*contract_parts)
-    expand_grad = added(*over_far(place, *expand_parts))
-    attend_keep = added(attend_keep, flipped(attend_send, "seq", 1)).reshape(peers, 2, group // 4, 3 * group)
-    attend_keep, attend_send = pick(attend_keep, y, 1), pick(attend_keep, 1 - y, 1)
-
-    attend_grad = to_all(added(attend_keep, flipped(attend_send, "seq", 2)))
-
-    contract_grad = in_order(contract_grad, flipped(contract_grad, "seq", 2), y, 0)
-    contract_grad = in_order(contract_grad, flipped(contract_grad, "seq", 1), core, 0).astype(jnp.float32)
-    span = part * (peers // 2 + 1)
-    expand_grad = in_order(expand_grad, flipped(expand_grad, "seq", 2), y, 0)
-    expand_other = flipped(expand_grad, "seq", 1)
-    halves = [jnp.where(core == side, expand_grad, expand_other).astype(jnp.float32) for side in range(2)]
-    at = [part * peer if peer < peers // 2 else part * (peer + 1) for peer in range(peers)]
-    expand_grad = jnp.concatenate([halves[side][:, start : start + part] for start in at for side in range(2)], axis=1)
-    merge_grad = jnp.concatenate([halves[side][:, start - part : start] for side in range(2) for start in (span, 2 * span)], axis=1)
-    attend_grad = in_order(attend_grad, flipped(attend_grad, "seq", 2), y, 1)
-    attend_grad = in_order(attend_grad, flipped(attend_grad, "seq", 1), core, 1)
-    attend_grad = attend_grad.reshape(peers, group, 3, group).transpose(1, 2, 0, 3).reshape(group, 3 * width).astype(jnp.float32)
-
-    table_mine = jnp.dot(hot, line_grad.T, precision=highest)
-    table_local = lax.dynamic_update_slice(jnp.zeros((buckets, heads), jnp.float32), table_mine, (0, 2 * me))
-    table_row = jnp.pad(table_local.reshape(1, buckets * heads), ((0, 0), (0, width - buckets * heads)))
-    small = jnp.concatenate([sums_first, sums_second, table_row])
-    for axis, mask in (("seq", 1), ("seq", 2), ("blk", 1), ("blk", 2), ("blk", 4)):
-        small = small + flipped(small, axis, mask)
-    table_grad = small[4, : buckets * heads].reshape(buckets, heads)
-    vectors = lax.dynamic_slice_in_dim(small, me * group, group, 1)
+    table_mine = jnp.dot(hot, line_grad.T, precision=highest).reshape(1, 2 * buckets)
+    table_row = jnp.broadcast_to(jnp.pad(table_mine, ((0, 0), (0, group - 2 * buckets)))[:, None], (1, peers, group))
+    small = jnp.concatenate([sums_first.reshape(2, peers, group), sums_second.reshape(2, peers, group), table_row]).transpose(1, 0, 2)
+    small = jnp.pad(small, ((0, 0), (0, 3), (0, 0)))
+
+    sums = lax.optimization_barrier((*attend_parts, *contract_parts, *expand_parts))
+    attend_parts = send_second(*over_second(here, *sums[:4]))
+    contract_own = over_all(*sums[4:6])
+    contract_across = flipped(contract_own, "seq", 2)
+    expand_parts = over_far(here, *sums[6:])
+    small, *sums = lax.optimization_barrier((small, *attend_parts, contract_across, *expand_parts))
+    attend_parts = over_near(here, *sums[:4])
+    contract_grad = (contract_own, sums[4], flipped(contract_own, "seq", 1), flipped(sums[4], "seq", 1))
+    small = small + flipped(small, "seq", 1)
+    expand_own = over_all(*sums[5:])
+    expand_across = flipped(expand_own, "seq", 2)
+    small, expand_across, *attend_parts = lax.optimization_barrier((small, expand_across, *attend_parts))
+    attend_parts = over_far(here, *attend_parts)
+    small = small + flipped(small, "seq", 2)
+    expand_grad = (expand_own, expand_across, flipped(expand_own, "seq", 1), flipped(expand_across, "seq", 1))
+    small = to_all(small)
+    contract_grad = _small_call(finish_contract_kernel, "finish_contract", [(2 * part, width)], jnp.float32, here, *contract_grad)[0]
+    expand_grad, merge_grad = _small_call(
+        partial(finish_expand_kernel, part), "finish_expand", [(group, hidden), (group, width)], jnp.float32, here, *expand_grad
+    )
+    attend_grad = of_all(over_all(*attend_parts))
+    attend_grad = _small_call(finish_attend_kernel, "finish_attend", [(group, 3 * width)], jnp.float32, here, *attend_grad)[0]
+    table_grad = small[:, 4, : 2 * buckets].reshape(peers, buckets, 2).transpose(1, 0, 2).reshape(buckets, heads)
+    vectors = jnp.sum(small[:, :4], axis=0)
     return (
         output[None],
         tokens_grad[None],

time: 342 us -> 322 us (0.942)
  other arithmetic: 31.6 us -> 3.67 us
  Pallas kernels: 85 us -> 106 us
  waiting for transfers between devices: 76.4 us -> 94.5 us
  between operations: 15.7 us -> 1.86 us
  blocking collectives: 35.8 us -> 25.8 us
  local copies, waits for them, and re-layouts: 42 us -> 35 us
    pallas_call x0 -> x16, Pallas kernels: none -> 29.3 us  [the longest x15 22.7 us: _small_call(): pl.pallas_call(kernel, out_shape=[jax.ShapeDtypeStruct(shape, kind) for s...]
    ppermute x38 -> x44, waiting for transfers between devices: 67.5 us -> 94.4 us  [flipped(): return lax.ppermute(array, axis, [(i, i ^ mask) for i in range(peers)])]
    convert_element_type x19 -> x0, other arithmetic: 21.3 us -> none  [the longest x16 18.2 us: added(): return (a.astype(jnp.float32) + b.astype(jnp.float32)).astype(jnp.bfloat16)]
    all_to_all x1, blocking collectives: 35.8 us -> 25.8 us  [to_all(): return lax.all_to_all(array, 'blk', split_axis=0, concat_axis=0, tiled=True)]
    all_to_all x3, waiting for transfers between devices: 8.83 us -> 0.01 us  [to_all(): return lax.all_to_all(array, 'blk', split_axis=0, concat_axis=0, tiled=True)]
    pallas_call x1, Pallas kernels: 18.8 us -> 10.9 us  [feed(): pl.pallas_call(partial(feed_kernel, rows, part), out_shape=[jax.ShapeDtyp...]
    concatenate x9 -> x1, other arithmetic: 3.7 us -> 0.01 us  [local_by_heads(): jnp.concatenate([sums_first.reshape(2, peers, group), sums_second.reshape...]
    unnamed x167 -> x128, local copies, waits for them, and re-layouts: 35 us -> 33.4 us
  transfers between devices with their start and end apart: 42 -> 47, of which waited for: 15 -> 19; matrix products, arithmetic and copies ran while one was open for 11% -> 2% of each run, Pallas kernels for 20% -> 22%
where the time goes in v3:
time: 322 us; the launch traced here: 321 us
  Pallas kernels  106 us (33%)
  waiting for transfers between devices  94.5 us (29%)
  starting transfers between devices  53.7 us (17%)
  local copies, waits for them, and re-layouts  35 us (11%)
  blocking collectives  25.8 us (8%)
  other arithmetic  3.67 us (1%)
    ppermute x44, waiting for transfers between devices, flipped(): return lax.ppermute(array, axis, [(i, i ^ mask) for i in range(peers)])  94.4 us
    ppermute x44, starting transfers between devices, flipped(): return lax.ppermute(array, axis, [(i, i ^ mask) for i in range(peers)])  39.9 us
    unnamed x128, local copies, waits for them, and re-layouts  33.4 us
    all_to_all x1, blocking collectives, to_all(): return lax.all_to_all(array, 'blk', split_axis=0, concat_axis=0, tiled=True)  25.8 us
    pallas_call x15, Pallas kernels, _small_call(): pl.pallas_call(kernel, out_shape=[jax.ShapeDtypeStruct(shape, kind) for s...  22.7 us
    pallas_call x1, Pallas kernels, attend_back(): pl.pallas_call(partial(attend_back_kernel, peers, items, rows), out_shape...  21.7 us
    all_to_all x3, starting transfers between devices, to_all(): return lax.all_to_all(array, 'blk', split_axis=0, concat_axis=0, tiled=True)  13.8 us
    pallas_call x1, Pallas kernels, attend(): pl.pallas_call(partial(attend_kernel, peers, items, rows), out_shape=shap...  12.6 us
  transfers between devices with their start and end apart: 47, of which 19 were waited for; matrix products, arithmetic and copies ran while one was open for 2% of the time, Pallas kernels for 22%

profile of v3, /device:TPU:0, one launch (start us, length us, event | category | flops | bytes accessed | tf_op | source)
XLA Modules:
  0.0 320.8 jit_solution(16701786124098823905)
XLA Ops:
  1.8 6.4 %project.1 = (bf16[3,256,128]{2,1,0:T(8,128)(2,1)}, bf16[3,256,128]{2,1,0:T(8,128)(2,1)}, bf16[3,256,128]{2,1,0:T(8,128)(2,1)}, bf16[3,256,128]{2,1,0:T(8,128)(2...) custom-call(s32[4]{0:T(128)} %pad_add_fusion.1.meta_ref, ...), custom_call_target="tpu_custom_call" | custom-call | flops 4000000000 | bytes 8388608 | tf_op jit(solution)/shard_map/project/pallas_call | solution.py:608
  8.1 2.6 collective-permute-start.1
  12.3 3.0 collective-permute-start.4
  16.7 3.6 %collective-permute-start.5 = (bf16[3,256,128]{2,1,0:T(8,128)(2,1)}, bf16[3,256,128]{2,1,0:T(8,128)(2,1)S(1)}, u32[]{:S(2)}, u32[]{:S(2)}) collective-permute-start(bf16[3,256,128]{2,1,0:T(8,128)(2,1)} %get-tuple-element.126), channel_id=1, source_target_pairs={{0,5},{1,4},{2,7},{3,6},{4,1},{5,0},{6,3},{7,2},{8,13},{9,12},{10,... | collective-permute-start | bytes 589832 | tf_op jit(solution)/shard_map/ppermute | solution.py:1090
  20.2 5.7 %collective-permute-done.2.refs_2_ = bf16[3,256,128]{2,1,0:T(8,128)(2,1)S(1)} collective-permute-done((bf16[3,256,128]{2,1,0:T(8,128)(2,1)}, bf16[3,256,128]{2,1,0:T(8,128)(2,1)S(1)}, u32[]{:S(2)}, u32[]{:S(2)}) %collective-permute-start.2) | collective-permute-done | bytes 196640 | tf_op jit(solution)/shard_map/ppermute | solution.py:1090
  29.2 3.4 %copy-done.2 = bf16[4096,1024]{1,0:T(8,128)(2,1)S(1)} copy-done((bf16[4096,1024]{1,0:T(8,128)(2,1)S(1)}, bf16[4096,1024]{1,0:T(8,128)(2,1)}, u32[]{:S(2)}) %copy-start.2) | copy-done | bytes 8388632
  32.6 4.7 %pull.1.pulled_ref = f32[512,2048]{1,0:T(8,128)S(1)} custom-call(s32[4]{0:T(128)S(1)} %copy-done.52, bf16[256,1024]{1,0:T(8,128)(2,1)S(1)} %bitcast.50, bf16[256,1024]{1,0:T(8,128)(2,1)S(1)} %collective-permute-done.other.grad_other, bf16[4096,1024]{1,0:T(8,128)(2,1)S(1)} %copy-done.2), custom_call_target="tpu_custom_call" | custom-call | flops 3000000000 | bytes 9437184 | tf_op jit(solution)/shard_map/pull/pallas_call | solution.py:670
  37.3 6.0 %collective-permute-done.5.refs_5_ = bf16[3,256,128]{2,1,0:T(8,128)(2,1)S(1)} collective-permute-done((bf16[3,256,128]{2,1,0:T(8,128)(2,1)}, bf16[3,256,128]{2,1,0:T(8,128)(2,1)S(1)}, u32[]{:S(2)}, u32[]{:S(2)}) %collective-permute-start.5) | collective-permute-done | bytes 196640 | tf_op jit(solution)/shard_map/ppermute | solution.py:1090
  43.4 12.6 %attend.1 = (bf16[8,256,128]{2,1,0:T(8,128)(2,1)S(1)}, f32[8,128,256]{2,1,0:T(8,128)S(1)}, f32[8,8,256]{2,1,0:T(8,128)S(1)}, bf16[8,3,256,128]{3,2,1,0:T(8,128)(2,1)S(1)}) custom-call(s32[18]{0:T(128)S(1)} %pad_add_fusion.meta_ref, f32[2]{0:T(128)S(1)} %slice_reduce_fusion.1.far_ref, f32[2,512]{1,0:T(2,128)S(1)} %fusion.2.line_ref, ...), custom_call_target="tpu_custom_call" | custom-call | flops 8000000000 | bytes 4194304 | tf_op jit(solution)/shard_map/attend/pallas_call | solution.py:420
  56.0 25.8 %all_to_all.20.parts_ref = bf16[8,256,128]{2,1,0:T(8,128)(2,1)S(1)} all-to-all(bf16[8,256,128]{2,1,0:T(8,128)(2,1)S(1)} %get-tuple-element.129), channel_id=1, replica_groups=mesh['seq'=4,'blk'=8] {'blk'}, dimensions={0} | all-to-all | bytes 1048576 | tf_op jit(solution)/shard_map/all_to_all | solution.py:1186
  85.0 10.9 %feed.1 = (f32[256,1024]{1,0:T(8,128)S(1)}, f32[256,1024]{1,0:T(8,128)S(1)}, bf16[512,2048]{1,0:T(8,128)(2,1)S(1)}, bf16[512,2048]{1,0:T(8,128)(2,1)S(1)}) custom-call(s32[4]{0:T(128)S(1)} %copy-done.52, bf16[256,1024]{1,0:T(8,128)(2,1)S(1)} %get-tuple-element.131.act_mine, bf16[256,1024]{1,0:T(8,128)(2,1)S(1)} %collective-permute-done.8.act_other, ...), custom_call_target="tpu_custom_call" | custom-call | flops 8000000000 | bytes 20971520 | tf_op jit(solution)/shard_map/feed/pallas_call | solution.py:733
  96.1 2.5 collective-permute-done.10.in_other
  103.4 4.4 %all-to-all-start.1 = ((bf16[8,256,128]{2,1,0:T(8,128)(2,1)}), bf16[8,256,128]{2,1,0:T(8,128)(2,1)}, u32[]{:S(2)}, u32[]{:S(2)}) async-start(bf16[8,256,128]{2,1,0:T(8,128)(2,1)} %copy-done.41), calls=%async_computation.1 | async-start | bytes 1048576 | tf_op jit(solution)/shard_map/all_to_all | solution.py:1186
  108.3 6.6 %contract_weigh.1 = (bf16[4,256,512]{2,1,0:T(8,128)(2,1)S(1)}, bf16[4,256,512]{2,1,0:T(8,128)(2,1)}, bf16[8,128,512]{2,1,0:T(8,128)(2,1)S(1)}, bf16[8,128,512]{2,1,0:T(8,128)(2,1)}) custom-call(s32[4]{0:T(128)S(1)} %copy-done.52, bf16[256,1024]{1,0:T(8,128)(2,1)S(1)} %bitcast.52, bf16[256,1024]{1,0:T(8,128)(2,1)S(1)} %collective-permute-done.other.grad_other, ...), custom_call_target="tpu_custom_call" | custom-call | flops 100000000 | bytes 1048576 | tf_op jit(solution)/shard_map/contract_weigh/pallas_call | solution.py:785
  120.0 3.4 %copy-done.3 = bf16[4096,1024]{1,0:T(8,128)(2,1)S(1)} copy-done((bf16[4096,1024]{1,0:T(8,128)(2,1)S(1)}, bf16[4096,1024]{1,0:T(8,128)(2,1)}, u32[]{:S(2)}) %copy-start.3) | copy-done | bytes 8388632
  125.4 10.3 %weigh.1 = (f32[256,1024]{1,0:T(8,128)S(1)}, bf16[256,1024]{1,0:T(8,128)(2,1)}, bf16[4,128,1280]{2,1,0:T(8,128)(2,1)S(1)}, bf16[4,128,1280]{2,1,0:T(8,128)(2,1)}...) custom-call(s32[4]{0:T(128)S(1)} %copy-done.52, bf16[256,1024]{1,0:T(8,128)(2,1)S(1)} %copy-done.38, ...), custom_call_target="tpu_custom_call" | custom-call | flops 100000000 | bytes 1048576 | tf_op jit(solution)/shard_map/weigh/pallas_call | solution.py:864
  141.3 21.7 %attend_back.1 = (bf16[8,3,256,128]{3,2,1,0:T(8,128)(2,1)}, f32[2,8,512]{2,1,0:T(8,128)S(1)}) custom-call(s32[18]{0:T(128)S(1)} %pad_add_fusion.meta_ref, f32[2]{0:T(128)S(1)} %slice_reduce_fusion.1.far_ref, f32[2,512]{1,0:T(2,128)S(1)} %fusion.2.line_ref, f32[8,128,256]{2,1,0:T(8,128)S(1)} %copy-done.62, f32[8,8,256]{2,1,0:T(8,128)S(1)} %get-tuple-element.144.log_ref, ...), custom_call_target="tpu_custom_call" | custom-call | flops 20000000000 | bytes 8388608 | tf_op jit(solution)/shard_map/attend_back/pallas_call | solution.py:519
  163.0 7.9 %collective-permute-done.15.one_got = bf16[4,128,1280]{2,1,0:T(8,128)(2,1)S(1)} collective-permute-done((bf16[4,128,1280]{2,1,0:T(8,128)(2,1)}, bf16[4,128,1280]{2,1,0:T(8,128)(2,1)S(1)}, u32[]{:S(2)}, u32[]{:S(2)}) %collective-permute-start.15) | collective-permute-done | bytes 1310752 | tf_op jit(solution)/shard_map/ppermute | solution.py:1090
  172.0 5.0 %all-to-all-start.2 = ((bf16[8,3,256,128]{3,2,1,0:T(8,128)(2,1)}), bf16[8,3,256,128]{3,2,1,0:T(8,128)(2,1)S(1)}, u32[]{:S(2)}, u32[]{:S(2)}) async-start(bf16[8,3,256,128]{3,2,1,0:T(8,128)(2,1)} %get-tuple-element.157), calls=%async_computation.2 | async-start | bytes 3145728 | tf_op jit(solution)/shard_map/all_to_all | solution.py:1186
  185.2 2.9 second.4
  190.3 6.2 %collective-permute-done.17.one_got = bf16[4,128,512]{2,1,0:T(8,128)(2,1)S(1)} collective-permute-done((bf16[4,128,512]{2,1,0:T(8,128)(2,1)S(1)}, bf16[4,128,512]{2,1,0:T(8,128)(2,1)S(1)}, u32[]{:S(2)}, u32[]{:S(2)}) %collective-permute-start.17) | collective-permute-done | bytes 524320 | tf_op jit(solution)/shard_map/ppermute | solution.py:1090
  196.5 10.9 %collective-permute-done.18.two_got = bf16[4,128,512]{2,1,0:T(8,128)(2,1)S(1)} collective-permute-done((bf16[4,128,512]{2,1,0:T(8,128)(2,1)S(1)}, bf16[4,128,512]{2,1,0:T(8,128)(2,1)S(1)}, u32[]{:S(2)}, u32[]{:S(2)}) %collective-permute-start.18) | collective-permute-done | bytes 524320 | tf_op jit(solution)/shard_map/ppermute | solution.py:1090
  209.8 11.0 %collective-permute-done.21.two_got = bf16[4,64,1280]{2,1,0:T(8,128)(2,1)S(1)} collective-permute-done((bf16[4,64,1280]{2,1,0:T(8,128)(2,1)}, bf16[4,64,1280]{2,1,0:T(8,128)(2,1)S(1)}, u32[]{:S(2)}, u32[]{:S(2)}) %collective-permute-start.21) | collective-permute-done | bytes 655392 | tf_op jit(solution)/shard_map/ppermute | solution.py:1090
  220.9 3.7 %collective-permute-done.19.got = bf16[2,128,1024]{2,1,0:T(8,128)(2,1)S(1)} collective-permute-done((bf16[2,128,1024]{2,1,0:T(8,128)(2,1)}, bf16[2,128,1024]{2,1,0:T(8,128)(2,1)S(1)}, u32[]{:S(2)}, u32[]{:S(2)}) %collective-permute-start.19) | collective-permute-done | bytes 524320 | tf_op jit(solution)/shard_map/ppermute | solution.py:1090
  228.7 3.6 %attend_weigh.1 = (bf16[4,128,768]{2,1,0:T(8,128)(2,1)S(1)}, bf16[4,128,768]{2,1,0:T(8,128)(2,1)}, bf16[8,64,768]{2,1,0:T(8,128)(2,1)S(1)}, bf16[8,64,768]{2,1,0:T(8,128)(2,1)}) custom-call(s32[4]{0:T(128)S(1)} %copy-done.52, bf16[256,1024]{1,0:T(8,128)(2,1)S(1)} %copy-done.56, bf16[256,1024]{1,0:T(8,128)(2,1)S(1)} %collective-permute-done.22.act_other, ...), custom_call_target="tpu_custom_call" | custom-call | flops 2000000000 | bytes 7340032 | tf_op jit(solution)/shard_map/attend_weigh/pallas_call | solution.py:1072
  241.4 16.0 %collective-permute-done.26.got = bf16[128,1024]{1,0:T(8,128)(2,1)} collective-permute-done((bf16[128,1024]{1,0:T(8,128)(2,1)}, bf16[128,1024]{1,0:T(8,128)(2,1)}, u32[]{:S(2)}, u32[]{:S(2)}) %collective-permute-start.26) | collective-permute-done | bytes 262176 | tf_op jit(solution)/shard_map/ppermute | solution.py:1090
  268.0 2.8 copy-done.4
  270.8 3.4 %close.1 = (f32[256,1024]{1,0:T(8,128)}, f32[2,1024]{1,0:T(2,128)S(1)}) custom-call(bf16[8,3,256,128]{3,2,1,0:T(8,128)(2,1)S(1)} %all-to-all-done.2.parts_ref.owned_ref, bf16[256,1024]{1,0:T(8,128)(2,1)S(1)} %bitcast.55, f32[256,1024]{1,0:T(8,128)S(1)} %copy-done.18, f32[1,1024]{1,0:T(1,128)S(1)} %bitcast.59, bf16[1024,3072]{1,0:T(8,128)(2,1)S(1)} %copy-done.4), custom_call_target="tpu_custom_call" | custom-call | flops 2000000000 | bytes 10485760 | tf_op jit(solution)/shard_map/close/pallas_call | solution.py:943
  274.2 2.7 collective-permute-done.30.refs_1_
  276.9 2.9 collective-permute-done.31.got
  283.9 6.5 %collective-permute-done.33.refs_1_ = bf16[64,2560]{1,0:T(8,128)(2,1)S(1)} collective-permute-done((bf16[64,2560]{1,0:T(8,128)(2,1)S(1)}, bf16[64,2560]{1,0:T(8,128)(2,1)S(1)}, u32[]{:S(2)}, u32[]{:S(2)}) %collective-permute-start.33) | collective-permute-done | bytes 327712 | tf_op jit(solution)/shard_map/ppermute | solution.py:1090
  298.2 4.5 %all-to-all-start.3 = ((f32[8,8,128]{2,1,0:T(8,128)}), f32[8,8,128]{2,1,0:T(8,128)S(1)}, u32[]{:S(2)}, u32[]{:S(2)}) async-start(f32[8,8,128]{2,1,0:T(8,128)} %add.210), calls=%async_computation.3 | async-start | bytes 65536 | tf_op jit(solution)/shard_map/all_to_all | solution.py:1186
  (243 shorter events, 95.4 us)
Async XLA Ops:
  0.7 26.8 %collective-permute-start = (bf16[256,1024]{1,0:T(8,128)(2,1)}, bf16[256,1024]{1,0:T(8,128)(2,1)S(1)}, u32[]{:S(2)}, u32[]{:S(2)}) collective-permute-start(bf16[256,1024]{1,0:T(8,128)(2,1)} %bitcast.49), channel_id=1, source_target_pairs={{0,8},{8,0},{16,24},{24,16},{1,9},{9,1},{17,25},{25,17},{2,10},{10... | collective-permute-start | bytes 1572872 | tf_op jit(solution)/shard_map/ppermute | solution.py:1090
  10.7 15.2 %collective-permute-start.2 = (bf16[3,256,128]{2,1,0:T(8,128)(2,1)}, bf16[3,256,128]{2,1,0:T(8,128)(2,1)S(1)}, u32[]{:S(2)}, u32[]{:S(2)}) collective-permute-start(bf16[3,256,128]{2,1,0:T(8,128)(2,1)} %get-tuple-element.123), channel_id=1, source_target_pairs={{0,2},{1,3},{2,0},{3,1},{4,6},{5,7},{6,4},{7,5},{8,10},{9,11},{10,... | collective-permute-start | bytes 589832 | tf_op jit(solution)/shard_map/ppermute | solution.py:1090
  12.3 25.0 %collective-permute-start.3 = (bf16[3,256,128]{2,1,0:T(8,128)(2,1)}, bf16[3,256,128]{2,1,0:T(8,128)(2,1)S(1)}, u32[]{:S(2)}, u32[]{:S(2)}) collective-permute-start(bf16[3,256,128]{2,1,0:T(8,128)(2,1)} %get-tuple-element.124), channel_id=1, source_target_pairs={{0,3},{1,2},{2,1},{3,0},{4,7},{5,6},{6,5},{7,4},{8,11},{9,10},{10,... | collective-permute-start | bytes 589832 | tf_op jit(solution)/shard_map/ppermute | solution.py:1090
  12.3 25.0 %collective-permute-start.4 = (bf16[3,256,128]{2,1,0:T(8,128)(2,1)}, bf16[3,256,128]{2,1,0:T(8,128)(2,1)S(1)}, u32[]{:S(2)}, u32[]{:S(2)}) collective-permute-start(bf16[3,256,128]{2,1,0:T(8,128)(2,1)} %get-tuple-element.125), channel_id=1, source_target_pairs={{0,4},{1,5},{2,6},{3,7},{4,0},{5,1},{6,2},{7,3},{8,12},{9,13},{10,... | collective-permute-start | bytes 589832 | tf_op jit(solution)/shard_map/ppermute | solution.py:1090
  16.7 26.7 %collective-permute-start.5 = (bf16[3,256,128]{2,1,0:T(8,128)(2,1)}, bf16[3,256,128]{2,1,0:T(8,128)(2,1)S(1)}, u32[]{:S(2)}, u32[]{:S(2)}) collective-permute-start(bf16[3,256,128]{2,1,0:T(8,128)(2,1)} %get-tuple-element.126), channel_id=1, source_target_pairs={{0,5},{1,4},{2,7},{3,6},{4,1},{5,0},{6,3},{7,2},{8,13},{9,12},{10,... | collective-permute-start | bytes 589832 | tf_op jit(solution)/shard_map/ppermute | solution.py:1090
  26.0 17.4 %collective-permute-start.6 = (bf16[3,256,128]{2,1,0:T(8,128)(2,1)}, bf16[3,256,128]{2,1,0:T(8,128)(2,1)S(1)}, u32[]{:S(2)}, u32[]{:S(2)}) collective-permute-start(bf16[3,256,128]{2,1,0:T(8,128)(2,1)} %get-tuple-element.127), channel_id=1, source_target_pairs={{0,6},{1,7},{2,4},{3,5},{4,2},{5,3},{6,0},{7,1},{8,14},{9,15},{10,... | collective-permute-start | bytes 589832 | tf_op jit(solution)/shard_map/ppermute | solution.py:1090
  27.5 15.9 %collective-permute-start.7 = (bf16[3,256,128]{2,1,0:T(8,128)(2,1)}, bf16[3,256,128]{2,1,0:T(8,128)(2,1)S(1)}, u32[]{:S(2)}, u32[]{:S(2)}) collective-permute-start(bf16[3,256,128]{2,1,0:T(8,128)(2,1)} %get-tuple-element.128), channel_id=1, source_target_pairs={{0,7},{1,6},{2,5},{3,4},{4,3},{5,2},{6,1},{7,0},{8,15},{9,14},{10,... | collective-permute-start | bytes 589832 | tf_op jit(solution)/shard_map/ppermute | solution.py:1090
  103.4 35.3 %all-to-all-start.1 = ((bf16[8,256,128]{2,1,0:T(8,128)(2,1)}), bf16[8,256,128]{2,1,0:T(8,128)(2,1)}, u32[]{:S(2)}, u32[]{:S(2)}) async-start(bf16[8,256,128]{2,1,0:T(8,128)(2,1)} %copy-done.41), calls=%async_computation.1 | async-start | bytes 1048576 | tf_op jit(solution)/shard_map/all_to_all | solution.py:1186
  107.7 12.3 %collective-permute-start.9 = (bf16[256,1024]{1,0:T(8,128)(2,1)}, bf16[256,1024]{1,0:T(8,128)(2,1)S(1)}, u32[]{:S(2)}, u32[]{:S(2)}) collective-permute-start(bf16[256,1024]{1,0:T(8,128)(2,1)} %copy-done.35), channel_id=1, source_target_pairs={{0,8},{8,0},{16,24},{24,16},{1,9},{9,1},{17,25},{25,17},{2,10},{10... | collective-permute-start | bytes 1572872 | tf_op jit(solution)/shard_map/ppermute | solution.py:1090
  107.9 12.1 %collective-permute-start.11 = (bf16[256,512]{1,0:T(8,128)(2,1)S(1)}, bf16[256,512]{1,0:T(8,128)(2,1)S(1)}, u32[]{:S(2)}, u32[]{:S(2)}) collective-permute-start(bf16[256,512]{1,0:T(8,128)(2,1)S(1)} %get-tuple-element.136), channel_id=1, source_target_pairs={{0,8},{8,0},{16,24},{24,16},{1,9},{9,1},{17,25},{25,17},{2,10},{10... | collective-permute-start | bytes 786440 | tf_op jit(solution)/shard_map/ppermute | solution.py:1090
  116.9 46.1 %collective-permute-start.13 = (bf16[4,256,512]{2,1,0:T(8,128)(2,1)}, bf16[4,256,512]{2,1,0:T(8,128)(2,1)}, u32[]{:S(2)}, u32[]{:S(2)}) collective-permute-start(bf16[4,256,512]{2,1,0:T(8,128)(2,1)} %get-tuple-element.150), channel_id=1, source_target_pairs={{0,1},{1,0},{2,3},{3,2},{4,5},{5,4},{6,7},{7,6},{8,9},{9,8},{10,11... | collective-permute-start | bytes 3145736 | tf_op jit(solution)/shard_map/ppermute | solution.py:1090
  118.5 44.5 %collective-permute-start.14 = (bf16[8,128,512]{2,1,0:T(8,128)(2,1)}, bf16[8,128,512]{2,1,0:T(8,128)(2,1)}, u32[]{:S(2)}, u32[]{:S(2)}) collective-permute-start(bf16[8,128,512]{2,1,0:T(8,128)(2,1)} %get-tuple-element.152), channel_id=1, source_target_pairs={{0,16},{8,24},{16,0},{24,8},{1,17},{9,25},{17,1},{25,9},{2,18},{10... | collective-permute-start | bytes 3145736 | tf_op jit(solution)/shard_map/ppermute | solution.py:1090
  137.8 33.2 %collective-permute-start.15 = (bf16[4,128,1280]{2,1,0:T(8,128)(2,1)}, bf16[4,128,1280]{2,1,0:T(8,128)(2,1)S(1)}, u32[]{:S(2)}, u32[]{:S(2)}) collective-permute-start(bf16[4,128,1280]{2,1,0:T(8,128)(2,1)} %get-tuple-element.154), channel_id=1, source_target_pairs={{0,1},{1,0},{2,3},{3,2},{4,5},{5,4},{6,7},{7,6},{8,9},{9,8},{10,11... | collective-permute-start | bytes 3932168 | tf_op jit(solution)/shard_map/ppermute | solution.py:1090
  138.2 33.8 %collective-permute-start.16 = (bf16[8,64,1280]{2,1,0:T(8,128)(2,1)}, bf16[8,64,1280]{2,1,0:T(8,128)(2,1)}, u32[]{:S(2)}, u32[]{:S(2)}) collective-permute-start(bf16[8,64,1280]{2,1,0:T(8,128)(2,1)} %get-tuple-element.156), channel_id=1, source_target_pairs={{0,16},{8,24},{16,0},{24,8},{1,17},{9,25},{17,1},{25,9},{2,18},{10... | collective-permute-start | bytes 3932168 | tf_op jit(solution)/shard_map/ppermute | solution.py:1090
  172.0 53.5 %all-to-all-start.2 = ((bf16[8,3,256,128]{3,2,1,0:T(8,128)(2,1)}), bf16[8,3,256,128]{3,2,1,0:T(8,128)(2,1)S(1)}, u32[]{:S(2)}, u32[]{:S(2)}) async-start(bf16[8,3,256,128]{3,2,1,0:T(8,128)(2,1)} %get-tuple-element.157), calls=%async_computation.2 | async-start | bytes 3145728 | tf_op jit(solution)/shard_map/all_to_all | solution.py:1186
  181.6 14.9 %collective-permute-start.17 = (bf16[4,128,512]{2,1,0:T(8,128)(2,1)S(1)}, bf16[4,128,512]{2,1,0:T(8,128)(2,1)S(1)}, u32[]{:S(2)}, u32[]{:S(2)}) collective-permute-start(bf16[4,128,512]{2,1,0:T(8,128)(2,1)S(1)} %get-tuple-element.163), channel_id=1, source_target_pairs={{0,16},{8,24},{16,0},{24,8},{1,17},{9,25},{17,1},{25,9},{2,18},{10... | collective-permute-start | bytes 1572872 | tf_op jit(solution)/shard_map/ppermute | solution.py:1090
  183.2 24.3 %collective-permute-start.18 = (bf16[4,128,512]{2,1,0:T(8,128)(2,1)S(1)}, bf16[4,128,512]{2,1,0:T(8,128)(2,1)S(1)}, u32[]{:S(2)}, u32[]{:S(2)}) collective-permute-start(bf16[4,128,512]{2,1,0:T(8,128)(2,1)S(1)} %get-tuple-element.165), channel_id=1, source_target_pairs={{0,1},{1,0},{2,3},{3,2},{4,5},{5,4},{6,7},{7,6},{8,9},{9,8},{10,11... | collective-permute-start | bytes 1572872 | tf_op jit(solution)/shard_map/ppermute | solution.py:1090
  189.8 20.0 %collective-permute-start.20 = (bf16[4,64,1280]{2,1,0:T(8,128)(2,1)}, bf16[4,64,1280]{2,1,0:T(8,128)(2,1)S(1)}, u32[]{:S(2)}, u32[]{:S(2)}) collective-permute-start(bf16[4,64,1280]{2,1,0:T(8,128)(2,1)} %get-tuple-element.173), channel_id=1, source_target_pairs={{0,16},{8,24},{16,0},{24,8},{1,17},{9,25},{17,1},{25,9},{2,18},{10... | collective-permute-start | bytes 1966088 | tf_op jit(solution)/shard_map/ppermute | solution.py:1090
  190.3 30.5 %collective-permute-start.21 = (bf16[4,64,1280]{2,1,0:T(8,128)(2,1)}, bf16[4,64,1280]{2,1,0:T(8,128)(2,1)S(1)}, u32[]{:S(2)}, u32[]{:S(2)}) collective-permute-start(bf16[4,64,1280]{2,1,0:T(8,128)(2,1)} %get-tuple-element.175), channel_id=1, source_target_pairs={{0,1},{1,0},{2,3},{3,2},{4,5},{5,4},{6,7},{7,6},{8,9},{9,8},{10,11... | collective-permute-start | bytes 1966088 | tf_op jit(solution)/shard_map/ppermute | solution.py:1090
  209.8 14.8 %collective-permute-start.19 = (bf16[2,128,1024]{2,1,0:T(8,128)(2,1)}, bf16[2,128,1024]{2,1,0:T(8,128)(2,1)S(1)}, u32[]{:S(2)}, u32[]{:S(2)}) collective-permute-start(bf16[2,128,1024]{2,1,0:T(8,128)(2,1)} %get-tuple-element.167), channel_id=1, source_target_pairs={{0,2},{1,3},{2,0},{3,1},{4,6},{5,7},{6,4},{7,5},{8,10},{9,11},{10,... | collective-permute-start | bytes 1572872 | tf_op jit(solution)/shard_map/ppermute | solution.py:1090
  232.3 27.4 %collective-permute-start.24 = (bf16[4,128,768]{2,1,0:T(8,128)(2,1)}, bf16[4,128,768]{2,1,0:T(8,128)(2,1)}, u32[]{:S(2)}, u32[]{:S(2)}) collective-permute-start(bf16[4,128,768]{2,1,0:T(8,128)(2,1)} %get-tuple-element.184), channel_id=1, source_target_pairs={{0,1},{1,0},{2,3},{3,2},{4,5},{5,4},{6,7},{7,6},{8,9},{9,8},{10,11... | collective-permute-start | bytes 2359304 | tf_op jit(solution)/shard_map/ppermute | solution.py:1090
  233.6 26.1 %collective-permute-start.25 = (bf16[8,64,768]{2,1,0:T(8,128)(2,1)}, bf16[8,64,768]{2,1,0:T(8,128)(2,1)}, u32[]{:S(2)}, u32[]{:S(2)}) collective-permute-start(bf16[8,64,768]{2,1,0:T(8,128)(2,1)} %get-tuple-element.186), channel_id=1, source_target_pairs={{0,16},{8,24},{16,0},{24,8},{1,17},{9,25},{17,1},{25,9},{2,18},{10... | collective-permute-start | bytes 2359304 | tf_op jit(solution)/shard_map/ppermute | solution.py:1090
  237.5 22.1 %collective-permute-start.27 = (bf16[2,64,2560]{2,1,0:T(8,128)(2,1)}, bf16[2,64,2560]{2,1,0:T(8,128)(2,1)}, u32[]{:S(2)}, u32[]{:S(2)}) collective-permute-start(bf16[2,64,2560]{2,1,0:T(8,128)(2,1)} %get-tuple-element.196), channel_id=1, source_target_pairs={{0,2},{1,3},{2,0},{3,1},{4,6},{5,7},{6,4},{7,5},{8,10},{9,11},{10,... | collective-permute-start | bytes 1966088 | tf_op jit(solution)/shard_map/ppermute | solution.py:1090
  238.8 18.6 %collective-permute-start.26 = (bf16[128,1024]{1,0:T(8,128)(2,1)}, bf16[128,1024]{1,0:T(8,128)(2,1)}, u32[]{:S(2)}, u32[]{:S(2)}) collective-permute-start(bf16[128,1024]{1,0:T(8,128)(2,1)} %get-tuple-element.190), channel_id=1, source_target_pairs={{0,4},{1,5},{2,6},{3,7},{4,0},{5,1},{6,2},{7,3},{8,12},{9,13},{10,... | collective-permute-start | bytes 786440 | tf_op jit(solution)/shard_map/ppermute | solution.py:1090
  261.5 18.3 %collective-permute-start.28 = (bf16[4,64,768]{2,1,0:T(8,128)(2,1)S(1)}, bf16[4,64,768]{2,1,0:T(8,128)(2,1)S(1)}, u32[]{:S(2)}, u32[]{:S(2)}) collective-permute-start(bf16[4,64,768]{2,1,0:T(8,128)(2,1)S(1)} %get-tuple-element.202), channel_id=1, source_target_pairs={{0,16},{8,24},{16,0},{24,8},{1,17},{9,25},{17,1},{25,9},{2,18},{10... | collective-permute-start | bytes 1179656 | tf_op jit(solution)/shard_map/ppermute | solution.py:1090
  262.1 17.7 %collective-permute-start.29 = (bf16[4,64,768]{2,1,0:T(8,128)(2,1)S(1)}, bf16[4,64,768]{2,1,0:T(8,128)(2,1)S(1)}, u32[]{:S(2)}, u32[]{:S(2)}) collective-permute-start(bf16[4,64,768]{2,1,0:T(8,128)(2,1)S(1)} %get-tuple-element.204), channel_id=1, source_target_pairs={{0,1},{1,0},{2,3},{3,2},{4,5},{5,4},{6,7},{7,6},{8,9},{9,8},{10,11... | collective-permute-start | bytes 1179656 | tf_op jit(solution)/shard_map/ppermute | solution.py:1090
  264.1 15.7 %collective-permute-start.31 = (bf16[64,2560]{1,0:T(8,128)(2,1)S(1)}, bf16[64,2560]{1,0:T(8,128)(2,1)S(1)}, u32[]{:S(2)}, u32[]{:S(2)}) collective-permute-start(bf16[64,2560]{1,0:T(8,128)(2,1)S(1)} %get-tuple-element.210), channel_id=1, source_target_pairs={{0,4},{1,5},{2,6},{3,7},{4,0},{5,1},{6,2},{7,3},{8,12},{9,13},{10,... | collective-permute-start | bytes 983048 | tf_op jit(solution)/shard_map/ppermute | solution.py:1090
  282.3 27.1 %collective-permute-start.12 = (bf16[256,1024]{1,0:T(8,128)(2,1)}, bf16[256,1024]{1,0:T(8,128)(2,1)}, u32[]{:S(2)}, u32[]{:S(2)}) collective-permute-start(bf16[256,1024]{1,0:T(8,128)(2,1)} %get-tuple-element.142), channel_id=1, source_target_pairs={{0,8},{8,0},{16,24},{24,16},{1,9},{9,1},{17,25},{25,17},{2,10},{10... | collective-permute-start | bytes 1572872 | tf_op jit(solution)/shard_map/ppermute | solution.py:1090
  293.6 11.4 %collective-permute-start.35 = (bf16[64,1536]{1,0:T(8,128)(2,1)}, bf16[64,1536]{1,0:T(8,128)(2,1)S(1)}, u32[]{:S(2)}, u32[]{:S(2)}) collective-permute-start(bf16[64,1536]{1,0:T(8,128)(2,1)} %get-tuple-element.223), channel_id=1, source_target_pairs={{0,4},{1,5},{2,6},{3,7},{4,0},{5,1},{6,2},{7,3},{8,12},{9,13},{10,... | collective-permute-start | bytes 589832 | tf_op jit(solution)/shard_map/ppermute | solution.py:1090
  295.2 16.4 %collective-permute-start.41 = (bf16[128,1024]{1,0:T(8,128)(2,1)S(1)}, bf16[128,1024]{1,0:T(8,128)(2,1)}, u32[]{:S(2)}, u32[]{:S(2)}) collective-permute-start(bf16[128,1024]{1,0:T(8,128)(2,1)S(1)} %last.3.refs_0_), channel_id=1, source_target_pairs={{0,8},{8,0},{16,24},{24,16},{1,9},{9,1},{17,25},{25,17},{2,10},{10... | collective-permute-start | bytes 786440 | tf_op jit(solution)/shard_map/ppermute | solution.py:1090
  295.2 16.4 %collective-permute-start.42 = (bf16[128,1024]{1,0:T(8,128)(2,1)S(1)}, bf16[128,1024]{1,0:T(8,128)(2,1)}, u32[]{:S(2)}, u32[]{:S(2)}) collective-permute-start(bf16[128,1024]{1,0:T(8,128)(2,1)S(1)} %collective-permute-done.30.refs_1_), channel_id=1, source_target_pairs={{0,8},{8,0},{16,24},{24,16},{1,9},{9,1},{17,25},{25,17},{2,10},{10... | collective-permute-start | bytes 786440 | tf_op jit(solution)/shard_map/ppermute | solution.py:1090
  298.2 16.4 %all-to-all-start.3 = ((f32[8,8,128]{2,1,0:T(8,128)}), f32[8,8,128]{2,1,0:T(8,128)S(1)}, u32[]{:S(2)}, u32[]{:S(2)}) async-start(f32[8,8,128]{2,1,0:T(8,128)} %add.210), calls=%async_computation.3 | async-start | bytes 65536 | tf_op jit(solution)/shard_map/all_to_all | solution.py:1186
  (78 other events, 645.9 us)

commit v4 on v3

--- a/solution.py
+++ b/solution.py
@@ -307,13 +307,13 @@
         total = total + (position >= meta_ref[first + item]).astype(jnp.int32)
     return total
 
-def _allowed(meta_ref, peers, items, rows, i, j, diagonal):
+def _allowed(meta_ref, peers, items, rows, i, j, which, needed):
     first = 1 + 2 * peers
     q_seg = _segments(i * rows + lax.broadcasted_iota(jnp.int32, (1, rows), 1), meta_ref, first, items)
     k_seg = _segments(j * rows + lax.broadcasted_iota(jnp.int32, (rows, 1), 0), meta_ref, first, items)
-    k_seg = jnp.where(k_seg < items, k_seg, -1)
+    k_seg = jnp.where((k_seg < items) & needed if which == 1 else k_seg < items, k_seg, -1)
     same = q_seg == k_seg
-    if diagonal:
+    if which == 0:
         key = lax.broadcasted_iota(jnp.int32, (rows, rows), 0)
         query = lax.broadcasted_iota(jnp.int32, (rows, rows), 1)
         return (same & (key < query)) | (key == query)
@@ -363,39 +363,42 @@
         whole = jnp.minimum(meta_ref[1 + peers + i], i - 1)
         queries = _split(qkv[i, 0].astype(jnp.float32) * 0.125)
 
-        def put(j, which, masked, peaks):
+        def put(j, slot, which, masked, peaks):
             key = qkv[j, 1]
             if masked:
-                allowed = _allowed(meta_ref, peers, items, rows, i, j, which == 0)
+                allowed = _allowed(meta_ref, peers, items, rows, i, j, which, low < i)
             new = []
             for head in range(2):
                 raw = _biased(_dot(key, queries[head], ((1,), (1,))), bias, far_ref, head, which, rows)
                 if masked:
                     raw = jnp.where(allowed, raw, masked_score)
-                scores[head, j] = raw
+                scores[head, slot] = raw
                 new.append(jnp.maximum(peaks[head], _fold(raw, jnp.maximum)))
             return tuple(new)
 
         start = jnp.full((8, rows), masked_score, jnp.float32)
-        peaks = put(i, 0, True, (start, start))
-        peaks = lax.cond(low < i, lambda p: put(i - 1, 1, True, p), lambda p: p, peaks)
-        peaks = lax.fori_loop(low, whole, lambda j, p: put(j, 2, True, p), peaks)
-        peaks = lax.fori_loop(jnp.maximum(low, whole), i - 1, lambda j, p: put(j, 2, False, p), peaks)
+        before = jnp.maximum(i - 1, 0)
+        peaks = put(i, peers, 0, True, (start, start))
+        peaks = put(before, peers + 1, 1, True, peaks)
+        peaks = lax.fori_loop(low, whole, lambda j, p: put(j, j, 2, True, p), peaks)
+        peaks = lax.fori_loop(jnp.maximum(low, whole), i - 1, lambda j, p: put(j, j, 2, False, p), peaks)
         tops = [jnp.max(peak, axis=0, keepdims=True) for peak in peaks]
 
-        def mix(j, carry):
+        def mix(j, slot, carry):
             sums, total = carry
             value = turned[j]
             new = []
             both = []
             for head in range(2):
-                weight = jnp.exp(scores[head, j] - tops[head])
+                weight = jnp.exp(scores[head, slot] - tops[head])
                 new.append(sums[head] + _fold(weight, jnp.add))
                 both.append(_dot(value[64 * head:64 * head + 64], weight.astype(jnp.bfloat16), ((1,), (0,))))
             return tuple(new), total + jnp.concatenate(both)
 
         nothing = jnp.zeros((8, rows), jnp.float32)
-        sums, total = lax.fori_loop(low, i + 1, mix, ((nothing, nothing), jnp.zeros((128, rows), jnp.float32)))
+        carry = ((nothing, nothing), jnp.zeros((128, rows), jnp.float32))
+        carry = mix(before, peers + 1, mix(i, peers, carry))
+        sums, total = lax.fori_loop(low, i - 1, lambda j, c: mix(j, j, c), carry)
         sums = [jnp.sum(s, axis=0, keepdims=True) for s in sums]
         total = total / jnp.where(upper, sums[0], sums[1])
         wide_ref[i] = total
@@ -425,7 +428,7 @@
         scratch_shapes=[
             pltpu.VMEM((peers, 128, rows), jnp.bfloat16),
             pltpu.VMEM((2, rows, 2 * rows), jnp.float32),
-            pltpu.VMEM((2, peers, rows, rows), jnp.float32),
+            pltpu.VMEM((2, peers + 2, rows, rows), jnp.float32),
         ],
         compiler_params=pltpu.CompilerParams(vmem_limit_bytes=18 * 2**20),
         cost_estimate=pl.CostEstimate(flops=8 * 10**9, bytes_accessed=4 * 2**20, transcendentals=3 * 10**6),
@@ -458,7 +461,7 @@
             value = qkv[j, 2]
             across = turned[j]
             if masked:
-                allowed = _allowed(meta_ref, peers, items, rows, i, j, which == 0)
+                allowed = _allowed(meta_ref, peers, items, rows, i, j, which, low < i)
             dk = jnp.zeros((rows, 128), jnp.float32)
             dv = jnp.zeros((rows, 128), jnp.float32)
             both = []
@@ -484,7 +487,7 @@
             return dquery + jnp.concatenate(both)
 
         dquery = step(i, 0, True, jnp.zeros((128, rows), jnp.float32))
-        dquery = lax.cond(low < i, lambda d: step(i - 1, 1, True, d), lambda d: d, dquery)
+        dquery = step(jnp.maximum(i - 1, 0), 1, True, dquery)
         dquery = lax.fori_loop(low, whole, lambda j, d: step(j, 2, True, d), dquery)
         dquery = lax.fori_loop(jnp.maximum(low, whole), i - 1, lambda j, d: step(j, 2, False, d), dquery)
         all_ref[i, 0] = (jnp.transpose(dquery) * 0.125).astype(jnp.bfloat16)
@@ -747,35 +750,26 @@
     )(meta, act_mine, act_other, pulled, expand_weight)
 
 
-def contract_weigh_kernel(part, meta_ref, grad_mine, grad_other, low_ref, one_keep, one_send, two_keep, two_send, grads):
-    step = pl.program_id(0)
-    x, y = meta_ref[1], meta_ref[2]
-    cut, half = one_keep.shape[2], part // 2
-
-    @pl.when(step == 0)
-    def _():
-        _both(grads, grad_mine, grad_other)
-
-    grad = _dot(low_ref[...], grads[...], ((0,), (0,))).astype(jnp.bfloat16)
-    level = step // 2
-
-    @pl.when(step % 2 == x)
-    def _():
-        one_keep[level] = grad[:, :cut]
-
-    @pl.when(step % 2 != x)
-    def _():
-        one_send[level] = grad[:, :cut]
-
-    @pl.when(y == 0)
-    def _():
-        two_keep[step] = grad[:half, cut:]
-        two_send[step] = grad[half:, cut:]
-
-    @pl.when(y != 0)
-    def _():
-        two_keep[step] = grad[half:, cut:]
-        two_send[step] = grad[:half, cut:]
+def _split_rows(held, x, y, one_keep, one_send, two_keep, two_send):
+    peers, rows, _ = held.shape
+    cut, half = one_keep.shape[2], rows // 2
+    mine = pl.ds(pl.multiple_of(y * half, half), half)
+    other = pl.ds(pl.multiple_of((1 - y) * half, half), half)
+    for place in range(peers // 2):
+        one_keep[place] = held[2 * place + x, :, :cut]
+        one_send[place] = held[2 * place + 1 - x, :, :cut]
+    for place in range(peers):
+        two_keep[place] = held[place, mine, cut:]
+        two_send[place] = held[place, other, cut:]
+
+
+def contract_weigh_kernel(meta_ref, grad_mine, grad_other, low_ref, *refs):
+    outs, grads, held = refs[:4], refs[4], refs[5]
+    _both(grads, grad_mine, grad_other)
+    part = held.shape[1]
+    for piece in range(held.shape[0]):
+        held[piece] = _dot(low_ref[:, piece * part : (piece + 1) * part], grads[...], ((0,), (0,))).astype(jnp.bfloat16)
+    _split_rows(held, meta_ref[1], meta_ref[2], *outs)
 
 
 def contract_weigh(meta, grad_mine, grad_other, low, peers):
@@ -783,105 +777,78 @@
     part, cut = low.shape[1] // peers, width // 2
     shapes = [(peers // 2, part, cut), (peers // 2, part, cut), (peers, part // 2, cut), (peers, part // 2, cut)]
     return pl.pallas_call(
-        partial(contract_weigh_kernel, part),
+        contract_weigh_kernel,
         out_shape=[jax.ShapeDtypeStruct(shape, jnp.bfloat16) for shape in shapes],
-        grid_spec=pltpu.PrefetchScalarGridSpec(
-            num_scalar_prefetch=1,
-            grid=(peers,),
-            in_specs=[_whole(rows, width)] * 2 + [_across(2 * rows, part)],
-            out_specs=[_whole(*shape) for shape in shapes],
-            scratch_shapes=[pltpu.VMEM((2 * rows, width), jnp.bfloat16)],
-        ),
-        compiler_params=_params(12),
+        in_specs=_specs("svvv"),
+        out_specs=_specs("vvvv"),
+        scratch_shapes=[pltpu.VMEM((2 * rows, width), jnp.bfloat16), pltpu.VMEM((peers, part, width), jnp.bfloat16)],
+        compiler_params=_params(14),
         cost_estimate=pl.CostEstimate(flops=10**8, bytes_accessed=2**20, transcendentals=0),
         name="contract_weigh",
     )(meta, grad_mine, grad_other, low)
 
 
-def weigh_kernel(
-    peers, rows, part, meta_ref, act_mine, act_other, mix_mine, mix_other, right_mine, right_other, low_ref, back_ref, contract_ref,
-    out_keep, out_send, one_keep, one_send, two_keep, two_send, turned, total, block_grad,
-):
-    step = pl.program_id(0)
-    x, y = meta_ref[1], meta_ref[2]
-    group = block_grad.shape[1]
-    half, near = group // 2, peers // 2
-
-    def over_x(columns):
-        for place in range(near):
-            one_keep[place, :, columns] = block_grad[2 * place + x]
-            one_send[place, :, columns] = block_grad[2 * place + 1 - x]
-
-    def over_y(columns):
-        for place in range(peers):
-            two_keep[place, :, columns] = block_grad[place, pl.ds(pl.multiple_of(y * half, half), half), :]
-            two_send[place, :, columns] = block_grad[place, pl.ds(pl.multiple_of((1 - y) * half, half), half), :]
-
-    @pl.when(step == 0)
-    def _():
-        turned[:, :rows] = _turned(mix_mine[...]).astype(jnp.bfloat16)
-        turned[:, rows:] = _turned(mix_other[...]).astype(jnp.bfloat16)
-        right = jnp.concatenate([right_mine[...], right_other[...]])
-        grad = _dot(turned[...], right, ((1,), (0,))).astype(jnp.bfloat16)
-        tail = pl.ds(near * part, part)
-        block_grad[...] = grad[:, :part].reshape(peers, group, part)
-        over_x(tail)
-        block_grad[...] = grad[:, part:].reshape(peers, group, part)
-        over_y(tail)
-        turned[:, :rows] = _turned(act_mine[...]).astype(jnp.bfloat16)
-        turned[:, rows:] = _turned(act_other[...]).astype(jnp.bfloat16)
-        total[...] = jnp.zeros_like(total)
-
-    total[...] += _dot(low_ref[...], contract_ref[...], ((1,), (0,)))
-    block_grad[...] = _dot(turned[...], back_ref[...], ((1,), (0,))).astype(jnp.bfloat16).reshape(peers, group, part)
-
-    @pl.when(step < near)
-    def _():
-        over_x(pl.ds(pl.multiple_of(step * part, part), part))
-
-    @pl.when(step >= near)
-    def _():
-        over_y(pl.ds(pl.multiple_of((step - near) * part, part), part))
-
-    @pl.when(step == peers - 1)
-    def _():
-        out_keep[...] = total[:rows]
-        out_send[...] = total[rows:].astype(jnp.bfloat16)
-
-
-def weigh(meta, act_mine, act_other, mix_mine, mix_other, right_mine, right_other, low, back, contract_weight, peers):
+def weigh_kernel(meta_ref, act_mine, act_other, mix_mine, mix_other, right_mine, right_other, back_ref, *refs):
+    outs, left, held = refs[:4], refs[4], refs[5]
+    peers, group, span = held.shape
+    wide = back_ref.shape[1] // 2
+    cut = span // 2
+    _both(left, mix_mine, mix_other)
+    right = jnp.concatenate([right_mine[...], right_other[...]])
+    grad = _dot(left[...], right, ((0,), (0,))).astype(jnp.bfloat16)
+    quarter = grad.shape[1] // 2
+    held[:, :, wide:cut] = grad[:, :quarter].reshape(peers, group, quarter)
+    held[:, :, cut + wide :] = grad[:, quarter:].reshape(peers, group, quarter)
+    _both(left, act_mine, act_other)
+    for side in range(2):
+        grad = _dot(left[...], back_ref[:, side * wide : (side + 1) * wide], ((0,), (0,))).astype(jnp.bfloat16)
+        held[:, :, side * cut : side * cut + wide] = grad.reshape(peers, group, wide)
+    _split_rows(held, meta_ref[1], meta_ref[2], *outs)
+
+
+def weigh(meta, act_mine, act_other, mix_mine, mix_other, right_mine, right_other, back, peers):
     rows, width = act_mine.shape
-    part = contract_weight.shape[0] // (2 * peers)
-    group, span = width // peers, part * (peers // 2 + 1)
-    shapes = [
-        ((rows, width), jnp.float32),
-        ((rows, width), jnp.bfloat16),
-        ((peers // 2, group, span), jnp.bfloat16),
-        ((peers // 2, group, span), jnp.bfloat16),
-        ((peers, group // 2, span), jnp.bfloat16),
-        ((peers, group // 2, span), jnp.bfloat16),
-    ]
+    group, cut = width // peers, back.shape[1] // 2 + width // 4
+    shapes = [(peers // 2, group, cut), (peers // 2, group, cut), (peers, group // 2, cut), (peers, group // 2, cut)]
     return pl.pallas_call(
-        partial(weigh_kernel, peers, rows, part),
-        out_shape=[jax.ShapeDtypeStruct(*shape) for shape in shapes],
-        grid_spec=pltpu.PrefetchScalarGridSpec(
-            num_scalar_prefetch=1,
-            grid=(peers,),
-            in_specs=[_whole(rows, width)] * 4
-            + [_whole(rows, width // 2)] * 2
-            + [_across(2 * rows, part)] * 2
-            + [pl.BlockSpec((part, width), lambda step, meta_ref: (2 * step + meta_ref[3], 0))],
-            out_specs=[_whole(*shape) for shape, _ in shapes],
-            scratch_shapes=[
-                pltpu.VMEM((width, 2 * rows), jnp.bfloat16),
-                pltpu.VMEM((2 * rows, width), jnp.float32),
-                pltpu.VMEM((peers, group, part), jnp.bfloat16),
-            ],
-        ),
-        compiler_params=_params(28),
+        weigh_kernel,
+        out_shape=[jax.ShapeDtypeStruct(shape, jnp.bfloat16) for shape in shapes],
+        in_specs=_specs("svvvvvvv"),
+        out_specs=_specs("vvvv"),
+        scratch_shapes=[pltpu.VMEM((2 * rows, width), jnp.bfloat16), pltpu.VMEM((peers, group, 2 * cut), jnp.bfloat16)],
+        compiler_params=_params(20),
         cost_estimate=pl.CostEstimate(flops=10**8, bytes_accessed=2**20, transcendentals=0),
         name="weigh",
-    )(meta, act_mine, act_other, mix_mine, mix_other, right_mine, right_other, low, back, contract_weight)
+    )(meta, act_mine, act_other, mix_mine, mix_other, right_mine, right_other, back)
+
+
+def emit_kernel(meta_ref, low_ref, contract_ref, keep_ref, send_ref, weights, arrived):
+    core = meta_ref[3]
+    rows, pieces = keep_ref.shape[0], arrived.shape[0]
+    part = weights.shape[0] // pieces
+    copies = []
+    for piece in range(pieces):
+        at = pl.ds(pl.multiple_of((2 * piece + core) * part, part), part)
+        copies.append(pltpu.make_async_copy(contract_ref.at[at], weights.at[pl.ds(piece * part, part)], arrived.at[piece]))
+        copies[-1].start()
+    for copy in copies:
+        copy.wait()
+    keep_ref[...] = _dot(low_ref[:rows], weights[...], ((1,), (0,)))
+    send_ref[...] = _dot(low_ref[rows:], weights[...], ((1,), (0,))).astype(jnp.bfloat16)
+
+
+def emit(meta, low, contract_weight, peers):
+    rows, width = low.shape[0] // 2, contract_weight.shape[1]
+    return pl.pallas_call(
+        emit_kernel,
+        out_shape=[jax.ShapeDtypeStruct((rows, width), jnp.float32), jax.ShapeDtypeStruct((rows, width), jnp.bfloat16)],
+        in_specs=_specs("svh"),
+        out_specs=_specs("vv"),
+        scratch_shapes=[pltpu.VMEM((low.shape[1], width), jnp.bfloat16), pltpu.SemaphoreType.DMA((peers,))],
+        compiler_params=_params(30),
+        cost_estimate=pl.CostEstimate(flops=2 * 10**9, bytes_accessed=8 * 2**20, transcendentals=0),
+        name="emit",
+    )(meta, low, contract_weight)
 
 
 def turn_kernel(meta_ref, in_mine, in_other, middle_ref, grad_ref, gain_ref, weight_ref, heads_ref, total_ref, keep_ref, send_ref, sums_ref):
@@ -1194,22 +1161,25 @@
     act_other = flipped(act_second, "seq", 1)
     attn_other = flipped(attn_low, "seq", 1)
     in_keep, in_send, hidden_low, hidden_back = feed(here, act_second, act_other, pulled, expand_weight, peers)
+    in_send = flipped(in_send, "seq", 1)
+    contract_keep, *contract_parts = contract_weigh(here, grad_out, grad_other, hidden_low, peers)
+    in_send, contract_keep, *contract_parts = lax.optimization_barrier((in_send, contract_keep, *contract_parts))
+    contract_parts = over_first(contract_keep, *contract_parts)
     grad_heads, grad_middle, keep_low, send_low, sums_second = turn(
-        here, in_keep, flipped(in_send, "seq", 1), middle, grad_out, gain_second, merge_weight, peers
-    )
-    contract_parts = over_first(*contract_weigh(here, grad_out, grad_other, after(hidden_low, grad_heads), peers))
-    out_keep, out_send, *expand_parts = weigh(
-        here, act_second, act_other, attn_low, attn_other, keep_low, flipped(send_low, "seq", 1), hidden_low, hidden_back, contract_weight, peers
-    )
-    expand_parts = over_first(*expand_parts)
-
-    grad_heads, out_send = lax.optimization_barrier((to_all(grad_heads), out_send))
+        here, in_keep, in_send, middle, grad_out, gain_second, merge_weight, peers
+    )
+    expand_parts = weigh(here, act_second, act_other, attn_low, attn_other, keep_low, flipped(send_low, "seq", 1), hidden_back, peers)
+    expand_keep = expand_parts[0]
+    _, *expand_parts = over_first(*expand_parts)
+
+    grad_heads, expand_keep, *contract_parts = lax.optimization_barrier((to_all(grad_heads), expand_keep, *contract_parts))
     back_all, line_grad = attend_back(meta, far, lines, wide, logs, qkv, grad_heads, items)
-    back_all, *sums = lax.optimization_barrier((back_all, *contract_parts, *expand_parts))
+    back_all, *sums = lax.optimization_barrier((back_all, *contract_parts, expand_keep, *expand_parts))
     owned = to_all(back_all)
+    out_keep, out_send = emit(here, after(hidden_low, back_all), contract_weight, peers)
     contract_parts = over_near(here, *send_second(*over_second(here, *sums[:4])))
     expand_parts = send_second(*over_second(here, *sums[4:]))
-    owned, *sums = lax.optimization_barrier((owned, *contract_parts, *expand_parts))
+    owned, out_keep, *sums = lax.optimization_barrier((owned, out_keep, *contract_parts, *expand_parts))
     contract_parts = over_far(here, *sums[:2])
     expand_parts = over_near(here, *sums[2:])
     owned_send = pick(owned.reshape(2, levels, 3, rows, group), 1 - core, 0)

time: 322 us -> 310 us (0.963)
  waiting for transfers between devices: 94.5 us -> 77.3 us
  local copies, waits for them, and re-layouts: 35 us -> 46.3 us
  Pallas kernels: 106 us -> 102 us
    ppermute x44, waiting for transfers between devices: 94.4 us -> 73.1 us  [flipped(): return lax.ppermute(array, axis, [(i, i ^ mask) for i in range(peers)])]
    unnamed x128 -> x134, local copies, waits for them, and re-layouts: 33.4 us -> 44.6 us
    all_to_all x3, waiting for transfers between devices: 0.01 us -> 4.17 us  [to_all(): return lax.all_to_all(array, 'blk', split_axis=0, concat_axis=0, tiled=True)]
    pallas_call x2 -> x3, Pallas kernels: 16.9 us -> 13.7 us  [the longest x1 5.17 us: weigh(): pl.pallas_call(weigh_kernel, out_shape=[jax.ShapeDtypeStruct(shape, jnp.b...]
  transfers between devices with their start and end apart: 47 -> 47, of which waited for: 19 -> 19; matrix products, arithmetic and copies ran while one was open for 2% -> 2% of each run, Pallas kernels for 22% -> 23%
where the time goes in v4:
time: 310 us; the launch traced here: 309 us
  Pallas kernels  102 us (33%)
  waiting for transfers between devices  77.3 us (25%)
  starting transfers between devices  51.7 us (17%)
  local copies, waits for them, and re-layouts  46.3 us (15%)
  blocking collectives  25.8 us (8%)
  other arithmetic  3.66 us (1%)
    ppermute x44, waiting for transfers between devices, flipped(): return lax.ppermute(array, axis, [(i, i ^ mask) for i in range(peers)])  73.1 us
    unnamed x134, local copies, waits for them, and re-layouts  44.6 us
    ppermute x44, starting transfers between devices, flipped(): return lax.ppermute(array, axis, [(i, i ^ mask) for i in range(peers)])  40.3 us
    all_to_all x1, blocking collectives, to_all(): return lax.all_to_all(array, 'blk', split_axis=0, concat_axis=0, tiled=True)  25.8 us
    pallas_call x15, Pallas kernels, _small_call(): pl.pallas_call(kernel, out_shape=[jax.ShapeDtypeStruct(shape, kind) for s...  23.3 us
    pallas_call x1, Pallas kernels, attend_back(): pl.pallas_call(partial(attend_back_kernel, peers, items, rows), out_shape...  21.4 us
    pallas_call x1, Pallas kernels, attend(): pl.pallas_call(partial(attend_kernel, peers, items, rows), out_shape=shap...  11.8 us
    all_to_all x3, starting transfers between devices, to_all(): return lax.all_to_all(array, 'blk', split_axis=0, concat_axis=0, tiled=True)  11.4 us
  transfers between devices with their start and end apart: 47, of which 19 were waited for; matrix products, arithmetic and copies ran while one was open for 2% of the time, Pallas kernels for 23%

profile of v4, /device:TPU:0, one launch (start us, length us, event | category | flops | bytes accessed | tf_op | source)
XLA Modules:
  0.0 309.1 jit_solution(12723739532088749926)
XLA Ops:
  1.8 6.3 %project.1 = (bf16[3,256,128]{2,1,0:T(8,128)(2,1)}, bf16[3,256,128]{2,1,0:T(8,128)(2,1)}, bf16[3,256,128]{2,1,0:T(8,128)(2,1)}, bf16[3,256,128]{2,1,0:T(8,128)(2...) custom-call(s32[4]{0:T(128)} %pad_add_fusion.1.meta_ref, ...), custom_call_target="tpu_custom_call" | custom-call | flops 4000000000 | bytes 8388608 | tf_op jit(solution)/shard_map/project/pallas_call | solution.py:611
  8.1 2.6 collective-permute-start.1
  12.3 3.0 collective-permute-start.4
  16.6 3.6 %collective-permute-start.5 = (bf16[3,256,128]{2,1,0:T(8,128)(2,1)}, bf16[3,256,128]{2,1,0:T(8,128)(2,1)S(1)}, u32[]{:S(2)}, u32[]{:S(2)}) collective-permute-start(bf16[3,256,128]{2,1,0:T(8,128)(2,1)} %get-tuple-element.136), channel_id=1, source_target_pairs={{0,5},{1,4},{2,7},{3,6},{4,1},{5,0},{6,3},{7,2},{8,13},{9,12},{10,... | collective-permute-start | bytes 589832 | tf_op jit(solution)/shard_map/ppermute | solution.py:1057
  20.2 5.7 %collective-permute-done.2.refs_2_ = bf16[3,256,128]{2,1,0:T(8,128)(2,1)S(1)} collective-permute-done((bf16[3,256,128]{2,1,0:T(8,128)(2,1)}, bf16[3,256,128]{2,1,0:T(8,128)(2,1)S(1)}, u32[]{:S(2)}, u32[]{:S(2)}) %collective-permute-start.2) | collective-permute-done | bytes 196640 | tf_op jit(solution)/shard_map/ppermute | solution.py:1057
  29.2 3.4 %copy-done.2 = bf16[4096,1024]{1,0:T(8,128)(2,1)S(1)} copy-done((bf16[4096,1024]{1,0:T(8,128)(2,1)S(1)}, bf16[4096,1024]{1,0:T(8,128)(2,1)}, u32[]{:S(2)}) %copy-start.2) | copy-done | bytes 8388632
  32.6 4.7 %pull.1.pulled_ref = f32[512,2048]{1,0:T(8,128)S(1)} custom-call(s32[4]{0:T(128)S(1)} %copy-done.55, bf16[256,1024]{1,0:T(8,128)(2,1)S(1)} %bitcast.50, bf16[256,1024]{1,0:T(8,128)(2,1)S(1)} %collective-permute-done.other.grad_other, bf16[4096,1024]{1,0:T(8,128)(2,1)S(1)} %copy-done.2), custom_call_target="tpu_custom_call" | custom-call | flops 3000000000 | bytes 9437184 | tf_op jit(solution)/shard_map/pull/pallas_call | solution.py:673
  37.3 6.0 %collective-permute-done.5.refs_5_ = bf16[3,256,128]{2,1,0:T(8,128)(2,1)S(1)} collective-permute-done((bf16[3,256,128]{2,1,0:T(8,128)(2,1)}, bf16[3,256,128]{2,1,0:T(8,128)(2,1)S(1)}, u32[]{:S(2)}, u32[]{:S(2)}) %collective-permute-start.5) | collective-permute-done | bytes 196640 | tf_op jit(solution)/shard_map/ppermute | solution.py:1057
  43.4 11.8 %attend.1 = (bf16[8,256,128]{2,1,0:T(8,128)(2,1)S(1)}, f32[8,128,256]{2,1,0:T(8,128)S(1)}, f32[8,8,256]{2,1,0:T(8,128)S(1)}, bf16[8,3,256,128]{3,2,1,0:T(8,128)(2,1)S(1)}) custom-call(s32[18]{0:T(128)S(1)} %pad_add_fusion.meta_ref, f32[2]{0:T(128)S(1)} %slice_reduce_fusion.1.far_ref, f32[2,512]{1,0:T(2,128)S(1)} %fusion.2.line_ref, ...), custom_call_target="tpu_custom_call" | custom-call | flops 8000000000 | bytes 4194304 | tf_op jit(solution)/shard_map/attend/pallas_call | solution.py:423
  56.3 25.8 %all_to_all.20.parts_ref = bf16[8,256,128]{2,1,0:T(8,128)(2,1)S(1)} all-to-all(bf16[8,256,128]{2,1,0:T(8,128)(2,1)S(1)} %get-tuple-element.139), channel_id=1, replica_groups=mesh['seq'=4,'blk'=8] {'blk'}, dimensions={0} | all-to-all | bytes 1048576 | tf_op jit(solution)/shard_map/all_to_all | solution.py:1153
  85.9 10.8 %feed.1 = (f32[256,1024]{1,0:T(8,128)S(1)}, f32[256,1024]{1,0:T(8,128)S(1)}, bf16[512,2048]{1,0:T(8,128)(2,1)S(1)}, bf16[512,2048]{1,0:T(8,128)(2,1)S(1)}) custom-call(s32[4]{0:T(128)S(1)} %copy-done.55, bf16[256,1024]{1,0:T(8,128)(2,1)S(1)} %get-tuple-element.143.act_mine, bf16[256,1024]{1,0:T(8,128)(2,1)S(1)} %collective-permute-done.8.act_other, ...), custom_call_target="tpu_custom_call" | custom-call | flops 8000000000 | bytes 20971520 | tf_op jit(solution)/shard_map/feed/pallas_call | solution.py:736
  98.2 4.5 %contract_weigh.1 = (bf16[4,256,512]{2,1,0:T(8,128)(2,1)S(1)}, bf16[4,256,512]{2,1,0:T(8,128)(2,1)}, bf16[8,128,512]{2,1,0:T(8,128)(2,1)S(1)}, bf16[8,128,512]{2,1,0:T(8,128)(2,1)}) custom-call(s32[4]{0:T(128)S(1)} %copy-done.55, bf16[256,1024]{1,0:T(8,128)(2,1)S(1)} %bitcast.51, bf16[256,1024]{1,0:T(8,128)(2,1)S(1)} %collective-permute-done.other.grad_other, ...), custom_call_target="tpu_custom_call" | custom-call | flops 100000000 | bytes 1048576 | tf_op jit(solution)/shard_map/contract_weigh/pallas_call | solution.py:779
  112.3 4.4 %all-to-all-start.1 = ((bf16[8,256,128]{2,1,0:T(8,128)(2,1)}), bf16[8,256,128]{2,1,0:T(8,128)(2,1)}, u32[]{:S(2)}, u32[]{:S(2)}) async-start(bf16[8,256,128]{2,1,0:T(8,128)(2,1)} %copy-done.46), calls=%async_computation.1 | async-start | bytes 1048576 | tf_op jit(solution)/shard_map/all_to_all | solution.py:1153
  122.9 5.2 %weigh.1 = (bf16[4,128,1280]{2,1,0:T(8,128)(2,1)S(1)}, bf16[4,128,1280]{2,1,0:T(8,128)(2,1)}, bf16[8,64,1280]{2,1,0:T(8,128)(2,1)S(1)}, bf16[8,64,1280]{2,1,0:T(8,128)(2,1)}) custom-call(s32[4]{0:T(128)S(1)} %copy-done.55, bf16[256,1024]{1,0:T(8,128)(2,1)S(1)} %copy-done.43, bf16[256,1024]{1,0:T(8,128)(2,1)S(1)} %copy-done.45, ...), custom_call_target="tpu_custom_call" | custom-call | flops 100000000 | bytes 1048576 | tf_op jit(solution)/shard_map/weigh/pallas_call | solution.py:813
  132.4 4.2 %all-to-all-done.1.cot = bf16[8,256,128]{2,1,0:T(8,128)(2,1)} async-done(((bf16[8,256,128]{2,1,0:T(8,128)(2,1)}), bf16[8,256,128]{2,1,0:T(8,128)(2,1)}, u32[]{:S(2)}, u32[]{:S(2)}) %all-to-all-start.1) | async-done | bytes 524320 | tf_op jit(solution)/shard_map/all_to_all | solution.py:1153
  139.6 21.4 %attend_back.1 = (bf16[8,3,256,128]{3,2,1,0:T(8,128)(2,1)S(1)}, f32[2,8,512]{2,1,0:T(8,128)S(1)}) custom-call(s32[18]{0:T(128)S(1)} %pad_add_fusion.meta_ref, f32[2]{0:T(128)S(1)} %slice_reduce_fusion.1.far_ref, f32[2,512]{1,0:T(2,128)S(1)} %fusion.2.line_ref, f32[8,128,256]{2,1,0:T(8,128)S(1)} %copy-done.65, f32[8,8,256]{2,1,0:T(8,128)S(1)} %get-tuple-element.142.log_ref, ...), custom_call_target="tpu_custom_call" | custom-call | flops 20000000000 | bytes 8388608 | tf_op jit(solution)/shard_map/attend_back/pallas_call | solution.py:522
  165.0 3.6 %all-to-all-start.2 = ((bf16[8,3,256,128]{3,2,1,0:T(8,128)(2,1)}), bf16[8,3,256,128]{3,2,1,0:T(8,128)(2,1)S(1)}, u32[]{:S(2)}, u32[]{:S(2)}) async-start(bf16[8,3,256,128]{3,2,1,0:T(8,128)(2,1)} %copy-done.11), calls=%async_computation.2 | async-start | bytes 3145728 | tf_op jit(solution)/shard_map/all_to_all | solution.py:1153
  177.8 2.9 second.4
  182.9 6.2 %collective-permute-done.16.one_got = bf16[4,128,512]{2,1,0:T(8,128)(2,1)S(1)} collective-permute-done((bf16[4,128,512]{2,1,0:T(8,128)(2,1)S(1)}, bf16[4,128,512]{2,1,0:T(8,128)(2,1)S(1)}, u32[]{:S(2)}, u32[]{:S(2)}) %collective-permute-start.16) | collective-permute-done | bytes 524320 | tf_op jit(solution)/shard_map/ppermute | solution.py:1057
  189.1 10.7 %collective-permute-done.17.two_got = bf16[4,128,512]{2,1,0:T(8,128)(2,1)S(1)} collective-permute-done((bf16[4,128,512]{2,1,0:T(8,128)(2,1)S(1)}, bf16[4,128,512]{2,1,0:T(8,128)(2,1)S(1)}, u32[]{:S(2)}, u32[]{:S(2)}) %collective-permute-start.17) | collective-permute-done | bytes 524320 | tf_op jit(solution)/shard_map/ppermute | solution.py:1057
  202.2 3.4 %copy-done.3 = bf16[4096,1024]{1,0:T(8,128)(2,1)S(1)} copy-done((bf16[4096,1024]{1,0:T(8,128)(2,1)S(1)}, bf16[4096,1024]{1,0:T(8,128)(2,1)}, u32[]{:S(2)}) %copy-start.3) | copy-done | bytes 8388632
  207.1 4.0 %emit.1 = (f32[256,1024]{1,0:T(8,128)S(1)}, bf16[256,1024]{1,0:T(8,128)(2,1)}) custom-call(s32[4]{0:T(128)S(1)} %copy-done.55, bf16[512,2048]{1,0:T(8,128)(2,1)S(1)} %copy-done.5, bf16[4096,1024]{1,0:T(8,128)(2,1)S(1)} %copy-done.3), custom_call_target="tpu_custom_call" | custom-call | flops 2000000000 | bytes 8388608 | tf_op jit(solution)/shard_map/emit/pallas_call | solution.py:842
  213.5 3.4 %collective-permute-done.18.got = bf16[2,128,1024]{2,1,0:T(8,128)(2,1)} collective-permute-done((bf16[2,128,1024]{2,1,0:T(8,128)(2,1)}, bf16[2,128,1024]{2,1,0:T(8,128)(2,1)}, u32[]{:S(2)}, u32[]{:S(2)}) %collective-permute-start.18) | collective-permute-done | bytes 524320 | tf_op jit(solution)/shard_map/ppermute | solution.py:1057
  220.1 3.6 %attend_weigh.1 = (bf16[4,128,768]{2,1,0:T(8,128)(2,1)S(1)}, bf16[4,128,768]{2,1,0:T(8,128)(2,1)}, bf16[8,64,768]{2,1,0:T(8,128)(2,1)S(1)}, bf16[8,64,768]{2,1,0:T(8,128)(2,1)}) custom-call(s32[4]{0:T(128)S(1)} %copy-done.55, bf16[256,1024]{1,0:T(8,128)(2,1)S(1)} %copy-done.58, bf16[256,1024]{1,0:T(8,128)(2,1)S(1)} %collective-permute-done.22.act_other, ...), custom_call_target="tpu_custom_call" | custom-call | flops 2000000000 | bytes 7340032 | tf_op jit(solution)/shard_map/attend_weigh/pallas_call | solution.py:1039
  235.4 14.8 %collective-permute-done.26.got = bf16[128,1024]{1,0:T(8,128)(2,1)} collective-permute-done((bf16[128,1024]{1,0:T(8,128)(2,1)}, bf16[128,1024]{1,0:T(8,128)(2,1)}, u32[]{:S(2)}, u32[]{:S(2)}) %collective-permute-start.26) | collective-permute-done | bytes 262176 | tf_op jit(solution)/shard_map/ppermute | solution.py:1057
  261.8 2.8 copy-done.6
  264.6 3.3 %close.1 = (f32[256,1024]{1,0:T(8,128)}, f32[2,1024]{1,0:T(2,128)S(1)}) custom-call(bf16[8,3,256,128]{3,2,1,0:T(8,128)(2,1)S(1)} %all-to-all-done.2.parts_ref.owned_ref, bf16[256,1024]{1,0:T(8,128)(2,1)S(1)} %bitcast.55, f32[256,1024]{1,0:T(8,128)S(1)} %copy-done.19, f32[1,1024]{1,0:T(1,128)S(1)} %bitcast.59, bf16[1024,3072]{1,0:T(8,128)(2,1)S(1)} %copy-done.6), custom_call_target="tpu_custom_call" | custom-call | flops 2000000000 | bytes 10485760 | tf_op jit(solution)/shard_map/close/pallas_call | solution.py:910
  268.0 5.2 %collective-permute-done.30.refs_1_ = bf16[128,1024]{1,0:T(8,128)(2,1)S(1)} collective-permute-done((bf16[128,1024]{1,0:T(8,128)(2,1)S(1)}, bf16[128,1024]{1,0:T(8,128)(2,1)S(1)}, u32[]{:S(2)}, u32[]{:S(2)}) %collective-permute-start.30) | collective-permute-done | bytes 262176 | tf_op jit(solution)/shard_map/ppermute | solution.py:1057
  277.1 4.9 %collective-permute-done.33.refs_1_ = bf16[64,2560]{1,0:T(8,128)(2,1)S(1)} collective-permute-done((bf16[64,2560]{1,0:T(8,128)(2,1)S(1)}, bf16[64,2560]{1,0:T(8,128)(2,1)S(1)}, u32[]{:S(2)}, u32[]{:S(2)}) %collective-permute-start.33) | collective-permute-done | bytes 327712 | tf_op jit(solution)/shard_map/ppermute | solution.py:1057
  287.0 2.8 collective-permute-done.43
  290.4 3.4 %all-to-all-start.3 = ((f32[8,8,128]{2,1,0:T(8,128)}), f32[8,8,128]{2,1,0:T(8,128)S(1)}, u32[]{:S(2)}, u32[]{:S(2)}) async-start(f32[8,8,128]{2,1,0:T(8,128)} %add.210), calls=%async_computation.3 | async-start | bytes 65536 | tf_op jit(solution)/shard_map/all_to_all | solution.py:1153
  299.8 2.5 finish_contract.1
  (250 shorter events, 106.3 us)
Async XLA Ops:
  0.7 26.8 %collective-permute-start = (bf16[256,1024]{1,0:T(8,128)(2,1)}, bf16[256,1024]{1,0:T(8,128)(2,1)S(1)}, u32[]{:S(2)}, u32[]{:S(2)}) collective-permute-start(bf16[256,1024]{1,0:T(8,128)(2,1)} %bitcast.49), channel_id=1, source_target_pairs={{0,8},{8,0},{16,24},{24,16},{1,9},{9,1},{17,25},{25,17},{2,10},{10... | collective-permute-start | bytes 1572872 | tf_op jit(solution)/shard_map/ppermute | solution.py:1057
  10.7 15.2 %collective-permute-start.2 = (bf16[3,256,128]{2,1,0:T(8,128)(2,1)}, bf16[3,256,128]{2,1,0:T(8,128)(2,1)S(1)}, u32[]{:S(2)}, u32[]{:S(2)}) collective-permute-start(bf16[3,256,128]{2,1,0:T(8,128)(2,1)} %get-tuple-element.133), channel_id=1, source_target_pairs={{0,2},{1,3},{2,0},{3,1},{4,6},{5,7},{6,4},{7,5},{8,10},{9,11},{10,... | collective-permute-start | bytes 589832 | tf_op jit(solution)/shard_map/ppermute | solution.py:1057
  12.3 25.0 %collective-permute-start.3 = (bf16[3,256,128]{2,1,0:T(8,128)(2,1)}, bf16[3,256,128]{2,1,0:T(8,128)(2,1)S(1)}, u32[]{:S(2)}, u32[]{:S(2)}) collective-permute-start(bf16[3,256,128]{2,1,0:T(8,128)(2,1)} %get-tuple-element.134), channel_id=1, source_target_pairs={{0,3},{1,2},{2,1},{3,0},{4,7},{5,6},{6,5},{7,4},{8,11},{9,10},{10,... | collective-permute-start | bytes 589832 | tf_op jit(solution)/shard_map/ppermute | solution.py:1057
  12.3 25.0 %collective-permute-start.4 = (bf16[3,256,128]{2,1,0:T(8,128)(2,1)}, bf16[3,256,128]{2,1,0:T(8,128)(2,1)S(1)}, u32[]{:S(2)}, u32[]{:S(2)}) collective-permute-start(bf16[3,256,128]{2,1,0:T(8,128)(2,1)} %get-tuple-element.135), channel_id=1, source_target_pairs={{0,4},{1,5},{2,6},{3,7},{4,0},{5,1},{6,2},{7,3},{8,12},{9,13},{10,... | collective-permute-start | bytes 589832 | tf_op jit(solution)/shard_map/ppermute | solution.py:1057
  16.6 26.7 %collective-permute-start.5 = (bf16[3,256,128]{2,1,0:T(8,128)(2,1)}, bf16[3,256,128]{2,1,0:T(8,128)(2,1)S(1)}, u32[]{:S(2)}, u32[]{:S(2)}) collective-permute-start(bf16[3,256,128]{2,1,0:T(8,128)(2,1)} %get-tuple-element.136), channel_id=1, source_target_pairs={{0,5},{1,4},{2,7},{3,6},{4,1},{5,0},{6,3},{7,2},{8,13},{9,12},{10,... | collective-permute-start | bytes 589832 | tf_op jit(solution)/shard_map/ppermute | solution.py:1057
  25.9 17.4 %collective-permute-start.6 = (bf16[3,256,128]{2,1,0:T(8,128)(2,1)}, bf16[3,256,128]{2,1,0:T(8,128)(2,1)S(1)}, u32[]{:S(2)}, u32[]{:S(2)}) collective-permute-start(bf16[3,256,128]{2,1,0:T(8,128)(2,1)} %get-tuple-element.137), channel_id=1, source_target_pairs={{0,6},{1,7},{2,4},{3,5},{4,2},{5,3},{6,0},{7,1},{8,14},{9,15},{10,... | collective-permute-start | bytes 589832 | tf_op jit(solution)/shard_map/ppermute | solution.py:1057
  27.5 15.9 %collective-permute-start.7 = (bf16[3,256,128]{2,1,0:T(8,128)(2,1)}, bf16[3,256,128]{2,1,0:T(8,128)(2,1)S(1)}, u32[]{:S(2)}, u32[]{:S(2)}) collective-permute-start(bf16[3,256,128]{2,1,0:T(8,128)(2,1)} %get-tuple-element.138), channel_id=1, source_target_pairs={{0,7},{1,6},{2,5},{3,4},{4,3},{5,2},{6,1},{7,0},{8,15},{9,14},{10,... | collective-permute-start | bytes 589832 | tf_op jit(solution)/shard_map/ppermute | solution.py:1057
  104.6 31.9 %collective-permute-start.12 = (bf16[4,256,512]{2,1,0:T(8,128)(2,1)}, bf16[4,256,512]{2,1,0:T(8,128)(2,1)S(1)}, u32[]{:S(2)}, u32[]{:S(2)}) collective-permute-start(bf16[4,256,512]{2,1,0:T(8,128)(2,1)} %get-tuple-element.159), channel_id=1, source_target_pairs={{0,1},{1,0},{2,3},{3,2},{4,5},{5,4},{6,7},{7,6},{8,9},{9,8},{10,11... | collective-permute-start | bytes 3145736 | tf_op jit(solution)/shard_map/ppermute | solution.py:1057
  106.1 30.4 %collective-permute-start.13 = (bf16[8,128,512]{2,1,0:T(8,128)(2,1)}, bf16[8,128,512]{2,1,0:T(8,128)(2,1)}, u32[]{:S(2)}, u32[]{:S(2)}) collective-permute-start(bf16[8,128,512]{2,1,0:T(8,128)(2,1)} %get-tuple-element.161), channel_id=1, source_target_pairs={{0,16},{8,24},{16,0},{24,8},{1,17},{9,25},{17,1},{25,9},{2,18},{10... | collective-permute-start | bytes 3145736 | tf_op jit(solution)/shard_map/ppermute | solution.py:1057
  112.3 24.2 %all-to-all-start.1 = ((bf16[8,256,128]{2,1,0:T(8,128)(2,1)}), bf16[8,256,128]{2,1,0:T(8,128)(2,1)}, u32[]{:S(2)}, u32[]{:S(2)}) async-start(bf16[8,256,128]{2,1,0:T(8,128)(2,1)} %copy-done.46), calls=%async_computation.1 | async-start | bytes 1048576 | tf_op jit(solution)/shard_map/all_to_all | solution.py:1153
  130.2 33.7 %collective-permute-start.14 = (bf16[4,128,1280]{2,1,0:T(8,128)(2,1)}, bf16[4,128,1280]{2,1,0:T(8,128)(2,1)S(1)}, u32[]{:S(2)}, u32[]{:S(2)}) collective-permute-start(bf16[4,128,1280]{2,1,0:T(8,128)(2,1)} %get-tuple-element.170), channel_id=1, source_target_pairs={{0,1},{1,0},{2,3},{3,2},{4,5},{5,4},{6,7},{7,6},{8,9},{9,8},{10,11... | collective-permute-start | bytes 3932168 | tf_op jit(solution)/shard_map/ppermute | solution.py:1057
  131.8 33.2 %collective-permute-start.15 = (bf16[8,64,1280]{2,1,0:T(8,128)(2,1)}, bf16[8,64,1280]{2,1,0:T(8,128)(2,1)}, u32[]{:S(2)}, u32[]{:S(2)}) collective-permute-start(bf16[8,64,1280]{2,1,0:T(8,128)(2,1)} %get-tuple-element.172), channel_id=1, source_target_pairs={{0,16},{8,24},{16,0},{24,8},{1,17},{9,25},{17,1},{25,9},{2,18},{10... | collective-permute-start | bytes 3932168 | tf_op jit(solution)/shard_map/ppermute | solution.py:1057
  165.0 51.9 %all-to-all-start.2 = ((bf16[8,3,256,128]{3,2,1,0:T(8,128)(2,1)}), bf16[8,3,256,128]{3,2,1,0:T(8,128)(2,1)S(1)}, u32[]{:S(2)}, u32[]{:S(2)}) async-start(bf16[8,3,256,128]{3,2,1,0:T(8,128)(2,1)} %copy-done.11), calls=%async_computation.2 | async-start | bytes 3145728 | tf_op jit(solution)/shard_map/all_to_all | solution.py:1153
  174.2 14.9 %collective-permute-start.16 = (bf16[4,128,512]{2,1,0:T(8,128)(2,1)S(1)}, bf16[4,128,512]{2,1,0:T(8,128)(2,1)S(1)}, u32[]{:S(2)}, u32[]{:S(2)}) collective-permute-start(bf16[4,128,512]{2,1,0:T(8,128)(2,1)S(1)} %get-tuple-element.181), channel_id=1, source_target_pairs={{0,16},{8,24},{16,0},{24,8},{1,17},{9,25},{17,1},{25,9},{2,18},{10... | collective-permute-start | bytes 1572872 | tf_op jit(solution)/shard_map/ppermute | solution.py:1057
  175.8 24.1 %collective-permute-start.17 = (bf16[4,128,512]{2,1,0:T(8,128)(2,1)S(1)}, bf16[4,128,512]{2,1,0:T(8,128)(2,1)S(1)}, u32[]{:S(2)}, u32[]{:S(2)}) collective-permute-start(bf16[4,128,512]{2,1,0:T(8,128)(2,1)S(1)} %get-tuple-element.183), channel_id=1, source_target_pairs={{0,1},{1,0},{2,3},{3,2},{4,5},{5,4},{6,7},{7,6},{8,9},{9,8},{10,11... | collective-permute-start | bytes 1572872 | tf_op jit(solution)/shard_map/ppermute | solution.py:1057
  182.4 29.8 %collective-permute-start.19 = (bf16[4,64,1280]{2,1,0:T(8,128)(2,1)}, bf16[4,64,1280]{2,1,0:T(8,128)(2,1)S(1)}, u32[]{:S(2)}, u32[]{:S(2)}) collective-permute-start(bf16[4,64,1280]{2,1,0:T(8,128)(2,1)} %get-tuple-element.191), channel_id=1, source_target_pairs={{0,16},{8,24},{16,0},{24,8},{1,17},{9,25},{17,1},{25,9},{2,18},{10... | collective-permute-start | bytes 1966088 | tf_op jit(solution)/shard_map/ppermute | solution.py:1057
  182.9 30.6 %collective-permute-start.20 = (bf16[4,64,1280]{2,1,0:T(8,128)(2,1)}, bf16[4,64,1280]{2,1,0:T(8,128)(2,1)}, u32[]{:S(2)}, u32[]{:S(2)}) collective-permute-start(bf16[4,64,1280]{2,1,0:T(8,128)(2,1)} %get-tuple-element.193), channel_id=1, source_target_pairs={{0,1},{1,0},{2,3},{3,2},{4,5},{5,4},{6,7},{7,6},{8,9},{9,8},{10,11... | collective-permute-start | bytes 1966088 | tf_op jit(solution)/shard_map/ppermute | solution.py:1057
  202.2 14.8 %collective-permute-start.18 = (bf16[2,128,1024]{2,1,0:T(8,128)(2,1)}, bf16[2,128,1024]{2,1,0:T(8,128)(2,1)}, u32[]{:S(2)}, u32[]{:S(2)}) collective-permute-start(bf16[2,128,1024]{2,1,0:T(8,128)(2,1)} %get-tuple-element.185), channel_id=1, source_target_pairs={{0,2},{1,3},{2,0},{3,1},{4,6},{5,7},{6,4},{7,5},{8,10},{9,11},{10,... | collective-permute-start | bytes 1572872 | tf_op jit(solution)/shard_map/ppermute | solution.py:1057
  224.6 27.8 %collective-permute-start.24 = (bf16[4,128,768]{2,1,0:T(8,128)(2,1)}, bf16[4,128,768]{2,1,0:T(8,128)(2,1)}, u32[]{:S(2)}, u32[]{:S(2)}) collective-permute-start(bf16[4,128,768]{2,1,0:T(8,128)(2,1)} %get-tuple-element.204), channel_id=1, source_target_pairs={{0,1},{1,0},{2,3},{3,2},{4,5},{5,4},{6,7},{7,6},{8,9},{9,8},{10,11... | collective-permute-start | bytes 2359304 | tf_op jit(solution)/shard_map/ppermute | solution.py:1057
  225.9 26.5 %collective-permute-start.25 = (bf16[8,64,768]{2,1,0:T(8,128)(2,1)}, bf16[8,64,768]{2,1,0:T(8,128)(2,1)}, u32[]{:S(2)}, u32[]{:S(2)}) collective-permute-start(bf16[8,64,768]{2,1,0:T(8,128)(2,1)} %get-tuple-element.206), channel_id=1, source_target_pairs={{0,16},{8,24},{16,0},{24,8},{1,17},{9,25},{17,1},{25,9},{2,18},{10... | collective-permute-start | bytes 2359304 | tf_op jit(solution)/shard_map/ppermute | solution.py:1057
  230.3 22.1 %collective-permute-start.27 = (bf16[2,64,2560]{2,1,0:T(8,128)(2,1)}, bf16[2,64,2560]{2,1,0:T(8,128)(2,1)}, u32[]{:S(2)}, u32[]{:S(2)}) collective-permute-start(bf16[2,64,2560]{2,1,0:T(8,128)(2,1)} %get-tuple-element.216), channel_id=1, source_target_pairs={{0,2},{1,3},{2,0},{3,1},{4,6},{5,7},{6,4},{7,5},{8,10},{9,11},{10,... | collective-permute-start | bytes 1966088 | tf_op jit(solution)/shard_map/ppermute | solution.py:1057
  232.8 17.4 %collective-permute-start.26 = (bf16[128,1024]{1,0:T(8,128)(2,1)}, bf16[128,1024]{1,0:T(8,128)(2,1)}, u32[]{:S(2)}, u32[]{:S(2)}) collective-permute-start(bf16[128,1024]{1,0:T(8,128)(2,1)} %get-tuple-element.210), channel_id=1, source_target_pairs={{0,4},{1,5},{2,6},{3,7},{4,0},{5,1},{6,2},{7,3},{8,12},{9,13},{10,... | collective-permute-start | bytes 786440 | tf_op jit(solution)/shard_map/ppermute | solution.py:1057
  254.8 18.4 %collective-permute-start.31 = (bf16[64,2560]{1,0:T(8,128)(2,1)S(1)}, bf16[64,2560]{1,0:T(8,128)(2,1)S(1)}, u32[]{:S(2)}, u32[]{:S(2)}) collective-permute-start(bf16[64,2560]{1,0:T(8,128)(2,1)S(1)} %get-tuple-element.230), channel_id=1, source_target_pairs={{0,4},{1,5},{2,6},{3,7},{4,0},{5,1},{6,2},{7,3},{8,12},{9,13},{10,... | collective-permute-start | bytes 983048 | tf_op jit(solution)/shard_map/ppermute | solution.py:1057
  257.8 15.4 %collective-permute-start.28 = (bf16[4,64,768]{2,1,0:T(8,128)(2,1)S(1)}, bf16[4,64,768]{2,1,0:T(8,128)(2,1)S(1)}, u32[]{:S(2)}, u32[]{:S(2)}) collective-permute-start(bf16[4,64,768]{2,1,0:T(8,128)(2,1)S(1)} %get-tuple-element.222), channel_id=1, source_target_pairs={{0,16},{8,24},{16,0},{24,8},{1,17},{9,25},{17,1},{25,9},{2,18},{10... | collective-permute-start | bytes 1179656 | tf_op jit(solution)/shard_map/ppermute | solution.py:1057
  258.5 14.7 %collective-permute-start.29 = (bf16[4,64,768]{2,1,0:T(8,128)(2,1)S(1)}, bf16[4,64,768]{2,1,0:T(8,128)(2,1)S(1)}, u32[]{:S(2)}, u32[]{:S(2)}) collective-permute-start(bf16[4,64,768]{2,1,0:T(8,128)(2,1)S(1)} %get-tuple-element.224), channel_id=1, source_target_pairs={{0,1},{1,0},{2,3},{3,2},{4,5},{5,4},{6,7},{7,6},{8,9},{9,8},{10,11... | collective-permute-start | bytes 1179656 | tf_op jit(solution)/shard_map/ppermute | solution.py:1057
  260.3 12.9 %collective-permute-start.30 = (bf16[128,1024]{1,0:T(8,128)(2,1)S(1)}, bf16[128,1024]{1,0:T(8,128)(2,1)S(1)}, u32[]{:S(2)}, u32[]{:S(2)}) collective-permute-start(bf16[128,1024]{1,0:T(8,128)(2,1)S(1)} %last.3.refs_0_), channel_id=1, source_target_pairs={{0,16},{8,24},{16,0},{24,8},{1,17},{9,25},{17,1},{25,9},{2,18},{10... | collective-permute-start | bytes 786440 | tf_op jit(solution)/shard_map/ppermute | solution.py:1057
  274.0 8.9 %collective-permute-start.34 = (bf16[2,64,1536]{2,1,0:T(8,128)(2,1)S(1)}, bf16[2,64,1536]{2,1,0:T(8,128)(2,1)S(1)}, u32[]{:S(2)}, u32[]{:S(2)}) collective-permute-start(bf16[2,64,1536]{2,1,0:T(8,128)(2,1)S(1)} %get-tuple-element.239), channel_id=1, source_target_pairs={{0,2},{1,3},{2,0},{3,1},{4,6},{5,7},{6,4},{7,5},{8,10},{9,11},{10,... | collective-permute-start | bytes 1179656 | tf_op jit(solution)/shard_map/ppermute | solution.py:1057
  275.6 22.1 %collective-permute-start.21 = (bf16[256,1024]{1,0:T(8,128)(2,1)}, bf16[256,1024]{1,0:T(8,128)(2,1)}, u32[]{:S(2)}, u32[]{:S(2)}) collective-permute-start(bf16[256,1024]{1,0:T(8,128)(2,1)} %get-tuple-element.195), channel_id=1, source_target_pairs={{0,8},{8,0},{16,24},{24,16},{1,9},{9,1},{17,25},{25,17},{2,10},{10... | collective-permute-start | bytes 1572872 | tf_op jit(solution)/shard_map/ppermute | solution.py:1057
  284.8 9.0 %collective-permute-start.35 = (bf16[64,1536]{1,0:T(8,128)(2,1)}, bf16[64,1536]{1,0:T(8,128)(2,1)S(1)}, u32[]{:S(2)}, u32[]{:S(2)}) collective-permute-start(bf16[64,1536]{1,0:T(8,128)(2,1)} %get-tuple-element.243), channel_id=1, source_target_pairs={{0,4},{1,5},{2,6},{3,7},{4,0},{5,1},{6,2},{7,3},{8,12},{9,13},{10,... | collective-permute-start | bytes 589832 | tf_op jit(solution)/shard_map/ppermute | solution.py:1057
  286.5 13.2 %collective-permute-start.41 = (bf16[128,1024]{1,0:T(8,128)(2,1)S(1)}, bf16[128,1024]{1,0:T(8,128)(2,1)}, u32[]{:S(2)}, u32[]{:S(2)}) collective-permute-start(bf16[128,1024]{1,0:T(8,128)(2,1)S(1)} %last.3.refs_0_), channel_id=1, source_target_pairs={{0,8},{8,0},{16,24},{24,16},{1,9},{9,1},{17,25},{25,17},{2,10},{10... | collective-permute-start | bytes 786440 | tf_op jit(solution)/shard_map/ppermute | solution.py:1057
  286.5 13.2 %collective-permute-start.42 = (bf16[128,1024]{1,0:T(8,128)(2,1)S(1)}, bf16[128,1024]{1,0:T(8,128)(2,1)}, u32[]{:S(2)}, u32[]{:S(2)}) collective-permute-start(bf16[128,1024]{1,0:T(8,128)(2,1)S(1)} %collective-permute-done.30.refs_1_), channel_id=1, source_target_pairs={{0,8},{8,0},{16,24},{24,16},{1,9},{9,1},{17,25},{25,17},{2,10},{10... | collective-permute-start | bytes 786440 | tf_op jit(solution)/shard_map/ppermute | solution.py:1057
  290.4 12.3 %all-to-all-start.3 = ((f32[8,8,128]{2,1,0:T(8,128)}), f32[8,8,128]{2,1,0:T(8,128)S(1)}, u32[]{:S(2)}, u32[]{:S(2)}) async-start(f32[8,8,128]{2,1,0:T(8,128)} %add.210), calls=%async_computation.3 | async-start | bytes 65536 | tf_op jit(solution)/shard_map/all_to_all | solution.py:1153
  (81 other events, 559.3 us)

commit v5 on v4

--- a/solution.py
+++ b/solution.py
@@ -639,7 +639,7 @@
         out_shape=[jax.ShapeDtypeStruct(tokens.shape, t) for t in (jnp.bfloat16, jnp.float32, jnp.bfloat16)],
         in_specs=_specs("vvvvv"),
         out_specs=_specs("vvv"),
-        compiler_params=_params(16),
+        compiler_params=_params(12),
         cost_estimate=pl.CostEstimate(flops=10**9, bytes_accessed=5 * 2**20, transcendentals=0),
         name="merge",
     )(parts, tokens, gain, shift, weight)
@@ -888,7 +888,7 @@
         out_shape=[jax.ShapeDtypeStruct(*shape) for shape in shapes],
         in_specs=_specs("svvvvvv"),
         out_specs=_specs("v" * len(shapes)),
-        compiler_params=_params(14),
+        compiler_params=_params(12),
         cost_estimate=pl.CostEstimate(flops=10**9, bytes_accessed=8 * 2**20, transcendentals=0),
         name="turn",
     )(meta, in_mine, in_other, middle, grad, gain, weight)
@@ -913,7 +913,7 @@
         in_specs=_specs("vvvvv"),
         out_specs=_specs("vv"),
         scratch_shapes=[pltpu.VMEM((rows, 3 * width), jnp.bfloat16)],
-        compiler_params=_params(20),
+        compiler_params=_params(16),
         cost_estimate=pl.CostEstimate(flops=2 * 10**9, bytes_accessed=10 * 2**20, transcendentals=0),
         name="close",
     )(parts, tokens, grad, gain, weight)
@@ -961,7 +961,7 @@
         out_shape=[jax.ShapeDtypeStruct(shape, kind) for shape in shapes],
         in_specs=_specs(*("s" if a.dtype == jnp.int32 else "v" for a in arguments)),
         out_specs=_specs("v" * len(shapes)),
-        compiler_params=_params(24),
+        compiler_params=_params(10),
         cost_estimate=pl.CostEstimate(flops=size, bytes_accessed=3 * size, transcendentals=0),
         name=name,
     )(*arguments)
@@ -1046,7 +1046,7 @@
             pltpu.VMEM((2 * rows, span), jnp.bfloat16),
             pltpu.VMEM((peers, group, cut), jnp.bfloat16),
         ],
-        compiler_params=_params(20),
+        compiler_params=_params(12),
         cost_estimate=pl.CostEstimate(flops=2 * 10**9, bytes_accessed=7 * 2**20, transcendentals=0),
         name="attend_weigh",
     )(meta, act_mine, act_other, owned, other)
@@ -1172,12 +1172,13 @@
     expand_keep = expand_parts[0]
     _, *expand_parts = over_first(*expand_parts)
 
+    contract_parts = over_second(here, *contract_parts)
     grad_heads, expand_keep, *contract_parts = lax.optimization_barrier((to_all(grad_heads), expand_keep, *contract_parts))
     back_all, line_grad = attend_back(meta, far, lines, wide, logs, qkv, grad_heads, items)
     back_all, *sums = lax.optimization_barrier((back_all, *contract_parts, expand_keep, *expand_parts))
     owned = to_all(back_all)
     out_keep, out_send = emit(here, after(hidden_low, back_all), contract_weight, peers)
-    contract_parts = over_near(here, *send_second(*over_second(here, *sums[:4])))
+    contract_parts = over_near(here, *send_second(*sums[:4]))
     expand_parts = send_second(*over_second(here, *sums[4:]))
     owned, out_keep, *sums = lax.optimization_barrier((owned, out_keep, *contract_parts, *expand_parts))
     contract_parts = over_far(here, *sums[:2])

time: 310 us -> 309 us (level)
  waiting for transfers between devices: 77.3 us -> 73 us
    all_to_all x3, waiting for transfers between devices: 4.17 us -> 0.01 us  [to_all(): return lax.all_to_all(array, 'blk', split_axis=0, concat_axis=0, tiled=True)]
    unnamed x134 -> x132, local copies, waits for them, and re-layouts: 44.6 us -> 45.6 us
  transfers between devices with their start and end apart: 47 -> 47, of which waited for: 19 -> 17; matrix products, arithmetic and copies ran while one was open for 2% -> 2% of each run, Pallas kernels for 23% -> 24%
where the time goes in v5:
time: 309 us; the launch traced here: 307 us
  Pallas kernels  104 us (34%)
  waiting for transfers between devices  73 us (24%)
  starting transfers between devices  51.2 us (17%)
  local copies, waits for them, and re-layouts  47.3 us (15%)
  blocking collectives  25.8 us (8%)
  other arithmetic  3.69 us (1%)
    ppermute x44, waiting for transfers between devices, flipped(): return lax.ppermute(array, axis, [(i, i ^ mask) for i in range(peers)])  73 us
    unnamed x132, local copies, waits for them, and re-layouts  45.6 us
    ppermute x44, starting transfers between devices, flipped(): return lax.ppermute(array, axis, [(i, i ^ mask) for i in range(peers)])  39.6 us
    all_to_all x1, blocking collectives, to_all(): return lax.all_to_all(array, 'blk', split_axis=0, concat_axis=0, tiled=True)  25.8 us
    pallas_call x15, Pallas kernels, _small_call(): pl.pallas_call(kernel, out_shape=[jax.ShapeDtypeStruct(shape, kind) for s...  24.4 us
    pallas_call x1, Pallas kernels, attend_back(): pl.pallas_call(partial(attend_back_kernel, peers, items, rows), out_shape...  21.5 us
    pallas_call x1, Pallas kernels, attend(): pl.pallas_call(partial(attend_kernel, peers, items, rows), out_shape=shap...  11.9 us
    all_to_all x3, starting transfers between devices, to_all(): return lax.all_to_all(array, 'blk', split_axis=0, concat_axis=0, tiled=True)  11.6 us
  transfers between devices with their start and end apart: 47, of which 17 were waited for; matrix products, arithmetic and copies ran while one was open for 2% of the time, Pallas kernels for 24%

profile of v5, /device:TPU:0, one launch (start us, length us, event | category | flops | bytes accessed | tf_op | source)
XLA Modules:
  0.0 307.4 jit_solution(15260417092818005754)
XLA Ops:
  1.8 6.3 %project.1 = (bf16[3,256,128]{2,1,0:T(8,128)(2,1)}, bf16[3,256,128]{2,1,0:T(8,128)(2,1)}, bf16[3,256,128]{2,1,0:T(8,128)(2,1)}, bf16[3,256,128]{2,1,0:T(8,128)(2...) custom-call(s32[4]{0:T(128)} %pad_add_fusion.1.meta_ref, ...), custom_call_target="tpu_custom_call" | custom-call | flops 4000000000 | bytes 8388608 | tf_op jit(solution)/shard_map/project/pallas_call | solution.py:611
  8.1 2.6 collective-permute-start.1
  12.3 3.0 collective-permute-start.4
  16.6 3.6 %collective-permute-start.5 = (bf16[3,256,128]{2,1,0:T(8,128)(2,1)}, bf16[3,256,128]{2,1,0:T(8,128)(2,1)S(1)}, u32[]{:S(2)}, u32[]{:S(2)}) collective-permute-start(bf16[3,256,128]{2,1,0:T(8,128)(2,1)} %get-tuple-element.136), channel_id=1, source_target_pairs={{0,5},{1,4},{2,7},{3,6},{4,1},{5,0},{6,3},{7,2},{8,13},{9,12},{10,... | collective-permute-start | bytes 589832 | tf_op jit(solution)/shard_map/ppermute | solution.py:1057
  20.2 5.7 %collective-permute-done.2.refs_2_ = bf16[3,256,128]{2,1,0:T(8,128)(2,1)S(1)} collective-permute-done((bf16[3,256,128]{2,1,0:T(8,128)(2,1)}, bf16[3,256,128]{2,1,0:T(8,128)(2,1)S(1)}, u32[]{:S(2)}, u32[]{:S(2)}) %collective-permute-start.2) | collective-permute-done | bytes 196640 | tf_op jit(solution)/shard_map/ppermute | solution.py:1057
  29.2 3.4 %copy-done.2 = bf16[4096,1024]{1,0:T(8,128)(2,1)S(1)} copy-done((bf16[4096,1024]{1,0:T(8,128)(2,1)S(1)}, bf16[4096,1024]{1,0:T(8,128)(2,1)}, u32[]{:S(2)}) %copy-start.2) | copy-done | bytes 8388632
  32.6 4.7 %pull.1.pulled_ref = f32[512,2048]{1,0:T(8,128)S(1)} custom-call(s32[4]{0:T(128)S(1)} %copy-done.54, bf16[256,1024]{1,0:T(8,128)(2,1)S(1)} %bitcast.50, bf16[256,1024]{1,0:T(8,128)(2,1)S(1)} %collective-permute-done.other.grad_other, bf16[4096,1024]{1,0:T(8,128)(2,1)S(1)} %copy-done.2), custom_call_target="tpu_custom_call" | custom-call | flops 3000000000 | bytes 9437184 | tf_op jit(solution)/shard_map/pull/pallas_call | solution.py:673
  37.3 6.0 %collective-permute-done.5.refs_5_ = bf16[3,256,128]{2,1,0:T(8,128)(2,1)S(1)} collective-permute-done((bf16[3,256,128]{2,1,0:T(8,128)(2,1)}, bf16[3,256,128]{2,1,0:T(8,128)(2,1)S(1)}, u32[]{:S(2)}, u32[]{:S(2)}) %collective-permute-start.5) | collective-permute-done | bytes 196640 | tf_op jit(solution)/shard_map/ppermute | solution.py:1057
  43.4 11.9 %attend.1 = (bf16[8,256,128]{2,1,0:T(8,128)(2,1)S(1)}, f32[8,128,256]{2,1,0:T(8,128)S(1)}, f32[8,8,256]{2,1,0:T(8,128)S(1)}, bf16[8,3,256,128]{3,2,1,0:T(8,128)(2,1)S(1)}) custom-call(s32[18]{0:T(128)S(1)} %pad_add_fusion.meta_ref, f32[2]{0:T(128)S(1)} %slice_reduce_fusion.1.far_ref, f32[2,512]{1,0:T(2,128)S(1)} %fusion.2.line_ref, ...), custom_call_target="tpu_custom_call" | custom-call | flops 8000000000 | bytes 4194304 | tf_op jit(solution)/shard_map/attend/pallas_call | solution.py:423
  56.4 25.8 %all_to_all.20.parts_ref = bf16[8,256,128]{2,1,0:T(8,128)(2,1)S(1)} all-to-all(bf16[8,256,128]{2,1,0:T(8,128)(2,1)S(1)} %get-tuple-element.139), channel_id=1, replica_groups=mesh['seq'=4,'blk'=8] {'blk'}, dimensions={0} | all-to-all | bytes 1048576 | tf_op jit(solution)/shard_map/all_to_all | solution.py:1153
  85.3 10.9 %feed.1 = (f32[256,1024]{1,0:T(8,128)S(1)}, f32[256,1024]{1,0:T(8,128)S(1)}, bf16[512,2048]{1,0:T(8,128)(2,1)S(1)}, bf16[512,2048]{1,0:T(8,128)(2,1)S(1)}) custom-call(s32[4]{0:T(128)S(1)} %copy-done.54, bf16[256,1024]{1,0:T(8,128)(2,1)S(1)} %get-tuple-element.143.act_mine, bf16[256,1024]{1,0:T(8,128)(2,1)S(1)} %collective-permute-done.8.act_other, ...), custom_call_target="tpu_custom_call" | custom-call | flops 8000000000 | bytes 20971520 | tf_op jit(solution)/shard_map/feed/pallas_call | solution.py:736
  97.7 4.4 %contract_weigh.1 = (bf16[4,256,512]{2,1,0:T(8,128)(2,1)S(1)}, bf16[4,256,512]{2,1,0:T(8,128)(2,1)}, bf16[8,128,512]{2,1,0:T(8,128)(2,1)S(1)}, bf16[8,128,512]{2,1,0:T(8,128)(2,1)}) custom-call(s32[4]{0:T(128)S(1)} %copy-done.54, bf16[256,1024]{1,0:T(8,128)(2,1)S(1)} %bitcast.51, bf16[256,1024]{1,0:T(8,128)(2,1)S(1)} %collective-permute-done.other.grad_other, ...), custom_call_target="tpu_custom_call" | custom-call | flops 100000000 | bytes 1048576 | tf_op jit(solution)/shard_map/contract_weigh/pallas_call | solution.py:779
  106.2 3.0 turn.1
  110.8 4.4 %all-to-all-start.1 = ((bf16[8,256,128]{2,1,0:T(8,128)(2,1)}), bf16[8,256,128]{2,1,0:T(8,128)(2,1)}, u32[]{:S(2)}, u32[]{:S(2)}) async-start(bf16[8,256,128]{2,1,0:T(8,128)(2,1)} %get-tuple-element.152), calls=%async_computation.1 | async-start | bytes 1048576 | tf_op jit(solution)/shard_map/all_to_all | solution.py:1153
  122.5 5.1 %weigh.1 = (bf16[4,128,1280]{2,1,0:T(8,128)(2,1)S(1)}, bf16[4,128,1280]{2,1,0:T(8,128)(2,1)}, bf16[8,64,1280]{2,1,0:T(8,128)(2,1)S(1)}, bf16[8,64,1280]{2,1,0:T(8,128)(2,1)}) custom-call(s32[4]{0:T(128)S(1)} %copy-done.54, bf16[256,1024]{1,0:T(8,128)(2,1)S(1)} %copy-done.39, bf16[256,1024]{1,0:T(8,128)(2,1)S(1)} %copy-done.45, ...), custom_call_target="tpu_custom_call" | custom-call | flops 100000000 | bytes 1048576 | tf_op jit(solution)/shard_map/weigh/pallas_call | solution.py:813
  133.7 2.9 second.3
  140.9 21.5 %attend_back.1 = (bf16[8,3,256,128]{3,2,1,0:T(8,128)(2,1)S(1)}, f32[2,8,512]{2,1,0:T(8,128)S(1)}) custom-call(s32[18]{0:T(128)S(1)} %pad_add_fusion.meta_ref, f32[2]{0:T(128)S(1)} %slice_reduce_fusion.1.far_ref, f32[2,512]{1,0:T(2,128)S(1)} %fusion.2.line_ref, f32[8,128,256]{2,1,0:T(8,128)S(1)} %copy-done.64, f32[8,8,256]{2,1,0:T(8,128)S(1)} %get-tuple-element.142.log_ref, ...), custom_call_target="tpu_custom_call" | custom-call | flops 20000000000 | bytes 8388608 | tf_op jit(solution)/shard_map/attend_back/pallas_call | solution.py:522
  164.7 3.8 %all-to-all-start.2 = ((bf16[8,3,256,128]{3,2,1,0:T(8,128)(2,1)}), bf16[8,3,256,128]{3,2,1,0:T(8,128)(2,1)S(1)}, u32[]{:S(2)}, u32[]{:S(2)}) async-start(bf16[8,3,256,128]{3,2,1,0:T(8,128)(2,1)} %copy-done.11), calls=%async_computation.2 | async-start | bytes 3145728 | tf_op jit(solution)/shard_map/all_to_all | solution.py:1153
  175.8 3.0 second.4
  181.9 18.2 %collective-permute-done.17.two_got = bf16[4,128,512]{2,1,0:T(8,128)(2,1)S(1)} collective-permute-done((bf16[4,128,512]{2,1,0:T(8,128)(2,1)}, bf16[4,128,512]{2,1,0:T(8,128)(2,1)S(1)}, u32[]{:S(2)}, u32[]{:S(2)}) %collective-permute-start.17) | collective-permute-done | bytes 524320 | tf_op jit(solution)/shard_map/ppermute | solution.py:1057
  202.4 3.4 %copy-done.3 = bf16[4096,1024]{1,0:T(8,128)(2,1)S(1)} copy-done((bf16[4096,1024]{1,0:T(8,128)(2,1)S(1)}, bf16[4096,1024]{1,0:T(8,128)(2,1)}, u32[]{:S(2)}) %copy-start.3) | copy-done | bytes 8388632
  207.4 4.1 %emit.1 = (f32[256,1024]{1,0:T(8,128)S(1)}, bf16[256,1024]{1,0:T(8,128)(2,1)}) custom-call(s32[4]{0:T(128)S(1)} %copy-done.54, bf16[512,2048]{1,0:T(8,128)(2,1)S(1)} %copy-done.5, bf16[4096,1024]{1,0:T(8,128)(2,1)S(1)} %copy-done.3), custom_call_target="tpu_custom_call" | custom-call | flops 2000000000 | bytes 8388608 | tf_op jit(solution)/shard_map/emit/pallas_call | solution.py:842
  212.4 3.5 %collective-permute-done.18.got = bf16[2,128,1024]{2,1,0:T(8,128)(2,1)} collective-permute-done((bf16[2,128,1024]{2,1,0:T(8,128)(2,1)}, bf16[2,128,1024]{2,1,0:T(8,128)(2,1)}, u32[]{:S(2)}, u32[]{:S(2)}) %collective-permute-start.18) | collective-permute-done | bytes 524320 | tf_op jit(solution)/shard_map/ppermute | solution.py:1057
  219.1 3.6 %attend_weigh.1 = (bf16[4,128,768]{2,1,0:T(8,128)(2,1)S(1)}, bf16[4,128,768]{2,1,0:T(8,128)(2,1)}, bf16[8,64,768]{2,1,0:T(8,128)(2,1)S(1)}, bf16[8,64,768]{2,1,0:T(8,128)(2,1)}) custom-call(s32[4]{0:T(128)S(1)} %copy-done.54, bf16[256,1024]{1,0:T(8,128)(2,1)S(1)} %copy-done.57, bf16[256,1024]{1,0:T(8,128)(2,1)S(1)} %collective-permute-done.22.act_other, ...), custom_call_target="tpu_custom_call" | custom-call | flops 2000000000 | bytes 7340032 | tf_op jit(solution)/shard_map/attend_weigh/pallas_call | solution.py:1039
  234.5 14.8 %collective-permute-done.26.got = bf16[128,1024]{1,0:T(8,128)(2,1)} collective-permute-done((bf16[128,1024]{1,0:T(8,128)(2,1)}, bf16[128,1024]{1,0:T(8,128)(2,1)}, u32[]{:S(2)}, u32[]{:S(2)}) %collective-permute-start.26) | collective-permute-done | bytes 262176 | tf_op jit(solution)/shard_map/ppermute | solution.py:1057
  260.9 2.8 copy-done.6
  263.7 3.4 %close.1 = (f32[256,1024]{1,0:T(8,128)}, f32[2,1024]{1,0:T(2,128)S(1)}) custom-call(bf16[8,3,256,128]{3,2,1,0:T(8,128)(2,1)S(1)} %all-to-all-done.2.parts_ref.owned_ref, bf16[256,1024]{1,0:T(8,128)(2,1)S(1)} %bitcast.55, f32[256,1024]{1,0:T(8,128)S(1)} %copy-done.19, f32[1,1024]{1,0:T(1,128)S(1)} %bitcast.59, bf16[1024,3072]{1,0:T(8,128)(2,1)S(1)} %copy-done.6), custom_call_target="tpu_custom_call" | custom-call | flops 2000000000 | bytes 10485760 | tf_op jit(solution)/shard_map/close/pallas_call | solution.py:910
  267.1 5.2 %collective-permute-done.30.refs_1_ = bf16[128,1024]{1,0:T(8,128)(2,1)S(1)} collective-permute-done((bf16[128,1024]{1,0:T(8,128)(2,1)S(1)}, bf16[128,1024]{1,0:T(8,128)(2,1)S(1)}, u32[]{:S(2)}, u32[]{:S(2)}) %collective-permute-start.30) | collective-permute-done | bytes 262176 | tf_op jit(solution)/shard_map/ppermute | solution.py:1057
  276.2 5.0 %collective-permute-done.33.refs_1_ = bf16[64,2560]{1,0:T(8,128)(2,1)S(1)} collective-permute-done((bf16[64,2560]{1,0:T(8,128)(2,1)S(1)}, bf16[64,2560]{1,0:T(8,128)(2,1)S(1)}, u32[]{:S(2)}, u32[]{:S(2)}) %collective-permute-start.33) | collective-permute-done | bytes 327712 | tf_op jit(solution)/shard_map/ppermute | solution.py:1057
  286.0 2.9 collective-permute-done.43
  289.5 3.3 %all-to-all-start.3 = ((f32[8,8,128]{2,1,0:T(8,128)}), f32[8,8,128]{2,1,0:T(8,128)S(1)}, u32[]{:S(2)}, u32[]{:S(2)}) async-start(f32[8,8,128]{2,1,0:T(8,128)} %add.210), calls=%async_computation.3 | async-start | bytes 65536 | tf_op jit(solution)/shard_map/all_to_all | solution.py:1153
  298.2 2.5 finish_contract.1
  (248 shorter events, 100.9 us)
Async XLA Ops:
  0.7 26.8 %collective-permute-start = (bf16[256,1024]{1,0:T(8,128)(2,1)}, bf16[256,1024]{1,0:T(8,128)(2,1)S(1)}, u32[]{:S(2)}, u32[]{:S(2)}) collective-permute-start(bf16[256,1024]{1,0:T(8,128)(2,1)} %bitcast.49), channel_id=1, source_target_pairs={{0,8},{8,0},{16,24},{24,16},{1,9},{9,1},{17,25},{25,17},{2,10},{10... | collective-permute-start | bytes 1572872 | tf_op jit(solution)/shard_map/ppermute | solution.py:1057
  10.7 15.2 %collective-permute-start.2 = (bf16[3,256,128]{2,1,0:T(8,128)(2,1)}, bf16[3,256,128]{2,1,0:T(8,128)(2,1)S(1)}, u32[]{:S(2)}, u32[]{:S(2)}) collective-permute-start(bf16[3,256,128]{2,1,0:T(8,128)(2,1)} %get-tuple-element.133), channel_id=1, source_target_pairs={{0,2},{1,3},{2,0},{3,1},{4,6},{5,7},{6,4},{7,5},{8,10},{9,11},{10,... | collective-permute-start | bytes 589832 | tf_op jit(solution)/shard_map/ppermute | solution.py:1057
  12.3 25.0 %collective-permute-start.3 = (bf16[3,256,128]{2,1,0:T(8,128)(2,1)}, bf16[3,256,128]{2,1,0:T(8,128)(2,1)S(1)}, u32[]{:S(2)}, u32[]{:S(2)}) collective-permute-start(bf16[3,256,128]{2,1,0:T(8,128)(2,1)} %get-tuple-element.134), channel_id=1, source_target_pairs={{0,3},{1,2},{2,1},{3,0},{4,7},{5,6},{6,5},{7,4},{8,11},{9,10},{10,... | collective-permute-start | bytes 589832 | tf_op jit(solution)/shard_map/ppermute | solution.py:1057
  12.3 25.0 %collective-permute-start.4 = (bf16[3,256,128]{2,1,0:T(8,128)(2,1)}, bf16[3,256,128]{2,1,0:T(8,128)(2,1)S(1)}, u32[]{:S(2)}, u32[]{:S(2)}) collective-permute-start(bf16[3,256,128]{2,1,0:T(8,128)(2,1)} %get-tuple-element.135), channel_id=1, source_target_pairs={{0,4},{1,5},{2,6},{3,7},{4,0},{5,1},{6,2},{7,3},{8,12},{9,13},{10,... | collective-permute-start | bytes 589832 | tf_op jit(solution)/shard_map/ppermute | solution.py:1057
  16.6 26.7 %collective-permute-start.5 = (bf16[3,256,128]{2,1,0:T(8,128)(2,1)}, bf16[3,256,128]{2,1,0:T(8,128)(2,1)S(1)}, u32[]{:S(2)}, u32[]{:S(2)}) collective-permute-start(bf16[3,256,128]{2,1,0:T(8,128)(2,1)} %get-tuple-element.136), channel_id=1, source_target_pairs={{0,5},{1,4},{2,7},{3,6},{4,1},{5,0},{6,3},{7,2},{8,13},{9,12},{10,... | collective-permute-start | bytes 589832 | tf_op jit(solution)/shard_map/ppermute | solution.py:1057
  25.9 17.4 %collective-permute-start.6 = (bf16[3,256,128]{2,1,0:T(8,128)(2,1)}, bf16[3,256,128]{2,1,0:T(8,128)(2,1)S(1)}, u32[]{:S(2)}, u32[]{:S(2)}) collective-permute-start(bf16[3,256,128]{2,1,0:T(8,128)(2,1)} %get-tuple-element.137), channel_id=1, source_target_pairs={{0,6},{1,7},{2,4},{3,5},{4,2},{5,3},{6,0},{7,1},{8,14},{9,15},{10,... | collective-permute-start | bytes 589832 | tf_op jit(solution)/shard_map/ppermute | solution.py:1057
  27.5 15.9 %collective-permute-start.7 = (bf16[3,256,128]{2,1,0:T(8,128)(2,1)}, bf16[3,256,128]{2,1,0:T(8,128)(2,1)S(1)}, u32[]{:S(2)}, u32[]{:S(2)}) collective-permute-start(bf16[3,256,128]{2,1,0:T(8,128)(2,1)} %get-tuple-element.138), channel_id=1, source_target_pairs={{0,7},{1,6},{2,5},{3,4},{4,3},{5,2},{6,1},{7,0},{8,15},{9,14},{10,... | collective-permute-start | bytes 589832 | tf_op jit(solution)/shard_map/ppermute | solution.py:1057
  103.1 30.5 %collective-permute-start.12 = (bf16[4,256,512]{2,1,0:T(8,128)(2,1)}, bf16[4,256,512]{2,1,0:T(8,128)(2,1)}, u32[]{:S(2)}, u32[]{:S(2)}) collective-permute-start(bf16[4,256,512]{2,1,0:T(8,128)(2,1)} %get-tuple-element.159), channel_id=1, source_target_pairs={{0,1},{1,0},{2,3},{3,2},{4,5},{5,4},{6,7},{7,6},{8,9},{9,8},{10,11... | collective-permute-start | bytes 3145736 | tf_op jit(solution)/shard_map/ppermute | solution.py:1057
  104.7 29.0 %collective-permute-start.13 = (bf16[8,128,512]{2,1,0:T(8,128)(2,1)}, bf16[8,128,512]{2,1,0:T(8,128)(2,1)}, u32[]{:S(2)}, u32[]{:S(2)}) collective-permute-start(bf16[8,128,512]{2,1,0:T(8,128)(2,1)} %get-tuple-element.161), channel_id=1, source_target_pairs={{0,16},{8,24},{16,0},{24,8},{1,17},{9,25},{17,1},{25,9},{2,18},{10... | collective-permute-start | bytes 3145736 | tf_op jit(solution)/shard_map/ppermute | solution.py:1057
  110.8 27.5 %all-to-all-start.1 = ((bf16[8,256,128]{2,1,0:T(8,128)(2,1)}), bf16[8,256,128]{2,1,0:T(8,128)(2,1)}, u32[]{:S(2)}, u32[]{:S(2)}) async-start(bf16[8,256,128]{2,1,0:T(8,128)(2,1)} %get-tuple-element.152), calls=%async_computation.1 | async-start | bytes 1048576 | tf_op jit(solution)/shard_map/all_to_all | solution.py:1153
  129.8 33.8 %collective-permute-start.14 = (bf16[4,128,1280]{2,1,0:T(8,128)(2,1)}, bf16[4,128,1280]{2,1,0:T(8,128)(2,1)S(1)}, u32[]{:S(2)}, u32[]{:S(2)}) collective-permute-start(bf16[4,128,1280]{2,1,0:T(8,128)(2,1)} %get-tuple-element.174), channel_id=1, source_target_pairs={{0,1},{1,0},{2,3},{3,2},{4,5},{5,4},{6,7},{7,6},{8,9},{9,8},{10,11... | collective-permute-start | bytes 3932168 | tf_op jit(solution)/shard_map/ppermute | solution.py:1057
  131.4 33.3 %collective-permute-start.15 = (bf16[8,64,1280]{2,1,0:T(8,128)(2,1)}, bf16[8,64,1280]{2,1,0:T(8,128)(2,1)}, u32[]{:S(2)}, u32[]{:S(2)}) collective-permute-start(bf16[8,64,1280]{2,1,0:T(8,128)(2,1)} %get-tuple-element.176), channel_id=1, source_target_pairs={{0,16},{8,24},{16,0},{24,8},{1,17},{9,25},{17,1},{25,9},{2,18},{10... | collective-permute-start | bytes 3932168 | tf_op jit(solution)/shard_map/ppermute | solution.py:1057
  164.7 51.3 %all-to-all-start.2 = ((bf16[8,3,256,128]{3,2,1,0:T(8,128)(2,1)}), bf16[8,3,256,128]{3,2,1,0:T(8,128)(2,1)S(1)}, u32[]{:S(2)}, u32[]{:S(2)}) async-start(bf16[8,3,256,128]{3,2,1,0:T(8,128)(2,1)} %copy-done.11), calls=%async_computation.2 | async-start | bytes 3145728 | tf_op jit(solution)/shard_map/all_to_all | solution.py:1153
  168.5 13.4 %collective-permute-start.16 = (bf16[4,128,512]{2,1,0:T(8,128)(2,1)}, bf16[4,128,512]{2,1,0:T(8,128)(2,1)S(1)}, u32[]{:S(2)}, u32[]{:S(2)}) collective-permute-start(bf16[4,128,512]{2,1,0:T(8,128)(2,1)} %get-tuple-element.181), channel_id=1, source_target_pairs={{0,16},{8,24},{16,0},{24,8},{1,17},{9,25},{17,1},{25,9},{2,18},{10... | collective-permute-start | bytes 1572872 | tf_op jit(solution)/shard_map/ppermute | solution.py:1057
  170.1 30.0 %collective-permute-start.17 = (bf16[4,128,512]{2,1,0:T(8,128)(2,1)}, bf16[4,128,512]{2,1,0:T(8,128)(2,1)S(1)}, u32[]{:S(2)}, u32[]{:S(2)}) collective-permute-start(bf16[4,128,512]{2,1,0:T(8,128)(2,1)} %get-tuple-element.183), channel_id=1, source_target_pairs={{0,1},{1,0},{2,3},{3,2},{4,5},{5,4},{6,7},{7,6},{8,9},{9,8},{10,11... | collective-permute-start | bytes 1572872 | tf_op jit(solution)/shard_map/ppermute | solution.py:1057
  180.5 32.0 %collective-permute-start.19 = (bf16[4,64,1280]{2,1,0:T(8,128)(2,1)}, bf16[4,64,1280]{2,1,0:T(8,128)(2,1)S(1)}, u32[]{:S(2)}, u32[]{:S(2)}) collective-permute-start(bf16[4,64,1280]{2,1,0:T(8,128)(2,1)} %get-tuple-element.191), channel_id=1, source_target_pairs={{0,16},{8,24},{16,0},{24,8},{1,17},{9,25},{17,1},{25,9},{2,18},{10... | collective-permute-start | bytes 1966088 | tf_op jit(solution)/shard_map/ppermute | solution.py:1057
  181.0 31.5 %collective-permute-start.20 = (bf16[4,64,1280]{2,1,0:T(8,128)(2,1)}, bf16[4,64,1280]{2,1,0:T(8,128)(2,1)}, u32[]{:S(2)}, u32[]{:S(2)}) collective-permute-start(bf16[4,64,1280]{2,1,0:T(8,128)(2,1)} %get-tuple-element.193), channel_id=1, source_target_pairs={{0,1},{1,0},{2,3},{3,2},{4,5},{5,4},{6,7},{7,6},{8,9},{9,8},{10,11... | collective-permute-start | bytes 1966088 | tf_op jit(solution)/shard_map/ppermute | solution.py:1057
  202.4 13.6 %collective-permute-start.18 = (bf16[2,128,1024]{2,1,0:T(8,128)(2,1)}, bf16[2,128,1024]{2,1,0:T(8,128)(2,1)}, u32[]{:S(2)}, u32[]{:S(2)}) collective-permute-start(bf16[2,128,1024]{2,1,0:T(8,128)(2,1)} %get-tuple-element.185), channel_id=1, source_target_pairs={{0,2},{1,3},{2,0},{3,1},{4,6},{5,7},{6,4},{7,5},{8,10},{9,11},{10,... | collective-permute-start | bytes 1572872 | tf_op jit(solution)/shard_map/ppermute | solution.py:1057
  223.6 27.9 %collective-permute-start.24 = (bf16[4,128,768]{2,1,0:T(8,128)(2,1)}, bf16[4,128,768]{2,1,0:T(8,128)(2,1)}, u32[]{:S(2)}, u32[]{:S(2)}) collective-permute-start(bf16[4,128,768]{2,1,0:T(8,128)(2,1)} %get-tuple-element.204), channel_id=1, source_target_pairs={{0,1},{1,0},{2,3},{3,2},{4,5},{5,4},{6,7},{7,6},{8,9},{9,8},{10,11... | collective-permute-start | bytes 2359304 | tf_op jit(solution)/shard_map/ppermute | solution.py:1057
  224.9 26.6 %collective-permute-start.25 = (bf16[8,64,768]{2,1,0:T(8,128)(2,1)}, bf16[8,64,768]{2,1,0:T(8,128)(2,1)}, u32[]{:S(2)}, u32[]{:S(2)}) collective-permute-start(bf16[8,64,768]{2,1,0:T(8,128)(2,1)} %get-tuple-element.206), channel_id=1, source_target_pairs={{0,16},{8,24},{16,0},{24,8},{1,17},{9,25},{17,1},{25,9},{2,18},{10... | collective-permute-start | bytes 2359304 | tf_op jit(solution)/shard_map/ppermute | solution.py:1057
  229.3 22.1 %collective-permute-start.27 = (bf16[2,64,2560]{2,1,0:T(8,128)(2,1)}, bf16[2,64,2560]{2,1,0:T(8,128)(2,1)}, u32[]{:S(2)}, u32[]{:S(2)}) collective-permute-start(bf16[2,64,2560]{2,1,0:T(8,128)(2,1)} %get-tuple-element.216), channel_id=1, source_target_pairs={{0,2},{1,3},{2,0},{3,1},{4,6},{5,7},{6,4},{7,5},{8,10},{9,11},{10,... | collective-permute-start | bytes 1966088 | tf_op jit(solution)/shard_map/ppermute | solution.py:1057
  231.9 17.4 %collective-permute-start.26 = (bf16[128,1024]{1,0:T(8,128)(2,1)}, bf16[128,1024]{1,0:T(8,128)(2,1)}, u32[]{:S(2)}, u32[]{:S(2)}) collective-permute-start(bf16[128,1024]{1,0:T(8,128)(2,1)} %get-tuple-element.210), channel_id=1, source_target_pairs={{0,4},{1,5},{2,6},{3,7},{4,0},{5,1},{6,2},{7,3},{8,12},{9,13},{10,... | collective-permute-start | bytes 786440 | tf_op jit(solution)/shard_map/ppermute | solution.py:1057
  253.9 18.4 %collective-permute-start.31 = (bf16[64,2560]{1,0:T(8,128)(2,1)S(1)}, bf16[64,2560]{1,0:T(8,128)(2,1)S(1)}, u32[]{:S(2)}, u32[]{:S(2)}) collective-permute-start(bf16[64,2560]{1,0:T(8,128)(2,1)S(1)} %get-tuple-element.230), channel_id=1, source_target_pairs={{0,4},{1,5},{2,6},{3,7},{4,0},{5,1},{6,2},{7,3},{8,12},{9,13},{10,... | collective-permute-start | bytes 983048 | tf_op jit(solution)/shard_map/ppermute | solution.py:1057
  256.9 15.4 %collective-permute-start.28 = (bf16[4,64,768]{2,1,0:T(8,128)(2,1)S(1)}, bf16[4,64,768]{2,1,0:T(8,128)(2,1)S(1)}, u32[]{:S(2)}, u32[]{:S(2)}) collective-permute-start(bf16[4,64,768]{2,1,0:T(8,128)(2,1)S(1)} %get-tuple-element.222), channel_id=1, source_target_pairs={{0,16},{8,24},{16,0},{24,8},{1,17},{9,25},{17,1},{25,9},{2,18},{10... | collective-permute-start | bytes 1179656 | tf_op jit(solution)/shard_map/ppermute | solution.py:1057
  257.5 14.8 %collective-permute-start.29 = (bf16[4,64,768]{2,1,0:T(8,128)(2,1)S(1)}, bf16[4,64,768]{2,1,0:T(8,128)(2,1)S(1)}, u32[]{:S(2)}, u32[]{:S(2)}) collective-permute-start(bf16[4,64,768]{2,1,0:T(8,128)(2,1)S(1)} %get-tuple-element.224), channel_id=1, source_target_pairs={{0,1},{1,0},{2,3},{3,2},{4,5},{5,4},{6,7},{7,6},{8,9},{9,8},{10,11... | collective-permute-start | bytes 1179656 | tf_op jit(solution)/shard_map/ppermute | solution.py:1057
  259.3 13.0 %collective-permute-start.30 = (bf16[128,1024]{1,0:T(8,128)(2,1)S(1)}, bf16[128,1024]{1,0:T(8,128)(2,1)S(1)}, u32[]{:S(2)}, u32[]{:S(2)}) collective-permute-start(bf16[128,1024]{1,0:T(8,128)(2,1)S(1)} %last.3.refs_0_), channel_id=1, source_target_pairs={{0,16},{8,24},{16,0},{24,8},{1,17},{9,25},{17,1},{25,9},{2,18},{10... | collective-permute-start | bytes 786440 | tf_op jit(solution)/shard_map/ppermute | solution.py:1057
  273.1 8.9 %collective-permute-start.34 = (bf16[2,64,1536]{2,1,0:T(8,128)(2,1)S(1)}, bf16[2,64,1536]{2,1,0:T(8,128)(2,1)S(1)}, u32[]{:S(2)}, u32[]{:S(2)}) collective-permute-start(bf16[2,64,1536]{2,1,0:T(8,128)(2,1)S(1)} %get-tuple-element.239), channel_id=1, source_target_pairs={{0,2},{1,3},{2,0},{3,1},{4,6},{5,7},{6,4},{7,5},{8,10},{9,11},{10,... | collective-permute-start | bytes 1179656 | tf_op jit(solution)/shard_map/ppermute | solution.py:1057
  274.6 21.4 %collective-permute-start.21 = (bf16[256,1024]{1,0:T(8,128)(2,1)}, bf16[256,1024]{1,0:T(8,128)(2,1)}, u32[]{:S(2)}, u32[]{:S(2)}) collective-permute-start(bf16[256,1024]{1,0:T(8,128)(2,1)} %get-tuple-element.195), channel_id=1, source_target_pairs={{0,8},{8,0},{16,24},{24,16},{1,9},{9,1},{17,25},{25,17},{2,10},{10... | collective-permute-start | bytes 1572872 | tf_op jit(solution)/shard_map/ppermute | solution.py:1057
  283.9 9.0 %collective-permute-start.35 = (bf16[64,1536]{1,0:T(8,128)(2,1)}, bf16[64,1536]{1,0:T(8,128)(2,1)S(1)}, u32[]{:S(2)}, u32[]{:S(2)}) collective-permute-start(bf16[64,1536]{1,0:T(8,128)(2,1)} %get-tuple-element.243), channel_id=1, source_target_pairs={{0,4},{1,5},{2,6},{3,7},{4,0},{5,1},{6,2},{7,3},{8,12},{9,13},{10,... | collective-permute-start | bytes 589832 | tf_op jit(solution)/shard_map/ppermute | solution.py:1057
  285.5 12.7 %collective-permute-start.41 = (bf16[128,1024]{1,0:T(8,128)(2,1)S(1)}, bf16[128,1024]{1,0:T(8,128)(2,1)}, u32[]{:S(2)}, u32[]{:S(2)}) collective-permute-start(bf16[128,1024]{1,0:T(8,128)(2,1)S(1)} %last.3.refs_0_), channel_id=1, source_target_pairs={{0,8},{8,0},{16,24},{24,16},{1,9},{9,1},{17,25},{25,17},{2,10},{10... | collective-permute-start | bytes 786440 | tf_op jit(solution)/shard_map/ppermute | solution.py:1057
  285.5 12.7 %collective-permute-start.42 = (bf16[128,1024]{1,0:T(8,128)(2,1)S(1)}, bf16[128,1024]{1,0:T(8,128)(2,1)}, u32[]{:S(2)}, u32[]{:S(2)}) collective-permute-start(bf16[128,1024]{1,0:T(8,128)(2,1)S(1)} %collective-permute-done.30.refs_1_), channel_id=1, source_target_pairs={{0,8},{8,0},{16,24},{24,16},{1,9},{9,1},{17,25},{25,17},{2,10},{10... | collective-permute-start | bytes 786440 | tf_op jit(solution)/shard_map/ppermute | solution.py:1057
  289.5 11.7 %all-to-all-start.3 = ((f32[8,8,128]{2,1,0:T(8,128)}), f32[8,8,128]{2,1,0:T(8,128)S(1)}, u32[]{:S(2)}, u32[]{:S(2)}) async-start(f32[8,8,128]{2,1,0:T(8,128)} %add.210), calls=%async_computation.3 | async-start | bytes 65536 | tf_op jit(solution)/shard_map/all_to_all | solution.py:1153
  (80 other events, 568.6 us)

commit v6 on v5

--- a/solution.py
+++ b/solution.py
@@ -1089,11 +1089,15 @@
     return one_left, flipped(one_send, "seq", 2), two_left, flipped(two_send, "blk", 1)
 
 
-def over_near(here, one_keep, one_got, two_keep, two_got):
+def near_sums(here, one_keep, one_got, two_keep, two_got):
     levels, half, cut = one_keep.shape
-    left, send = _small_call(
+    return _small_call(
         near_kernel, "near", [(levels // 2, half, 2 * cut)] * 2, jnp.bfloat16, here, one_keep, one_got, two_keep, two_got
     )
+
+
+def over_near(here, *parts):
+    left, send = near_sums(here, *parts)
     return left, flipped(send, "blk", 2)
 
 
@@ -1180,9 +1184,10 @@
     out_keep, out_send = emit(here, after(hidden_low, back_all), contract_weight, peers)
     contract_parts = over_near(here, *send_second(*sums[:4]))
     expand_parts = send_second(*over_second(here, *sums[4:]))
-    owned, out_keep, *sums = lax.optimization_barrier((owned, out_keep, *contract_parts, *expand_parts))
-    contract_parts = over_far(here, *sums[:2])
-    expand_parts = over_near(here, *sums[2:])
+    expand_left, expand_send = near_sums(here, *expand_parts)
+    owned, out_keep, expand_left, expand_send, *sums = lax.optimization_barrier((owned, out_keep, expand_left, expand_send, *contract_parts))
+    expand_parts = expand_left, flipped(expand_send, "blk", 2)
+    contract_parts = over_far(here, *sums)
     owned_send = pick(owned.reshape(2, levels, 3, rows, group), 1 - core, 0)
     attend_parts = over_first(*attend_weigh(here, act_first, first_other, owned, flipped(owned_send, "seq", 1)))
     output = (middle + out_keep + flipped(out_send, "seq", 1).astype(jnp.float32)).astype(jnp.bfloat16)

time: 309 us -> 307 us (level)
  starting transfers between devices: 51.2 us -> 54.6 us
    ppermute x44, starting transfers between devices: 39.6 us -> 43 us  [flipped(): return lax.ppermute(array, axis, [(i, i ^ mask) for i in range(peers)])]
    unnamed x132 -> x126, local copies, waits for them, and re-layouts: 45.6 us -> 43.2 us
where the time goes in v6:
time: 307 us; the launch traced here: 306 us
  Pallas kernels  105 us (34%)
  waiting for transfers between devices  70 us (23%)
  starting transfers between devices  54.6 us (18%)
  local copies, waits for them, and re-layouts  44.9 us (15%)
  blocking collectives  25.8 us (8%)
  other arithmetic  3.69 us (1%)
    ppermute x44, waiting for transfers between devices, flipped(): return lax.ppermute(array, axis, [(i, i ^ mask) for i in range(peers)])  70 us
    unnamed x126, local copies, waits for them, and re-layouts  43.2 us
    ppermute x44, starting transfers between devices, flipped(): return lax.ppermute(array, axis, [(i, i ^ mask) for i in range(peers)])  43 us
    all_to_all x1, blocking collectives, to_all(): return lax.all_to_all(array, 'blk', split_axis=0, concat_axis=0, tiled=True)  25.8 us
    pallas_call x15, Pallas kernels, _small_call(): pl.pallas_call(kernel, out_shape=[jax.ShapeDtypeStruct(shape, kind) for s...  24.6 us
    pallas_call x1, Pallas kernels, attend_back(): pl.pallas_call(partial(attend_back_kernel, peers, items, rows), out_shape...  21.5 us
    pallas_call x1, Pallas kernels, attend(): pl.pallas_call(partial(attend_kernel, peers, items, rows), out_shape=shap...  11.9 us
    all_to_all x3, starting transfers between devices, to_all(): return lax.all_to_all(array, 'blk', split_axis=0, concat_axis=0, tiled=True)  11.6 us
  transfers between devices with their start and end apart: 47, of which 17 were waited for; matrix products, arithmetic and copies ran while one was open for 2% of the time, Pallas kernels for 24%

profile of v6, /device:TPU:0, one launch (start us, length us, event | category | flops | bytes accessed | tf_op | source)
XLA Modules:
  0.0 305.6 jit_solution(2249002217108558025)
XLA Ops:
  1.8 6.4 %project.1 = (bf16[3,256,128]{2,1,0:T(8,128)(2,1)}, bf16[3,256,128]{2,1,0:T(8,128)(2,1)}, bf16[3,256,128]{2,1,0:T(8,128)(2,1)}, bf16[3,256,128]{2,1,0:T(8,128)(2...) custom-call(s32[4]{0:T(128)} %pad_add_fusion.1.meta_ref, ...), custom_call_target="tpu_custom_call" | custom-call | flops 4000000000 | bytes 8388608 | tf_op jit(solution)/shard_map/project/pallas_call | solution.py:611
  8.1 2.6 collective-permute-start.1
  12.3 3.0 collective-permute-start.4
  16.7 3.6 %collective-permute-start.5 = (bf16[3,256,128]{2,1,0:T(8,128)(2,1)}, bf16[3,256,128]{2,1,0:T(8,128)(2,1)S(1)}, u32[]{:S(2)}, u32[]{:S(2)}) collective-permute-start(bf16[3,256,128]{2,1,0:T(8,128)(2,1)} %get-tuple-element.134), channel_id=1, source_target_pairs={{0,5},{1,4},{2,7},{3,6},{4,1},{5,0},{6,3},{7,2},{8,13},{9,12},{10,... | collective-permute-start | bytes 589832 | tf_op jit(solution)/shard_map/ppermute | solution.py:1057
  20.2 5.7 %collective-permute-done.2.refs_2_ = bf16[3,256,128]{2,1,0:T(8,128)(2,1)S(1)} collective-permute-done((bf16[3,256,128]{2,1,0:T(8,128)(2,1)}, bf16[3,256,128]{2,1,0:T(8,128)(2,1)S(1)}, u32[]{:S(2)}, u32[]{:S(2)}) %collective-permute-start.2) | collective-permute-done | bytes 196640 | tf_op jit(solution)/shard_map/ppermute | solution.py:1057
  29.2 3.4 %copy-done.2 = bf16[4096,1024]{1,0:T(8,128)(2,1)S(1)} copy-done((bf16[4096,1024]{1,0:T(8,128)(2,1)S(1)}, bf16[4096,1024]{1,0:T(8,128)(2,1)}, u32[]{:S(2)}) %copy-start.2) | copy-done | bytes 8388632
  32.6 4.7 %pull.1.pulled_ref = f32[512,2048]{1,0:T(8,128)S(1)} custom-call(s32[4]{0:T(128)S(1)} %copy-done.50, bf16[256,1024]{1,0:T(8,128)(2,1)S(1)} %bitcast.50, bf16[256,1024]{1,0:T(8,128)(2,1)S(1)} %collective-permute-done.other.grad_other, bf16[4096,1024]{1,0:T(8,128)(2,1)S(1)} %copy-done.2), custom_call_target="tpu_custom_call" | custom-call | flops 3000000000 | bytes 9437184 | tf_op jit(solution)/shard_map/pull/pallas_call | solution.py:673
  37.3 6.0 %collective-permute-done.5.refs_5_ = bf16[3,256,128]{2,1,0:T(8,128)(2,1)S(1)} collective-permute-done((bf16[3,256,128]{2,1,0:T(8,128)(2,1)}, bf16[3,256,128]{2,1,0:T(8,128)(2,1)S(1)}, u32[]{:S(2)}, u32[]{:S(2)}) %collective-permute-start.5) | collective-permute-done | bytes 196640 | tf_op jit(solution)/shard_map/ppermute | solution.py:1057
  43.4 11.9 %attend.1 = (bf16[8,256,128]{2,1,0:T(8,128)(2,1)S(1)}, f32[8,128,256]{2,1,0:T(8,128)S(1)}, f32[8,8,256]{2,1,0:T(8,128)S(1)}, bf16[8,3,256,128]{3,2,1,0:T(8,128)(2,1)S(1)}) custom-call(s32[18]{0:T(128)S(1)} %pad_add_fusion.meta_ref, f32[2]{0:T(128)S(1)} %slice_reduce_fusion.1.far_ref, f32[2,512]{1,0:T(2,128)S(1)} %fusion.2.line_ref, ...), custom_call_target="tpu_custom_call" | custom-call | flops 8000000000 | bytes 4194304 | tf_op jit(solution)/shard_map/attend/pallas_call | solution.py:423
  56.5 25.8 %all_to_all.20.parts_ref = bf16[8,256,128]{2,1,0:T(8,128)(2,1)S(1)} all-to-all(bf16[8,256,128]{2,1,0:T(8,128)(2,1)S(1)} %get-tuple-element.137), channel_id=1, replica_groups=mesh['seq'=4,'blk'=8] {'blk'}, dimensions={0} | all-to-all | bytes 1048576 | tf_op jit(solution)/shard_map/all_to_all | solution.py:1157
  85.3 10.9 %feed.1 = (f32[256,1024]{1,0:T(8,128)S(1)}, f32[256,1024]{1,0:T(8,128)S(1)}, bf16[512,2048]{1,0:T(8,128)(2,1)S(1)}, bf16[512,2048]{1,0:T(8,128)(2,1)S(1)}) custom-call(s32[4]{0:T(128)S(1)} %copy-done.50, bf16[256,1024]{1,0:T(8,128)(2,1)S(1)} %get-tuple-element.141.act_mine, bf16[256,1024]{1,0:T(8,128)(2,1)S(1)} %collective-permute-done.8.act_other, ...), custom_call_target="tpu_custom_call" | custom-call | flops 8000000000 | bytes 20971520 | tf_op jit(solution)/shard_map/feed/pallas_call | solution.py:736
  97.7 4.4 %contract_weigh.1 = (bf16[4,256,512]{2,1,0:T(8,128)(2,1)S(1)}, bf16[4,256,512]{2,1,0:T(8,128)(2,1)}, bf16[8,128,512]{2,1,0:T(8,128)(2,1)S(1)}, bf16[8,128,512]{2,1,0:T(8,128)(2,1)}) custom-call(s32[4]{0:T(128)S(1)} %copy-done.50, bf16[256,1024]{1,0:T(8,128)(2,1)S(1)} %bitcast.51, bf16[256,1024]{1,0:T(8,128)(2,1)S(1)} %collective-permute-done.other.grad_other, ...), custom_call_target="tpu_custom_call" | custom-call | flops 100000000 | bytes 1048576 | tf_op jit(solution)/shard_map/contract_weigh/pallas_call | solution.py:779
  106.2 3.0 turn.1
  110.8 4.4 %all-to-all-start.1 = ((bf16[8,256,128]{2,1,0:T(8,128)(2,1)}), bf16[8,256,128]{2,1,0:T(8,128)(2,1)}, u32[]{:S(2)}, u32[]{:S(2)}) async-start(bf16[8,256,128]{2,1,0:T(8,128)(2,1)} %get-tuple-element.150), calls=%async_computation.1 | async-start | bytes 1048576 | tf_op jit(solution)/shard_map/all_to_all | solution.py:1157
  122.5 5.1 %weigh.1 = (bf16[4,128,1280]{2,1,0:T(8,128)(2,1)S(1)}, bf16[4,128,1280]{2,1,0:T(8,128)(2,1)}, bf16[8,64,1280]{2,1,0:T(8,128)(2,1)S(1)}, bf16[8,64,1280]{2,1,0:T(8,128)(2,1)}) custom-call(s32[4]{0:T(128)S(1)} %copy-done.50, bf16[256,1024]{1,0:T(8,128)(2,1)S(1)} %copy-done.35, bf16[256,1024]{1,0:T(8,128)(2,1)S(1)} %copy-done.41, ...), custom_call_target="tpu_custom_call" | custom-call | flops 100000000 | bytes 1048576 | tf_op jit(solution)/shard_map/weigh/pallas_call | solution.py:813
  133.7 2.9 second.3
  140.9 21.5 %attend_back.1 = (bf16[8,3,256,128]{3,2,1,0:T(8,128)(2,1)S(1)}, f32[2,8,512]{2,1,0:T(8,128)S(1)}) custom-call(s32[18]{0:T(128)S(1)} %pad_add_fusion.meta_ref, f32[2]{0:T(128)S(1)} %slice_reduce_fusion.1.far_ref, f32[2,512]{1,0:T(2,128)S(1)} %fusion.2.line_ref, f32[8,128,256]{2,1,0:T(8,128)S(1)} %copy-done.61, f32[8,8,256]{2,1,0:T(8,128)S(1)} %get-tuple-element.140.log_ref, ...), custom_call_target="tpu_custom_call" | custom-call | flops 20000000000 | bytes 8388608 | tf_op jit(solution)/shard_map/attend_back/pallas_call | solution.py:522
  164.7 3.8 %all-to-all-start.2 = ((bf16[8,3,256,128]{3,2,1,0:T(8,128)(2,1)}), bf16[8,3,256,128]{3,2,1,0:T(8,128)(2,1)S(1)}, u32[]{:S(2)}, u32[]{:S(2)}) async-start(bf16[8,3,256,128]{3,2,1,0:T(8,128)(2,1)} %copy-done.11), calls=%async_computation.2 | async-start | bytes 3145728 | tf_op jit(solution)/shard_map/all_to_all | solution.py:1157
  175.8 3.0 second.4
  182.8 17.3 %collective-permute-done.19.two_got = bf16[4,128,512]{2,1,0:T(8,128)(2,1)S(1)} collective-permute-done((bf16[4,128,512]{2,1,0:T(8,128)(2,1)}, bf16[4,128,512]{2,1,0:T(8,128)(2,1)S(1)}, u32[]{:S(2)}, u32[]{:S(2)}) %collective-permute-start.19) | collective-permute-done | bytes 524320 | tf_op jit(solution)/shard_map/ppermute | solution.py:1057
  202.4 3.4 %copy-done.3 = bf16[4096,1024]{1,0:T(8,128)(2,1)S(1)} copy-done((bf16[4096,1024]{1,0:T(8,128)(2,1)S(1)}, bf16[4096,1024]{1,0:T(8,128)(2,1)}, u32[]{:S(2)}) %copy-start.3) | copy-done | bytes 8388632
  207.4 4.1 %emit.1 = (f32[256,1024]{1,0:T(8,128)S(1)}, bf16[256,1024]{1,0:T(8,128)(2,1)}) custom-call(s32[4]{0:T(128)S(1)} %copy-done.50, bf16[512,2048]{1,0:T(8,128)(2,1)S(1)} %copy-done.5, bf16[4096,1024]{1,0:T(8,128)(2,1)S(1)} %copy-done.3), custom_call_target="tpu_custom_call" | custom-call | flops 2000000000 | bytes 8388608 | tf_op jit(solution)/shard_map/emit/pallas_call | solution.py:842
  216.6 2.5 collective-permute-done.22.act_other
  219.1 3.6 %attend_weigh.1 = (bf16[4,128,768]{2,1,0:T(8,128)(2,1)S(1)}, bf16[4,128,768]{2,1,0:T(8,128)(2,1)}, bf16[8,64,768]{2,1,0:T(8,128)(2,1)S(1)}, bf16[8,64,768]{2,1,0:T(8,128)(2,1)}) custom-call(s32[4]{0:T(128)S(1)} %copy-done.50, bf16[256,1024]{1,0:T(8,128)(2,1)S(1)} %copy-done.54, bf16[256,1024]{1,0:T(8,128)(2,1)S(1)} %collective-permute-done.22.act_other, ...), custom_call_target="tpu_custom_call" | custom-call | flops 2000000000 | bytes 7340032 | tf_op jit(solution)/shard_map/attend_weigh/pallas_call | solution.py:1039
  231.8 14.5 %collective-permute-done.26.got = bf16[128,1024]{1,0:T(8,128)(2,1)} collective-permute-done((bf16[128,1024]{1,0:T(8,128)(2,1)}, bf16[128,1024]{1,0:T(8,128)(2,1)}, u32[]{:S(2)}, u32[]{:S(2)}) %collective-permute-start.26) | collective-permute-done | bytes 262176 | tf_op jit(solution)/shard_map/ppermute | solution.py:1057
  258.7 2.8 copy-done.6
  261.5 3.4 %close.1 = (f32[256,1024]{1,0:T(8,128)}, f32[2,1024]{1,0:T(2,128)S(1)}) custom-call(bf16[8,3,256,128]{3,2,1,0:T(8,128)(2,1)S(1)} %all-to-all-done.2.parts_ref.owned_ref, bf16[256,1024]{1,0:T(8,128)(2,1)S(1)} %bitcast.55, f32[256,1024]{1,0:T(8,128)S(1)} %copy-done.19, f32[1,1024]{1,0:T(1,128)S(1)} %bitcast.59, bf16[1024,3072]{1,0:T(8,128)(2,1)S(1)} %copy-done.6), custom_call_target="tpu_custom_call" | custom-call | flops 2000000000 | bytes 10485760 | tf_op jit(solution)/shard_map/close/pallas_call | solution.py:910
  264.9 4.2 %collective-permute-done.30.refs_1_ = bf16[128,1024]{1,0:T(8,128)(2,1)S(1)} collective-permute-done((bf16[128,1024]{1,0:T(8,128)(2,1)S(1)}, bf16[128,1024]{1,0:T(8,128)(2,1)S(1)}, u32[]{:S(2)}, u32[]{:S(2)}) %collective-permute-start.30) | collective-permute-done | bytes 262176 | tf_op jit(solution)/shard_map/ppermute | solution.py:1057
  273.6 4.9 %collective-permute-done.33.refs_1_ = bf16[64,2560]{1,0:T(8,128)(2,1)S(1)} collective-permute-done((bf16[64,2560]{1,0:T(8,128)(2,1)S(1)}, bf16[64,2560]{1,0:T(8,128)(2,1)S(1)}, u32[]{:S(2)}, u32[]{:S(2)}) %collective-permute-start.33) | collective-permute-done | bytes 327712 | tf_op jit(solution)/shard_map/ppermute | solution.py:1057
  280.5 2.6 collective-permute-start.35
  284.1 2.9 collective-permute-done.43
  287.6 3.4 %all-to-all-start.3 = ((f32[8,8,128]{2,1,0:T(8,128)}), f32[8,8,128]{2,1,0:T(8,128)S(1)}, u32[]{:S(2)}, u32[]{:S(2)}) async-start(f32[8,8,128]{2,1,0:T(8,128)} %add.210), calls=%async_computation.3 | async-start | bytes 65536 | tf_op jit(solution)/shard_map/all_to_all | solution.py:1157
  (242 shorter events, 102.3 us)
Async XLA Ops:
  0.7 26.8 %collective-permute-start = (bf16[256,1024]{1,0:T(8,128)(2,1)}, bf16[256,1024]{1,0:T(8,128)(2,1)S(1)}, u32[]{:S(2)}, u32[]{:S(2)}) collective-permute-start(bf16[256,1024]{1,0:T(8,128)(2,1)} %bitcast.49), channel_id=1, source_target_pairs={{0,8},{8,0},{16,24},{24,16},{1,9},{9,1},{17,25},{25,17},{2,10},{10... | collective-permute-start | bytes 1572872 | tf_op jit(solution)/shard_map/ppermute | solution.py:1057
  10.7 15.2 %collective-permute-start.2 = (bf16[3,256,128]{2,1,0:T(8,128)(2,1)}, bf16[3,256,128]{2,1,0:T(8,128)(2,1)S(1)}, u32[]{:S(2)}, u32[]{:S(2)}) collective-permute-start(bf16[3,256,128]{2,1,0:T(8,128)(2,1)} %get-tuple-element.131), channel_id=1, source_target_pairs={{0,2},{1,3},{2,0},{3,1},{4,6},{5,7},{6,4},{7,5},{8,10},{9,11},{10,... | collective-permute-start | bytes 589832 | tf_op jit(solution)/shard_map/ppermute | solution.py:1057
  12.3 25.0 %collective-permute-start.3 = (bf16[3,256,128]{2,1,0:T(8,128)(2,1)}, bf16[3,256,128]{2,1,0:T(8,128)(2,1)S(1)}, u32[]{:S(2)}, u32[]{:S(2)}) collective-permute-start(bf16[3,256,128]{2,1,0:T(8,128)(2,1)} %get-tuple-element.132), channel_id=1, source_target_pairs={{0,3},{1,2},{2,1},{3,0},{4,7},{5,6},{6,5},{7,4},{8,11},{9,10},{10,... | collective-permute-start | bytes 589832 | tf_op jit(solution)/shard_map/ppermute | solution.py:1057
  12.3 25.0 %collective-permute-start.4 = (bf16[3,256,128]{2,1,0:T(8,128)(2,1)}, bf16[3,256,128]{2,1,0:T(8,128)(2,1)S(1)}, u32[]{:S(2)}, u32[]{:S(2)}) collective-permute-start(bf16[3,256,128]{2,1,0:T(8,128)(2,1)} %get-tuple-element.133), channel_id=1, source_target_pairs={{0,4},{1,5},{2,6},{3,7},{4,0},{5,1},{6,2},{7,3},{8,12},{9,13},{10,... | collective-permute-start | bytes 589832 | tf_op jit(solution)/shard_map/ppermute | solution.py:1057
  16.7 26.7 %collective-permute-start.5 = (bf16[3,256,128]{2,1,0:T(8,128)(2,1)}, bf16[3,256,128]{2,1,0:T(8,128)(2,1)S(1)}, u32[]{:S(2)}, u32[]{:S(2)}) collective-permute-start(bf16[3,256,128]{2,1,0:T(8,128)(2,1)} %get-tuple-element.134), channel_id=1, source_target_pairs={{0,5},{1,4},{2,7},{3,6},{4,1},{5,0},{6,3},{7,2},{8,13},{9,12},{10,... | collective-permute-start | bytes 589832 | tf_op jit(solution)/shard_map/ppermute | solution.py:1057
  26.0 17.4 %collective-permute-start.6 = (bf16[3,256,128]{2,1,0:T(8,128)(2,1)}, bf16[3,256,128]{2,1,0:T(8,128)(2,1)S(1)}, u32[]{:S(2)}, u32[]{:S(2)}) collective-permute-start(bf16[3,256,128]{2,1,0:T(8,128)(2,1)} %get-tuple-element.135), channel_id=1, source_target_pairs={{0,6},{1,7},{2,4},{3,5},{4,2},{5,3},{6,0},{7,1},{8,14},{9,15},{10,... | collective-permute-start | bytes 589832 | tf_op jit(solution)/shard_map/ppermute | solution.py:1057
  27.5 15.9 %collective-permute-start.7 = (bf16[3,256,128]{2,1,0:T(8,128)(2,1)}, bf16[3,256,128]{2,1,0:T(8,128)(2,1)S(1)}, u32[]{:S(2)}, u32[]{:S(2)}) collective-permute-start(bf16[3,256,128]{2,1,0:T(8,128)(2,1)} %get-tuple-element.136), channel_id=1, source_target_pairs={{0,7},{1,6},{2,5},{3,4},{4,3},{5,2},{6,1},{7,0},{8,15},{9,14},{10,... | collective-permute-start | bytes 589832 | tf_op jit(solution)/shard_map/ppermute | solution.py:1057
  103.1 30.5 %collective-permute-start.12 = (bf16[4,256,512]{2,1,0:T(8,128)(2,1)}, bf16[4,256,512]{2,1,0:T(8,128)(2,1)}, u32[]{:S(2)}, u32[]{:S(2)}) collective-permute-start(bf16[4,256,512]{2,1,0:T(8,128)(2,1)} %get-tuple-element.157), channel_id=1, source_target_pairs={{0,1},{1,0},{2,3},{3,2},{4,5},{5,4},{6,7},{7,6},{8,9},{9,8},{10,11... | collective-permute-start | bytes 3145736 | tf_op jit(solution)/shard_map/ppermute | solution.py:1057
  104.7 29.0 %collective-permute-start.13 = (bf16[8,128,512]{2,1,0:T(8,128)(2,1)}, bf16[8,128,512]{2,1,0:T(8,128)(2,1)}, u32[]{:S(2)}, u32[]{:S(2)}) collective-permute-start(bf16[8,128,512]{2,1,0:T(8,128)(2,1)} %get-tuple-element.159), channel_id=1, source_target_pairs={{0,16},{8,24},{16,0},{24,8},{1,17},{9,25},{17,1},{25,9},{2,18},{10... | collective-permute-start | bytes 3145736 | tf_op jit(solution)/shard_map/ppermute | solution.py:1057
  110.8 27.5 %all-to-all-start.1 = ((bf16[8,256,128]{2,1,0:T(8,128)(2,1)}), bf16[8,256,128]{2,1,0:T(8,128)(2,1)}, u32[]{:S(2)}, u32[]{:S(2)}) async-start(bf16[8,256,128]{2,1,0:T(8,128)(2,1)} %get-tuple-element.150), calls=%async_computation.1 | async-start | bytes 1048576 | tf_op jit(solution)/shard_map/all_to_all | solution.py:1157
  129.8 33.8 %collective-permute-start.14 = (bf16[4,128,1280]{2,1,0:T(8,128)(2,1)}, bf16[4,128,1280]{2,1,0:T(8,128)(2,1)S(1)}, u32[]{:S(2)}, u32[]{:S(2)}) collective-permute-start(bf16[4,128,1280]{2,1,0:T(8,128)(2,1)} %get-tuple-element.172), channel_id=1, source_target_pairs={{0,1},{1,0},{2,3},{3,2},{4,5},{5,4},{6,7},{7,6},{8,9},{9,8},{10,11... | collective-permute-start | bytes 3932168 | tf_op jit(solution)/shard_map/ppermute | solution.py:1057
  131.4 33.3 %collective-permute-start.15 = (bf16[8,64,1280]{2,1,0:T(8,128)(2,1)}, bf16[8,64,1280]{2,1,0:T(8,128)(2,1)}, u32[]{:S(2)}, u32[]{:S(2)}) collective-permute-start(bf16[8,64,1280]{2,1,0:T(8,128)(2,1)} %get-tuple-element.174), channel_id=1, source_target_pairs={{0,16},{8,24},{16,0},{24,8},{1,17},{9,25},{17,1},{25,9},{2,18},{10... | collective-permute-start | bytes 3932168 | tf_op jit(solution)/shard_map/ppermute | solution.py:1057
  164.7 51.3 %all-to-all-start.2 = ((bf16[8,3,256,128]{3,2,1,0:T(8,128)(2,1)}), bf16[8,3,256,128]{3,2,1,0:T(8,128)(2,1)S(1)}, u32[]{:S(2)}, u32[]{:S(2)}) async-start(bf16[8,3,256,128]{3,2,1,0:T(8,128)(2,1)} %copy-done.11), calls=%async_computation.2 | async-start | bytes 3145728 | tf_op jit(solution)/shard_map/all_to_all | solution.py:1157
  168.5 14.3 %collective-permute-start.18 = (bf16[4,128,512]{2,1,0:T(8,128)(2,1)}, bf16[4,128,512]{2,1,0:T(8,128)(2,1)S(1)}, u32[]{:S(2)}, u32[]{:S(2)}) collective-permute-start(bf16[4,128,512]{2,1,0:T(8,128)(2,1)} %get-tuple-element.189), channel_id=1, source_target_pairs={{0,16},{8,24},{16,0},{24,8},{1,17},{9,25},{17,1},{25,9},{2,18},{10... | collective-permute-start | bytes 1572872 | tf_op jit(solution)/shard_map/ppermute | solution.py:1057
  170.1 30.0 %collective-permute-start.19 = (bf16[4,128,512]{2,1,0:T(8,128)(2,1)}, bf16[4,128,512]{2,1,0:T(8,128)(2,1)S(1)}, u32[]{:S(2)}, u32[]{:S(2)}) collective-permute-start(bf16[4,128,512]{2,1,0:T(8,128)(2,1)} %get-tuple-element.191), channel_id=1, source_target_pairs={{0,1},{1,0},{2,3},{3,2},{4,5},{5,4},{6,7},{7,6},{8,9},{9,8},{10,11... | collective-permute-start | bytes 1572872 | tf_op jit(solution)/shard_map/ppermute | solution.py:1057
  179.6 31.9 %collective-permute-start.16 = (bf16[4,64,1280]{2,1,0:T(8,128)(2,1)}, bf16[4,64,1280]{2,1,0:T(8,128)(2,1)}, u32[]{:S(2)}, u32[]{:S(2)}) collective-permute-start(bf16[4,64,1280]{2,1,0:T(8,128)(2,1)} %get-tuple-element.183), channel_id=1, source_target_pairs={{0,16},{8,24},{16,0},{24,8},{1,17},{9,25},{17,1},{25,9},{2,18},{10... | collective-permute-start | bytes 1966088 | tf_op jit(solution)/shard_map/ppermute | solution.py:1057
  180.1 32.1 %collective-permute-start.17 = (bf16[4,64,1280]{2,1,0:T(8,128)(2,1)}, bf16[4,64,1280]{2,1,0:T(8,128)(2,1)}, u32[]{:S(2)}, u32[]{:S(2)}) collective-permute-start(bf16[4,64,1280]{2,1,0:T(8,128)(2,1)} %get-tuple-element.185), channel_id=1, source_target_pairs={{0,1},{1,0},{2,3},{3,2},{4,5},{5,4},{6,7},{7,6},{8,9},{9,8},{10,11... | collective-permute-start | bytes 1966088 | tf_op jit(solution)/shard_map/ppermute | solution.py:1057
  202.4 13.6 %collective-permute-start.20 = (bf16[2,128,1024]{2,1,0:T(8,128)(2,1)}, bf16[2,128,1024]{2,1,0:T(8,128)(2,1)}, u32[]{:S(2)}, u32[]{:S(2)}) collective-permute-start(bf16[2,128,1024]{2,1,0:T(8,128)(2,1)} %get-tuple-element.193), channel_id=1, source_target_pairs={{0,2},{1,3},{2,0},{3,1},{4,6},{5,7},{6,4},{7,5},{8,10},{9,11},{10,... | collective-permute-start | bytes 1572872 | tf_op jit(solution)/shard_map/ppermute | solution.py:1057
  223.6 24.9 %collective-permute-start.24 = (bf16[4,128,768]{2,1,0:T(8,128)(2,1)}, bf16[4,128,768]{2,1,0:T(8,128)(2,1)}, u32[]{:S(2)}, u32[]{:S(2)}) collective-permute-start(bf16[4,128,768]{2,1,0:T(8,128)(2,1)} %get-tuple-element.204), channel_id=1, source_target_pairs={{0,1},{1,0},{2,3},{3,2},{4,5},{5,4},{6,7},{7,6},{8,9},{9,8},{10,11... | collective-permute-start | bytes 2359304 | tf_op jit(solution)/shard_map/ppermute | solution.py:1057
  224.9 23.7 %collective-permute-start.25 = (bf16[8,64,768]{2,1,0:T(8,128)(2,1)}, bf16[8,64,768]{2,1,0:T(8,128)(2,1)}, u32[]{:S(2)}, u32[]{:S(2)}) collective-permute-start(bf16[8,64,768]{2,1,0:T(8,128)(2,1)} %get-tuple-element.206), channel_id=1, source_target_pairs={{0,16},{8,24},{16,0},{24,8},{1,17},{9,25},{17,1},{25,9},{2,18},{10... | collective-permute-start | bytes 2359304 | tf_op jit(solution)/shard_map/ppermute | solution.py:1057
  226.4 22.1 %collective-permute-start.27 = (bf16[2,64,2560]{2,1,0:T(8,128)(2,1)}, bf16[2,64,2560]{2,1,0:T(8,128)(2,1)}, u32[]{:S(2)}, u32[]{:S(2)}) collective-permute-start(bf16[2,64,2560]{2,1,0:T(8,128)(2,1)} %get-tuple-element.212), channel_id=1, source_target_pairs={{0,2},{1,3},{2,0},{3,1},{4,6},{5,7},{6,4},{7,5},{8,10},{9,11},{10,... | collective-permute-start | bytes 1966088 | tf_op jit(solution)/shard_map/ppermute | solution.py:1057
  229.1 17.2 %collective-permute-start.26 = (bf16[128,1024]{1,0:T(8,128)(2,1)}, bf16[128,1024]{1,0:T(8,128)(2,1)}, u32[]{:S(2)}, u32[]{:S(2)}) collective-permute-start(bf16[128,1024]{1,0:T(8,128)(2,1)} %get-tuple-element.210), channel_id=1, source_target_pairs={{0,4},{1,5},{2,6},{3,7},{4,0},{5,1},{6,2},{7,3},{8,12},{9,13},{10,... | collective-permute-start | bytes 786440 | tf_op jit(solution)/shard_map/ppermute | solution.py:1057
  250.9 18.2 %collective-permute-start.31 = (bf16[64,2560]{1,0:T(8,128)(2,1)S(1)}, bf16[64,2560]{1,0:T(8,128)(2,1)S(1)}, u32[]{:S(2)}, u32[]{:S(2)}) collective-permute-start(bf16[64,2560]{1,0:T(8,128)(2,1)S(1)} %get-tuple-element.226), channel_id=1, source_target_pairs={{0,4},{1,5},{2,6},{3,7},{4,0},{5,1},{6,2},{7,3},{8,12},{9,13},{10,... | collective-permute-start | bytes 983048 | tf_op jit(solution)/shard_map/ppermute | solution.py:1057
  253.9 15.2 %collective-permute-start.28 = (bf16[4,64,768]{2,1,0:T(8,128)(2,1)S(1)}, bf16[4,64,768]{2,1,0:T(8,128)(2,1)S(1)}, u32[]{:S(2)}, u32[]{:S(2)}) collective-permute-start(bf16[4,64,768]{2,1,0:T(8,128)(2,1)S(1)} %get-tuple-element.218), channel_id=1, source_target_pairs={{0,16},{8,24},{16,0},{24,8},{1,17},{9,25},{17,1},{25,9},{2,18},{10... | collective-permute-start | bytes 1179656 | tf_op jit(solution)/shard_map/ppermute | solution.py:1057
  254.5 14.6 %collective-permute-start.29 = (bf16[4,64,768]{2,1,0:T(8,128)(2,1)S(1)}, bf16[4,64,768]{2,1,0:T(8,128)(2,1)S(1)}, u32[]{:S(2)}, u32[]{:S(2)}) collective-permute-start(bf16[4,64,768]{2,1,0:T(8,128)(2,1)S(1)} %get-tuple-element.220), channel_id=1, source_target_pairs={{0,1},{1,0},{2,3},{3,2},{4,5},{5,4},{6,7},{7,6},{8,9},{9,8},{10,11... | collective-permute-start | bytes 1179656 | tf_op jit(solution)/shard_map/ppermute | solution.py:1057
  257.1 12.0 %collective-permute-start.30 = (bf16[128,1024]{1,0:T(8,128)(2,1)S(1)}, bf16[128,1024]{1,0:T(8,128)(2,1)S(1)}, u32[]{:S(2)}, u32[]{:S(2)}) collective-permute-start(bf16[128,1024]{1,0:T(8,128)(2,1)S(1)} %last.3.refs_0_), channel_id=1, source_target_pairs={{0,16},{8,24},{16,0},{24,8},{1,17},{9,25},{17,1},{25,9},{2,18},{10... | collective-permute-start | bytes 786440 | tf_op jit(solution)/shard_map/ppermute | solution.py:1057
  269.9 8.7 %collective-permute-start.34 = (bf16[2,64,1536]{2,1,0:T(8,128)(2,1)S(1)}, bf16[2,64,1536]{2,1,0:T(8,128)(2,1)S(1)}, u32[]{:S(2)}, u32[]{:S(2)}) collective-permute-start(bf16[2,64,1536]{2,1,0:T(8,128)(2,1)S(1)} %get-tuple-element.235), channel_id=1, source_target_pairs={{0,2},{1,3},{2,0},{3,1},{4,6},{5,7},{6,4},{7,5},{8,10},{9,11},{10,... | collective-permute-start | bytes 1179656 | tf_op jit(solution)/shard_map/ppermute | solution.py:1057
  272.0 22.1 %collective-permute-start.21 = (bf16[256,1024]{1,0:T(8,128)(2,1)}, bf16[256,1024]{1,0:T(8,128)(2,1)}, u32[]{:S(2)}, u32[]{:S(2)}) collective-permute-start(bf16[256,1024]{1,0:T(8,128)(2,1)} %get-tuple-element.195), channel_id=1, source_target_pairs={{0,8},{8,0},{16,24},{24,16},{1,9},{9,1},{17,25},{25,17},{2,10},{10... | collective-permute-start | bytes 1572872 | tf_op jit(solution)/shard_map/ppermute | solution.py:1057
  280.5 10.4 %collective-permute-start.35 = (bf16[64,1536]{1,0:T(8,128)(2,1)}, bf16[64,1536]{1,0:T(8,128)(2,1)S(1)}, u32[]{:S(2)}, u32[]{:S(2)}) collective-permute-start(bf16[64,1536]{1,0:T(8,128)(2,1)} %get-tuple-element.239), channel_id=1, source_target_pairs={{0,4},{1,5},{2,6},{3,7},{4,0},{5,1},{6,2},{7,3},{8,12},{9,13},{10,... | collective-permute-start | bytes 589832 | tf_op jit(solution)/shard_map/ppermute | solution.py:1057
  283.6 12.7 %collective-permute-start.41 = (bf16[128,1024]{1,0:T(8,128)(2,1)S(1)}, bf16[128,1024]{1,0:T(8,128)(2,1)}, u32[]{:S(2)}, u32[]{:S(2)}) collective-permute-start(bf16[128,1024]{1,0:T(8,128)(2,1)S(1)} %last.3.refs_0_), channel_id=1, source_target_pairs={{0,8},{8,0},{16,24},{24,16},{1,9},{9,1},{17,25},{25,17},{2,10},{10... | collective-permute-start | bytes 786440 | tf_op jit(solution)/shard_map/ppermute | solution.py:1057
  283.6 12.7 %collective-permute-start.42 = (bf16[128,1024]{1,0:T(8,128)(2,1)S(1)}, bf16[128,1024]{1,0:T(8,128)(2,1)}, u32[]{:S(2)}, u32[]{:S(2)}) collective-permute-start(bf16[128,1024]{1,0:T(8,128)(2,1)S(1)} %collective-permute-done.30.refs_1_), channel_id=1, source_target_pairs={{0,8},{8,0},{16,24},{24,16},{1,9},{9,1},{17,25},{25,17},{2,10},{10... | collective-permute-start | bytes 786440 | tf_op jit(solution)/shard_map/ppermute | solution.py:1057
  287.6 11.7 %all-to-all-start.3 = ((f32[8,8,128]{2,1,0:T(8,128)}), f32[8,8,128]{2,1,0:T(8,128)S(1)}, u32[]{:S(2)}, u32[]{:S(2)}) async-start(f32[8,8,128]{2,1,0:T(8,128)} %add.210), calls=%async_computation.3 | async-start | bytes 65536 | tf_op jit(solution)/shard_map/all_to_all | solution.py:1157
  (77 other events, 554.7 us)

commit v7 on v6

--- a/solution.py
+++ b/solution.py
@@ -1217,6 +1217,7 @@
     expand_grad, merge_grad = _small_call(
         partial(finish_expand_kernel, part), "finish_expand", [(group, hidden), (group, width)], jnp.float32, here, *expand_grad
     )
+    output, *attend_parts = lax.optimization_barrier((output, *attend_parts))
     attend_grad = of_all(over_all(*attend_parts))
     attend_grad = _small_call(finish_attend_kernel, "finish_attend", [(group, 3 * width)], jnp.float32, here, *attend_grad)[0]
     table_grad = small[:, 4, : 2 * buckets].reshape(peers, buckets, 2).transpose(1, 0, 2).reshape(buckets, heads)

time: 307 us -> 306 us (level)
  waiting for transfers between devices: 70 us -> 82.6 us
  local copies, waits for them, and re-layouts: 44.9 us -> 34.2 us
    unnamed x126 -> x116, local copies, waits for them, and re-layouts: 43.2 us -> 32.6 us
    ppermute x44, waiting for transfers between devices: 70 us -> 78.8 us  [flipped(): return lax.ppermute(array, axis, [(i, i ^ mask) for i in range(peers)])]
    all_to_all x3, waiting for transfers between devices: 0.01 us -> 3.75 us  [to_all(): return lax.all_to_all(array, 'blk', split_axis=0, concat_axis=0, tiled=True)]
  transfers between devices with their start and end apart: 47 -> 47, of which waited for: 17 -> 19; matrix products, arithmetic and copies ran while one was open for 2% -> 1% of each run, Pallas kernels for 24% -> 24%
where the time goes in v7:
time: 306 us; the launch traced here: 305 us
  Pallas kernels  103 us (34%)
  waiting for transfers between devices  82.6 us (27%)
  starting transfers between devices  55.1 us (18%)
  local copies, waits for them, and re-layouts  34.2 us (11%)
  blocking collectives  25.8 us (8%)
    ppermute x44, waiting for transfers between devices, flipped(): return lax.ppermute(array, axis, [(i, i ^ mask) for i in range(peers)])  78.8 us
    ppermute x44, starting transfers between devices, flipped(): return lax.ppermute(array, axis, [(i, i ^ mask) for i in range(peers)])  42.5 us
    unnamed x116, local copies, waits for them, and re-layouts  32.6 us
    all_to_all x1, blocking collectives, to_all(): return lax.all_to_all(array, 'blk', split_axis=0, concat_axis=0, tiled=True)  25.8 us
    pallas_call x15, Pallas kernels, _small_call(): pl.pallas_call(kernel, out_shape=[jax.ShapeDtypeStruct(shape, kind) for s...  24 us
    pallas_call x1, Pallas kernels, attend_back(): pl.pallas_call(partial(attend_back_kernel, peers, items, rows), out_shape...  21.4 us
    all_to_all x3, starting transfers between devices, to_all(): return lax.all_to_all(array, 'blk', split_axis=0, concat_axis=0, tiled=True)  12.6 us
    pallas_call x1, Pallas kernels, attend(): pl.pallas_call(partial(attend_kernel, peers, items, rows), out_shape=shap...  11.8 us
  transfers between devices with their start and end apart: 47, of which 19 were waited for; matrix products, arithmetic and copies ran while one was open for 1% of the time, Pallas kernels for 24%

profile of v7, /device:TPU:0, one launch (start us, length us, event | category | flops | bytes accessed | tf_op | source)
XLA Modules:
  0.0 305.2 jit_solution(8797892740459130167)
XLA Ops:
  1.8 6.4 %project.1 = (bf16[3,256,128]{2,1,0:T(8,128)(2,1)}, bf16[3,256,128]{2,1,0:T(8,128)(2,1)}, bf16[3,256,128]{2,1,0:T(8,128)(2,1)}, bf16[3,256,128]{2,1,0:T(8,128)(2...) custom-call(s32[4]{0:T(128)} %pad_add_fusion.1.meta_ref, ...), custom_call_target="tpu_custom_call" | custom-call | flops 4000000000 | bytes 8388608 | tf_op jit(solution)/shard_map/project/pallas_call | solution.py:611
  12.3 3.0 collective-permute-start.4
  16.7 3.6 %collective-permute-start.5 = (bf16[3,256,128]{2,1,0:T(8,128)(2,1)}, bf16[3,256,128]{2,1,0:T(8,128)(2,1)S(1)}, u32[]{:S(2)}, u32[]{:S(2)}) collective-permute-start(bf16[3,256,128]{2,1,0:T(8,128)(2,1)} %get-tuple-element.137), channel_id=1, source_target_pairs={{0,5},{1,4},{2,7},{3,6},{4,1},{5,0},{6,3},{7,2},{8,13},{9,12},{10,... | collective-permute-start | bytes 589832 | tf_op jit(solution)/shard_map/ppermute | solution.py:1057
  20.3 5.7 %collective-permute-done.2.refs_2_ = bf16[3,256,128]{2,1,0:T(8,128)(2,1)S(1)} collective-permute-done((bf16[3,256,128]{2,1,0:T(8,128)(2,1)}, bf16[3,256,128]{2,1,0:T(8,128)(2,1)S(1)}, u32[]{:S(2)}, u32[]{:S(2)}) %collective-permute-start.2) | collective-permute-done | bytes 196640 | tf_op jit(solution)/shard_map/ppermute | solution.py:1057
  29.2 3.4 %copy-done.2 = bf16[4096,1024]{1,0:T(8,128)(2,1)S(1)} copy-done((bf16[4096,1024]{1,0:T(8,128)(2,1)S(1)}, bf16[4096,1024]{1,0:T(8,128)(2,1)}, u32[]{:S(2)}) %copy-start.2) | copy-done | bytes 8388632
  32.6 4.7 %pull.1.pulled_ref = f32[512,2048]{1,0:T(8,128)S(1)} custom-call(s32[4]{0:T(128)S(1)} %copy-done.44, bf16[256,1024]{1,0:T(8,128)(2,1)S(1)} %bitcast.49, bf16[256,1024]{1,0:T(8,128)(2,1)S(1)} %collective-permute-done.other.grad_other, bf16[4096,1024]{1,0:T(8,128)(2,1)S(1)} %copy-done.2), custom_call_target="tpu_custom_call" | custom-call | flops 3000000000 | bytes 9437184 | tf_op jit(solution)/shard_map/pull/pallas_call | solution.py:673
  37.3 6.0 %collective-permute-done.5.refs_5_ = bf16[3,256,128]{2,1,0:T(8,128)(2,1)S(1)} collective-permute-done((bf16[3,256,128]{2,1,0:T(8,128)(2,1)}, bf16[3,256,128]{2,1,0:T(8,128)(2,1)S(1)}, u32[]{:S(2)}, u32[]{:S(2)}) %collective-permute-start.5) | collective-permute-done | bytes 196640 | tf_op jit(solution)/shard_map/ppermute | solution.py:1057
  43.4 11.8 %attend.1 = (bf16[8,256,128]{2,1,0:T(8,128)(2,1)S(1)}, f32[8,128,256]{2,1,0:T(8,128)S(1)}, f32[8,8,256]{2,1,0:T(8,128)S(1)}, bf16[8,3,256,128]{3,2,1,0:T(8,128)(2,1)S(1)}) custom-call(s32[18]{0:T(128)S(1)} %pad_add_fusion.meta_ref, f32[2]{0:T(128)S(1)} %slice_reduce_fusion.1.far_ref, f32[2,512]{1,0:T(2,128)S(1)} %fusion.1.line_ref, ...), custom_call_target="tpu_custom_call" | custom-call | flops 8000000000 | bytes 4194304 | tf_op jit(solution)/shard_map/attend/pallas_call | solution.py:423
  56.2 25.8 %all_to_all.20.parts_ref = bf16[8,256,128]{2,1,0:T(8,128)(2,1)S(1)} all-to-all(bf16[8,256,128]{2,1,0:T(8,128)(2,1)S(1)} %get-tuple-element.140), channel_id=1, replica_groups=mesh['seq'=4,'blk'=8] {'blk'}, dimensions={0} | all-to-all | bytes 1048576 | tf_op jit(solution)/shard_map/all_to_all | solution.py:1157
  85.0 10.8 %feed.1 = (f32[256,1024]{1,0:T(8,128)S(1)}, f32[256,1024]{1,0:T(8,128)S(1)}, bf16[512,2048]{1,0:T(8,128)(2,1)S(1)}, bf16[512,2048]{1,0:T(8,128)(2,1)S(1)}) custom-call(s32[4]{0:T(128)S(1)} %copy-done.44, bf16[256,1024]{1,0:T(8,128)(2,1)S(1)} %get-tuple-element.144.act_mine, bf16[256,1024]{1,0:T(8,128)(2,1)S(1)} %collective-permute-done.8.act_other, ...), custom_call_target="tpu_custom_call" | custom-call | flops 8000000000 | bytes 20971520 | tf_op jit(solution)/shard_map/feed/pallas_call | solution.py:736
  97.3 4.5 %contract_weigh.1 = (bf16[4,256,512]{2,1,0:T(8,128)(2,1)S(1)}, bf16[4,256,512]{2,1,0:T(8,128)(2,1)}, bf16[8,128,512]{2,1,0:T(8,128)(2,1)S(1)}, bf16[8,128,512]{2,1,0:T(8,128)(2,1)}) custom-call(s32[4]{0:T(128)S(1)} %copy-done.44, bf16[256,1024]{1,0:T(8,128)(2,1)S(1)} %bitcast.50, bf16[256,1024]{1,0:T(8,128)(2,1)S(1)} %collective-permute-done.other.grad_other, ...), custom_call_target="tpu_custom_call" | custom-call | flops 100000000 | bytes 1048576 | tf_op jit(solution)/shard_map/contract_weigh/pallas_call | solution.py:779
  104.9 3.0 turn.1
  108.9 4.4 %all-to-all-start.1 = ((bf16[8,256,128]{2,1,0:T(8,128)(2,1)}), bf16[8,256,128]{2,1,0:T(8,128)(2,1)}, u32[]{:S(2)}, u32[]{:S(2)}) async-start(bf16[8,256,128]{2,1,0:T(8,128)(2,1)} %get-tuple-element.153), calls=%async_computation.1 | async-start | bytes 1048576 | tf_op jit(solution)/shard_map/all_to_all | solution.py:1157
  119.3 5.1 %weigh.1 = (bf16[4,128,1280]{2,1,0:T(8,128)(2,1)S(1)}, bf16[4,128,1280]{2,1,0:T(8,128)(2,1)}, bf16[8,64,1280]{2,1,0:T(8,128)(2,1)S(1)}, bf16[8,64,1280]{2,1,0:T(8,128)(2,1)}) custom-call(s32[4]{0:T(128)S(1)} %copy-done.44, bf16[256,1024]{1,0:T(8,128)(2,1)S(1)} %copy-done.33, bf16[256,1024]{1,0:T(8,128)(2,1)S(1)} %copy-done.39, ...), custom_call_target="tpu_custom_call" | custom-call | flops 100000000 | bytes 1048576 | tf_op jit(solution)/shard_map/weigh/pallas_call | solution.py:813
  128.7 3.7 %collective-permute-done.12.one_got = bf16[4,256,512]{2,1,0:T(8,128)(2,1)} collective-permute-done((bf16[4,256,512]{2,1,0:T(8,128)(2,1)}, bf16[4,256,512]{2,1,0:T(8,128)(2,1)}, u32[]{:S(2)}, u32[]{:S(2)}) %collective-permute-start.12) | collective-permute-done | bytes 1048608 | tf_op jit(solution)/shard_map/ppermute | solution.py:1057
  132.4 2.9 second.3
  138.2 21.4 %attend_back.1 = (bf16[8,3,256,128]{3,2,1,0:T(8,128)(2,1)S(1)}, f32[2,8,512]{2,1,0:T(8,128)S(1)}) custom-call(s32[18]{0:T(128)S(1)} %pad_add_fusion.meta_ref, f32[2]{0:T(128)S(1)} %slice_reduce_fusion.1.far_ref, f32[2,512]{1,0:T(2,128)S(1)} %fusion.1.line_ref, f32[8,128,256]{2,1,0:T(8,128)S(1)} %copy-done.56, f32[8,8,256]{2,1,0:T(8,128)S(1)} %get-tuple-element.143.log_ref, ...), custom_call_target="tpu_custom_call" | custom-call | flops 20000000000 | bytes 8388608 | tf_op jit(solution)/shard_map/attend_back/pallas_call | solution.py:522
  161.3 3.8 %all-to-all-start.2 = ((bf16[8,3,256,128]{3,2,1,0:T(8,128)(2,1)}), bf16[8,3,256,128]{3,2,1,0:T(8,128)(2,1)S(1)}, u32[]{:S(2)}, u32[]{:S(2)}) async-start(bf16[8,3,256,128]{3,2,1,0:T(8,128)(2,1)} %copy-done.11), calls=%async_computation.2 | async-start | bytes 3145728 | tf_op jit(solution)/shard_map/all_to_all | solution.py:1157
  171.2 3.4 %second.4 = (bf16[4,64,1280]{2,1,0:T(8,128)(2,1)S(1)}, bf16[4,64,1280]{2,1,0:T(8,128)(2,1)}, bf16[4,64,1280]{2,1,0:T(8,128)(2,1)S(1)}, bf16[4,64,1280]{2,1,0:T(8,128)(2,1)}) custom-call(s32[4]{0:T(128)S(1)} %copy-done.44, bf16[4,128,1280]{2,1,0:T(8,128)(2,1)S(1)} %copy-done.13, bf16[4,128,1280]{2,1,0:T(8,128)(2,1)} %collective-permute-done.14.one_got, ...), custom_call_target="tpu_custom_call" | custom-call | flops 5242880 | bytes 15728640 | tf_op jit(solution)/shard_map/second/pallas_call | solution.py:959
  176.2 4.1 %collective-permute-done.18.one_got = bf16[4,128,512]{2,1,0:T(8,128)(2,1)S(1)} collective-permute-done((bf16[4,128,512]{2,1,0:T(8,128)(2,1)}, bf16[4,128,512]{2,1,0:T(8,128)(2,1)S(1)}, u32[]{:S(2)}, u32[]{:S(2)}) %collective-permute-start.18) | collective-permute-done | bytes 524320 | tf_op jit(solution)/shard_map/ppermute | solution.py:1057
  180.3 16.6 %collective-permute-done.19.two_got = bf16[4,128,512]{2,1,0:T(8,128)(2,1)S(1)} collective-permute-done((bf16[4,128,512]{2,1,0:T(8,128)(2,1)}, bf16[4,128,512]{2,1,0:T(8,128)(2,1)S(1)}, u32[]{:S(2)}, u32[]{:S(2)}) %collective-permute-start.19) | collective-permute-done | bytes 524320 | tf_op jit(solution)/shard_map/ppermute | solution.py:1057
  199.3 3.4 %copy-done.3 = bf16[4096,1024]{1,0:T(8,128)(2,1)S(1)} copy-done((bf16[4096,1024]{1,0:T(8,128)(2,1)S(1)}, bf16[4096,1024]{1,0:T(8,128)(2,1)}, u32[]{:S(2)}) %copy-start.3) | copy-done | bytes 8388632
  204.3 3.3 %emit.1 = (f32[256,1024]{1,0:T(8,128)S(1)}, bf16[256,1024]{1,0:T(8,128)(2,1)S(1)}) custom-call(s32[4]{0:T(128)S(1)} %copy-done.44, bf16[512,2048]{1,0:T(8,128)(2,1)S(1)} %copy-done.5, bf16[4096,1024]{1,0:T(8,128)(2,1)S(1)} %copy-done.3), custom_call_target="tpu_custom_call" | custom-call | flops 2000000000 | bytes 8388608 | tf_op jit(solution)/shard_map/emit/pallas_call | solution.py:842
  216.4 3.6 %attend_weigh.1 = (bf16[4,128,768]{2,1,0:T(8,128)(2,1)S(1)}, bf16[4,128,768]{2,1,0:T(8,128)(2,1)}, bf16[8,64,768]{2,1,0:T(8,128)(2,1)S(1)}, bf16[8,64,768]{2,1,0:T(8,128)(2,1)}) custom-call(s32[4]{0:T(128)S(1)} %copy-done.44, bf16[256,1024]{1,0:T(8,128)(2,1)S(1)} %copy-done.48, bf16[256,1024]{1,0:T(8,128)(2,1)S(1)} %collective-permute-done.22.act_other, ...), custom_call_target="tpu_custom_call" | custom-call | flops 2000000000 | bytes 7340032 | tf_op jit(solution)/shard_map/attend_weigh/pallas_call | solution.py:1039
  229.1 14.5 %collective-permute-done.26.got = bf16[128,1024]{1,0:T(8,128)(2,1)} collective-permute-done((bf16[128,1024]{1,0:T(8,128)(2,1)}, bf16[128,1024]{1,0:T(8,128)(2,1)}, u32[]{:S(2)}, u32[]{:S(2)}) %collective-permute-start.26) | collective-permute-done | bytes 262176 | tf_op jit(solution)/shard_map/ppermute | solution.py:1057
  255.8 2.8 copy-done.6
  258.6 3.3 %close.1 = (f32[256,1024]{1,0:T(8,128)}, f32[2,1024]{1,0:T(2,128)S(1)}) custom-call(bf16[8,3,256,128]{3,2,1,0:T(8,128)(2,1)S(1)} %all-to-all-done.2.parts_ref.owned_ref, bf16[256,1024]{1,0:T(8,128)(2,1)S(1)} %bitcast.54, f32[256,1024]{1,0:T(8,128)S(1)} %copy-done.17, f32[1,1024]{1,0:T(1,128)S(1)} %bitcast.58, bf16[1024,3072]{1,0:T(8,128)(2,1)S(1)} %copy-done.6), custom_call_target="tpu_custom_call" | custom-call | flops 2000000000 | bytes 10485760 | tf_op jit(solution)/shard_map/close/pallas_call | solution.py:910
  261.9 4.4 %collective-permute-done.30.refs_1_ = bf16[128,1024]{1,0:T(8,128)(2,1)S(1)} collective-permute-done((bf16[128,1024]{1,0:T(8,128)(2,1)S(1)}, bf16[128,1024]{1,0:T(8,128)(2,1)S(1)}, u32[]{:S(2)}, u32[]{:S(2)}) %collective-permute-start.30) | collective-permute-done | bytes 262176 | tf_op jit(solution)/shard_map/ppermute | solution.py:1057
  270.6 5.5 %collective-permute-done.33.refs_1_ = bf16[64,2560]{1,0:T(8,128)(2,1)S(1)} collective-permute-done((bf16[64,2560]{1,0:T(8,128)(2,1)S(1)}, bf16[64,2560]{1,0:T(8,128)(2,1)S(1)}, u32[]{:S(2)}, u32[]{:S(2)}) %collective-permute-start.33) | collective-permute-done | bytes 327712 | tf_op jit(solution)/shard_map/ppermute | solution.py:1057
  280.1 6.1 %collective-permute-done.35.got = bf16[64,1536]{1,0:T(8,128)(2,1)S(1)} collective-permute-done((bf16[64,1536]{1,0:T(8,128)(2,1)S(1)}, bf16[64,1536]{1,0:T(8,128)(2,1)S(1)}, u32[]{:S(2)}, u32[]{:S(2)}) %collective-permute-start.35) | collective-permute-done | bytes 196640 | tf_op jit(solution)/shard_map/ppermute | solution.py:1057
  288.3 4.4 %all-to-all-start.3 = ((f32[8,8,128]{2,1,0:T(8,128)}), f32[8,8,128]{2,1,0:T(8,128)S(1)}, u32[]{:S(2)}, u32[]{:S(2)}) async-start(f32[8,8,128]{2,1,0:T(8,128)} %add.210), calls=%async_computation.3 | async-start | bytes 65536 | tf_op jit(solution)/shard_map/all_to_all | solution.py:1157
  295.6 3.7 %all-to-all-done.3 = f32[8,8,128]{2,1,0:T(8,128)S(1)} async-done(((f32[8,8,128]{2,1,0:T(8,128)}), f32[8,8,128]{2,1,0:T(8,128)S(1)}, u32[]{:S(2)}, u32[]{:S(2)}) %all-to-all-start.3) | async-done | bytes 32800 | tf_op jit(solution)/shard_map/all_to_all | solution.py:1157
  (232 shorter events, 94.5 us)
Async XLA Ops:
  0.7 26.8 %collective-permute-start = (bf16[256,1024]{1,0:T(8,128)(2,1)}, bf16[256,1024]{1,0:T(8,128)(2,1)S(1)}, u32[]{:S(2)}, u32[]{:S(2)}) collective-permute-start(bf16[256,1024]{1,0:T(8,128)(2,1)} %bitcast.48), channel_id=1, source_target_pairs={{0,8},{8,0},{16,24},{24,16},{1,9},{9,1},{17,25},{25,17},{2,10},{10... | collective-permute-start | bytes 1572872 | tf_op jit(solution)/shard_map/ppermute | solution.py:1057
  10.7 15.2 %collective-permute-start.2 = (bf16[3,256,128]{2,1,0:T(8,128)(2,1)}, bf16[3,256,128]{2,1,0:T(8,128)(2,1)S(1)}, u32[]{:S(2)}, u32[]{:S(2)}) collective-permute-start(bf16[3,256,128]{2,1,0:T(8,128)(2,1)} %get-tuple-element.134), channel_id=1, source_target_pairs={{0,2},{1,3},{2,0},{3,1},{4,6},{5,7},{6,4},{7,5},{8,10},{9,11},{10,... | collective-permute-start | bytes 589832 | tf_op jit(solution)/shard_map/ppermute | solution.py:1057
  12.3 25.0 %collective-permute-start.3 = (bf16[3,256,128]{2,1,0:T(8,128)(2,1)}, bf16[3,256,128]{2,1,0:T(8,128)(2,1)S(1)}, u32[]{:S(2)}, u32[]{:S(2)}) collective-permute-start(bf16[3,256,128]{2,1,0:T(8,128)(2,1)} %get-tuple-element.135), channel_id=1, source_target_pairs={{0,3},{1,2},{2,1},{3,0},{4,7},{5,6},{6,5},{7,4},{8,11},{9,10},{10,... | collective-permute-start | bytes 589832 | tf_op jit(solution)/shard_map/ppermute | solution.py:1057
  12.3 25.0 %collective-permute-start.4 = (bf16[3,256,128]{2,1,0:T(8,128)(2,1)}, bf16[3,256,128]{2,1,0:T(8,128)(2,1)S(1)}, u32[]{:S(2)}, u32[]{:S(2)}) collective-permute-start(bf16[3,256,128]{2,1,0:T(8,128)(2,1)} %get-tuple-element.136), channel_id=1, source_target_pairs={{0,4},{1,5},{2,6},{3,7},{4,0},{5,1},{6,2},{7,3},{8,12},{9,13},{10,... | collective-permute-start | bytes 589832 | tf_op jit(solution)/shard_map/ppermute | solution.py:1057
  16.7 26.7 %collective-permute-start.5 = (bf16[3,256,128]{2,1,0:T(8,128)(2,1)}, bf16[3,256,128]{2,1,0:T(8,128)(2,1)S(1)}, u32[]{:S(2)}, u32[]{:S(2)}) collective-permute-start(bf16[3,256,128]{2,1,0:T(8,128)(2,1)} %get-tuple-element.137), channel_id=1, source_target_pairs={{0,5},{1,4},{2,7},{3,6},{4,1},{5,0},{6,3},{7,2},{8,13},{9,12},{10,... | collective-permute-start | bytes 589832 | tf_op jit(solution)/shard_map/ppermute | solution.py:1057
  26.0 17.4 %collective-permute-start.6 = (bf16[3,256,128]{2,1,0:T(8,128)(2,1)}, bf16[3,256,128]{2,1,0:T(8,128)(2,1)S(1)}, u32[]{:S(2)}, u32[]{:S(2)}) collective-permute-start(bf16[3,256,128]{2,1,0:T(8,128)(2,1)} %get-tuple-element.138), channel_id=1, source_target_pairs={{0,6},{1,7},{2,4},{3,5},{4,2},{5,3},{6,0},{7,1},{8,14},{9,15},{10,... | collective-permute-start | bytes 589832 | tf_op jit(solution)/shard_map/ppermute | solution.py:1057
  27.5 15.9 %collective-permute-start.7 = (bf16[3,256,128]{2,1,0:T(8,128)(2,1)}, bf16[3,256,128]{2,1,0:T(8,128)(2,1)S(1)}, u32[]{:S(2)}, u32[]{:S(2)}) collective-permute-start(bf16[3,256,128]{2,1,0:T(8,128)(2,1)} %get-tuple-element.139), channel_id=1, source_target_pairs={{0,7},{1,6},{2,5},{3,4},{4,3},{5,2},{6,1},{7,0},{8,15},{9,14},{10,... | collective-permute-start | bytes 589832 | tf_op jit(solution)/shard_map/ppermute | solution.py:1057
  101.8 30.6 %collective-permute-start.12 = (bf16[4,256,512]{2,1,0:T(8,128)(2,1)}, bf16[4,256,512]{2,1,0:T(8,128)(2,1)}, u32[]{:S(2)}, u32[]{:S(2)}) collective-permute-start(bf16[4,256,512]{2,1,0:T(8,128)(2,1)} %get-tuple-element.160), channel_id=1, source_target_pairs={{0,1},{1,0},{2,3},{3,2},{4,5},{5,4},{6,7},{7,6},{8,9},{9,8},{10,11... | collective-permute-start | bytes 3145736 | tf_op jit(solution)/shard_map/ppermute | solution.py:1057
  103.4 29.0 %collective-permute-start.13 = (bf16[8,128,512]{2,1,0:T(8,128)(2,1)}, bf16[8,128,512]{2,1,0:T(8,128)(2,1)}, u32[]{:S(2)}, u32[]{:S(2)}) collective-permute-start(bf16[8,128,512]{2,1,0:T(8,128)(2,1)} %get-tuple-element.162), channel_id=1, source_target_pairs={{0,16},{8,24},{16,0},{24,8},{1,17},{9,25},{17,1},{25,9},{2,18},{10... | collective-permute-start | bytes 3145736 | tf_op jit(solution)/shard_map/ppermute | solution.py:1057
  108.9 28.0 %all-to-all-start.1 = ((bf16[8,256,128]{2,1,0:T(8,128)(2,1)}), bf16[8,256,128]{2,1,0:T(8,128)(2,1)}, u32[]{:S(2)}, u32[]{:S(2)}) async-start(bf16[8,256,128]{2,1,0:T(8,128)(2,1)} %get-tuple-element.153), calls=%async_computation.1 | async-start | bytes 1048576 | tf_op jit(solution)/shard_map/all_to_all | solution.py:1157
  126.6 34.7 %collective-permute-start.14 = (bf16[4,128,1280]{2,1,0:T(8,128)(2,1)}, bf16[4,128,1280]{2,1,0:T(8,128)(2,1)}, u32[]{:S(2)}, u32[]{:S(2)}) collective-permute-start(bf16[4,128,1280]{2,1,0:T(8,128)(2,1)} %get-tuple-element.175), channel_id=1, source_target_pairs={{0,1},{1,0},{2,3},{3,2},{4,5},{5,4},{6,7},{7,6},{8,9},{9,8},{10,11... | collective-permute-start | bytes 3932168 | tf_op jit(solution)/shard_map/ppermute | solution.py:1057
  128.2 33.1 %collective-permute-start.15 = (bf16[8,64,1280]{2,1,0:T(8,128)(2,1)}, bf16[8,64,1280]{2,1,0:T(8,128)(2,1)}, u32[]{:S(2)}, u32[]{:S(2)}) collective-permute-start(bf16[8,64,1280]{2,1,0:T(8,128)(2,1)} %get-tuple-element.177), channel_id=1, source_target_pairs={{0,16},{8,24},{16,0},{24,8},{1,17},{9,25},{17,1},{25,9},{2,18},{10... | collective-permute-start | bytes 3932168 | tf_op jit(solution)/shard_map/ppermute | solution.py:1057
  161.3 51.9 %all-to-all-start.2 = ((bf16[8,3,256,128]{3,2,1,0:T(8,128)(2,1)}), bf16[8,3,256,128]{3,2,1,0:T(8,128)(2,1)S(1)}, u32[]{:S(2)}, u32[]{:S(2)}) async-start(bf16[8,3,256,128]{3,2,1,0:T(8,128)(2,1)} %copy-done.11), calls=%async_computation.2 | async-start | bytes 3145728 | tf_op jit(solution)/shard_map/all_to_all | solution.py:1157
  165.2 15.1 %collective-permute-start.18 = (bf16[4,128,512]{2,1,0:T(8,128)(2,1)}, bf16[4,128,512]{2,1,0:T(8,128)(2,1)S(1)}, u32[]{:S(2)}, u32[]{:S(2)}) collective-permute-start(bf16[4,128,512]{2,1,0:T(8,128)(2,1)} %get-tuple-element.192), channel_id=1, source_target_pairs={{0,16},{8,24},{16,0},{24,8},{1,17},{9,25},{17,1},{25,9},{2,18},{10... | collective-permute-start | bytes 1572872 | tf_op jit(solution)/shard_map/ppermute | solution.py:1057
  166.8 30.1 %collective-permute-start.19 = (bf16[4,128,512]{2,1,0:T(8,128)(2,1)}, bf16[4,128,512]{2,1,0:T(8,128)(2,1)S(1)}, u32[]{:S(2)}, u32[]{:S(2)}) collective-permute-start(bf16[4,128,512]{2,1,0:T(8,128)(2,1)} %get-tuple-element.194), channel_id=1, source_target_pairs={{0,1},{1,0},{2,3},{3,2},{4,5},{5,4},{6,7},{7,6},{8,9},{9,8},{10,11... | collective-permute-start | bytes 1572872 | tf_op jit(solution)/shard_map/ppermute | solution.py:1057
  175.4 32.2 %collective-permute-start.16 = (bf16[4,64,1280]{2,1,0:T(8,128)(2,1)}, bf16[4,64,1280]{2,1,0:T(8,128)(2,1)}, u32[]{:S(2)}, u32[]{:S(2)}) collective-permute-start(bf16[4,64,1280]{2,1,0:T(8,128)(2,1)} %get-tuple-element.186), channel_id=1, source_target_pairs={{0,16},{8,24},{16,0},{24,8},{1,17},{9,25},{17,1},{25,9},{2,18},{10... | collective-permute-start | bytes 1966088 | tf_op jit(solution)/shard_map/ppermute | solution.py:1057
  175.9 33.6 %collective-permute-start.17 = (bf16[4,64,1280]{2,1,0:T(8,128)(2,1)}, bf16[4,64,1280]{2,1,0:T(8,128)(2,1)}, u32[]{:S(2)}, u32[]{:S(2)}) collective-permute-start(bf16[4,64,1280]{2,1,0:T(8,128)(2,1)} %get-tuple-element.188), channel_id=1, source_target_pairs={{0,1},{1,0},{2,3},{3,2},{4,5},{5,4},{6,7},{7,6},{8,9},{9,8},{10,11... | collective-permute-start | bytes 1966088 | tf_op jit(solution)/shard_map/ppermute | solution.py:1057
  199.3 14.0 %collective-permute-start.20 = (bf16[2,128,1024]{2,1,0:T(8,128)(2,1)}, bf16[2,128,1024]{2,1,0:T(8,128)(2,1)}, u32[]{:S(2)}, u32[]{:S(2)}) collective-permute-start(bf16[2,128,1024]{2,1,0:T(8,128)(2,1)} %get-tuple-element.196), channel_id=1, source_target_pairs={{0,2},{1,3},{2,0},{3,1},{4,6},{5,7},{6,4},{7,5},{8,10},{9,11},{10,... | collective-permute-start | bytes 1572872 | tf_op jit(solution)/shard_map/ppermute | solution.py:1057
  220.9 24.9 %collective-permute-start.24 = (bf16[4,128,768]{2,1,0:T(8,128)(2,1)}, bf16[4,128,768]{2,1,0:T(8,128)(2,1)}, u32[]{:S(2)}, u32[]{:S(2)}) collective-permute-start(bf16[4,128,768]{2,1,0:T(8,128)(2,1)} %get-tuple-element.206), channel_id=1, source_target_pairs={{0,1},{1,0},{2,3},{3,2},{4,5},{5,4},{6,7},{7,6},{8,9},{9,8},{10,11... | collective-permute-start | bytes 2359304 | tf_op jit(solution)/shard_map/ppermute | solution.py:1057
  222.1 23.7 %collective-permute-start.25 = (bf16[8,64,768]{2,1,0:T(8,128)(2,1)}, bf16[8,64,768]{2,1,0:T(8,128)(2,1)}, u32[]{:S(2)}, u32[]{:S(2)}) collective-permute-start(bf16[8,64,768]{2,1,0:T(8,128)(2,1)} %get-tuple-element.208), channel_id=1, source_target_pairs={{0,16},{8,24},{16,0},{24,8},{1,17},{9,25},{17,1},{25,9},{2,18},{10... | collective-permute-start | bytes 2359304 | tf_op jit(solution)/shard_map/ppermute | solution.py:1057
  223.6 22.1 %collective-permute-start.27 = (bf16[2,64,2560]{2,1,0:T(8,128)(2,1)}, bf16[2,64,2560]{2,1,0:T(8,128)(2,1)}, u32[]{:S(2)}, u32[]{:S(2)}) collective-permute-start(bf16[2,64,2560]{2,1,0:T(8,128)(2,1)} %get-tuple-element.214), channel_id=1, source_target_pairs={{0,2},{1,3},{2,0},{3,1},{4,6},{5,7},{6,4},{7,5},{8,10},{9,11},{10,... | collective-permute-start | bytes 1966088 | tf_op jit(solution)/shard_map/ppermute | solution.py:1057
  226.4 17.2 %collective-permute-start.26 = (bf16[128,1024]{1,0:T(8,128)(2,1)}, bf16[128,1024]{1,0:T(8,128)(2,1)}, u32[]{:S(2)}, u32[]{:S(2)}) collective-permute-start(bf16[128,1024]{1,0:T(8,128)(2,1)} %get-tuple-element.212), channel_id=1, source_target_pairs={{0,4},{1,5},{2,6},{3,7},{4,0},{5,1},{6,2},{7,3},{8,12},{9,13},{10,... | collective-permute-start | bytes 786440 | tf_op jit(solution)/shard_map/ppermute | solution.py:1057
  248.2 18.1 %collective-permute-start.31 = (bf16[64,2560]{1,0:T(8,128)(2,1)S(1)}, bf16[64,2560]{1,0:T(8,128)(2,1)S(1)}, u32[]{:S(2)}, u32[]{:S(2)}) collective-permute-start(bf16[64,2560]{1,0:T(8,128)(2,1)S(1)} %get-tuple-element.228), channel_id=1, source_target_pairs={{0,4},{1,5},{2,6},{3,7},{4,0},{5,1},{6,2},{7,3},{8,12},{9,13},{10,... | collective-permute-start | bytes 983048 | tf_op jit(solution)/shard_map/ppermute | solution.py:1057
  251.2 15.1 %collective-permute-start.28 = (bf16[4,64,768]{2,1,0:T(8,128)(2,1)S(1)}, bf16[4,64,768]{2,1,0:T(8,128)(2,1)S(1)}, u32[]{:S(2)}, u32[]{:S(2)}) collective-permute-start(bf16[4,64,768]{2,1,0:T(8,128)(2,1)S(1)} %get-tuple-element.220), channel_id=1, source_target_pairs={{0,16},{8,24},{16,0},{24,8},{1,17},{9,25},{17,1},{25,9},{2,18},{10... | collective-permute-start | bytes 1179656 | tf_op jit(solution)/shard_map/ppermute | solution.py:1057
  251.8 14.6 %collective-permute-start.29 = (bf16[4,64,768]{2,1,0:T(8,128)(2,1)S(1)}, bf16[4,64,768]{2,1,0:T(8,128)(2,1)S(1)}, u32[]{:S(2)}, u32[]{:S(2)}) collective-permute-start(bf16[4,64,768]{2,1,0:T(8,128)(2,1)S(1)} %get-tuple-element.222), channel_id=1, source_target_pairs={{0,1},{1,0},{2,3},{3,2},{4,5},{5,4},{6,7},{7,6},{8,9},{9,8},{10,11... | collective-permute-start | bytes 1179656 | tf_op jit(solution)/shard_map/ppermute | solution.py:1057
  253.2 25.8 %collective-permute-start.21 = (bf16[256,1024]{1,0:T(8,128)(2,1)S(1)}, bf16[256,1024]{1,0:T(8,128)(2,1)S(1)}, u32[]{:S(2)}, u32[]{:S(2)}) collective-permute-start(bf16[256,1024]{1,0:T(8,128)(2,1)S(1)} %copy-done.50), channel_id=1, source_target_pairs={{0,8},{8,0},{16,24},{24,16},{1,9},{9,1},{17,25},{25,17},{2,10},{10... | collective-permute-start | bytes 1572872 | tf_op jit(solution)/shard_map/ppermute | solution.py:1057
  254.2 12.1 %collective-permute-start.30 = (bf16[128,1024]{1,0:T(8,128)(2,1)S(1)}, bf16[128,1024]{1,0:T(8,128)(2,1)S(1)}, u32[]{:S(2)}, u32[]{:S(2)}) collective-permute-start(bf16[128,1024]{1,0:T(8,128)(2,1)S(1)} %last.3.refs_0_), channel_id=1, source_target_pairs={{0,16},{8,24},{16,0},{24,8},{1,17},{9,25},{17,1},{25,9},{2,18},{10... | collective-permute-start | bytes 786440 | tf_op jit(solution)/shard_map/ppermute | solution.py:1057
  269.2 23.5 %collective-permute-start.41 = (bf16[128,1024]{1,0:T(8,128)(2,1)S(1)}, bf16[128,1024]{1,0:T(8,128)(2,1)S(1)}, u32[]{:S(2)}, u32[]{:S(2)}) collective-permute-start(bf16[128,1024]{1,0:T(8,128)(2,1)S(1)} %last.3.refs_0_), channel_id=1, source_target_pairs={{0,8},{8,0},{16,24},{24,16},{1,9},{9,1},{17,25},{25,17},{2,10},{10... | collective-permute-start | bytes 786440 | tf_op jit(solution)/shard_map/ppermute | solution.py:1057
  270.4 22.3 %collective-permute-start.42 = (bf16[128,1024]{1,0:T(8,128)(2,1)S(1)}, bf16[128,1024]{1,0:T(8,128)(2,1)}, u32[]{:S(2)}, u32[]{:S(2)}) collective-permute-start(bf16[128,1024]{1,0:T(8,128)(2,1)S(1)} %collective-permute-done.30.refs_1_), channel_id=1, source_target_pairs={{0,8},{8,0},{16,24},{24,16},{1,9},{9,1},{17,25},{25,17},{2,10},{10... | collective-permute-start | bytes 786440 | tf_op jit(solution)/shard_map/ppermute | solution.py:1057
  276.1 11.5 %collective-permute-start.43 = (f32[8,8,128]{2,1,0:T(8,128)S(1)}, f32[8,8,128]{2,1,0:T(8,128)S(1)}, u32[]{:S(2)}, u32[]{:S(2)}) collective-permute-start(f32[8,8,128]{2,1,0:T(8,128)S(1)} %add.209), channel_id=1, source_target_pairs={{0,16},{8,24},{16,0},{24,8},{1,17},{9,25},{17,1},{25,9},{2,18},{10... | collective-permute-start | bytes 98312 | tf_op jit(solution)/shard_map/ppermute | solution.py:1057
  286.2 13.9 %collective-permute-start.36 = (bf16[64,1536]{1,0:T(8,128)(2,1)S(1)}, bf16[64,1536]{1,0:T(8,128)(2,1)S(1)}, u32[]{:S(2)}, u32[]{:S(2)}) collective-permute-start(bf16[64,1536]{1,0:T(8,128)(2,1)S(1)} %last.5.refs_0_), channel_id=1, source_target_pairs={{0,16},{8,24},{16,0},{24,8},{1,17},{9,25},{17,1},{25,9},{2,18},{10... | collective-permute-start | bytes 589832 | tf_op jit(solution)/shard_map/ppermute | solution.py:1057
  288.3 11.1 %all-to-all-start.3 = ((f32[8,8,128]{2,1,0:T(8,128)}), f32[8,8,128]{2,1,0:T(8,128)S(1)}, u32[]{:S(2)}, u32[]{:S(2)}) async-start(f32[8,8,128]{2,1,0:T(8,128)} %add.210), calls=%async_computation.3 | async-start | bytes 65536 | tf_op jit(solution)/shard_map/all_to_all | solution.py:1157
  (72 other events, 593.0 us)

commit v8 on v7

--- a/solution.py
+++ b/solution.py
@@ -1177,7 +1177,9 @@
     _, *expand_parts = over_first(*expand_parts)
 
     contract_parts = over_second(here, *contract_parts)
-    grad_heads, expand_keep, *contract_parts = lax.optimization_barrier((to_all(grad_heads), expand_keep, *contract_parts))
+    grad_heads, expand_keep, first_other, *contract_parts = lax.optimization_barrier(
+        (to_all(grad_heads), expand_keep, first_other, *contract_parts)
+    )
     back_all, line_grad = attend_back(meta, far, lines, wide, logs, qkv, grad_heads, items)
     back_all, *sums = lax.optimization_barrier((back_all, *contract_parts, expand_keep, *expand_parts))
     owned = to_all(back_all)

time: 306 us -> 308 us (level)
    unnamed x116 -> x118, local copies, waits for them, and re-layouts: 32.6 us -> 34.5 us
  transfers between devices with their start and end apart: 47 -> 47, of which waited for: 19 -> 18; matrix products, arithmetic and copies ran while one was open for 1% -> 1% of each run, Pallas kernels for 24% -> 24%
where the time goes in v8:
time: 308 us; the launch traced here: 307 us
  Pallas kernels  103 us (33%)
  waiting for transfers between devices  81.3 us (26%)
  starting transfers between devices  55.8 us (18%)
  local copies, waits for them, and re-layouts  36.1 us (12%)
  blocking collectives  25.9 us (8%)
    ppermute x44, waiting for transfers between devices, flipped(): return lax.ppermute(array, axis, [(i, i ^ mask) for i in range(peers)])  77.6 us
    ppermute x44, starting transfers between devices, flipped(): return lax.ppermute(array, axis, [(i, i ^ mask) for i in range(peers)])  43 us
    unnamed x118, local copies, waits for them, and re-layouts  34.5 us
    all_to_all x1, blocking collectives, to_all(): return lax.all_to_all(array, 'blk', split_axis=0, concat_axis=0, tiled=True)  25.9 us
    pallas_call x15, Pallas kernels, _small_call(): pl.pallas_call(kernel, out_shape=[jax.ShapeDtypeStruct(shape, kind) for s...  23.9 us
    pallas_call x1, Pallas kernels, attend_back(): pl.pallas_call(partial(attend_back_kernel, peers, items, rows), out_shape...  21.5 us
    all_to_all x3, starting transfers between devices, to_all(): return lax.all_to_all(array, 'blk', split_axis=0, concat_axis=0, tiled=True)  12.7 us
    pallas_call x1, Pallas kernels, attend(): pl.pallas_call(partial(attend_kernel, peers, items, rows), out_shape=shap...  11.9 us
  transfers between devices with their start and end apart: 47, of which 18 were waited for; matrix products, arithmetic and copies ran while one was open for 1% of the time, Pallas kernels for 24%

profile of v8, /device:TPU:0, one launch (start us, length us, event | category | flops | bytes accessed | tf_op | source)
XLA Modules:
  0.0 307.1 jit_solution(2593339740662655058)
XLA Ops:
  1.8 6.4 %project.1 = (bf16[3,256,128]{2,1,0:T(8,128)(2,1)}, bf16[3,256,128]{2,1,0:T(8,128)(2,1)}, bf16[3,256,128]{2,1,0:T(8,128)(2,1)}, bf16[3,256,128]{2,1,0:T(8,128)(2...) custom-call(s32[4]{0:T(128)} %pad_add_fusion.1.meta_ref, ...), custom_call_target="tpu_custom_call" | custom-call | flops 4000000000 | bytes 8388608 | tf_op jit(solution)/shard_map/project/pallas_call | solution.py:611
  12.3 3.0 collective-permute-start.4
  16.7 3.6 %collective-permute-start.5 = (bf16[3,256,128]{2,1,0:T(8,128)(2,1)}, bf16[3,256,128]{2,1,0:T(8,128)(2,1)S(1)}, u32[]{:S(2)}, u32[]{:S(2)}) collective-permute-start(bf16[3,256,128]{2,1,0:T(8,128)(2,1)} %get-tuple-element.138), channel_id=1, source_target_pairs={{0,5},{1,4},{2,7},{3,6},{4,1},{5,0},{6,3},{7,2},{8,13},{9,12},{10,... | collective-permute-start | bytes 589832 | tf_op jit(solution)/shard_map/ppermute | solution.py:1057
  20.2 5.7 %collective-permute-done.2.refs_2_ = bf16[3,256,128]{2,1,0:T(8,128)(2,1)S(1)} collective-permute-done((bf16[3,256,128]{2,1,0:T(8,128)(2,1)}, bf16[3,256,128]{2,1,0:T(8,128)(2,1)S(1)}, u32[]{:S(2)}, u32[]{:S(2)}) %collective-permute-start.2) | collective-permute-done | bytes 196640 | tf_op jit(solution)/shard_map/ppermute | solution.py:1057
  29.2 3.4 %copy-done.2 = bf16[4096,1024]{1,0:T(8,128)(2,1)S(1)} copy-done((bf16[4096,1024]{1,0:T(8,128)(2,1)S(1)}, bf16[4096,1024]{1,0:T(8,128)(2,1)}, u32[]{:S(2)}) %copy-start.2) | copy-done | bytes 8388632
  32.6 4.7 %pull.1.pulled_ref = f32[512,2048]{1,0:T(8,128)S(1)} custom-call(s32[4]{0:T(128)S(1)} %copy-done.44, bf16[256,1024]{1,0:T(8,128)(2,1)S(1)} %bitcast.49, bf16[256,1024]{1,0:T(8,128)(2,1)S(1)} %collective-permute-done.other.grad_other, bf16[4096,1024]{1,0:T(8,128)(2,1)S(1)} %copy-done.2), custom_call_target="tpu_custom_call" | custom-call | flops 3000000000 | bytes 9437184 | tf_op jit(solution)/shard_map/pull/pallas_call | solution.py:673
  37.3 6.0 %collective-permute-done.5.refs_5_ = bf16[3,256,128]{2,1,0:T(8,128)(2,1)S(1)} collective-permute-done((bf16[3,256,128]{2,1,0:T(8,128)(2,1)}, bf16[3,256,128]{2,1,0:T(8,128)(2,1)S(1)}, u32[]{:S(2)}, u32[]{:S(2)}) %collective-permute-start.5) | collective-permute-done | bytes 196640 | tf_op jit(solution)/shard_map/ppermute | solution.py:1057
  43.4 11.9 %attend.1 = (bf16[8,256,128]{2,1,0:T(8,128)(2,1)S(1)}, f32[8,128,256]{2,1,0:T(8,128)S(1)}, f32[8,8,256]{2,1,0:T(8,128)S(1)}, bf16[8,3,256,128]{3,2,1,0:T(8,128)(2,1)S(1)}) custom-call(s32[18]{0:T(128)S(1)} %pad_add_fusion.meta_ref, f32[2]{0:T(128)S(1)} %slice_reduce_fusion.1.far_ref, f32[2,512]{1,0:T(2,128)S(1)} %fusion.1.line_ref, ...), custom_call_target="tpu_custom_call" | custom-call | flops 8000000000 | bytes 4194304 | tf_op jit(solution)/shard_map/attend/pallas_call | solution.py:423
  55.3 25.9 %all_to_all.20.parts_ref = bf16[8,256,128]{2,1,0:T(8,128)(2,1)S(1)} all-to-all(bf16[8,256,128]{2,1,0:T(8,128)(2,1)S(1)} %get-tuple-element.141), channel_id=1, replica_groups=mesh['seq'=4,'blk'=8] {'blk'}, dimensions={0} | all-to-all | bytes 1048576 | tf_op jit(solution)/shard_map/all_to_all | solution.py:1157
  84.2 10.9 %feed.1 = (f32[256,1024]{1,0:T(8,128)S(1)}, f32[256,1024]{1,0:T(8,128)S(1)}, bf16[512,2048]{1,0:T(8,128)(2,1)S(1)}, bf16[512,2048]{1,0:T(8,128)(2,1)S(1)}) custom-call(s32[4]{0:T(128)S(1)} %copy-done.44, bf16[256,1024]{1,0:T(8,128)(2,1)S(1)} %get-tuple-element.145.act_mine, bf16[256,1024]{1,0:T(8,128)(2,1)S(1)} %collective-permute-done.8.act_other, ...), custom_call_target="tpu_custom_call" | custom-call | flops 8000000000 | bytes 20971520 | tf_op jit(solution)/shard_map/feed/pallas_call | solution.py:736
  96.6 4.5 %contract_weigh.1 = (bf16[4,256,512]{2,1,0:T(8,128)(2,1)S(1)}, bf16[4,256,512]{2,1,0:T(8,128)(2,1)}, bf16[8,128,512]{2,1,0:T(8,128)(2,1)S(1)}, bf16[8,128,512]{2,1,0:T(8,128)(2,1)}) custom-call(s32[4]{0:T(128)S(1)} %copy-done.44, bf16[256,1024]{1,0:T(8,128)(2,1)S(1)} %bitcast.50, bf16[256,1024]{1,0:T(8,128)(2,1)S(1)} %collective-permute-done.other.grad_other, ...), custom_call_target="tpu_custom_call" | custom-call | flops 100000000 | bytes 1048576 | tf_op jit(solution)/shard_map/contract_weigh/pallas_call | solution.py:779
  104.2 3.0 turn.1
  108.2 4.4 %all-to-all-start.1 = ((bf16[8,256,128]{2,1,0:T(8,128)(2,1)}), bf16[8,256,128]{2,1,0:T(8,128)(2,1)}, u32[]{:S(2)}, u32[]{:S(2)}) async-start(bf16[8,256,128]{2,1,0:T(8,128)(2,1)} %get-tuple-element.154), calls=%async_computation.1 | async-start | bytes 1048576 | tf_op jit(solution)/shard_map/all_to_all | solution.py:1157
  119.0 5.1 %weigh.1 = (bf16[4,128,1280]{2,1,0:T(8,128)(2,1)S(1)}, bf16[4,128,1280]{2,1,0:T(8,128)(2,1)}, bf16[8,64,1280]{2,1,0:T(8,128)(2,1)S(1)}, bf16[8,64,1280]{2,1,0:T(8,128)(2,1)}) custom-call(s32[4]{0:T(128)S(1)} %copy-done.44, bf16[256,1024]{1,0:T(8,128)(2,1)S(1)} %copy-done.33, bf16[256,1024]{1,0:T(8,128)(2,1)S(1)} %copy-done.39, ...), custom_call_target="tpu_custom_call" | custom-call | flops 100000000 | bytes 1048576 | tf_op jit(solution)/shard_map/weigh/pallas_call | solution.py:813
  127.7 4.0 %collective-permute-done.13.one_got = bf16[4,256,512]{2,1,0:T(8,128)(2,1)} collective-permute-done((bf16[4,256,512]{2,1,0:T(8,128)(2,1)}, bf16[4,256,512]{2,1,0:T(8,128)(2,1)}, u32[]{:S(2)}, u32[]{:S(2)}) %collective-permute-start.13) | collective-permute-done | bytes 1048608 | tf_op jit(solution)/shard_map/ppermute | solution.py:1057
  131.7 3.0 second.3
  139.7 21.5 %attend_back.1 = (bf16[8,3,256,128]{3,2,1,0:T(8,128)(2,1)S(1)}, f32[2,8,512]{2,1,0:T(8,128)S(1)}) custom-call(s32[18]{0:T(128)S(1)} %pad_add_fusion.meta_ref, f32[2]{0:T(128)S(1)} %slice_reduce_fusion.1.far_ref, f32[2,512]{1,0:T(2,128)S(1)} %fusion.1.line_ref, f32[8,128,256]{2,1,0:T(8,128)S(1)} %copy-done.57, f32[8,8,256]{2,1,0:T(8,128)S(1)} %get-tuple-element.144.log_ref, ...), custom_call_target="tpu_custom_call" | custom-call | flops 20000000000 | bytes 8388608 | tf_op jit(solution)/shard_map/attend_back/pallas_call | solution.py:522
  162.3 3.8 %all-to-all-start.2 = ((bf16[8,3,256,128]{3,2,1,0:T(8,128)(2,1)}), bf16[8,3,256,128]{3,2,1,0:T(8,128)(2,1)S(1)}, u32[]{:S(2)}, u32[]{:S(2)}) async-start(bf16[8,3,256,128]{3,2,1,0:T(8,128)(2,1)} %copy-done.11), calls=%async_computation.2 | async-start | bytes 3145728 | tf_op jit(solution)/shard_map/all_to_all | solution.py:1157
  172.1 3.4 %second.4 = (bf16[4,64,1280]{2,1,0:T(8,128)(2,1)S(1)}, bf16[4,64,1280]{2,1,0:T(8,128)(2,1)}, bf16[4,64,1280]{2,1,0:T(8,128)(2,1)S(1)}, bf16[4,64,1280]{2,1,0:T(8,128)(2,1)}) custom-call(s32[4]{0:T(128)S(1)} %copy-done.44, bf16[4,128,1280]{2,1,0:T(8,128)(2,1)S(1)} %copy-done.13, bf16[4,128,1280]{2,1,0:T(8,128)(2,1)} %collective-permute-done.15.one_got, ...), custom_call_target="tpu_custom_call" | custom-call | flops 5242880 | bytes 15728640 | tf_op jit(solution)/shard_map/second/pallas_call | solution.py:959
  177.2 4.0 %collective-permute-done.19.one_got = bf16[4,128,512]{2,1,0:T(8,128)(2,1)S(1)} collective-permute-done((bf16[4,128,512]{2,1,0:T(8,128)(2,1)}, bf16[4,128,512]{2,1,0:T(8,128)(2,1)S(1)}, u32[]{:S(2)}, u32[]{:S(2)}) %collective-permute-start.19) | collective-permute-done | bytes 524320 | tf_op jit(solution)/shard_map/ppermute | solution.py:1057
  181.2 16.5 %collective-permute-done.20.two_got = bf16[4,128,512]{2,1,0:T(8,128)(2,1)S(1)} collective-permute-done((bf16[4,128,512]{2,1,0:T(8,128)(2,1)}, bf16[4,128,512]{2,1,0:T(8,128)(2,1)S(1)}, u32[]{:S(2)}, u32[]{:S(2)}) %collective-permute-start.20) | collective-permute-done | bytes 524320 | tf_op jit(solution)/shard_map/ppermute | solution.py:1057
  200.1 3.4 %copy-done.3 = bf16[4096,1024]{1,0:T(8,128)(2,1)S(1)} copy-done((bf16[4096,1024]{1,0:T(8,128)(2,1)S(1)}, bf16[4096,1024]{1,0:T(8,128)(2,1)}, u32[]{:S(2)}) %copy-start.3) | copy-done | bytes 8388632
  205.1 3.3 %emit.1 = (f32[256,1024]{1,0:T(8,128)S(1)}, bf16[256,1024]{1,0:T(8,128)(2,1)S(1)}) custom-call(s32[4]{0:T(128)S(1)} %copy-done.44, bf16[512,2048]{1,0:T(8,128)(2,1)S(1)} %copy-done.5, bf16[4096,1024]{1,0:T(8,128)(2,1)S(1)} %copy-done.3), custom_call_target="tpu_custom_call" | custom-call | flops 2000000000 | bytes 8388608 | tf_op jit(solution)/shard_map/emit/pallas_call | solution.py:842
  218.1 3.6 %attend_weigh.1 = (bf16[4,128,768]{2,1,0:T(8,128)(2,1)S(1)}, bf16[4,128,768]{2,1,0:T(8,128)(2,1)}, bf16[8,64,768]{2,1,0:T(8,128)(2,1)S(1)}, bf16[8,64,768]{2,1,0:T(8,128)(2,1)}) custom-call(s32[4]{0:T(128)S(1)} %copy-done.44, bf16[256,1024]{1,0:T(8,128)(2,1)S(1)} %copy-done.47, bf16[256,1024]{1,0:T(8,128)(2,1)S(1)} %copy-done.51, ...), custom_call_target="tpu_custom_call" | custom-call | flops 2000000000 | bytes 7340032 | tf_op jit(solution)/shard_map/attend_weigh/pallas_call | solution.py:1039
  230.8 14.6 %collective-permute-done.26.got = bf16[128,1024]{1,0:T(8,128)(2,1)} collective-permute-done((bf16[128,1024]{1,0:T(8,128)(2,1)}, bf16[128,1024]{1,0:T(8,128)(2,1)}, u32[]{:S(2)}, u32[]{:S(2)}) %collective-permute-start.26) | collective-permute-done | bytes 262176 | tf_op jit(solution)/shard_map/ppermute | solution.py:1057
  257.5 2.8 copy-done.6
  260.3 3.4 %close.1 = (f32[256,1024]{1,0:T(8,128)}, f32[2,1024]{1,0:T(2,128)S(1)}) custom-call(bf16[8,3,256,128]{3,2,1,0:T(8,128)(2,1)S(1)} %all-to-all-done.2.parts_ref.owned_ref, bf16[256,1024]{1,0:T(8,128)(2,1)S(1)} %bitcast.54, f32[256,1024]{1,0:T(8,128)S(1)} %copy-done.17, f32[1,1024]{1,0:T(1,128)S(1)} %bitcast.58, bf16[1024,3072]{1,0:T(8,128)(2,1)S(1)} %copy-done.6), custom_call_target="tpu_custom_call" | custom-call | flops 2000000000 | bytes 10485760 | tf_op jit(solution)/shard_map/close/pallas_call | solution.py:910
  263.7 4.4 %collective-permute-done.30.refs_1_ = bf16[128,1024]{1,0:T(8,128)(2,1)S(1)} collective-permute-done((bf16[128,1024]{1,0:T(8,128)(2,1)S(1)}, bf16[128,1024]{1,0:T(8,128)(2,1)S(1)}, u32[]{:S(2)}, u32[]{:S(2)}) %collective-permute-start.30) | collective-permute-done | bytes 262176 | tf_op jit(solution)/shard_map/ppermute | solution.py:1057
  272.3 5.5 %collective-permute-done.33.refs_1_ = bf16[64,2560]{1,0:T(8,128)(2,1)S(1)} collective-permute-done((bf16[64,2560]{1,0:T(8,128)(2,1)S(1)}, bf16[64,2560]{1,0:T(8,128)(2,1)S(1)}, u32[]{:S(2)}, u32[]{:S(2)}) %collective-permute-start.33) | collective-permute-done | bytes 327712 | tf_op jit(solution)/shard_map/ppermute | solution.py:1057
  282.4 5.5 %collective-permute-done.35.got = bf16[64,1536]{1,0:T(8,128)(2,1)S(1)} collective-permute-done((bf16[64,1536]{1,0:T(8,128)(2,1)S(1)}, bf16[64,1536]{1,0:T(8,128)(2,1)S(1)}, u32[]{:S(2)}, u32[]{:S(2)}) %collective-permute-start.35) | collective-permute-done | bytes 196640 | tf_op jit(solution)/shard_map/ppermute | solution.py:1057
  290.0 4.5 %all-to-all-start.3 = ((f32[8,8,128]{2,1,0:T(8,128)}), f32[8,8,128]{2,1,0:T(8,128)S(1)}, u32[]{:S(2)}, u32[]{:S(2)}) async-start(f32[8,8,128]{2,1,0:T(8,128)} %add.210), calls=%async_computation.3 | async-start | bytes 65536 | tf_op jit(solution)/shard_map/all_to_all | solution.py:1157
  297.5 3.7 %all-to-all-done.3 = f32[8,8,128]{2,1,0:T(8,128)S(1)} async-done(((f32[8,8,128]{2,1,0:T(8,128)}), f32[8,8,128]{2,1,0:T(8,128)S(1)}, u32[]{:S(2)}, u32[]{:S(2)}) %all-to-all-start.3) | async-done | bytes 32800 | tf_op jit(solution)/shard_map/all_to_all | solution.py:1157
  (234 shorter events, 95.9 us)
Async XLA Ops:
  0.7 26.8 %collective-permute-start = (bf16[256,1024]{1,0:T(8,128)(2,1)}, bf16[256,1024]{1,0:T(8,128)(2,1)S(1)}, u32[]{:S(2)}, u32[]{:S(2)}) collective-permute-start(bf16[256,1024]{1,0:T(8,128)(2,1)} %bitcast.48), channel_id=1, source_target_pairs={{0,8},{8,0},{16,24},{24,16},{1,9},{9,1},{17,25},{25,17},{2,10},{10... | collective-permute-start | bytes 1572872 | tf_op jit(solution)/shard_map/ppermute | solution.py:1057
  10.7 15.2 %collective-permute-start.2 = (bf16[3,256,128]{2,1,0:T(8,128)(2,1)}, bf16[3,256,128]{2,1,0:T(8,128)(2,1)S(1)}, u32[]{:S(2)}, u32[]{:S(2)}) collective-permute-start(bf16[3,256,128]{2,1,0:T(8,128)(2,1)} %get-tuple-element.135), channel_id=1, source_target_pairs={{0,2},{1,3},{2,0},{3,1},{4,6},{5,7},{6,4},{7,5},{8,10},{9,11},{10,... | collective-permute-start | bytes 589832 | tf_op jit(solution)/shard_map/ppermute | solution.py:1057
  12.3 25.0 %collective-permute-start.3 = (bf16[3,256,128]{2,1,0:T(8,128)(2,1)}, bf16[3,256,128]{2,1,0:T(8,128)(2,1)S(1)}, u32[]{:S(2)}, u32[]{:S(2)}) collective-permute-start(bf16[3,256,128]{2,1,0:T(8,128)(2,1)} %get-tuple-element.136), channel_id=1, source_target_pairs={{0,3},{1,2},{2,1},{3,0},{4,7},{5,6},{6,5},{7,4},{8,11},{9,10},{10,... | collective-permute-start | bytes 589832 | tf_op jit(solution)/shard_map/ppermute | solution.py:1057
  12.3 25.0 %collective-permute-start.4 = (bf16[3,256,128]{2,1,0:T(8,128)(2,1)}, bf16[3,256,128]{2,1,0:T(8,128)(2,1)S(1)}, u32[]{:S(2)}, u32[]{:S(2)}) collective-permute-start(bf16[3,256,128]{2,1,0:T(8,128)(2,1)} %get-tuple-element.137), channel_id=1, source_target_pairs={{0,4},{1,5},{2,6},{3,7},{4,0},{5,1},{6,2},{7,3},{8,12},{9,13},{10,... | collective-permute-start | bytes 589832 | tf_op jit(solution)/shard_map/ppermute | solution.py:1057
  16.7 26.7 %collective-permute-start.5 = (bf16[3,256,128]{2,1,0:T(8,128)(2,1)}, bf16[3,256,128]{2,1,0:T(8,128)(2,1)S(1)}, u32[]{:S(2)}, u32[]{:S(2)}) collective-permute-start(bf16[3,256,128]{2,1,0:T(8,128)(2,1)} %get-tuple-element.138), channel_id=1, source_target_pairs={{0,5},{1,4},{2,7},{3,6},{4,1},{5,0},{6,3},{7,2},{8,13},{9,12},{10,... | collective-permute-start | bytes 589832 | tf_op jit(solution)/shard_map/ppermute | solution.py:1057
  26.0 17.4 %collective-permute-start.6 = (bf16[3,256,128]{2,1,0:T(8,128)(2,1)}, bf16[3,256,128]{2,1,0:T(8,128)(2,1)S(1)}, u32[]{:S(2)}, u32[]{:S(2)}) collective-permute-start(bf16[3,256,128]{2,1,0:T(8,128)(2,1)} %get-tuple-element.139), channel_id=1, source_target_pairs={{0,6},{1,7},{2,4},{3,5},{4,2},{5,3},{6,0},{7,1},{8,14},{9,15},{10,... | collective-permute-start | bytes 589832 | tf_op jit(solution)/shard_map/ppermute | solution.py:1057
  27.5 15.9 %collective-permute-start.7 = (bf16[3,256,128]{2,1,0:T(8,128)(2,1)}, bf16[3,256,128]{2,1,0:T(8,128)(2,1)S(1)}, u32[]{:S(2)}, u32[]{:S(2)}) collective-permute-start(bf16[3,256,128]{2,1,0:T(8,128)(2,1)} %get-tuple-element.140), channel_id=1, source_target_pairs={{0,7},{1,6},{2,5},{3,4},{4,3},{5,2},{6,1},{7,0},{8,15},{9,14},{10,... | collective-permute-start | bytes 589832 | tf_op jit(solution)/shard_map/ppermute | solution.py:1057
  101.1 30.6 %collective-permute-start.13 = (bf16[4,256,512]{2,1,0:T(8,128)(2,1)}, bf16[4,256,512]{2,1,0:T(8,128)(2,1)}, u32[]{:S(2)}, u32[]{:S(2)}) collective-permute-start(bf16[4,256,512]{2,1,0:T(8,128)(2,1)} %get-tuple-element.162), channel_id=1, source_target_pairs={{0,1},{1,0},{2,3},{3,2},{4,5},{5,4},{6,7},{7,6},{8,9},{9,8},{10,11... | collective-permute-start | bytes 3145736 | tf_op jit(solution)/shard_map/ppermute | solution.py:1057
  102.7 29.0 %collective-permute-start.14 = (bf16[8,128,512]{2,1,0:T(8,128)(2,1)}, bf16[8,128,512]{2,1,0:T(8,128)(2,1)}, u32[]{:S(2)}, u32[]{:S(2)}) collective-permute-start(bf16[8,128,512]{2,1,0:T(8,128)(2,1)} %get-tuple-element.164), channel_id=1, source_target_pairs={{0,16},{8,24},{16,0},{24,8},{1,17},{9,25},{17,1},{25,9},{2,18},{10... | collective-permute-start | bytes 3145736 | tf_op jit(solution)/shard_map/ppermute | solution.py:1057
  108.2 28.8 %all-to-all-start.1 = ((bf16[8,256,128]{2,1,0:T(8,128)(2,1)}), bf16[8,256,128]{2,1,0:T(8,128)(2,1)}, u32[]{:S(2)}, u32[]{:S(2)}) async-start(bf16[8,256,128]{2,1,0:T(8,128)(2,1)} %get-tuple-element.154), calls=%async_computation.1 | async-start | bytes 1048576 | tf_op jit(solution)/shard_map/all_to_all | solution.py:1157
  112.6 23.6 %collective-permute-start.12 = (bf16[256,1024]{1,0:T(8,128)(2,1)}, bf16[256,1024]{1,0:T(8,128)(2,1)S(1)}, u32[]{:S(2)}, u32[]{:S(2)}) collective-permute-start(bf16[256,1024]{1,0:T(8,128)(2,1)} %get-tuple-element.160.act_mine), channel_id=1, source_target_pairs={{0,8},{8,0},{16,24},{24,16},{1,9},{9,1},{17,25},{25,17},{2,10},{10... | collective-permute-start | bytes 1572872 | tf_op jit(solution)/shard_map/ppermute | solution.py:1057
  125.2 37.2 %collective-permute-start.15 = (bf16[4,128,1280]{2,1,0:T(8,128)(2,1)}, bf16[4,128,1280]{2,1,0:T(8,128)(2,1)}, u32[]{:S(2)}, u32[]{:S(2)}) collective-permute-start(bf16[4,128,1280]{2,1,0:T(8,128)(2,1)} %get-tuple-element.177), channel_id=1, source_target_pairs={{0,1},{1,0},{2,3},{3,2},{4,5},{5,4},{6,7},{7,6},{8,9},{9,8},{10,11... | collective-permute-start | bytes 3932168 | tf_op jit(solution)/shard_map/ppermute | solution.py:1057
  127.2 35.2 %collective-permute-start.16 = (bf16[8,64,1280]{2,1,0:T(8,128)(2,1)}, bf16[8,64,1280]{2,1,0:T(8,128)(2,1)}, u32[]{:S(2)}, u32[]{:S(2)}) collective-permute-start(bf16[8,64,1280]{2,1,0:T(8,128)(2,1)} %get-tuple-element.179), channel_id=1, source_target_pairs={{0,16},{8,24},{16,0},{24,8},{1,17},{9,25},{17,1},{25,9},{2,18},{10... | collective-permute-start | bytes 3932168 | tf_op jit(solution)/shard_map/ppermute | solution.py:1057
  162.3 51.3 %all-to-all-start.2 = ((bf16[8,3,256,128]{3,2,1,0:T(8,128)(2,1)}), bf16[8,3,256,128]{3,2,1,0:T(8,128)(2,1)S(1)}, u32[]{:S(2)}, u32[]{:S(2)}) async-start(bf16[8,3,256,128]{3,2,1,0:T(8,128)(2,1)} %copy-done.11), calls=%async_computation.2 | async-start | bytes 3145728 | tf_op jit(solution)/shard_map/all_to_all | solution.py:1157
  166.2 15.0 %collective-permute-start.19 = (bf16[4,128,512]{2,1,0:T(8,128)(2,1)}, bf16[4,128,512]{2,1,0:T(8,128)(2,1)S(1)}, u32[]{:S(2)}, u32[]{:S(2)}) collective-permute-start(bf16[4,128,512]{2,1,0:T(8,128)(2,1)} %get-tuple-element.194), channel_id=1, source_target_pairs={{0,16},{8,24},{16,0},{24,8},{1,17},{9,25},{17,1},{25,9},{2,18},{10... | collective-permute-start | bytes 1572872 | tf_op jit(solution)/shard_map/ppermute | solution.py:1057
  167.7 30.0 %collective-permute-start.20 = (bf16[4,128,512]{2,1,0:T(8,128)(2,1)}, bf16[4,128,512]{2,1,0:T(8,128)(2,1)S(1)}, u32[]{:S(2)}, u32[]{:S(2)}) collective-permute-start(bf16[4,128,512]{2,1,0:T(8,128)(2,1)} %get-tuple-element.196), channel_id=1, source_target_pairs={{0,1},{1,0},{2,3},{3,2},{4,5},{5,4},{6,7},{7,6},{8,9},{9,8},{10,11... | collective-permute-start | bytes 1572872 | tf_op jit(solution)/shard_map/ppermute | solution.py:1057
  176.4 32.0 %collective-permute-start.17 = (bf16[4,64,1280]{2,1,0:T(8,128)(2,1)}, bf16[4,64,1280]{2,1,0:T(8,128)(2,1)}, u32[]{:S(2)}, u32[]{:S(2)}) collective-permute-start(bf16[4,64,1280]{2,1,0:T(8,128)(2,1)} %get-tuple-element.188), channel_id=1, source_target_pairs={{0,16},{8,24},{16,0},{24,8},{1,17},{9,25},{17,1},{25,9},{2,18},{10... | collective-permute-start | bytes 1966088 | tf_op jit(solution)/shard_map/ppermute | solution.py:1057
  176.9 33.0 %collective-permute-start.18 = (bf16[4,64,1280]{2,1,0:T(8,128)(2,1)}, bf16[4,64,1280]{2,1,0:T(8,128)(2,1)}, u32[]{:S(2)}, u32[]{:S(2)}) collective-permute-start(bf16[4,64,1280]{2,1,0:T(8,128)(2,1)} %get-tuple-element.190), channel_id=1, source_target_pairs={{0,1},{1,0},{2,3},{3,2},{4,5},{5,4},{6,7},{7,6},{8,9},{9,8},{10,11... | collective-permute-start | bytes 1966088 | tf_op jit(solution)/shard_map/ppermute | solution.py:1057
  200.1 13.5 %collective-permute-start.21 = (bf16[2,128,1024]{2,1,0:T(8,128)(2,1)}, bf16[2,128,1024]{2,1,0:T(8,128)(2,1)}, u32[]{:S(2)}, u32[]{:S(2)}) collective-permute-start(bf16[2,128,1024]{2,1,0:T(8,128)(2,1)} %get-tuple-element.198), channel_id=1, source_target_pairs={{0,2},{1,3},{2,0},{3,1},{4,6},{5,7},{6,4},{7,5},{8,10},{9,11},{10,... | collective-permute-start | bytes 1572872 | tf_op jit(solution)/shard_map/ppermute | solution.py:1057
  222.6 24.9 %collective-permute-start.24 = (bf16[4,128,768]{2,1,0:T(8,128)(2,1)}, bf16[4,128,768]{2,1,0:T(8,128)(2,1)}, u32[]{:S(2)}, u32[]{:S(2)}) collective-permute-start(bf16[4,128,768]{2,1,0:T(8,128)(2,1)} %get-tuple-element.208), channel_id=1, source_target_pairs={{0,1},{1,0},{2,3},{3,2},{4,5},{5,4},{6,7},{7,6},{8,9},{9,8},{10,11... | collective-permute-start | bytes 2359304 | tf_op jit(solution)/shard_map/ppermute | solution.py:1057
  223.9 23.6 %collective-permute-start.25 = (bf16[8,64,768]{2,1,0:T(8,128)(2,1)}, bf16[8,64,768]{2,1,0:T(8,128)(2,1)}, u32[]{:S(2)}, u32[]{:S(2)}) collective-permute-start(bf16[8,64,768]{2,1,0:T(8,128)(2,1)} %get-tuple-element.210), channel_id=1, source_target_pairs={{0,16},{8,24},{16,0},{24,8},{1,17},{9,25},{17,1},{25,9},{2,18},{10... | collective-permute-start | bytes 2359304 | tf_op jit(solution)/shard_map/ppermute | solution.py:1057
  225.4 22.1 %collective-permute-start.27 = (bf16[2,64,2560]{2,1,0:T(8,128)(2,1)}, bf16[2,64,2560]{2,1,0:T(8,128)(2,1)}, u32[]{:S(2)}, u32[]{:S(2)}) collective-permute-start(bf16[2,64,2560]{2,1,0:T(8,128)(2,1)} %get-tuple-element.216), channel_id=1, source_target_pairs={{0,2},{1,3},{2,0},{3,1},{4,6},{5,7},{6,4},{7,5},{8,10},{9,11},{10,... | collective-permute-start | bytes 1966088 | tf_op jit(solution)/shard_map/ppermute | solution.py:1057
  228.1 17.2 %collective-permute-start.26 = (bf16[128,1024]{1,0:T(8,128)(2,1)}, bf16[128,1024]{1,0:T(8,128)(2,1)}, u32[]{:S(2)}, u32[]{:S(2)}) collective-permute-start(bf16[128,1024]{1,0:T(8,128)(2,1)} %get-tuple-element.214), channel_id=1, source_target_pairs={{0,4},{1,5},{2,6},{3,7},{4,0},{5,1},{6,2},{7,3},{8,12},{9,13},{10,... | collective-permute-start | bytes 786440 | tf_op jit(solution)/shard_map/ppermute | solution.py:1057
  250.0 18.2 %collective-permute-start.31 = (bf16[64,2560]{1,0:T(8,128)(2,1)S(1)}, bf16[64,2560]{1,0:T(8,128)(2,1)S(1)}, u32[]{:S(2)}, u32[]{:S(2)}) collective-permute-start(bf16[64,2560]{1,0:T(8,128)(2,1)S(1)} %get-tuple-element.230), channel_id=1, source_target_pairs={{0,4},{1,5},{2,6},{3,7},{4,0},{5,1},{6,2},{7,3},{8,12},{9,13},{10,... | collective-permute-start | bytes 983048 | tf_op jit(solution)/shard_map/ppermute | solution.py:1057
  253.0 15.2 %collective-permute-start.28 = (bf16[4,64,768]{2,1,0:T(8,128)(2,1)S(1)}, bf16[4,64,768]{2,1,0:T(8,128)(2,1)S(1)}, u32[]{:S(2)}, u32[]{:S(2)}) collective-permute-start(bf16[4,64,768]{2,1,0:T(8,128)(2,1)S(1)} %get-tuple-element.222), channel_id=1, source_target_pairs={{0,16},{8,24},{16,0},{24,8},{1,17},{9,25},{17,1},{25,9},{2,18},{10... | collective-permute-start | bytes 1179656 | tf_op jit(solution)/shard_map/ppermute | solution.py:1057
  253.6 14.6 %collective-permute-start.29 = (bf16[4,64,768]{2,1,0:T(8,128)(2,1)S(1)}, bf16[4,64,768]{2,1,0:T(8,128)(2,1)S(1)}, u32[]{:S(2)}, u32[]{:S(2)}) collective-permute-start(bf16[4,64,768]{2,1,0:T(8,128)(2,1)S(1)} %get-tuple-element.224), channel_id=1, source_target_pairs={{0,1},{1,0},{2,3},{3,2},{4,5},{5,4},{6,7},{7,6},{8,9},{9,8},{10,11... | collective-permute-start | bytes 1179656 | tf_op jit(solution)/shard_map/ppermute | solution.py:1057
  254.9 26.4 %collective-permute-start.22 = (bf16[256,1024]{1,0:T(8,128)(2,1)S(1)}, bf16[256,1024]{1,0:T(8,128)(2,1)S(1)}, u32[]{:S(2)}, u32[]{:S(2)}) collective-permute-start(bf16[256,1024]{1,0:T(8,128)(2,1)S(1)} %copy-done.49), channel_id=1, source_target_pairs={{0,8},{8,0},{16,24},{24,16},{1,9},{9,1},{17,25},{25,17},{2,10},{10... | collective-permute-start | bytes 1572872 | tf_op jit(solution)/shard_map/ppermute | solution.py:1057
  256.0 12.2 %collective-permute-start.30 = (bf16[128,1024]{1,0:T(8,128)(2,1)S(1)}, bf16[128,1024]{1,0:T(8,128)(2,1)S(1)}, u32[]{:S(2)}, u32[]{:S(2)}) collective-permute-start(bf16[128,1024]{1,0:T(8,128)(2,1)S(1)} %last.3.refs_0_), channel_id=1, source_target_pairs={{0,16},{8,24},{16,0},{24,8},{1,17},{9,25},{17,1},{25,9},{2,18},{10... | collective-permute-start | bytes 786440 | tf_op jit(solution)/shard_map/ppermute | solution.py:1057
  271.0 23.6 %collective-permute-start.41 = (bf16[128,1024]{1,0:T(8,128)(2,1)S(1)}, bf16[128,1024]{1,0:T(8,128)(2,1)S(1)}, u32[]{:S(2)}, u32[]{:S(2)}) collective-permute-start(bf16[128,1024]{1,0:T(8,128)(2,1)S(1)} %last.3.refs_0_), channel_id=1, source_target_pairs={{0,8},{8,0},{16,24},{24,16},{1,9},{9,1},{17,25},{25,17},{2,10},{10... | collective-permute-start | bytes 786440 | tf_op jit(solution)/shard_map/ppermute | solution.py:1057
  272.2 22.4 %collective-permute-start.42 = (bf16[128,1024]{1,0:T(8,128)(2,1)S(1)}, bf16[128,1024]{1,0:T(8,128)(2,1)}, u32[]{:S(2)}, u32[]{:S(2)}) collective-permute-start(bf16[128,1024]{1,0:T(8,128)(2,1)S(1)} %collective-permute-done.30.refs_1_), channel_id=1, source_target_pairs={{0,8},{8,0},{16,24},{24,16},{1,9},{9,1},{17,25},{25,17},{2,10},{10... | collective-permute-start | bytes 786440 | tf_op jit(solution)/shard_map/ppermute | solution.py:1057
  277.9 11.5 %collective-permute-start.43 = (f32[8,8,128]{2,1,0:T(8,128)S(1)}, f32[8,8,128]{2,1,0:T(8,128)S(1)}, u32[]{:S(2)}, u32[]{:S(2)}) collective-permute-start(f32[8,8,128]{2,1,0:T(8,128)S(1)} %add.209), channel_id=1, source_target_pairs={{0,16},{8,24},{16,0},{24,8},{1,17},{9,25},{17,1},{25,9},{2,18},{10... | collective-permute-start | bytes 98312 | tf_op jit(solution)/shard_map/ppermute | solution.py:1057
  288.0 14.1 %collective-permute-start.36 = (bf16[64,1536]{1,0:T(8,128)(2,1)S(1)}, bf16[64,1536]{1,0:T(8,128)(2,1)S(1)}, u32[]{:S(2)}, u32[]{:S(2)}) collective-permute-start(bf16[64,1536]{1,0:T(8,128)(2,1)S(1)} %last.5.refs_0_), channel_id=1, source_target_pairs={{0,16},{8,24},{16,0},{24,8},{1,17},{9,25},{17,1},{25,9},{2,18},{10... | collective-permute-start | bytes 589832 | tf_op jit(solution)/shard_map/ppermute | solution.py:1057
  (73 other events, 622.6 us)
